TPU v7x, 32 devices: a whole 2x2x4 slice. The times are simulated.
32 devices in a mesh: clip: 4 (over x, core), row: 8 (over z, y).
Axes of the slice: x: 2, y: 2, z: 4, core: 2. Of those that a mesh axis runs over, the one named last changes fastest.
Arguments:
- features: bfloat16 [4, 16, 128, 48, 128], P('clip', None, 'row'), may hold values from -6 to 6
- target: bfloat16 [4, 16, 128, 3, 48], P('clip', None, 'row'), may hold values from -6 to 6
- conv_weight: bfloat16 [3, 3, 3, 128], replicated, may hold values from -0.4375 to 0.4375
- disc_first: bfloat16 [4, 4, 3, 64], replicated, may hold values from -0.875 to 0.875
- disc_second: bfloat16 [4, 4, 64, 128], replicated, may hold values from -0.1875 to 0.1875
- disc_third: bfloat16 [4, 4, 128, 256], replicated, may hold values from -0.125 to 0.125
- disc_fourth: bfloat16 [4, 4, 256, 512], replicated, may hold values from -0.09375 to 0.09375
- disc_head: bfloat16 [4, 4, 512, 1], replicated, may hold values from -0.0625 to 0.0625
Outputs:
- feature_grad: bfloat16 [4, 16, 128, 48, 128], P('clip', None, 'row')
- gan_grad: bfloat16 [4, 16, 128, 3, 48], P('clip', None, 'row')
- weight_grad: float32 [3, 3, 3, 128], replicated
- adaptive: float32 [], replicated
All inputs are finite; a program needn't handle non-finite values.
Results may differ from a plain program's by a relative error of at most 0.015.
Values may be sent and summed in bfloat16 or wider, within the bound.
No kernel may reach another device: no remote copies, remote signals or barrier semaphores. Data moves between devices by JAX's collectives and lax.ppermute only.
A program may use at most 64 MiB of HBM per device.

v0:
```python
import jax
import jax.numpy as jnp
from jax import lax
from jax.sharding import PartitionSpec as P

loss_scale = 64.0
epsilon = 0.0001


def padded_2(cells, sides, width):
    for axis, dim in sides:
        count = lax.axis_size(axis)
        ends = count - 1
        head = lax.slice_in_dim(cells, 0, width, axis=dim)
        tail = lax.slice_in_dim(cells, cells.shape[dim] - width, cells.shape[dim], axis=dim)
        cells = jnp.concatenate(
            [
                lax.ppermute(tail, axis, [(i, (i + 1) % count) for i in range(ends)]),
                cells,
                lax.ppermute(head, axis, [((i + 1) % count, i) for i in range(ends)]),
            ],
            axis=dim,
        )
    return cells


def forward_conv(padded, conv_weight):
    return lax.conv_general_dilated(
        padded,
        conv_weight,
        (1, 1),
        "VALID",
        dimension_numbers=("NHWC", "HWOI", "NHCW"),
        preferred_element_type=jnp.float32,
    )


def weight_terms(padded, grads):
    return lax.conv_general_dilated(
        padded,
        grads,
        (1, 1),
        "VALID",
        dimension_numbers=("CHWN", "IHOW", "HWCN"),
        preferred_element_type=jnp.float32,
    )


def input_grad(grad_rows, conv_weight):
    flipped = conv_weight[::-1, ::-1]
    result = lax.conv_general_dilated(
        grad_rows,
        flipped,
        (1, 1),
        ((0, 0), (1, 1)),
        dimension_numbers=("NHCW", "HWIO", "NHWC"),
        preferred_element_type=jnp.float32,
    )
    return result.astype(jnp.bfloat16)


def down_conv(values, weight, stride, layout_spec):
    return lax.conv_general_dilated(
        values,
        weight,
        (stride, stride),
        ((1, 1), (1, 1)),
        dimension_numbers=layout_spec,
        preferred_element_type=jnp.float32,
    )


def back_conv(cotangent, weight, stride, layout_spec):
    return lax.conv_general_dilated(
        cotangent,
        weight[::-1, ::-1],
        (1, 1),
        ((2, 2), (2, 2)),
        lhs_dilation=(stride, stride),
        dimension_numbers=layout_spec,
        preferred_element_type=jnp.float32,
    )


def silu_slope(values):
    logistic = jax.nn.sigmoid(values)
    return logistic * (1.0 + values * (1.0 - logistic))


def disc_gradient(images, layer_one, layer_two, layer_three, layer_four, layer_head):
    plain = ("NHWC", "HWIO", "NHWC")
    pre_one = down_conv(images, layer_one, 2, ("NHCW", "HWIO", "NHWC"))
    act_one = jax.nn.silu(pre_one).astype(jnp.bfloat16)
    pre_two = down_conv(act_one, layer_two, 2, plain)
    act_two = jax.nn.silu(pre_two).astype(jnp.bfloat16)
    pre_three = down_conv(act_two, layer_three, 2, plain)
    act_three = jax.nn.silu(pre_three).astype(jnp.bfloat16)
    pre_four = down_conv(act_three, layer_four, 1, plain)
    act_four = jax.nn.silu(pre_four).astype(jnp.bfloat16)
    back_spec = ("NHWC", "HWOI", "NHWC")
    cot_head = jnp.full(
        (act_four.shape[0], act_four.shape[1] - 1, act_four.shape[2] - 1, 1),
        -loss_scale,
        jnp.bfloat16,
    )
    cot_four = (back_conv(cot_head, layer_head, 1, back_spec) * silu_slope(pre_four)).astype(
        jnp.bfloat16
    )
    cot_three = (back_conv(cot_four, layer_four, 1, back_spec) * silu_slope(pre_three)).astype(
        jnp.bfloat16
    )
    cot_two = (back_conv(cot_three, layer_three, 2, back_spec) * silu_slope(pre_two)).astype(
        jnp.bfloat16
    )
    cot_one = (back_conv(cot_two, layer_two, 2, back_spec) * silu_slope(pre_one)).astype(
        jnp.bfloat16
    )
    return back_conv(cot_one, layer_one, 2, ("NHWC", "HWOI", "NHCW")).astype(jnp.bfloat16)


def per_device(
    features, target, conv_weight, disc_first, disc_second, disc_third, disc_fourth, disc_head
):
    row_count = lax.axis_size("row")
    clip_count = lax.axis_size("clip")
    pixels = clip_count * features.shape[1] * features.shape[2] * row_count * features.shape[3]
    row_block = padded_2(features, (("row", 2),), 1)
    padded = jnp.pad(row_block[0], ((0, 0), (0, 0), (1, 1), (0, 0)))
    wanted = target[0]
    rebuilt = forward_conv(padded, conv_weight)
    rec_grad = loss_scale * (rebuilt - wanted.astype(jnp.float32))
    rec_part = weight_terms(padded, rec_grad.astype(jnp.bfloat16))
    images = rebuilt.astype(jnp.bfloat16)
    frame_total = images.shape[0]
    group_frames = frame_total // row_count
    grouped = images.reshape((row_count, group_frames) + images.shape[1:])
    framed = disc_gradient(
        lax.all_to_all(grouped, "row", split_axis=0, concat_axis=2, tiled=True)[0],
        disc_first,
        disc_second,
        disc_third,
        disc_fourth,
        disc_head,
    )[None]
    returned = lax.all_to_all(framed, "row", split_axis=2, concat_axis=0, tiled=True)
    gan_grad = returned.reshape((frame_total,) + returned.shape[2:])
    gan_part = weight_terms(padded, gan_grad)
    rec_weight, gan_weight = lax.psum((rec_part, gan_part), ("clip", "row"))
    adaptive = jnp.sqrt(jnp.sum(rec_weight * rec_weight)) / (
        jnp.sqrt(jnp.sum(gan_weight * gan_weight)) + epsilon
    )
    weight_grad = (rec_weight + adaptive * gan_weight) / pixels
    combined = (rec_grad + adaptive * gan_grad.astype(jnp.float32)).astype(jnp.bfloat16)
    grad_rows = padded_2(combined[None], (("row", 2),), 1)[0]
    feature_grad = input_grad(grad_rows, conv_weight)[None]
    image_back = gan_grad[None]
    return (feature_grad, image_back, weight_grad, adaptive)


def solution(mesh):
    return jax.shard_map(
        per_device,
        mesh=mesh,
        in_specs=(
            P("clip", None, "row", None, None),
            P("clip", None, "row", None, None),
            P(),
            P(),
            P(),
            P(),
            P(),
            P(),
        ),
        out_specs=(
            P("clip", None, "row", None, None),
            P("clip", None, "row", None, None),
            P(),
            P(),
        ),
        check_vma=False,
    )
```

profile of v0, /device:TPU:0, one launch (start us, length us, event | category | flops | bytes accessed | tf_op | source)
XLA Modules:
  0.0 201.7 jit_solution(16517008344910199247)
XLA Ops:
  0.7 4.0 %copy.131 = bf16[1,16,16,48,128]{4,1,3,2,0:T(8,128)(2,1)S(1)} copy(bf16[1,16,16,48,128]{4,3,2,1,0:T(8,128)(2,1)} %param.8) | data formatting | bytes 6291456 | tf_op args[0]
  4.7 4.9 %collective-permute-start = (bf16[1,16,1,48,128]{4,1,3,2,0:T(8,128)(2,1)S(1)}, bf16[1,16,1,48,128]{4,1,3,2,0:T(8,128)(2,1)S(1)}, u32[]{:S(2)}, u32[]{:S(2)}) collective-permute-start(bf16[1,16,1,48,128]{4,1,3,2,0:T(8,128)(2,1)S(1)} %get-tuple-element.30), channel_id=1, source_target_pairs={{0,1},{1,2},{2,3},{3,4},{4,5},{5,6},{6,7},{8,9},{9,10},{10,11},{11... | collective-permute-start | bytes 589832 | tf_op jit(solution)/shard_map/ppermute | solution.py:18
  11.5 2.2 %collective-permute-done = bf16[1,16,1,48,128]{4,1,3,2,0:T(8,128)(2,1)S(1)} collective-permute-done((bf16[1,16,1,48,128]{4,1,3,2,0:T(8,128)(2,1)S(1)}, bf16[1,16,1,48,128]{4,1,3,2,0:T(8,128)(2,1)S(1)}, u32[]{:S(2)}, u32[]{:S(2)}) %collective-permute-start) | collective-permute-done | bytes 196640 | tf_op jit(solution)/shard_map/ppermute | solution.py:18
  13.7 4.3 %collective-permute-done.1 = bf16[1,16,1,48,128]{4,1,3,2,0:T(8,128)(2,1)S(1)} collective-permute-done((bf16[1,16,1,48,128]{4,1,3,2,0:T(8,128)(2,1)S(1)}, bf16[1,16,1,48,128]{4,1,3,2,0:T(8,128)(2,1)S(1)}, u32[]{:S(2)}, u32[]{:S(2)}) %collective-permute-start.1) | collective-permute-done | bytes 196640 | tf_op jit(solution)/shard_map/ppermute | solution.py:20
  18.0 37.6 %fusion.69 = (bf16[16,16,3,48]{0,2,3,1:T(4,128)(2,1)S(1)}, f32[16,16,3,48]{0,2,3,1:T(4,128)}) fusion(bf16[3,3,3,128]{3,2,1,0:T(4,128)(2,1)S(1)} %copy-done.14, bf16[1,16,1,48,128]{4,1,3,2,0:T(8,128)(2,1)S(1)} %collective-permute-done.1, bf16[1,16,16,48,128]{4,1,3,2,0:T(8,128)(2,1)S(1)} %copy.131, bf16[1,16,1,48,128]{4,1,3,2,0:T(8,128)(2,1)S(1)} %collective-permute-done), kind=kOutput, calls=%fused_computation.92 | convolution fusion | flops 94408704 | bytes 3767040 | tf_op jit(solution)/shard_map/conv_general_dilated | solution.py:28
  57.1 6.7 %all-to-all-start = ((bf16[8,2,2304]{2,1,0:T(2,128)(2,1)}), bf16[8,2,2304]{2,1,0:T(2,128)(2,1)S(1)}, u32[]{:S(2)}, u32[]{:S(2)}) async-start(bf16[8,2,2304]{2,1,0:T(2,128)(2,1)} %reshape.51), calls=%async_computation | async-start | bytes 147456 | tf_op jit(solution)/shard_map/all_to_all | solution.py:138
  64.5 6.3 %all-to-all-done = bf16[8,2,2304]{2,1,0:T(2,128)(2,1)S(1)} async-done(((bf16[8,2,2304]{2,1,0:T(2,128)(2,1)}), bf16[8,2,2304]{2,1,0:T(2,128)(2,1)S(1)}, u32[]{:S(2)}, u32[]{:S(2)}) %all-to-all-start) | async-done | bytes 73760 | tf_op jit(solution)/shard_map/all_to_all | solution.py:138
  71.3 3.7 %copy.140 = bf16[128,3,16,11]{2,1,3,0:T(4,128)(2,1)S(1)} copy(bf16[128,3,16,11]{0,3,2,1:T(8,128)(2,1)S(1)} %bitcast.92) | data formatting | bytes 270336 | tf_op jit(solution)/shard_map/conv_general_dilated | solution.py:63
  83.3 2.9 %fusion.48 = f32[2,15,5,512]{3,0,2,1:T(2,128)} fusion(bf16[4,4,256,512]{3,2,1,0:T(8,128)(2,1)S(1)} %copy-done.7, f32[2,16,6,256]{3,0,2,1:T(2,128)S(1)} %fusion.45), kind=kOutput, calls=%fused_computation.69 | convolution fusion | flops 547602432 | bytes 4698112 | tf_op jit(solution)/shard_map/conv_general_dilated | solution.py:63
  86.2 6.9 %fusion.23 = bf16[2,16,6,256]{3,0,2,1:T(2,128)(2,1)} fusion(bf16[4,4,256,512]{3,2,1,0:T(8,128)(2,1)} %param.14, f32[2,15,5,512]{3,0,2,1:T(2,128)} %fusion.48, f32[2,16,6,256]{3,0,2,1:T(2,128)} %copy-done.15, bf16[4,4,512,1]{2,1,3,0:T(4,128)(2,1)S(1)} %copy-done.12), kind=kOutput, calls=%fused_computation.35 | convolution fusion | flops 550038528 | bytes 4812800 | tf_op jit(solution)/shard_map/conv_general_dilated | solution.py:74
  93.2 2.8 %fusion.21 = bf16[2,32,12,128]{3,0,2,1:T(2,128)(2,1)S(1)} fusion(bf16[2,16,6,256]{3,0,2,1:T(2,128)(2,1)} %fusion.23, bf16[4,4,128,256]{3,2,1,0:T(8,128)(2,1)S(1)} %copy-done, f32[32,2,12,128]{3,0,2,1:T(8,128)} %slice.30), kind=kOutput, calls=%fused_computation.32 | convolution fusion | flops 178978816 | bytes 1736704 | tf_op jit(solution)/shard_map/conv_general_dilated | solution.py:74
  96.0 5.0 %fusion.20 = bf16[64,2,24,64]{3,1,2,0:T(2,128)(2,1)S(1)} fusion(f32[64,2,24,64]{3,0,2,1:T(8,128)S(1)} %slice.31, bf16[2,32,12,128]{3,0,2,1:T(2,128)(2,1)S(1)} %fusion.21, bf16[4,4,64,128]{3,2,1,0:T(8,128)(2,1)S(1)} %copy-done.9), kind=kOutput, calls=%fused_computation.29 | convolution fusion | flops 190316544 | bytes 1638400 | tf_op jit(solution)/shard_map/conv_general_dilated | solution.py:74
  102.6 4.3 %fusion.13 = bf16[64,2,8,6,64]{4,1,3,2,0:T(2,128)(2,1)S(1)} fusion(bf16[64,2,7,2,64]{4,1,3,2,0:T(2,128)(2,1)S(1)} %slice.32, bf16[64,2,8,4,64]{4,1,3,2,0:T(2,128)(2,1)S(1)} %bitcast.89), kind=kLoop, calls=%fused_computation.19 | loop fusion | flops 2359296 | bytes 1540096 | tf_op jit(solution)/shard_map/conv_general_dilated | solution.py:74
  106.9 10.5 %fusion.17 = bf16[128,16,8,3]{1,3,2,0:T(4,128)(2,1)} fusion(bf16[64,2,8,6,64]{4,1,3,2,0:T(2,128)(2,1)S(1)} %fusion.13, bf16[4,4,3,64]{3,1,2,0:T(4,128)(2,1)S(1)} %copy-done.13), kind=kOutput, calls=%fused_computation.25 | convolution fusion | flops 24969216 | bytes 890880 | tf_op jit(solution)/shard_map/conv_general_dilated | solution.py:74
  117.4 2.3 %copy.150 = bf16[128,16,8,3]{0,2,3,1:T(8,128)(2,1)S(1)} copy(bf16[128,16,8,3]{1,3,2,0:T(4,128)(2,1)} %fusion.17) | data formatting | bytes 196608 | tf_op jit(solution)/shard_map/conv_general_dilated | solution.py:74
  122.5 3.6 %all-to-all-start.1 = ((bf16[8,2,2304]{2,1,0:T(2,128)(2,1)}), bf16[8,2,2304]{2,1,0:T(2,128)(2,1)S(1)}, u32[]{:S(2)}, u32[]{:S(2)}) async-start(bf16[8,2,2304]{2,1,0:T(2,128)(2,1)} %reshape.53), calls=%async_computation.1 | async-start | bytes 147456 | tf_op jit(solution)/shard_map/all_to_all | solution.py:145
  126.2 5.9 %fusion.30 = f32[3,3,3,128]{3,2,1,0:T(4,128)S(1)} fusion(f32[16,16,3,48]{0,2,3,1:T(4,128)S(1)} %copy-done.2, bf16[1,16,16,3,48]{1,3,4,2,0:T(4,128)(2,1)S(1)} %copy.134, bf16[1,16,1,48,128]{4,1,3,2,0:T(8,128)(2,1)} %copy-done.11, bf16[1,16,16,48,128]{4,1,3,2,0:T(8,128)(2,1)} %copy-done.1, bf16[1,16,1,48,128]{4,1,3,2,0:T(8,128)(2,1)} %copy-done.10), kind=kOutput, calls=%fused_computation.44 | convolution fusion | flops 94519296 | bytes 3773952 | tf_op jit(solution)/shard_map/conv_general_dilated | solution.py:39
  134.0 5.9 %fusion.65 = f32[3,3,3,128]{3,2,1,0:T(4,128)S(1)} fusion(bf16[16,16,3,48]{0,2,3,1:T(4,128)(2,1)S(1)} %copy.155, bf16[1,16,1,48,128]{4,1,3,2,0:T(8,128)(2,1)} %copy-done.11, bf16[1,16,16,48,128]{4,1,3,2,0:T(8,128)(2,1)} %copy-done.1, bf16[1,16,1,48,128]{4,1,3,2,0:T(8,128)(2,1)} %copy-done.10), kind=kOutput, calls=%fused_computation.88 | convolution fusion | flops 94371840 | bytes 3626496 | tf_op jit(solution)/shard_map/conv_general_dilated | solution.py:39
  139.9 40.3 %all-reduce = (f32[3,3,3,128]{3,2,1,0:T(4,128)S(1)}, f32[3,3,3,128]{3,2,1,0:T(4,128)S(1)}) all-reduce(f32[3,3,3,128]{3,2,1,0:T(4,128)S(1)} %fusion.30, f32[3,3,3,128]{3,2,1,0:T(4,128)S(1)} %fusion.65), channel_id=1, replica_groups=mesh['clip'=4,'row'=8] {'clip','row'}, use_global_device_ids=true, to_apply=%region_0.1 | all-reduce | flops 6912 | bytes 55296 | tf_op jit(solution)/shard_map/psum | solution.py:148
  182.3 2.1 %fusion.32 = bf16[1,16,16,3,48]{1,3,4,2,0:T(4,128)(2,1)S(1)} fusion(bf16[16,16,3,48]{0,2,3,1:T(4,128)(2,1)S(1)} %copy.155, f32[16,16,3,48]{0,2,3,1:T(4,128)} %get-tuple-element.37, bf16[1,16,16,3,48]{1,3,4,2,0:T(4,128)(2,1)S(1)} %copy.134, f32[]{:T(128)} %div.31), kind=kLoop, calls=%fused_computation.45 | loop fusion | flops 258048 | bytes 368644 | tf_op jit(solution)/shard_map/broadcast_in_dim | solution.py:154
  184.5 4.2 %collective-permute-start.2 = (bf16[1,16,1,3,48]{1,3,4,2,0:T(4,128)(2,1)S(1)}, bf16[1,16,1,3,48]{1,3,4,2,0:T(4,128)(2,1)S(1)}, u32[]{:S(2)}, u32[]{:S(2)}) collective-permute-start(bf16[1,16,1,3,48]{1,3,4,2,0:T(4,128)(2,1)S(1)} %get-tuple-element.32), channel_id=1, source_target_pairs={{0,1},{1,2},{2,3},{3,4},{4,5},{5,6},{6,7},{8,9},{9,10},{10,11},{11... | collective-permute-start | bytes 13832 | tf_op jit(solution)/shard_map/ppermute | solution.py:18
  190.6 4.1 %collective-permute-done.3 = bf16[1,16,1,3,48]{1,3,4,2,0:T(4,128)(2,1)S(1)} collective-permute-done((bf16[1,16,1,3,48]{1,3,4,2,0:T(4,128)(2,1)S(1)}, bf16[1,16,1,3,48]{1,3,4,2,0:T(4,128)(2,1)S(1)}, u32[]{:S(2)}, u32[]{:S(2)}) %collective-permute-start.3) | collective-permute-done | bytes 4640 | tf_op jit(solution)/shard_map/ppermute | solution.py:20
  194.6 3.0 %convert_bitcast_fusion = bf16[1,16,16,48,128]{4,1,3,2,0:T(8,128)(2,1)S(1)} fusion(bf16[3,3,3,128]{3,2,1,0:T(4,128)(2,1)S(1)} %copy-done.14, bf16[1,16,1,3,48]{1,3,4,2,0:T(4,128)(2,1)S(1)} %collective-permute-done.3, bf16[1,16,16,3,48]{1,3,4,2,0:T(4,128)(2,1)S(1)} %fusion.32, bf16[1,16,1,3,48]{1,3,4,2,0:T(4,128)(2,1)S(1)} %collective-permute-done.2), kind=kOutput, calls=%fused_computation.6 | convolution fusion | flops 85576704 | bytes 3235584 | tf_op jit(solution)/shard_map/conv_general_dilated | solution.py:51
  197.7 2.5 %copy.158 = bf16[1,16,16,48,128]{4,3,2,1,0:T(8,128)(2,1)} copy(bf16[1,16,16,48,128]{4,1,3,2,0:T(8,128)(2,1)S(1)} %convert_bitcast_fusion) | data formatting | bytes 6291456
  (73 shorter events, 21.5 us)
Async XLA Ops:
  0.6 80.6 %copy-start = (bf16[4,4,128,256]{3,2,1,0:T(8,128)(2,1)S(1)}, bf16[4,4,128,256]{3,2,1,0:T(8,128)(2,1)}, u32[]{:S(2)}) copy-start(bf16[4,4,128,256]{3,2,1,0:T(8,128)(2,1)} %param.13) | copy-start | bytes 3145732
  0.6 17.4 %copy-start.14 = (bf16[3,3,3,128]{3,2,1,0:T(4,128)(2,1)S(1)}, bf16[3,3,3,128]{3,2,1,0:T(4,128)(2,1)}, u32[]{:S(2)}) copy-start(bf16[3,3,3,128]{3,2,1,0:T(4,128)(2,1)} %param.10) | copy-start | bytes 20740
  4.7 51.0 %copy-start.1 = (bf16[1,16,16,48,128]{4,1,3,2,0:T(8,128)(2,1)}, bf16[1,16,16,48,128]{4,1,3,2,0:T(8,128)(2,1)S(1)}, u32[]{:S(2)}) copy-start(bf16[1,16,16,48,128]{4,1,3,2,0:T(8,128)(2,1)S(1)} %copy.131) | copy-start | bytes 9437188
  4.7 9.0 %collective-permute-start = (bf16[1,16,1,48,128]{4,1,3,2,0:T(8,128)(2,1)S(1)}, bf16[1,16,1,48,128]{4,1,3,2,0:T(8,128)(2,1)S(1)}, u32[]{:S(2)}, u32[]{:S(2)}) collective-permute-start(bf16[1,16,1,48,128]{4,1,3,2,0:T(8,128)(2,1)S(1)} %get-tuple-element.30), channel_id=1, source_target_pairs={{0,1},{1,2},{2,3},{3,4},{4,5},{5,6},{6,7},{8,9},{9,10},{10,11},{11... | collective-permute-start | bytes 589832 | tf_op jit(solution)/shard_map/ppermute | solution.py:18
  9.6 54.2 %copy-start.4 = (bf16[1,16,16,3,48]{4,2,3,1,0:T(8,128)(2,1)S(1)}, bf16[1,16,16,3,48]{4,2,3,1,0:T(8,128)(2,1)}, u32[]{:S(2)}) copy-start(bf16[1,16,16,3,48]{4,2,3,1,0:T(8,128)(2,1)} %param.9) | copy-start | bytes 221188
  9.6 8.4 %collective-permute-start.1 = (bf16[1,16,1,48,128]{4,1,3,2,0:T(8,128)(2,1)S(1)}, bf16[1,16,1,48,128]{4,1,3,2,0:T(8,128)(2,1)S(1)}, u32[]{:S(2)}, u32[]{:S(2)}) collective-permute-start(bf16[1,16,1,48,128]{4,1,3,2,0:T(8,128)(2,1)S(1)} %get-tuple-element.31), channel_id=1, source_target_pairs={{1,0},{2,1},{3,2},{4,3},{5,4},{6,5},{7,6},{9,8},{10,9},{11,10},{12... | collective-permute-start | bytes 589832 | tf_op jit(solution)/shard_map/ppermute | solution.py:20
  13.7 41.9 %copy-start.10 = (bf16[1,16,1,48,128]{4,1,3,2,0:T(8,128)(2,1)}, bf16[1,16,1,48,128]{4,1,3,2,0:T(8,128)(2,1)S(1)}, u32[]{:S(2)}) copy-start(bf16[1,16,1,48,128]{4,1,3,2,0:T(8,128)(2,1)S(1)} %collective-permute-done) | copy-start | bytes 589828
  18.0 37.7 %copy-start.11 = (bf16[1,16,1,48,128]{4,1,3,2,0:T(8,128)(2,1)}, bf16[1,16,1,48,128]{4,1,3,2,0:T(8,128)(2,1)S(1)}, u32[]{:S(2)}) copy-start(bf16[1,16,1,48,128]{4,1,3,2,0:T(8,128)(2,1)S(1)} %collective-permute-done.1) | copy-start | bytes 589828
  57.1 13.6 %all-to-all-start = ((bf16[8,2,2304]{2,1,0:T(2,128)(2,1)}), bf16[8,2,2304]{2,1,0:T(2,128)(2,1)S(1)}, u32[]{:S(2)}, u32[]{:S(2)}) async-start(bf16[8,2,2304]{2,1,0:T(2,128)(2,1)} %reshape.51), calls=%async_computation | async-start | bytes 147456 | tf_op jit(solution)/shard_map/all_to_all | solution.py:138
  63.8 11.2 %copy-start.6 = (pred[16,4]{0,1:T(4,128)(4,1)S(1)}, pred[16,4]{0,1:T(4,128)(4,1)}, u32[]{:S(2)}) copy-start(pred[16,4]{0,1:T(4,128)(4,1)} %constant.38) | copy-start | bytes 196
  63.8 11.2 %copy-start.13 = (bf16[4,4,3,64]{3,1,2,0:T(4,128)(2,1)S(1)}, bf16[4,4,3,64]{3,1,2,0:T(4,128)(2,1)}, u32[]{:S(2)}) copy-start(bf16[4,4,3,64]{3,1,2,0:T(4,128)(2,1)} %param.11) | copy-start | bytes 18436
  76.9 1.0 copy-start.8
  81.1 2.3 %copy-start.7 = (bf16[4,4,256,512]{3,2,1,0:T(8,128)(2,1)S(1)}, bf16[4,4,256,512]{3,2,1,0:T(8,128)(2,1)}, u32[]{:S(2)}) copy-start(bf16[4,4,256,512]{3,2,1,0:T(8,128)(2,1)} %param.14) | copy-start | bytes 12582916
  82.2 0.7 copy-start.15
  83.3 2.9 %copy-start.12 = (bf16[4,4,512,1]{2,1,3,0:T(4,128)(2,1)S(1)}, bf16[4,4,512,1]{2,1,3,0:T(4,128)(2,1)}, u32[]{:S(2)}) copy-start(bf16[4,4,512,1]{2,1,3,0:T(4,128)(2,1)} %param.15) | copy-start | bytes 49156
  93.2 2.8 %copy-start.9 = (bf16[4,4,64,128]{3,2,1,0:T(8,128)(2,1)S(1)}, bf16[4,4,64,128]{3,2,1,0:T(8,128)(2,1)}, u32[]{:S(2)}) copy-start(bf16[4,4,64,128]{3,2,1,0:T(8,128)(2,1)} %param.12) | copy-start | bytes 786436
  106.9 12.9 %copy-start.5 = (pred[16,8]{1,0:T(8,128)(4,1)S(1)}, pred[16,8]{1,0:T(8,128)(4,1)}, u32[]{:S(2)}) copy-start(pred[16,8]{1,0:T(8,128)(4,1)} %constant.37) | copy-start | bytes 388
  117.4 8.7 %copy-start.2 = (f32[16,16,3,48]{0,2,3,1:T(4,128)S(1)}, f32[16,16,3,48]{0,2,3,1:T(4,128)}, u32[]{:S(2)}) copy-start(f32[16,16,3,48]{0,2,3,1:T(4,128)} %get-tuple-element.37) | copy-start | bytes 442372
  122.5 10.5 %all-to-all-start.1 = ((bf16[8,2,2304]{2,1,0:T(2,128)(2,1)}), bf16[8,2,2304]{2,1,0:T(2,128)(2,1)S(1)}, u32[]{:S(2)}, u32[]{:S(2)}) async-start(bf16[8,2,2304]{2,1,0:T(2,128)(2,1)} %reshape.53), calls=%async_computation.1 | async-start | bytes 147456 | tf_op jit(solution)/shard_map/all_to_all | solution.py:145
  133.3 6.6 %copy-start.3 = (bf16[8,1,2,16,3,48]{5,3,4,2,1,0:T(8,128)(2,1)}, bf16[8,1,2,16,3,48]{5,3,4,2,1,0:T(8,128)(2,1)S(1)}, u32[]{:S(2)}) copy-start(bf16[8,1,2,16,3,48]{5,3,4,2,1,0:T(8,128)(2,1)S(1)} %copy.154) | copy-start | bytes 221188
  184.5 6.1 %collective-permute-start.2 = (bf16[1,16,1,3,48]{1,3,4,2,0:T(4,128)(2,1)S(1)}, bf16[1,16,1,3,48]{1,3,4,2,0:T(4,128)(2,1)S(1)}, u32[]{:S(2)}, u32[]{:S(2)}) collective-permute-start(bf16[1,16,1,3,48]{1,3,4,2,0:T(4,128)(2,1)S(1)} %get-tuple-element.32), channel_id=1, source_target_pairs={{0,1},{1,2},{2,3},{3,4},{4,5},{5,6},{6,7},{8,9},{9,10},{10,11},{11... | collective-permute-start | bytes 13832 | tf_op jit(solution)/shard_map/ppermute | solution.py:18
  188.7 6.0 %collective-permute-start.3 = (bf16[1,16,1,3,48]{1,3,4,2,0:T(4,128)(2,1)S(1)}, bf16[1,16,1,3,48]{1,3,4,2,0:T(4,128)(2,1)S(1)}, u32[]{:S(2)}, u32[]{:S(2)}) collective-permute-start(bf16[1,16,1,3,48]{1,3,4,2,0:T(4,128)(2,1)S(1)} %get-tuple-element.33), channel_id=1, source_target_pairs={{1,0},{2,1},{3,2},{4,3},{5,4},{6,5},{7,6},{9,8},{10,9},{11,10},{12... | collective-permute-start | bytes 13832 | tf_op jit(solution)/shard_map/ppermute | solution.py:20
where the time goes:
time: 205 us; the launch traced here: 202 us
  matrix products  84.3 us (41%)
  blocking collectives  40.3 us (20%)
  local copies, waits for them, and re-layouts  24.3 us (12%)
  starting transfers between devices  22.5 us (11%)
  waiting for transfers between devices  17.8 us (9%)
  other arithmetic  8.41 us (4%)
  between operations  4.09 us (2%)
    psum x1, blocking collectives, per_device(): rec_weight, gan_weight = lax.psum((rec_part, gan_part), ('clip', 'row'))  40.3 us
    conv_general_dilated x1, matrix products, forward_conv(): lax.conv_general_dilated(padded, conv_weight, (1, 1), 'VALID', dimension_...  37.6 us
    conv_general_dilated x4, matrix products, back_conv(): lax.conv_general_dilated(cotangent, weight[::-1, ::-1], (1, 1), ((2, 2),...  25.3 us
    conv_general_dilated x2, matrix products, weight_terms(): lax.conv_general_dilated(padded, grads, (1, 1), 'VALID', dimension_number...  11.9 us
    unnamed x40, local copies, waits for them, and re-layouts  11.8 us
    ppermute x2, starting transfers between devices, padded_2(): lax.ppermute(tail, axis, [(i, (i + 1) % count) for i in range(ends)])  9.05 us
    ppermute x2, waiting for transfers between devices, padded_2(): lax.ppermute(head, axis, [((i + 1) % count, i) for i in range(ends)])  8.33 us
    all_to_all x1, starting transfers between devices, per_device(): lax.all_to_all(grouped, 'row', split_axis=0, concat_axis=2, tiled=True)[0]  6.68 us
  transfers between devices with their start and end apart: 6, of which 5 were waited for; matrix products, arithmetic and copies ran while one was open for 4% of the time, Pallas kernels for 0%

commit v1 on v0

v1 whole, which is shorter than its diff:
```python
import functools

import jax
import jax.numpy as jnp
import numpy as np
from jax import lax
from jax.experimental import pallas as pl
from jax.experimental.pallas import tpu as pltpu
from jax.sharding import PartitionSpec as P

loss_scale = 64.0
epsilon = 0.0001
F32 = jnp.float32
BF16 = jnp.bfloat16
LANES = 128
NN = (((1,), (0,)), ((), ()))
NT = (((1,), (1,)), ((), ()))
TN = (((0,), (0,)), ((), ()))


def up_to(value, step):
    return -(-value // step) * step


def mat(left, right, dims=NN):
    return lax.dot_general(left, right, dims, preferred_element_type=F32)


def slot_of(frame, devices, group):
    return (frame % group) * devices + frame // group


def forward_kernel(feat_ref, weight_ref, pay_ref, own_ref, taps_ref, out_ref, *, frames, devices, group, cols, lanes):
    pixels = feat_ref.shape[0] // frames
    pieces = pixels // LANES
    pitch = out_ref.shape[1] // devices
    taps = weight_ref.shape[0]
    weight = weight_ref[...]
    for frame in range(frames):
        product = mat(weight, feat_ref[frame * pixels : (frame + 1) * pixels, :], NT)
        slot = slot_of(frame, devices, group)
        for k in range(pieces):
            taps_ref[k, pl.ds(slot, taps, stride=frames), :] = product[:, k * LANES : (k + 1) * LANES]
    column = lax.broadcasted_iota(jnp.int32, (frames, pixels), 1) % cols
    out_ref[...] = jnp.zeros_like(out_ref)

    def tap(a, b, o):
        rows = pl.ds(((a * 3 + b) * 3 + o) * frames, frames)
        return jnp.concatenate([taps_ref[k, rows, :] for k in range(pieces)], axis=1)

    for o in range(3):
        total = None
        for a in range(3):
            part = tap(a, 1, o)
            part = part + jnp.where(column == 0, 0.0, pltpu.roll(tap(a, 0, o), 1, 1))
            part = part + jnp.where(column == cols - 1, 0.0, pltpu.roll(tap(a, 2, o), pixels - 1, 1))
            part = jnp.concatenate([part, jnp.zeros((frames, lanes - pixels), F32)], axis=1)
            if a < 2:
                part = pltpu.roll(part, (2 - a) * cols, 1)
            total = part if total is None else total + part
        own_ref[o * frames : (o + 1) * frames, :] = total
        for part in range(group):
            rows = total[part * devices : (part + 1) * devices, :]
            for k in range(lanes // LANES):
                out_ref[k, pl.ds(o * group + part, devices, stride=pitch), :] = rows[:, k * LANES : (k + 1) * LANES]
    for k in range(lanes // LANES):
        pay_ref[:, k * LANES : (k + 1) * LANES] = out_ref[k].astype(BF16)


def forward_call(features, weight, frames, devices, group, cols, lanes, pitch):
    pixels = features.shape[0] // frames
    return pl.pallas_call(
        functools.partial(forward_kernel, frames=frames, devices=devices, group=group, cols=cols, lanes=lanes),
        out_shape=(
            jax.ShapeDtypeStruct((devices * pitch, lanes), BF16),
            jax.ShapeDtypeStruct((3 * frames, lanes), F32),
        ),
        in_specs=[pl.BlockSpec(memory_space=pltpu.VMEM)] * 2,
        out_specs=(pl.BlockSpec(memory_space=pltpu.VMEM),) * 2,
        scratch_shapes=[
            pltpu.VMEM((pixels // LANES, weight.shape[0] * frames, LANES), F32),
            pltpu.VMEM((lanes // LANES, devices * pitch, LANES), F32),
        ],
        compiler_params=pltpu.CompilerParams(vmem_limit_bytes=24 * 2**20),
        cost_estimate=pl.CostEstimate(flops=2 * features.size * 27, bytes_accessed=2 * features.size, transcendentals=0),
        name="forward_taps",
    )(features, weight)


def shift_rows(values, step, period):
    size = values.shape[0]
    row = lax.broadcasted_iota(jnp.int32, values.shape, 0) % period
    rolled = pltpu.roll(values, step % size, 0)
    source = row - step
    return jnp.where((source >= 0) & (source < period), rolled, 0.0)


def gate_of(values):
    logistic = 1.0 / (1.0 + jnp.exp(-values))
    return (values * logistic).astype(BF16), logistic * (1.0 + values * (1.0 - logistic))


def disc_kernel(
    pay_ref, gather_ref, scatter_ref, band_hbm, second_hbm, third_hbm, fourth_hbm, head_ref, out_ref,
    zin, band, second, third, fourth, rows_in, act_one, slope_one, cols_two, act_two, slope_two, act_three, cols_four,
    pull_four, pull_three, pull_two, zout, sems, *, devices, group, cols, block_rows, period,
):
    lanes = pay_ref.shape[1]
    pitch = pay_ref.shape[0] // devices
    span = block_rows + 2
    unit = group * period
    wide = 3 * cols
    d1 = (act_one.shape[1]) // (cols // 2 + 2)
    d2, d3, d4 = second.shape[1], third.shape[1], fourth.shape[1]
    x1, x2, x3 = cols // 2, cols // 4, cols // 8
    x4 = x3 - 1
    copies = [
        pltpu.make_async_copy(source, target, sems.at[i])
        for i, (source, target) in enumerate(
            ((band_hbm, band), (second_hbm, second), (third_hbm, third), (fourth_hbm, fourth))
        )
    ]
    for copy in copies:
        copy.start()
    for k in range(lanes // LANES):
        zin[k] = pay_ref[:, k * LANES : (k + 1) * LANES].astype(F32)
    for part in range(group):
        planes = []
        for o in range(3):
            pieces = [zin[k, pl.ds(o * group + part, devices, stride=pitch), :] for k in range(lanes // LANES)]
            planes.append(jnp.concatenate(pieces, axis=1))
        for i in range(span):
            row = jnp.concatenate([plane[:, i * cols : (i + 1) * cols] for plane in planes], axis=1)
            rows_in[pl.ds((i * group + part) * devices, devices), :] = row
    image = mat(gather_ref[...], rows_in[...].astype(BF16)).astype(BF16).astype(F32)
    ext = [image[r * unit : (r + 1) * unit] for r in range(8)]
    ext = [shift_rows(ext[7], 1, period)] + ext + [shift_rows(ext[0], -1, period)]
    ext = [piece.astype(BF16) for piece in ext]
    copies[0].wait()
    left = [jnp.concatenate([ext[a + 2 * p] for p in range(4)], axis=0) for a in range(4)]
    width_one = act_one.shape[1]
    step = 256
    for start in range(0, width_one, step):
        end = min(start + step, width_one)
        pre = mat(left[0], band[0:wide, start:end])
        for a in range(1, 4):
            pre = pre + mat(left[a], band[a * wide : (a + 1) * wide, start:end])
        act, slope = gate_of(pre)
        slope_one[:, start:end] = slope
        act_one[unit : 5 * unit, start:end] = act
        actual = act.astype(F32)
        act_one[0:unit, start:end] = shift_rows(actual[3 * unit :], 1, period).astype(BF16)
        act_one[5 * unit :, start:end] = shift_rows(actual[:unit], -1, period).astype(BF16)
    copies[1].wait()
    for x in range(x2):
        for a in range(4):
            for p in range(2):
                cols_two[(x * 2 + p) * unit : (x * 2 + p + 1) * unit, a * 4 * d1 : (a + 1) * 4 * d1] = act_one[
                    (2 * p + a) * unit : (2 * p + a + 1) * unit, 2 * x * d1 : (2 * x + 4) * d1
                ]
    pre = mat(cols_two[...], second[...])
    act, slope = gate_of(pre)
    slope_two[...] = slope
    act_two[:, 0:d2] = jnp.zeros((4 * unit, d2), BF16)
    act_two[:, (x2 + 1) * d2 :] = jnp.zeros((4 * unit, d2), BF16)
    for x in range(x2):
        block = act[x * 2 * unit : (x + 1) * 2 * unit]
        actual = block.astype(F32)
        at = slice((x + 1) * d2, (x + 2) * d2)
        act_two[unit : 3 * unit, at] = block
        act_two[0:unit, at] = shift_rows(actual[unit:], 1, period).astype(BF16)
        act_two[3 * unit :, at] = shift_rows(actual[:unit], -1, period).astype(BF16)
    copies[2].wait()
    left = jnp.concatenate(
        [
            jnp.concatenate([act_two[a * unit : (a + 1) * unit, 2 * x * d2 : (2 * x + 4) * d2] for a in range(4)], axis=1)
            for x in range(x3)
        ],
        axis=0,
    )
    act, slope_three = gate_of(mat(left, third[...]))
    act_three[:, 0:d3] = jnp.zeros((4 * unit, d3), BF16)
    act_three[:, (x3 + 1) * d3 :] = jnp.zeros((4 * unit, d3), BF16)
    for x in range(x3):
        block = act[x * unit : (x + 1) * unit]
        actual = block.astype(F32)
        at = slice((x + 1) * d3, (x + 2) * d3)
        act_three[unit : 2 * unit, at] = block
        for a in (0, 2, 3):
            act_three[a * unit : (a + 1) * unit, at] = shift_rows(actual, 1 - a, period).astype(BF16)
    for x in range(x4):
        for a in range(4):
            cols_four[x * unit : (x + 1) * unit, a * 4 * d3 : (a + 1) * 4 * d3] = act_three[
                a * unit : (a + 1) * unit, x * d3 : (x + 4) * d3
            ]
    copies[3].wait()
    pre = mat(cols_four[...], fourth[...])
    _, slope = gate_of(pre)
    row = lax.broadcasted_iota(jnp.int32, (unit, d4), 0) % period
    head = head_ref[...].astype(F32) * -loss_scale
    heads = []
    for x in range(x4):
        total = None
        for a in range(4):
            taps = [head[a * 4 + b : a * 4 + b + 1, :] for b in range(4) if 0 <= x - b + 1 < x4 - 1]
            tap = functools.reduce(lambda u, v: u + v, taps)
            inside = (row - a + 1 >= 0) & (row - a + 1 < period - 2) & (row < period - 1)
            term = jnp.where(inside, jnp.broadcast_to(tap, (unit, d4)), 0.0)
            total = term if total is None else total + term
        heads.append(total)
    cot = (jnp.concatenate(heads, axis=0) * slope).astype(BF16)
    pull_four[...] = mat(cot, fourth[...], NT)
    cots = []
    for x in range(x3):
        total = None
        for a in range(4):
            term = None
            for b in range(4):
                source = x - b + 1
                if 0 <= source < x4:
                    piece = pull_four[source * unit : (source + 1) * unit, (a * 4 + b) * d3 : (a * 4 + b + 1) * d3]
                    term = piece if term is None else term + piece
            if a != 1:
                term = shift_rows(term, a - 1, period)
            total = term if total is None else total + term
        cots.append((total * slope_three[x * unit : (x + 1) * unit]).astype(BF16))
    pull_three[...] = mat(jnp.concatenate(cots, axis=0), third[...], NT)
    cots = []
    for x in range(x2):
        terms = []
        for a in range(4):
            term = None
            for b in range(4):
                if (x - b + 1) % 2 == 0 and 0 <= (x - b + 1) // 2 < x3:
                    source = (x - b + 1) // 2
                    piece = pull_three[source * unit : (source + 1) * unit, (a * 4 + b) * d2 : (a * 4 + b + 1) * d2]
                    term = piece if term is None else term + piece
            terms.append(term)
        even = terms[1] + shift_rows(terms[3], 1, period)
        odd = terms[2] + shift_rows(terms[0], -1, period)
        both = jnp.concatenate([even, odd], axis=0)
        cots.append((both * slope_two[x * 2 * unit : (x + 1) * 2 * unit]).astype(BF16))
    pull_two[...] = mat(jnp.concatenate(cots, axis=0), second[...], NT)
    strips = []
    for k in range(x2 + 1):
        terms = {}
        for p in range(2):
            for a in range(4):
                term = None
                if k < x2:
                    term = pull_two[(2 * k + p) * unit : (2 * k + p + 1) * unit, a * 4 * d1 : (a * 4 + 2) * d1]
                if k > 0:
                    other = pull_two[(2 * k - 2 + p) * unit : (2 * k - 1 + p) * unit, (a * 4 + 2) * d1 : (a + 1) * 4 * d1]
                    term = other if term is None else term + other
                terms[p, a] = term
        both = jnp.concatenate(
            [
                terms[0, 1] + shift_rows(terms[1, 3], 1, period),
                terms[0, 2] + terms[1, 0],
                terms[0, 3] + terms[1, 1],
                terms[1, 2] + shift_rows(terms[0, 0], -1, period),
            ],
            axis=0,
        )
        strips.append((both * slope_one[:, 2 * k * d1 : (2 * k + 2) * d1]).astype(BF16))
    cot = jnp.concatenate(strips, axis=1)
    pulls = [mat(cot, band[a * wide : (a + 1) * wide, :], NT) for a in range(4)]
    part = lambda p, a: pulls[a][p * unit : (p + 1) * unit]
    phases = []
    for r in range(8):
        terms = [part(p, a) for p in range(4) for a in range(4) if 2 * p + a - 1 == r]
        if r == 0:
            terms.append(shift_rows(part(3, 3), 1, period))
        if r == 7:
            terms.append(shift_rows(part(0, 0), -1, period))
        phases.append(functools.reduce(lambda u, v: u + v, terms))
    image = jnp.concatenate(phases, axis=0).astype(BF16)
    rows = mat(scatter_ref[...], image)
    zout[...] = jnp.zeros_like(zout)
    for part_at in range(group):
        picked = [rows[(i * group + part_at) * devices : (i * group + part_at + 1) * devices] for i in range(span)]
        for o in range(3):
            plane = [piece[:, o * cols : (o + 1) * cols] for piece in picked]
            plane.append(jnp.zeros((devices, lanes - span * cols), F32))
            plane = jnp.concatenate(plane, axis=1)
            for k in range(lanes // LANES):
                zout[k, pl.ds(o * group + part_at, devices, stride=pitch), :] = plane[:, k * LANES : (k + 1) * LANES]
    for k in range(lanes // LANES):
        out_ref[:, k * LANES : (k + 1) * LANES] = zout[k].astype(BF16)


def row_maps(devices, group, block_rows):
    height = devices * block_rows
    period = height // 8
    span = block_rows + 2
    gather = np.zeros((8 * group * period, span * group * devices), np.float32)
    for device in range(devices):
        for i in range(span):
            y = device * block_rows + i - 1
            if 0 <= y < height:
                for part in range(group):
                    gather[((y % 8) * group + part) * period + y // 8, (i * group + part) * devices + device] = 1.0
    return gather


def band_of(first, cols):
    d1 = first.shape[-1]
    width = (cols // 2 + 2) * d1
    x = np.arange(cols)[:, None]
    out_x = np.arange(width)[None, :] // d1 - 1
    tap = x - 2 * out_x + 1
    inside = (out_x >= 0) & (out_x < cols // 2)
    tiled = jnp.tile(first, (1, 1, 1, cols // 2 + 2))
    band = jnp.zeros((4, 3, cols, width), BF16)
    for b in range(4):
        band = jnp.where(jnp.asarray((tap == b) & inside), tiled[:, b, :, None, :], band)
    return band.reshape(4 * 3 * cols, width)


def disc_call(payload, first, second, third, fourth, head, devices, group, cols, block_rows):
    period = devices * block_rows // 8
    unit = group * period
    d1, d2, d3, d4 = first.shape[-1], second.shape[-1], third.shape[-1], fourth.shape[-1]
    x2, x3 = cols // 4, cols // 8
    x4 = x3 - 1
    gather = row_maps(devices, group, block_rows)
    band = band_of(first, cols)
    args = (
        payload,
        jnp.asarray(gather, BF16),
        jnp.asarray(gather.T, BF16),
        band,
        second.reshape(16 * d1, d2),
        third.reshape(16 * d2, d3),
        fourth.reshape(16 * d3, d4),
        head.reshape(16, d4),
    )
    lanes = payload.shape[1]
    vm = pl.BlockSpec(memory_space=pltpu.VMEM)
    hbm = pl.BlockSpec(memory_space=pl.ANY)
    return pl.pallas_call(
        functools.partial(
            disc_kernel, devices=devices, group=group, cols=cols, block_rows=block_rows, period=period
        ),
        out_shape=jax.ShapeDtypeStruct(payload.shape, BF16),
        in_specs=[vm, vm, vm, hbm, hbm, hbm, hbm, vm],
        out_specs=vm,
        scratch_shapes=[
            pltpu.VMEM((lanes // LANES, payload.shape[0], LANES), F32),
            pltpu.VMEM(band.shape, BF16),
            pltpu.VMEM((16 * d1, d2), BF16),
            pltpu.VMEM((16 * d2, d3), BF16),
            pltpu.VMEM((16 * d3, d4), BF16),
            pltpu.VMEM((gather.shape[1], 3 * cols), F32),
            pltpu.VMEM((6 * unit, band.shape[1]), BF16),
            pltpu.VMEM((4 * unit, band.shape[1]), F32),
            pltpu.VMEM((x2 * 2 * unit, 16 * d1), BF16),
            pltpu.VMEM((4 * unit, (x2 + 2) * d2), BF16),
            pltpu.VMEM((x2 * 2 * unit, d2), F32),
            pltpu.VMEM((4 * unit, (x3 + 2) * d3), BF16),
            pltpu.VMEM((x4 * unit, 16 * d3), BF16),
            pltpu.VMEM((x4 * unit, 16 * d3), F32),
            pltpu.VMEM((x3 * unit, 16 * d2), F32),
            pltpu.VMEM((x2 * 2 * unit, 16 * d1), F32),
            pltpu.VMEM((lanes // LANES, payload.shape[0], LANES), F32),
            pltpu.SemaphoreType.DMA((4,)),
        ],
        compiler_params=pltpu.CompilerParams(vmem_limit_bytes=48 * 2**20),
        cost_estimate=pl.CostEstimate(flops=4 * 10**9, bytes_accessed=8 * 10**6, transcendentals=10**6),
        name="disc_rows",
    )(*args)


def taps_kernel(plane_ref, feat_ref, taps_out, part_ref, taps_ref, zin, *, frames, devices, group, cols, packed):
    lanes = plane_ref.shape[1]
    pixels = feat_ref.shape[0] // frames
    pieces = pixels // LANES
    if packed:
        pitch = plane_ref.shape[0] // devices
        for k in range(lanes // LANES):
            zin[k] = plane_ref[:, k * LANES : (k + 1) * LANES].astype(F32)
        blocks = []
        for o in range(3):
            for part in range(group):
                row = pl.ds(o * group + part, devices, stride=pitch)
                blocks.append(jnp.concatenate([zin[k, row, :] for k in range(lanes // LANES)], axis=1))
        plane = jnp.concatenate(blocks, axis=0)
    else:
        plane = plane_ref[...]
    column = lax.broadcasted_iota(jnp.int32, plane.shape, 1) % cols
    for b in range(3):
        moved = plane
        if b == 0:
            moved = jnp.where(column == cols - 1, 0.0, pltpu.roll(plane, lanes - 1, 1))
        if b == 2:
            moved = jnp.where(column == 0, 0.0, pltpu.roll(plane, 1, 1))
        for a in range(3):
            turned = moved if a == 2 else pltpu.roll(moved, lanes - (2 - a) * cols, 1)
            for k in range(pieces):
                taps_ref[k, pl.ds((a * 3 + b) * 3 * frames, 3 * frames), :] = turned[:, k * LANES : (k + 1) * LANES]
    padded = taps_out.shape[1]
    for k in range(pieces):
        taps_ref[k, pl.ds(27 * frames, (padded - 27) * frames), :] = jnp.zeros(((padded - 27) * frames, LANES), F32)
    total = jnp.zeros(part_ref.shape, F32)
    for frame in range(frames):
        rows = pl.ds(slot_of(frame, devices, group), padded, stride=frames)
        taps = jnp.concatenate([taps_ref[k, rows, :] for k in range(pieces)], axis=1).astype(BF16)
        taps_out[frame] = taps
        total = total + mat(taps, feat_ref[frame * pixels : (frame + 1) * pixels, :])
    part_ref[...] = total


def taps_call(plane, features, frames, devices, group, cols, packed, name):
    pixels = features.shape[0] // frames
    channels = features.shape[1]
    vm = pl.BlockSpec(memory_space=pltpu.VMEM)
    return pl.pallas_call(
        functools.partial(
            taps_kernel, frames=frames, devices=devices, group=group, cols=cols, packed=packed
        ),
        out_shape=(
            jax.ShapeDtypeStruct((frames, 32, pixels), BF16),
            jax.ShapeDtypeStruct((32, channels), F32),
        ),
        in_specs=[vm, vm],
        out_specs=(vm, vm),
        scratch_shapes=[
            pltpu.VMEM((pixels // LANES, 32 * frames, LANES), F32),
            pltpu.VMEM((plane.shape[1] // LANES, plane.shape[0], LANES), F32),
        ],
        compiler_params=pltpu.CompilerParams(vmem_limit_bytes=24 * 2**20),
        cost_estimate=pl.CostEstimate(
            flops=2 * features.size * 27, bytes_accessed=2 * features.size, transcendentals=0
        ),
        name=name,
    )(plane, features)


def final_kernel(rec_ref, gan_ref, sums_ref, weight_ref, out_ref, grad_ref, adapt_ref, both_ref, *, pixels):
    half = weight_ref.shape[0]

    @pl.when(pl.program_id(0) == 0)
    def _():
        total = sums_ref[0].astype(F32)
        for i in range(1, sums_ref.shape[0]):
            total = total + sums_ref[i].astype(F32)
        rec, gan = total[:half], total[half:]
        norm = lambda values: jnp.sqrt(jnp.sum(jnp.sum(values * values, axis=1, keepdims=True), axis=0, keepdims=True))
        adaptive = norm(rec) / (norm(gan) + epsilon)
        grad_ref[...] = (rec + adaptive * gan) / pixels
        adapt_ref[...] = jnp.broadcast_to(adaptive, adapt_ref.shape)
        both_ref[:half] = weight_ref[...]
        both_ref[half:] = (adaptive * weight_ref[...].astype(F32)).astype(BF16)

    step_frames, _, block = rec_ref.shape
    for at in range(step_frames):
        left = jnp.concatenate([rec_ref[at], gan_ref[at]], axis=0)
        out_ref[at * block : (at + 1) * block] = mat(left, both_ref[...], TN).astype(BF16)


def final_call(rec_taps, gan_taps, sums, weight, pixels):
    frames, padded, block = rec_taps.shape
    channels = weight.shape[1]
    step = 2
    whole = lambda shape: pl.BlockSpec(shape, lambda i: (0,) * len(shape))
    return pl.pallas_call(
        functools.partial(final_kernel, pixels=pixels),
        grid=(frames // step,),
        out_shape=(
            jax.ShapeDtypeStruct((frames * block, channels), BF16),
            jax.ShapeDtypeStruct((padded, channels), F32),
            jax.ShapeDtypeStruct((8, LANES), F32),
        ),
        in_specs=[
            pl.BlockSpec((step, padded, block), lambda i: (i, 0, 0)),
            pl.BlockSpec((step, padded, block), lambda i: (i, 0, 0)),
            whole(sums.shape),
            whole(weight.shape),
        ],
        out_specs=(
            pl.BlockSpec((step * block, channels), lambda i: (i, 0)),
            whole((padded, channels)),
            whole((8, LANES)),
        ),
        scratch_shapes=[pltpu.VMEM((2 * padded, channels), BF16)],
        compiler_params=pltpu.CompilerParams(vmem_limit_bytes=24 * 2**20),
        cost_estimate=pl.CostEstimate(
            flops=4 * frames * block * channels * padded, bytes_accessed=4 * frames * block * channels, transcendentals=0
        ),
        name="feature_pull",
    )(rec_taps, gan_taps, sums, weight)


def spread(values, axis):
    count = lax.axis_size(axis)
    copies = jnp.broadcast_to(values[None], (count,) + values.shape)
    return lax.all_to_all(copies, axis, split_axis=0, concat_axis=0, tiled=True)


def per_device(
    features, target, conv_weight, disc_first, disc_second, disc_third, disc_fourth, disc_head
):
    devices = lax.axis_size("row")
    _, frames, block_rows, cols, channels = features.shape
    group = frames // devices
    pixels = lax.axis_size("clip") * devices * frames * block_rows * cols
    lanes = up_to((block_rows + 2) * cols, LANES)
    pitch = up_to(3 * group, 8)
    edge = lax.axis_index("row")
    feats = features.reshape(frames * block_rows * cols, channels)
    weight = jnp.pad(conv_weight.reshape(27, channels), ((0, 5), (0, 0)))
    payload, own = forward_call(feats, weight, frames, devices, group, cols, lanes, pitch)
    trade = lambda values: lax.all_to_all(
        values.reshape(devices, pitch, lanes), "row", split_axis=0, concat_axis=0, tiled=True
    ).reshape(devices * pitch, lanes)
    arrived = trade(payload)
    wanted = target[0].reshape(devices, group, block_rows, 3, cols).transpose(3, 1, 0, 2, 4)
    wanted = wanted.reshape(3 * frames, block_rows * cols)
    upward = jnp.concatenate([own[:, : 2 * cols].astype(BF16), wanted[:, :cols]], axis=1)
    downward = jnp.concatenate(
        [own[:, block_rows * cols : (block_rows + 2) * cols].astype(BF16), wanted[:, -cols:]], axis=1
    )
    below = lax.ppermute(upward, "row", [(i + 1, i) for i in range(devices - 1)]).astype(F32)
    above = lax.ppermute(downward, "row", [(i, i + 1) for i in range(devices - 1)]).astype(F32)
    none = lambda count: jnp.zeros((3 * frames, count), F32)
    rest = lanes - (block_rows + 2) * cols
    added = jnp.concatenate(
        [above[:, : 2 * cols], none((block_rows - 2) * cols), below[:, : 2 * cols], none(rest)], axis=1
    )
    asked = jnp.concatenate([above[:, 2 * cols :], wanted.astype(F32), below[:, 2 * cols :], none(rest)], axis=1)
    lane = jnp.arange(lanes)[None, :]
    first = jnp.where(edge == 0, cols, 0)
    last = jnp.where(edge == devices - 1, (block_rows + 1) * cols, (block_rows + 2) * cols)
    rec_plane = jnp.where((lane >= first) & (lane < last), loss_scale * (own + added - asked), 0.0)
    sent = disc_call(
        arrived, disc_first, disc_second, disc_third, disc_fourth, disc_head, devices, group, cols, block_rows
    )
    returned = trade(sent)
    rec_taps, rec_part = taps_call(rec_plane, feats, frames, devices, group, cols, False, "rec_taps")
    gan_taps, gan_part = taps_call(returned, feats, frames, devices, group, cols, True, "gan_taps")
    partial = jnp.concatenate([rec_part, gan_part], axis=0)
    partial = jnp.sum(spread(partial.astype(BF16), "clip").astype(F32), axis=0)
    sums = spread(partial.astype(BF16), "row")
    image_back = returned.reshape(devices, pitch, lanes)[:, : 3 * group, cols : (block_rows + 1) * cols]
    image_back = image_back.reshape(devices, 3, group, block_rows, cols).transpose(0, 2, 3, 1, 4)
    image_back = image_back.reshape(1, frames, block_rows, 3, cols)
    feature_grad, weight_grad, adaptive = final_call(rec_taps, gan_taps, sums, weight, pixels)
    return (
        feature_grad.reshape(features.shape),
        image_back,
        weight_grad[:27].reshape(3, 3, 3, channels),
        adaptive[0, 0],
    )


def solution(mesh):
    rows = P("clip", None, "row", None, None)
    return jax.shard_map(
        per_device,
        mesh=mesh,
        in_specs=(rows, rows, P(), P(), P(), P(), P(), P()),
        out_specs=(rows, rows, P(), P()),
        check_vma=False,
    )
```

time: 205 us -> 79 us (0.39); the launches traced: 202 us -> 78.3 us
  matrix products: 84.3 us -> 0 us
  blocking collectives: 40.3 us -> 6.81 us
  Pallas kernels: 0 us -> 17.3 us
  local copies, waits for them, and re-layouts: 24.3 us -> 15.2 us
  waiting for transfers between devices: 17.8 us -> 11.5 us
  other arithmetic: 8.41 us -> 5.09 us
  between operations: 4.09 us -> 0.91 us
    conv_general_dilated x12 -> x0, matrix products: 84.3 us -> none  [the longest x1 37.6 us: forward_conv(): lax.conv_general_dilated(padded, conv_weight, (1, 1), 'VALID', dimension_...]
    psum x1 -> x0, blocking collectives: 40.3 us -> none  [per_device(): rec_weight, gan_weight = lax.psum((rec_part, gan_part), ('clip', 'row'))]
    pallas_call x0 -> x5, Pallas kernels: none -> 17.3 us  [the longest x1 8.04 us: disc_call(): pl.pallas_call(functools.partial(disc_kernel, devices=devices, group=grou...]
    ppermute x4 -> x2, waiting for transfers between devices: 10.6 us -> 0.01 us  [the longest x1 0.01 us: per_device(): lax.ppermute(downward, 'row', [(i, i + 1) for i in range(devices - 1)])]
    all_to_all x0 -> x1, blocking collectives: none -> 6.81 us  [spread(): return lax.all_to_all(copies, axis, split_axis=0, concat_axis=0, tiled=True)]
    conv_general_dilated x5 -> x0, local copies, waits for them, and re-layouts: 6.43 us -> none  [the longest x3 3.77 us: down_conv(): lax.conv_general_dilated(values, weight, (stride, stride), ((1, 1), (1, 1...]
    ppermute x4 -> x2, starting transfers between devices: 12.2 us -> 6.15 us  [the longest x1 4.87 us: per_device(): lax.ppermute(downward, 'row', [(i, i + 1) for i in range(devices - 1)])]
    all_to_all x2 -> x3, starting transfers between devices: 10.3 us -> 15.2 us  [the longest x2 11.8 us: per_device(): lax.all_to_all(values.reshape(devices, pitch, lanes), 'row', split_axis=0...]
  transfers between devices with their start and end apart: 6 -> 5, of which waited for: 5 -> 3; matrix products, arithmetic and copies ran while one was open for 4% -> 10% of each run, Pallas kernels for 0% -> 1%
where the time goes in v1:
time: 79 us; the launch traced here: 78.3 us
  starting transfers between devices  21.4 us (27%)
  Pallas kernels  17.3 us (22%)
  local copies, waits for them, and re-layouts  15.2 us (19%)
  waiting for transfers between devices  11.5 us (15%)
  blocking collectives  6.81 us (9%)
  other arithmetic  5.09 us (6%)
  between operations  0.91 us (1%)
    all_to_all x2, starting transfers between devices, per_device(): lax.all_to_all(values.reshape(devices, pitch, lanes), 'row', split_axis=0...  11.8 us
    unnamed x36, local copies, waits for them, and re-layouts  9.24 us
    pallas_call x1, Pallas kernels, disc_call(): pl.pallas_call(functools.partial(disc_kernel, devices=devices, group=grou...  8.04 us
    all_to_all x1, blocking collectives, spread(): return lax.all_to_all(copies, axis, split_axis=0, concat_axis=0, tiled=True)  6.81 us
    all_to_all x1, waiting for transfers between devices, spread(): return lax.all_to_all(copies, axis, split_axis=0, concat_axis=0, tiled=True)  6.25 us
    all_to_all x2, waiting for transfers between devices, per_device(): lax.all_to_all(values.reshape(devices, pitch, lanes), 'row', split_axis=0...  5.27 us
    ppermute x1, starting transfers between devices, per_device(): lax.ppermute(downward, 'row', [(i, i + 1) for i in range(devices - 1)])  4.87 us
    pallas_call x1, Pallas kernels, final_call(): pl.pallas_call(functools.partial(final_kernel, pixels=pixels), grid=(fram...  4.61 us
  transfers between devices with their start and end apart: 5, of which 3 were waited for; matrix products, arithmetic and copies ran while one was open for 10% of the time, Pallas kernels for 1%

profile of v1, /device:TPU:0, one launch (start us, length us, event | category | flops | bytes accessed | tf_op | source)
XLA Modules:
  0.0 78.3 jit_solution(3197202977827657183)
XLA Ops:
  1.4 1.9 %copy-done = bf16[1,16,16,48,128]{4,3,2,1,0:T(8,128)(2,1)S(1)} copy-done((bf16[1,16,16,48,128]{4,3,2,1,0:T(8,128)(2,1)S(1)}, bf16[1,16,16,48,128]{4,3,2,1,0:T(8,128)(2,1)}, u32[]{:S(2)}) %copy-start) | copy-done | bytes 3145752
  3.3 2.4 %forward_taps.1 = (bf16[64,896]{1,0:T(8,128)(2,1)}, f32[48,896]{1,0:T(8,128)S(1)}) custom-call(bf16[12288,128]{1,0:T(8,128)(2,1)S(1)} %bitcast.38, bf16[32,128]{1,0:T(8,128)(2,1)S(1)} %pad.4.weight_ref), custom_call_target="tpu_custom_call" | custom-call | flops 84934656 | bytes 3145728 | tf_op jit(solution)/shard_map/forward_taps/pallas_call | solution.py:72
  6.1 4.9 %collective-permute-start = (bf16[48,144]{1,0:T(8,128)(2,1)S(1)}, bf16[48,144]{1,0:T(8,128)(2,1)S(1)}, u32[]{:S(2)}, u32[]{:S(2)}) collective-permute-start(bf16[48,144]{1,0:T(8,128)(2,1)S(1)} %pad_maximum_fusion), channel_id=1, source_target_pairs={{0,1},{1,2},{2,3},{3,4},{4,5},{5,6},{6,7},{8,9},{9,10},{10,11},{11... | collective-permute-start | bytes 41480 | tf_op jit(solution)/shard_map/ppermute | solution.py:524
  11.1 1.3 %collective-permute-start.1 = (bf16[48,144]{1,0:T(8,128)(2,1)S(1)}, bf16[48,144]{1,0:T(8,128)(2,1)S(1)}, u32[]{:S(2)}, u32[]{:S(2)}) collective-permute-start(bf16[48,144]{1,0:T(8,128)(2,1)S(1)} %pad_maximum_fusion.1), channel_id=1, source_target_pairs={{1,0},{2,1},{3,2},{4,3},{5,4},{6,5},{7,6},{9,8},{10,9},{11,10},{12... | collective-permute-start | bytes 41480 | tf_op jit(solution)/shard_map/ppermute | solution.py:523
  12.4 7.0 %all-to-all-start = ((bf16[8,8,896]{2,1,0:T(8,128)(2,1)}), bf16[8,8,896]{2,1,0:T(8,128)(2,1)S(1)}, u32[]{:S(2)}, u32[]{:S(2)}) async-start(bf16[8,8,896]{2,1,0:T(8,128)(2,1)} %bitcast.3), calls=%async_computation | async-start | bytes 229376 | tf_op jit(solution)/shard_map/all_to_all | solution.py:513
  20.1 2.6 %select_select_fusion = bf16[4,3,48,1664]{3,2,1,0:T(8,128)(2,1)} fusion(pred[48,1664]{1,0:T(8,128)(4,1)S(1)} %copy-done.12, pred[48,1664]{1,0:T(8,128)(4,1)S(1)} %copy-done.13, pred[48,1664]{1,0:T(8,128)(4,1)S(1)} %copy-done.14, pred[48,1664]{1,0:T(8,128)(4,1)S(1)} %copy-done.15, bf16[4,3,1664]{2,1,0:T(4,128)(2,1)S(1)} %get-tuple-element.30, ...), kind=kLoop, calls=%fused_computation | loop fusion | flops 3833856 | bytes 2396160 | tf_op jit(solution)/shard_map/jit(_where)/select_n | solution.py:316
  25.4 1.1 %all-to-all-done = bf16[8,8,896]{2,1,0:T(8,128)(2,1)S(1)} async-done(((bf16[8,8,896]{2,1,0:T(8,128)(2,1)}), bf16[8,8,896]{2,1,0:T(8,128)(2,1)S(1)}, u32[]{:S(2)}, u32[]{:S(2)}) %all-to-all-start) | async-done | bytes 114720 | tf_op jit(solution)/shard_map/all_to_all | solution.py:513
  26.6 1.5 %copy-done.2 = bf16[4,3,48,1664]{3,2,1,0:T(8,128)(2,1)S(1)} copy-done((bf16[4,3,48,1664]{3,2,1,0:T(8,128)(2,1)S(1)}, bf16[4,3,48,1664]{3,2,1,0:T(8,128)(2,1)}, u32[]{:S(2)}) %copy-start.2) | copy-done | bytes 1916952
  28.1 1.2 %copy-done.7 = bf16[4,4,128,256]{3,2,1,0:T(8,128)(2,1)S(1)} copy-done((bf16[4,4,128,256]{3,2,1,0:T(8,128)(2,1)S(1)}, bf16[4,4,128,256]{3,2,1,0:T(8,128)(2,1)}, u32[]{:S(2)}) %copy-start.7) | copy-done | bytes 1048600
  29.3 0.9 %copy-done.8 = bf16[4,4,64,128]{3,2,1,0:T(8,128)(2,1)S(1)} copy-done((bf16[4,4,64,128]{3,2,1,0:T(8,128)(2,1)S(1)}, bf16[4,4,64,128]{3,2,1,0:T(8,128)(2,1)}, u32[]{:S(2)}) %copy-start.8) | copy-done | bytes 262168
  30.3 0.9 %copy-done.9 = bf16[256,288]{1,0:T(8,128)(2,1)S(1)} copy-done((bf16[256,288]{1,0:T(8,128)(2,1)S(1)}, bf16[256,288]{1,0:T(8,128)(2,1)}, u32[]{:S(2)}) %copy-start.9) | copy-done | bytes 147480
  31.2 0.9 %copy-done.10 = bf16[288,256]{1,0:T(8,128)(2,1)S(1)} copy-done((bf16[288,256]{1,0:T(8,128)(2,1)S(1)}, bf16[288,256]{1,0:T(8,128)(2,1)}, u32[]{:S(2)}) %copy-start.10) | copy-done | bytes 147480
  32.1 8.0 %disc_rows.1 = bf16[64,896]{1,0:T(8,128)(2,1)} custom-call(bf16[64,896]{1,0:T(8,128)(2,1)S(1)} %bitcast.43, bf16[256,288]{1,0:T(8,128)(2,1)S(1)} %copy-done.9, bf16[288,256]{1,0:T(8,128)(2,1)S(1)} %copy-done.10, bf16[576,1664]{1,0:T(8,128)(2,1)S(1)} %bitcast.41, bf16[1024,128]{1,0:T(8,128)(2,1)S(1)} %bitcast.46, bf16[2048,256]{1,0:T(8,128)(2,1)S(1)} %bitcast.45, ...), custom_call_target="tpu_custom_call" | custom-call | flops 4000000000 | bytes 8000000 | tf_op jit(solution)/shard_map/disc_rows/pallas_call | solution.py:341
  40.2 4.9 %all-to-all-start.1 = ((bf16[8,8,896]{2,1,0:T(8,128)(2,1)}), bf16[8,8,896]{2,1,0:T(8,128)(2,1)S(1)}, u32[]{:S(2)}, u32[]{:S(2)}) async-start(bf16[8,8,896]{2,1,0:T(8,128)(2,1)} %bitcast.17), calls=%async_computation.1 | async-start | bytes 229376 | tf_op jit(solution)/shard_map/all_to_all | solution.py:513
  45.0 1.1 %fusion.2.plane_ref = f32[48,896]{1,0:T(8,128)S(1)} fusion(f32[48,896]{1,0:T(8,128)S(1)} %get-tuple-element.13, f32[48,96]{1,0:T(8,128)S(1)} %slice.67, f32[48,96]{1,0:T(8,128)S(1)} %slice.64, f32[48,48]{1,0:T(8,128)S(1)} %slice.69, f32[48,768]{1,0:T(8,128)} %convert_element_type.22, f32[48,48]{1,0:T(8,128)S(1)} %slice.68, f32[896]{0:T(1024)} %pad.14.clone, ...), kind=kLoop, calls=%fused_computation.5 | loop fusion | flops 430080 | bytes 554880 | tf_op jit(solution)/shard_map/jit(_where)/select_n | solution.py:534
  46.1 1.1 %rec_taps.1 = (bf16[16,32,768]{2,1,0:T(8,128)(2,1)S(1)}, f32[32,128]{1,0:T(8,128)S(1)}) custom-call(f32[48,896]{1,0:T(8,128)S(1)} %fusion.2.plane_ref, bf16[12288,128]{1,0:T(8,128)(2,1)S(1)} %bitcast.39), custom_call_target="tpu_custom_call" | custom-call | flops 84934656 | bytes 3145728 | tf_op jit(solution)/shard_map/rec_taps/pallas_call | solution.py:417
  47.2 0.9 %copy-done.3 = bf16[16,32,768]{2,1,0:T(8,128)(2,1)} copy-done((bf16[16,32,768]{2,1,0:T(8,128)(2,1)}, bf16[16,32,768]{2,1,0:T(8,128)(2,1)S(1)}, u32[]{:S(2)}) %copy-start.3) | copy-done | bytes 786456
  48.1 4.1 %all-to-all-done.1 = bf16[8,8,896]{2,1,0:T(8,128)(2,1)S(1)} async-done(((bf16[8,8,896]{2,1,0:T(8,128)(2,1)}), bf16[8,8,896]{2,1,0:T(8,128)(2,1)S(1)}, u32[]{:S(2)}, u32[]{:S(2)}) %all-to-all-start.1) | async-done | bytes 114720 | tf_op jit(solution)/shard_map/all_to_all | solution.py:513
  52.3 1.1 %gan_taps.1 = (bf16[16,32,768]{2,1,0:T(8,128)(2,1)S(1)}, f32[32,128]{1,0:T(8,128)S(1)}) custom-call(bf16[64,896]{1,0:T(8,128)(2,1)S(1)} %bitcast.42, bf16[12288,128]{1,0:T(8,128)(2,1)S(1)} %bitcast.40), custom_call_target="tpu_custom_call" | custom-call | flops 84934656 | bytes 3145728 | tf_op jit(solution)/shard_map/gan_taps/pallas_call | solution.py:417
  53.4 0.9 %copy-done.5 = bf16[16,32,768]{2,1,0:T(8,128)(2,1)} copy-done((bf16[16,32,768]{2,1,0:T(8,128)(2,1)}, bf16[16,32,768]{2,1,0:T(8,128)(2,1)S(1)}, u32[]{:S(2)}) %copy-start.5) | copy-done | bytes 786456
  54.4 6.8 %all_to_all.20 = bf16[4,64,128]{2,1,0:T(8,128)(2,1)S(1)} all-to-all(bf16[4,64,128]{2,1,0:T(8,128)(2,1)S(1)} %broadcast_in_dim.91), channel_id=1, replica_groups=mesh['clip'=4,'row'=8] {'clip'}, dimensions={0} | all-to-all | bytes 131072 | tf_op jit(solution)/shard_map/all_to_all | solution.py:497
  61.9 3.4 %all-to-all-start.3 = ((bf16[8,64,128]{2,1,0:T(8,128)(2,1)}), bf16[8,64,128]{2,1,0:T(8,128)(2,1)S(1)}, u32[]{:S(2)}, u32[]{:S(2)}) async-start(bf16[8,64,128]{2,1,0:T(8,128)(2,1)} %broadcast_in_dim.92), calls=%async_computation.3 | async-start | bytes 262144 | tf_op jit(solution)/shard_map/all_to_all | solution.py:497
  66.3 6.2 %all-to-all-done.3.sums_ref = bf16[8,64,128]{2,1,0:T(8,128)(2,1)S(1)} async-done(((bf16[8,64,128]{2,1,0:T(8,128)(2,1)}), bf16[8,64,128]{2,1,0:T(8,128)(2,1)S(1)}, u32[]{:S(2)}, u32[]{:S(2)}) %all-to-all-start.3) | async-done | bytes 131104 | tf_op jit(solution)/shard_map/all_to_all | solution.py:497
  72.5 4.6 %feature_pull.1 = (bf16[12288,128]{1,0:T(8,128)(2,1)}, f32[32,128]{1,0:T(8,128)S(1)}, f32[8,128]{1,0:T(8,128)S(1)}) custom-call(bf16[16,32,768]{2,1,0:T(8,128)(2,1)S(1)} %copy-done.4, bf16[16,32,768]{2,1,0:T(8,128)(2,1)S(1)} %copy-done.6, bf16[8,64,128]{2,1,0:T(8,128)(2,1)S(1)} %all-to-all-done.3.sums_ref, bf16[32,128]{1,0:T(8,128)(2,1)S(1)} %pad.4.weight_ref), custom_call_target="tpu_custom_call" | custom-call | flops 201326592 | bytes 6291456 | tf_op jit(solution)/shard_map/feature_pull/pallas_call | solution.py:466
  (67 shorter events, 7.5 us)
Async XLA Ops:
  1.4 1.9 %copy-start = (bf16[1,16,16,48,128]{4,3,2,1,0:T(8,128)(2,1)S(1)}, bf16[1,16,16,48,128]{4,3,2,1,0:T(8,128)(2,1)}, u32[]{:S(2)}) copy-start(bf16[1,16,16,48,128]{4,3,2,1,0:T(8,128)(2,1)} %param.14) | copy-start | bytes 9437188
  3.3 2.5 %copy-start.11 = (bf16[1,16,16,3,48]{4,2,3,1,0:T(8,128)(2,1)S(1)}, bf16[1,16,16,3,48]{4,2,3,1,0:T(8,128)(2,1)}, u32[]{:S(2)}) copy-start(bf16[1,16,16,3,48]{4,2,3,1,0:T(8,128)(2,1)} %param.15) | copy-start | bytes 221188
  3.3 16.1 %copy-start.17 = (bf16[4,4,3,64]{3,1,2,0:T(4,128)(2,1)S(1)}, bf16[4,4,3,64]{3,1,2,0:T(4,128)(2,1)}, u32[]{:S(2)}) copy-start(bf16[4,4,3,64]{3,1,2,0:T(4,128)(2,1)} %param.17) | copy-start | bytes 18436
  5.7 14.4 %copy-start.12 = (pred[48,1664]{1,0:T(8,128)(4,1)S(1)}, pred[48,1664]{1,0:T(8,128)(4,1)}, u32[]{:S(2)}) copy-start(pred[48,1664]{1,0:T(8,128)(4,1)} %constant.36.clone) | copy-start | bytes 239620
  5.7 14.4 %copy-start.13 = (pred[48,1664]{1,0:T(8,128)(4,1)S(1)}, pred[48,1664]{1,0:T(8,128)(4,1)}, u32[]{:S(2)}) copy-start(pred[48,1664]{1,0:T(8,128)(4,1)} %constant.37.clone) | copy-start | bytes 239620
  5.7 14.4 %copy-start.14 = (pred[48,1664]{1,0:T(8,128)(4,1)S(1)}, pred[48,1664]{1,0:T(8,128)(4,1)}, u32[]{:S(2)}) copy-start(pred[48,1664]{1,0:T(8,128)(4,1)} %constant.38.clone) | copy-start | bytes 239620
  5.7 14.4 %copy-start.15 = (pred[48,1664]{1,0:T(8,128)(4,1)S(1)}, pred[48,1664]{1,0:T(8,128)(4,1)}, u32[]{:S(2)}) copy-start(pred[48,1664]{1,0:T(8,128)(4,1)} %constant.39.clone) | copy-start | bytes 239620
  6.1 19.1 %collective-permute-start = (bf16[48,144]{1,0:T(8,128)(2,1)S(1)}, bf16[48,144]{1,0:T(8,128)(2,1)S(1)}, u32[]{:S(2)}, u32[]{:S(2)}) collective-permute-start(bf16[48,144]{1,0:T(8,128)(2,1)S(1)} %pad_maximum_fusion), channel_id=1, source_target_pairs={{0,1},{1,2},{2,3},{3,4},{4,5},{5,6},{6,7},{8,9},{9,10},{10,11},{11... | collective-permute-start | bytes 41480 | tf_op jit(solution)/shard_map/ppermute | solution.py:524
  11.1 14.3 %collective-permute-start.1 = (bf16[48,144]{1,0:T(8,128)(2,1)S(1)}, bf16[48,144]{1,0:T(8,128)(2,1)S(1)}, u32[]{:S(2)}, u32[]{:S(2)}) collective-permute-start(bf16[48,144]{1,0:T(8,128)(2,1)S(1)} %pad_maximum_fusion.1), channel_id=1, source_target_pairs={{1,0},{2,1},{3,2},{4,3},{5,4},{6,5},{7,6},{9,8},{10,9},{11,10},{12... | collective-permute-start | bytes 41480 | tf_op jit(solution)/shard_map/ppermute | solution.py:523
  12.4 14.2 %all-to-all-start = ((bf16[8,8,896]{2,1,0:T(8,128)(2,1)}), bf16[8,8,896]{2,1,0:T(8,128)(2,1)S(1)}, u32[]{:S(2)}, u32[]{:S(2)}) async-start(bf16[8,8,896]{2,1,0:T(8,128)(2,1)} %bitcast.3), calls=%async_computation | async-start | bytes 229376 | tf_op jit(solution)/shard_map/all_to_all | solution.py:513
  19.6 5.6 %copy-start.16 = (bf16[4,4,512,1]{2,1,3,0:T(4,128)(2,1)S(1)}, bf16[4,4,512,1]{2,1,3,0:T(4,128)(2,1)}, u32[]{:S(2)}) copy-start(bf16[4,4,512,1]{2,1,3,0:T(4,128)(2,1)} %param.21) | copy-start | bytes 49156
  26.6 1.5 %copy-start.2 = (bf16[4,3,48,1664]{3,2,1,0:T(8,128)(2,1)S(1)}, bf16[4,3,48,1664]{3,2,1,0:T(8,128)(2,1)}, u32[]{:S(2)}) copy-start(bf16[4,3,48,1664]{3,2,1,0:T(8,128)(2,1)} %select_select_fusion) | copy-start | bytes 5750788
  28.1 1.2 %copy-start.7 = (bf16[4,4,128,256]{3,2,1,0:T(8,128)(2,1)S(1)}, bf16[4,4,128,256]{3,2,1,0:T(8,128)(2,1)}, u32[]{:S(2)}) copy-start(bf16[4,4,128,256]{3,2,1,0:T(8,128)(2,1)} %param.19) | copy-start | bytes 3145732
  29.3 0.9 %copy-start.8 = (bf16[4,4,64,128]{3,2,1,0:T(8,128)(2,1)S(1)}, bf16[4,4,64,128]{3,2,1,0:T(8,128)(2,1)}, u32[]{:S(2)}) copy-start(bf16[4,4,64,128]{3,2,1,0:T(8,128)(2,1)} %param.18) | copy-start | bytes 786436
  30.3 0.9 %copy-start.9 = (bf16[256,288]{1,0:T(8,128)(2,1)S(1)}, bf16[256,288]{1,0:T(8,128)(2,1)}, u32[]{:S(2)}) copy-start(bf16[256,288]{1,0:T(8,128)(2,1)} %constant.40.clone.gather_ref) | copy-start | bytes 442372
  31.2 0.9 %copy-start.10 = (bf16[288,256]{1,0:T(8,128)(2,1)S(1)}, bf16[288,256]{1,0:T(8,128)(2,1)}, u32[]{:S(2)}) copy-start(bf16[288,256]{1,0:T(8,128)(2,1)} %constant.41.clone.scatter_ref) | copy-start | bytes 442372
  32.1 14.0 %copy-start.1 = (bf16[1,16,16,48,128]{4,3,2,1,0:T(8,128)(2,1)S(1)}, bf16[1,16,16,48,128]{4,3,2,1,0:T(8,128)(2,1)}, u32[]{:S(2)}) copy-start(bf16[1,16,16,48,128]{4,3,2,1,0:T(8,128)(2,1)} %param.14) | copy-start | bytes 9437188
  40.2 12.1 %all-to-all-start.1 = ((bf16[8,8,896]{2,1,0:T(8,128)(2,1)}), bf16[8,8,896]{2,1,0:T(8,128)(2,1)S(1)}, u32[]{:S(2)}, u32[]{:S(2)}) async-start(bf16[8,8,896]{2,1,0:T(8,128)(2,1)} %bitcast.17), calls=%async_computation.1 | async-start | bytes 229376 | tf_op jit(solution)/shard_map/all_to_all | solution.py:513
  47.2 0.9 %copy-start.3 = (bf16[16,32,768]{2,1,0:T(8,128)(2,1)}, bf16[16,32,768]{2,1,0:T(8,128)(2,1)S(1)}, u32[]{:S(2)}) copy-start(bf16[16,32,768]{2,1,0:T(8,128)(2,1)S(1)} %get-tuple-element.14.rec_ref) | copy-start | bytes 2359300
  53.4 0.9 %copy-start.5 = (bf16[16,32,768]{2,1,0:T(8,128)(2,1)}, bf16[16,32,768]{2,1,0:T(8,128)(2,1)S(1)}, u32[]{:S(2)}) copy-start(bf16[16,32,768]{2,1,0:T(8,128)(2,1)S(1)} %get-tuple-element.16.gan_ref) | copy-start | bytes 2359300
  54.3 18.2 %copy-start.4 = (bf16[16,32,768]{2,1,0:T(8,128)(2,1)S(1)}, bf16[16,32,768]{2,1,0:T(8,128)(2,1)}, u32[]{:S(2)}) copy-start(bf16[16,32,768]{2,1,0:T(8,128)(2,1)} %copy-done.3) | copy-start | bytes 2359300
  54.3 18.2 %copy-start.6 = (bf16[16,32,768]{2,1,0:T(8,128)(2,1)S(1)}, bf16[16,32,768]{2,1,0:T(8,128)(2,1)}, u32[]{:S(2)}) copy-start(bf16[16,32,768]{2,1,0:T(8,128)(2,1)} %copy-done.5) | copy-start | bytes 2359300
  61.9 10.7 %all-to-all-start.3 = ((bf16[8,64,128]{2,1,0:T(8,128)(2,1)}), bf16[8,64,128]{2,1,0:T(8,128)(2,1)S(1)}, u32[]{:S(2)}, u32[]{:S(2)}) async-start(bf16[8,64,128]{2,1,0:T(8,128)(2,1)} %broadcast_in_dim.92), calls=%async_computation.3 | async-start | bytes 262144 | tf_op jit(solution)/shard_map/all_to_all | solution.py:497

commit v2 on v1

--- a/solution.py
+++ b/solution.py
@@ -16,6 +16,9 @@
 NN = (((1,), (0,)), ((), ()))
 NT = (((1,), (1,)), ((), ()))
 TN = (((0,), (0,)), ((), ()))
+VM = pl.BlockSpec(memory_space=pltpu.VMEM)
+HBM = pl.BlockSpec(memory_space=pl.ANY)
+WHOLE = pltpu.CompilerParams(vmem_limit_bytes=60 * 2**20)
 
 
 def up_to(value, step):
@@ -30,19 +33,37 @@
     return (frame % group) * devices + frame // group
 
 
-def forward_kernel(feat_ref, weight_ref, pay_ref, own_ref, taps_ref, out_ref, *, frames, devices, group, cols, lanes):
+def forward_kernel(
+    feat_hbm, weight_ref, pay_ref, own_ref, flat_ref, feat_ref, weight_scr, taps_ref, out_ref, sems,
+    *, frames, devices, group, cols, lanes,
+):
     pixels = feat_ref.shape[0] // frames
     pieces = pixels // LANES
     pitch = out_ref.shape[1] // devices
-    taps = weight_ref.shape[0]
-    weight = weight_ref[...]
+    taps = flat_ref.shape[0]
+    copies = [
+        pltpu.make_async_copy(
+            feat_hbm.at[pl.ds(frame * pixels, pixels), :], feat_ref.at[pl.ds(frame * pixels, pixels), :], sems.at[frame]
+        )
+        for frame in range(frames)
+    ]
+    for copy in copies:
+        copy.start()
+    weight_scr[...] = jnp.zeros_like(weight_scr)
+    for a in range(3):
+        for b in range(3):
+            at = (a * 3 + b) * 3
+            weight_scr[at : at + 3, :] = weight_ref[a, b].astype(F32)
+    weight = weight_scr[...].astype(BF16)
+    flat_ref[...] = weight
+    out_ref[...] = jnp.zeros_like(out_ref)
     for frame in range(frames):
+        copies[frame].wait()
         product = mat(weight, feat_ref[frame * pixels : (frame + 1) * pixels, :], NT)
         slot = slot_of(frame, devices, group)
         for k in range(pieces):
             taps_ref[k, pl.ds(slot, taps, stride=frames), :] = product[:, k * LANES : (k + 1) * LANES]
     column = lax.broadcasted_iota(jnp.int32, (frames, pixels), 1) % cols
-    out_ref[...] = jnp.zeros_like(out_ref)
 
     def tap(a, b, o):
         rows = pl.ds(((a * 3 + b) * 3 + o) * frames, frames)
@@ -69,22 +90,65 @@
 
 def forward_call(features, weight, frames, devices, group, cols, lanes, pitch):
     pixels = features.shape[0] // frames
+    channels = features.shape[1]
     return pl.pallas_call(
         functools.partial(forward_kernel, frames=frames, devices=devices, group=group, cols=cols, lanes=lanes),
         out_shape=(
             jax.ShapeDtypeStruct((devices * pitch, lanes), BF16),
             jax.ShapeDtypeStruct((3 * frames, lanes), F32),
+            jax.ShapeDtypeStruct((32, channels), BF16),
         ),
-        in_specs=[pl.BlockSpec(memory_space=pltpu.VMEM)] * 2,
-        out_specs=(pl.BlockSpec(memory_space=pltpu.VMEM),) * 2,
+        in_specs=[pl.BlockSpec(memory_space=pl.ANY), VM],
+        out_specs=(VM,) * 3,
         scratch_shapes=[
-            pltpu.VMEM((pixels // LANES, weight.shape[0] * frames, LANES), F32),
+            pltpu.VMEM(features.shape, BF16),
+            pltpu.VMEM((32, channels), F32),
+            pltpu.VMEM((pixels // LANES, 32 * frames, LANES), F32),
             pltpu.VMEM((lanes // LANES, devices * pitch, LANES), F32),
+            pltpu.SemaphoreType.DMA((frames,)),
         ],
-        compiler_params=pltpu.CompilerParams(vmem_limit_bytes=24 * 2**20),
+        compiler_params=WHOLE,
         cost_estimate=pl.CostEstimate(flops=2 * features.size * 27, bytes_accessed=2 * features.size, transcendentals=0),
         name="forward_taps",
     )(features, weight)
+
+
+def edge_kernel(own_ref, target_ref, wanted_ref, up_ref, down_ref, scr, *, frames, devices, group, block_rows, cols):
+    scr[:, 0:cols] = target_ref[...].reshape(scr.shape[0], cols).astype(F32)
+    stride = group * 3 * block_rows
+    for o in range(3):
+        for part in range(group):
+            at = o * frames + part * devices
+            rows = [
+                scr[pl.ds((part * 3 + o) * block_rows + y, devices, stride=stride), :][:, 0:cols]
+                for y in range(block_rows)
+            ]
+            wanted_ref[at : at + devices, :] = jnp.concatenate(rows, axis=1)
+    own = own_ref[...]
+    wanted = wanted_ref[...]
+    up_ref[...] = jnp.concatenate([own[:, 0 : 2 * cols], wanted[:, 0:cols]], axis=1).astype(BF16)
+    down_ref[...] = jnp.concatenate(
+        [own[:, block_rows * cols : (block_rows + 2) * cols], wanted[:, (block_rows - 1) * cols :]], axis=1
+    ).astype(BF16)
+
+
+def edge_call(own, target, frames, devices, group, block_rows, cols):
+    return pl.pallas_call(
+        functools.partial(
+            edge_kernel, frames=frames, devices=devices, group=group, block_rows=block_rows, cols=cols
+        ),
+        out_shape=(
+            jax.ShapeDtypeStruct((3 * frames, block_rows * cols), F32),
+            jax.ShapeDtypeStruct((3 * frames, 3 * cols), BF16),
+            jax.ShapeDtypeStruct((3 * frames, 3 * cols), BF16),
+        ),
+        in_specs=[VM, VM],
+        out_specs=(VM,) * 3,
+        scratch_shapes=[pltpu.VMEM((frames * 3 * block_rows, LANES), F32)],
+        compiler_params=WHOLE,
+        cost_estimate=pl.CostEstimate(flops=10**9, bytes_accessed=10**7, transcendentals=0),
+        name="edge_rows",
+    )(own, target)
 
 
 def shift_rows(values, step, period):
@@ -336,15 +400,13 @@
         head.reshape(16, d4),
     )
     lanes = payload.shape[1]
-    vm = pl.BlockSpec(memory_space=pltpu.VMEM)
-    hbm = pl.BlockSpec(memory_space=pl.ANY)
     return pl.pallas_call(
         functools.partial(
             disc_kernel, devices=devices, group=group, cols=cols, block_rows=block_rows, period=period
         ),
         out_shape=jax.ShapeDtypeStruct(payload.shape, BF16),
-        in_specs=[vm, vm, vm, hbm, hbm, hbm, hbm, vm],
-        out_specs=vm,
+        in_specs=[VM, VM, VM, HBM, HBM, HBM, HBM, VM],
+        out_specs=VM,
         scratch_shapes=[
             pltpu.VMEM((lanes // LANES, payload.shape[0], LANES), F32),
             pltpu.VMEM(band.shape, BF16),
@@ -365,28 +427,14 @@
             pltpu.VMEM((lanes // LANES, payload.shape[0], LANES), F32),
             pltpu.SemaphoreType.DMA((4,)),
         ],
-        compiler_params=pltpu.CompilerParams(vmem_limit_bytes=48 * 2**20),
+        compiler_params=WHOLE,
         cost_estimate=pl.CostEstimate(flops=4 * 10**9, bytes_accessed=8 * 10**6, transcendentals=10**6),
         name="disc_rows",
     )(*args)
 
 
-def taps_kernel(plane_ref, feat_ref, taps_out, part_ref, taps_ref, zin, *, frames, devices, group, cols, packed):
-    lanes = plane_ref.shape[1]
-    pixels = feat_ref.shape[0] // frames
-    pieces = pixels // LANES
-    if packed:
-        pitch = plane_ref.shape[0] // devices
-        for k in range(lanes // LANES):
-            zin[k] = plane_ref[:, k * LANES : (k + 1) * LANES].astype(F32)
-        blocks = []
-        for o in range(3):
-            for part in range(group):
-                row = pl.ds(o * group + part, devices, stride=pitch)
-                blocks.append(jnp.concatenate([zin[k, row, :] for k in range(lanes // LANES)], axis=1))
-        plane = jnp.concatenate(blocks, axis=0)
-    else:
-        plane = plane_ref[...]
+def put_taps(plane, taps_ref, frames, cols, pieces, padded):
+    lanes = plane.shape[1]
     column = lax.broadcasted_iota(jnp.int32, plane.shape, 1) % cols
     for b in range(3):
         moved = plane
@@ -398,159 +446,215 @@
             turned = moved if a == 2 else pltpu.roll(moved, lanes - (2 - a) * cols, 1)
             for k in range(pieces):
                 taps_ref[k, pl.ds((a * 3 + b) * 3 * frames, 3 * frames), :] = turned[:, k * LANES : (k + 1) * LANES]
-    padded = taps_out.shape[1]
     for k in range(pieces):
         taps_ref[k, pl.ds(27 * frames, (padded - 27) * frames), :] = jnp.zeros(((padded - 27) * frames, LANES), F32)
-    total = jnp.zeros(part_ref.shape, F32)
+
+
+def weigh(taps_ref, taps_out, feat_ref, copies, frames, devices, group, pieces, padded):
+    pixels = pieces * LANES
+    total = jnp.zeros((padded, feat_ref.shape[1]), F32)
     for frame in range(frames):
         rows = pl.ds(slot_of(frame, devices, group), padded, stride=frames)
         taps = jnp.concatenate([taps_ref[k, rows, :] for k in range(pieces)], axis=1).astype(BF16)
         taps_out[frame] = taps
+        copies[frame].wait()
         total = total + mat(taps, feat_ref[frame * pixels : (frame + 1) * pixels, :])
-    part_ref[...] = total
-
-
-def taps_call(plane, features, frames, devices, group, cols, packed, name):
-    pixels = features.shape[0] // frames
-    channels = features.shape[1]
-    vm = pl.BlockSpec(memory_space=pltpu.VMEM)
+    return total
+
+
+def fetch(feat_hbm, feat_ref, sems, frames):
+    pixels = feat_ref.shape[0] // frames
+    copies = [
+        pltpu.make_async_copy(
+            feat_hbm.at[pl.ds(frame * pixels, pixels), :], feat_ref.at[pl.ds(frame * pixels, pixels), :], sems.at[frame]
+        )
+        for frame in range(frames)
+    ]
+    for copy in copies:
+        copy.start()
+    return copies
+
+
+def rec_kernel(
+    ends_ref, own_ref, wanted_ref, above_ref, below_ref, feat_hbm, taps_out, part_ref, feat_ref, taps_ref, sems,
+    *, frames, devices, group, cols, block_rows,
+):
+    copies = fetch(feat_hbm, feat_ref, sems, frames)
+    lanes = own_ref.shape[1]
+    pieces = block_rows * cols // LANES
+    none = lambda count: jnp.zeros((3 * frames, count), F32)
+    rest = none(lanes - (block_rows + 2) * cols)
+    above, below = above_ref[...].astype(F32), below_ref[...].astype(F32)
+    added = jnp.concatenate(
+        [above[:, : 2 * cols], none((block_rows - 2) * cols), below[:, : 2 * cols], rest], axis=1
+    )
+    asked = jnp.concatenate([above[:, 2 * cols :], wanted_ref[...], below[:, 2 * cols :], rest], axis=1)
+    lane = lax.broadcasted_iota(jnp.int32, (3 * frames, lanes), 1)
+    plane = loss_scale * (own_ref[...] + added - asked)
+    plane = jnp.where((lane >= ends_ref[0]) & (lane < ends_ref[1]), plane, 0.0)
+    put_taps(plane, taps_ref, frames, cols, pieces, taps_out.shape[1])
+    part_ref[...] = weigh(taps_ref, taps_out, feat_ref, copies, frames, devices, group, pieces, taps_out.shape[1])
+
+
+def gan_kernel(
+    plane_ref, feat_hbm, taps_out, part_ref, feat_ref, taps_ref, zin, sems, *, frames, devices, group, cols, block_rows
+):
+    copies = fetch(feat_hbm, feat_ref, sems, frames)
+    lanes = plane_ref.shape[1]
+    pieces = block_rows * cols // LANES
+    pitch = plane_ref.shape[0] // devices
+    for k in range(lanes // LANES):
+        zin[k] = plane_ref[:, k * LANES : (k + 1) * LANES].astype(F32)
+    blocks = []
+    for o in range(3):
+        for part in range(group):
+            row = pl.ds(o * group + part, devices, stride=pitch)
+            blocks.append(jnp.concatenate([zin[k, row, :] for k in range(lanes // LANES)], axis=1))
+    plane = jnp.concatenate(blocks, axis=0)
+    put_taps(plane, taps_ref, frames, cols, pieces, taps_out.shape[1])
+    total = weigh(taps_ref, taps_out, feat_ref, copies, frames, devices, group, pieces, taps_out.shape[1])
+    total = total.astype(BF16)
+    for i in range(part_ref.shape[0]):
+        part_ref[i] = total
+
+
+def taps_call(kernel, specs, operands, features, part, extra, frames, devices, group, cols, block_rows, name):
     return pl.pallas_call(
-        functools.partial(
-            taps_kernel, frames=frames, devices=devices, group=group, cols=cols, packed=packed
-        ),
-        out_shape=(
-            jax.ShapeDtypeStruct((frames, 32, pixels), BF16),
-            jax.ShapeDtypeStruct((32, channels), F32),
-        ),
-        in_specs=[vm, vm],
-        out_specs=(vm, vm),
+        functools.partial(kernel, frames=frames, devices=devices, group=group, cols=cols, block_rows=block_rows),
+        out_shape=(jax.ShapeDtypeStruct((frames, 32, block_rows * cols), BF16), part),
+        in_specs=specs + [HBM],
+        out_specs=(VM, VM),
         scratch_shapes=[
-            pltpu.VMEM((pixels // LANES, 32 * frames, LANES), F32),
-            pltpu.VMEM((plane.shape[1] // LANES, plane.shape[0], LANES), F32),
+            pltpu.VMEM(features.shape, BF16),
+            pltpu.VMEM((block_rows * cols // LANES, 32 * frames, LANES), F32),
+            *extra,
+            pltpu.SemaphoreType.DMA((frames,)),
         ],
-        compiler_params=pltpu.CompilerParams(vmem_limit_bytes=24 * 2**20),
+        compiler_params=WHOLE,
         cost_estimate=pl.CostEstimate(
             flops=2 * features.size * 27, bytes_accessed=2 * features.size, transcendentals=0
         ),
         name=name,
-    )(plane, features)
-
-
-def final_kernel(rec_ref, gan_ref, sums_ref, weight_ref, out_ref, grad_ref, adapt_ref, both_ref, *, pixels):
-    half = weight_ref.shape[0]
-
-    @pl.when(pl.program_id(0) == 0)
-    def _():
-        total = sums_ref[0].astype(F32)
-        for i in range(1, sums_ref.shape[0]):
-            total = total + sums_ref[i].astype(F32)
-        rec, gan = total[:half], total[half:]
-        norm = lambda values: jnp.sqrt(jnp.sum(jnp.sum(values * values, axis=1, keepdims=True), axis=0, keepdims=True))
-        adaptive = norm(rec) / (norm(gan) + epsilon)
-        grad_ref[...] = (rec + adaptive * gan) / pixels
-        adapt_ref[...] = jnp.broadcast_to(adaptive, adapt_ref.shape)
-        both_ref[:half] = weight_ref[...]
-        both_ref[half:] = (adaptive * weight_ref[...].astype(F32)).astype(BF16)
-
-    step_frames, _, block = rec_ref.shape
-    for at in range(step_frames):
-        left = jnp.concatenate([rec_ref[at], gan_ref[at]], axis=0)
-        out_ref[at * block : (at + 1) * block] = mat(left, both_ref[...], TN).astype(BF16)
-
-
-def final_call(rec_taps, gan_taps, sums, weight, pixels):
+    )(*operands, features)
+
+
+def final_kernel(
+    rec_hbm, gan_hbm, rec_sum, gan_sums, weight_ref, out_hbm, grad_ref, adapt_ref, rec_ref, gan_ref, both_ref, out_ref,
+    in_sems, out_sems, *, pixels, chunk,
+):
+    frames, padded, block = rec_ref.shape
+    loads = []
+    for at in range(0, frames, chunk):
+        part = pl.ds(at, chunk)
+        loads.append(pltpu.make_async_copy(rec_hbm.at[part], rec_ref.at[part], in_sems.at[0, at // chunk]))
+        loads.append(pltpu.make_async_copy(gan_hbm.at[part], gan_ref.at[part], in_sems.at[1, at // chunk]))
+    for copy in loads:
+        copy.start()
+    gan = gan_sums[0].astype(F32)
+    for i in range(1, gan_sums.shape[0]):
+        gan = gan + gan_sums[i].astype(F32)
+    rec = rec_sum[...]
+    norm = lambda values: jnp.sqrt(jnp.sum(jnp.sum(values * values, axis=1, keepdims=True), axis=0, keepdims=True))
+    adaptive = norm(rec) / (norm(gan) + epsilon)
+    grad = (rec + adaptive * gan) / pixels
+    for a in range(3):
+        for b in range(3):
+            at = (a * 3 + b) * 3
+            grad_ref[a, b] = grad[at : at + 3, :]
+    adapt_ref[...] = adaptive
+    weight = weight_ref[...]
+    both_ref[:padded] = weight
+    both_ref[padded:] = (adaptive * weight.astype(F32)).astype(BF16)
+    stores = []
+    for frame in range(frames):
+        if frame % chunk == 0:
+            loads[frame // chunk * 2].wait()
+            loads[frame // chunk * 2 + 1].wait()
+        left = jnp.concatenate([rec_ref[frame], gan_ref[frame]], axis=0)
+        out_ref[frame * block : (frame + 1) * block] = mat(left, both_ref[...], TN).astype(BF16)
+        rows = pl.ds(frame * block, block)
+        stores.append(pltpu.make_async_copy(out_ref.at[rows], out_hbm.at[rows], out_sems.at[frame]))
+        stores[-1].start()
+    for copy in stores:
+        copy.wait()
+
+
+def final_call(rec_taps, gan_taps, rec_sum, gan_sums, weight, pixels):
     frames, padded, block = rec_taps.shape
     channels = weight.shape[1]
-    step = 2
-    whole = lambda shape: pl.BlockSpec(shape, lambda i: (0,) * len(shape))
+    chunk = 4
     return pl.pallas_call(
-        functools.partial(final_kernel, pixels=pixels),
-        grid=(frames // step,),
+        functools.partial(final_kernel, pixels=pixels, chunk=chunk),
         out_shape=(
             jax.ShapeDtypeStruct((frames * block, channels), BF16),
-            jax.ShapeDtypeStruct((padded, channels), F32),
-            jax.ShapeDtypeStruct((8, LANES), F32),
+            jax.ShapeDtypeStruct((3, 3, 3, channels), F32),
+            jax.ShapeDtypeStruct((1, 1), F32),
         ),
-        in_specs=[
-            pl.BlockSpec((step, padded, block), lambda i: (i, 0, 0)),
-            pl.BlockSpec((step, padded, block), lambda i: (i, 0, 0)),
-            whole(sums.shape),
-            whole(weight.shape),
+        in_specs=[HBM, HBM, VM, VM, VM],
+        out_specs=(HBM, VM, VM),
+        scratch_shapes=[
+            pltpu.VMEM(rec_taps.shape, BF16),
+            pltpu.VMEM(gan_taps.shape, BF16),
+            pltpu.VMEM((2 * padded, channels), BF16),
+            pltpu.VMEM((frames * block, channels), BF16),
+            pltpu.SemaphoreType.DMA((2, frames // chunk)),
+            pltpu.SemaphoreType.DMA((frames,)),
         ],
-        out_specs=(
-            pl.BlockSpec((step * block, channels), lambda i: (i, 0)),
-            whole((padded, channels)),
-            whole((8, LANES)),
-        ),
-        scratch_shapes=[pltpu.VMEM((2 * padded, channels), BF16)],
-        compiler_params=pltpu.CompilerParams(vmem_limit_bytes=24 * 2**20),
+        compiler_params=WHOLE,
         cost_estimate=pl.CostEstimate(
             flops=4 * frames * block * channels * padded, bytes_accessed=4 * frames * block * channels, transcendentals=0
         ),
         name="feature_pull",
-    )(rec_taps, gan_taps, sums, weight)
-
-
-def spread(values, axis):
-    count = lax.axis_size(axis)
-    copies = jnp.broadcast_to(values[None], (count,) + values.shape)
-    return lax.all_to_all(copies, axis, split_axis=0, concat_axis=0, tiled=True)
+    )(rec_taps, gan_taps, rec_sum, gan_sums, weight)
 
 
 def per_device(
     features, target, conv_weight, disc_first, disc_second, disc_third, disc_fourth, disc_head
 ):
     devices = lax.axis_size("row")
+    clips = lax.axis_size("clip")
     _, frames, block_rows, cols, channels = features.shape
     group = frames // devices
-    pixels = lax.axis_size("clip") * devices * frames * block_rows * cols
+    pixels = clips * devices * frames * block_rows * cols
     lanes = up_to((block_rows + 2) * cols, LANES)
     pitch = up_to(3 * group, 8)
     edge = lax.axis_index("row")
     feats = features.reshape(frames * block_rows * cols, channels)
-    weight = jnp.pad(conv_weight.reshape(27, channels), ((0, 5), (0, 0)))
-    payload, own = forward_call(feats, weight, frames, devices, group, cols, lanes, pitch)
+    payload, own, weight = forward_call(feats, conv_weight, frames, devices, group, cols, lanes, pitch)
     trade = lambda values: lax.all_to_all(
         values.reshape(devices, pitch, lanes), "row", split_axis=0, concat_axis=0, tiled=True
     ).reshape(devices * pitch, lanes)
     arrived = trade(payload)
-    wanted = target[0].reshape(devices, group, block_rows, 3, cols).transpose(3, 1, 0, 2, 4)
-    wanted = wanted.reshape(3 * frames, block_rows * cols)
-    upward = jnp.concatenate([own[:, : 2 * cols].astype(BF16), wanted[:, :cols]], axis=1)
-    downward = jnp.concatenate(
-        [own[:, block_rows * cols : (block_rows + 2) * cols].astype(BF16), wanted[:, -cols:]], axis=1
-    )
-    below = lax.ppermute(upward, "row", [(i + 1, i) for i in range(devices - 1)]).astype(F32)
-    above = lax.ppermute(downward, "row", [(i, i + 1) for i in range(devices - 1)]).astype(F32)
-    none = lambda count: jnp.zeros((3 * frames, count), F32)
-    rest = lanes - (block_rows + 2) * cols
-    added = jnp.concatenate(
-        [above[:, : 2 * cols], none((block_rows - 2) * cols), below[:, : 2 * cols], none(rest)], axis=1
-    )
-    asked = jnp.concatenate([above[:, 2 * cols :], wanted.astype(F32), below[:, 2 * cols :], none(rest)], axis=1)
-    lane = jnp.arange(lanes)[None, :]
-    first = jnp.where(edge == 0, cols, 0)
-    last = jnp.where(edge == devices - 1, (block_rows + 1) * cols, (block_rows + 2) * cols)
-    rec_plane = jnp.where((lane >= first) & (lane < last), loss_scale * (own + added - asked), 0.0)
+    wanted, upward, downward = edge_call(
+        own, target[0].transpose(0, 2, 1, 3), frames, devices, group, block_rows, cols
+    )
+    below = lax.ppermute(upward, "row", [(i + 1, i) for i in range(devices - 1)])
+    above = lax.ppermute(downward, "row", [(i, i + 1) for i in range(devices - 1)])
+    ends = jnp.stack(
+        [
+            jnp.where(edge == 0, cols, 0),
+            jnp.where(edge == devices - 1, (block_rows + 1) * cols, (block_rows + 2) * cols),
+        ]
+    ).astype(jnp.int32)
+    rec_taps, rec_part = taps_call(
+        rec_kernel, [pl.BlockSpec(memory_space=pltpu.SMEM), VM, VM, VM, VM], (ends, own, wanted, above, below), feats,
+        jax.ShapeDtypeStruct((32, channels), F32), [], frames, devices, group, cols, block_rows, "rec_taps",
+    )
+    rec_sum = lax.psum(rec_part, ("clip", "row"))
     sent = disc_call(
         arrived, disc_first, disc_second, disc_third, disc_fourth, disc_head, devices, group, cols, block_rows
     )
     returned = trade(sent)
-    rec_taps, rec_part = taps_call(rec_plane, feats, frames, devices, group, cols, False, "rec_taps")
-    gan_taps, gan_part = taps_call(returned, feats, frames, devices, group, cols, True, "gan_taps")
-    partial = jnp.concatenate([rec_part, gan_part], axis=0)
-    partial = jnp.sum(spread(partial.astype(BF16), "clip").astype(F32), axis=0)
-    sums = spread(partial.astype(BF16), "row")
+    gan_taps, gan_part = taps_call(
+        gan_kernel, [VM], (returned,), feats, jax.ShapeDtypeStruct((clips * devices, 32, channels), BF16),
+        [pltpu.VMEM((lanes // LANES, devices * pitch, LANES), F32)], frames, devices, group, cols, block_rows, "gan_taps",
+    )
+    gan_sums = lax.all_to_all(gan_part, ("clip", "row"), split_axis=0, concat_axis=0, tiled=True)
     image_back = returned.reshape(devices, pitch, lanes)[:, : 3 * group, cols : (block_rows + 1) * cols]
     image_back = image_back.reshape(devices, 3, group, block_rows, cols).transpose(0, 2, 3, 1, 4)
     image_back = image_back.reshape(1, frames, block_rows, 3, cols)
-    feature_grad, weight_grad, adaptive = final_call(rec_taps, gan_taps, sums, weight, pixels)
-    return (
-        feature_grad.reshape(features.shape),
-        image_back,
-        weight_grad[:27].reshape(3, 3, 3, channels),
-        adaptive[0, 0],
-    )
+    feature_grad, weight_grad, adaptive = final_call(rec_taps, gan_taps, rec_sum, gan_sums, weight, pixels)
+    return (feature_grad.reshape(features.shape), image_back, weight_grad, adaptive[0, 0])
 
 
 def solution(mesh):

time: 79 us -> 120 us (1.52)
  blocking collectives: 6.81 us -> 52.8 us
  Pallas kernels: 17.3 us -> 35.4 us
  local copies, waits for them, and re-layouts: 15.2 us -> 4.27 us
  starting transfers between devices: 21.4 us -> 15.2 us
  waiting for transfers between devices: 11.5 us -> 7.07 us
  other arithmetic: 5.09 us -> 3.24 us
    psum x0 -> x1, blocking collectives: none -> 41.6 us  [per_device(): rec_sum = lax.psum(rec_part, ('clip', 'row'))]
    pallas_call x3 -> x4, Pallas kernels: 6.88 us -> 19.5 us  [the longest x2 12.3 us: taps_call(): pl.pallas_call(functools.partial(kernel, frames=frames, devices=devices,...]
    unnamed x36 -> x22, local copies, waits for them, and re-layouts: 9.24 us -> 1.99 us
    all_to_all x1, waiting for transfers between devices: 6.25 us -> 0.01 us  [per_device(): lax.all_to_all(gan_part, ('clip', 'row'), split_axis=0, concat_axis=0, ti...]
    all_to_all x2 -> x1, starting transfers between devices: 11.8 us -> 7.42 us  [per_device(): lax.all_to_all(values.reshape(devices, pitch, lanes), 'row', split_axis=0...]
    all_to_all x1, blocking collectives: 6.81 us -> 11.2 us  [per_device(): lax.all_to_all(values.reshape(devices, pitch, lanes), 'row', split_axis=0...]
    ppermute x1, waiting for transfers between devices: 0.01 us -> 3.78 us  [per_device(): lax.ppermute(upward, 'row', [(i + 1, i) for i in range(devices - 1)])]
    pallas_call x1, Pallas kernels: 2.4 us -> 6.06 us  [forward_call(): pl.pallas_call(functools.partial(forward_kernel, frames=frames, devices=d...]
  transfers between devices with their start and end apart: 5 -> 4, of which waited for: 3 -> 2; matrix products, arithmetic and copies ran while one was open for 10% -> 5% of each run, Pallas kernels for 1% -> 7%
where the time goes in v2:
time: 120 us; the launch traced here: 119 us
  blocking collectives  52.8 us (44%)
  Pallas kernels  35.4 us (30%)
  starting transfers between devices  15.2 us (13%)
  waiting for transfers between devices  7.07 us (6%)
  local copies, waits for them, and re-layouts  4.27 us (4%)
  other arithmetic  3.24 us (3%)
    psum x1, blocking collectives, per_device(): rec_sum = lax.psum(rec_part, ('clip', 'row'))  41.6 us
    pallas_call x2, Pallas kernels, taps_call(): pl.pallas_call(functools.partial(kernel, frames=frames, devices=devices,...  12.3 us
    all_to_all x1, blocking collectives, per_device(): lax.all_to_all(values.reshape(devices, pitch, lanes), 'row', split_axis=0...  11.2 us
    pallas_call x1, Pallas kernels, disc_call(): pl.pallas_call(functools.partial(disc_kernel, devices=devices, group=grou...  9.83 us
    all_to_all x1, starting transfers between devices, per_device(): lax.all_to_all(values.reshape(devices, pitch, lanes), 'row', split_axis=0...  7.42 us
    pallas_call x1, Pallas kernels, forward_call(): pl.pallas_call(functools.partial(forward_kernel, frames=frames, devices=d...  6.06 us
    pallas_call x1, Pallas kernels, final_call(): pl.pallas_call(functools.partial(final_kernel, pixels=pixels, chunk=chunk...  5.24 us
    ppermute x1, waiting for transfers between devices, per_device(): lax.ppermute(upward, 'row', [(i + 1, i) for i in range(devices - 1)])  3.78 us
  transfers between devices with their start and end apart: 4, of which 2 were waited for; matrix products, arithmetic and copies ran while one was open for 5% of the time, Pallas kernels for 7%

profile of v2, /device:TPU:0, one launch (start us, length us, event | category | flops | bytes accessed | tf_op | source)
XLA Modules:
  0.0 119.0 jit_solution(14621030427078606253)
XLA Ops:
  0.6 6.1 %forward_taps.1 = (bf16[64,896]{1,0:T(8,128)(2,1)}, f32[48,896]{1,0:T(8,128)}, bf16[32,128]{1,0:T(8,128)(2,1)}) custom-call(bf16[12288,128]{1,0:T(8,128)(2,1)} %bitcast.36, bf16[3,3,3,128]{3,2,1,0:T(4,128)(2,1)} %weight_ref.1), custom_call_target="tpu_custom_call" | custom-call | flops 84934656 | bytes 3145728 | tf_op jit(solution)/shard_map/forward_taps/pallas_call | solution.py:94
  6.8 7.4 %all-to-all-start = ((bf16[8,8,896]{2,1,0:T(8,128)(2,1)}), bf16[8,8,896]{2,1,0:T(8,128)(2,1)S(1)}, u32[]{:S(2)}, u32[]{:S(2)}) async-start(bf16[8,8,896]{2,1,0:T(8,128)(2,1)} %bitcast.44), calls=%async_computation | async-start | bytes 229376 | tf_op jit(solution)/shard_map/all_to_all | solution.py:624
  14.3 0.2 tile.10
  14.5 0.2 fusion
  14.9 2.6 %select_select_fusion = bf16[4,3,48,1664]{3,2,1,0:T(8,128)(2,1)} fusion(pred[48,1664]{1,0:T(8,128)(4,1)S(1)} %copy-done.3, pred[48,1664]{1,0:T(8,128)(4,1)S(1)} %copy-done.4, pred[48,1664]{1,0:T(8,128)(4,1)S(1)} %copy-done.5, pred[48,1664]{1,0:T(8,128)(4,1)S(1)} %copy-done.6, bf16[4,3,1664]{2,1,0:T(4,128)(2,1)S(1)} %get-tuple-element.34, ...), kind=kLoop, calls=%fused_computation | loop fusion | flops 3833856 | bytes 2396160 | tf_op jit(solution)/shard_map/jit(_where)/select_n | solution.py:380
  17.5 0.6 reshape.72.head_ref
  18.1 3.3 %all-to-all-done = bf16[8,8,896]{2,1,0:T(8,128)(2,1)S(1)} async-done(((bf16[8,8,896]{2,1,0:T(8,128)(2,1)}), bf16[8,8,896]{2,1,0:T(8,128)(2,1)S(1)}, u32[]{:S(2)}, u32[]{:S(2)}) %all-to-all-start) | async-done | bytes 114720 | tf_op jit(solution)/shard_map/all_to_all | solution.py:624
  21.4 0.6 copy-done.2
  22.1 9.8 %disc_rows.1 = bf16[64,896]{1,0:T(8,128)(2,1)} custom-call(bf16[64,896]{1,0:T(8,128)(2,1)} %bitcast.43, bf16[256,288]{1,0:T(8,128)(2,1)} %constant.32.clone.gather_ref, bf16[288,256]{1,0:T(8,128)(2,1)} %constant.33.clone.scatter_ref, bf16[576,1664]{1,0:T(8,128)(2,1)} %bitcast.39, bf16[1024,128]{1,0:T(8,128)(2,1)} %bitcast.49, bf16[2048,256]{1,0:T(8,128)(2,1)} %bitcast.48, ...), custom_call_target="tpu_custom_call" | custom-call | flops 4000000000 | bytes 8000000 | tf_op jit(solution)/shard_map/disc_rows/pallas_call | solution.py:403
  31.9 11.2 %all_to_all.15 = bf16[8,8,896]{2,1,0:T(8,128)(2,1)} all-to-all(bf16[8,8,896]{2,1,0:T(8,128)(2,1)} %bitcast.45), channel_id=1, replica_groups=mesh['clip'=4,'row'=8] {'row'}, dimensions={0} | all-to-all | bytes 229376 | tf_op jit(solution)/shard_map/all_to_all | solution.py:624
  43.1 6.1 %gan_taps.1 = (bf16[16,32,768]{2,1,0:T(8,128)(2,1)}, bf16[32,32,128]{2,1,0:T(8,128)(2,1)}) custom-call(bf16[64,896]{1,0:T(8,128)(2,1)} %bitcast.40, bf16[12288,128]{1,0:T(8,128)(2,1)} %bitcast.37), custom_call_target="tpu_custom_call" | custom-call | flops 84934656 | bytes 3145728 | tf_op jit(solution)/shard_map/gan_taps/pallas_call | solution.py:522
  49.2 2.6 %all-to-all-start.2 = ((bf16[32,32,128]{2,1,0:T(8,128)(2,1)}), bf16[32,32,128]{2,1,0:T(8,128)(2,1)S(1)}, u32[]{:S(2)}, u32[]{:S(2)}) async-start(bf16[32,32,128]{2,1,0:T(8,128)(2,1)} %get-tuple-element.25), calls=%async_computation.2 | async-start | bytes 524288 | tf_op jit(solution)/shard_map/all_to_all | solution.py:652
  51.8 2.0 %edge_rows.1 = (f32[48,768]{1,0:T(8,128)}, bf16[48,144]{1,0:T(8,128)(2,1)}, bf16[48,144]{1,0:T(8,128)(2,1)}) custom-call(f32[48,896]{1,0:T(8,128)} %get-tuple-element.17.own_ref, bf16[16,3,16,48]{3,2,1,0:T(8,128)(2,1)} %bitcast.50), custom_call_target="tpu_custom_call" | custom-call | flops 1000000000 | bytes 10000000 | tf_op jit(solution)/shard_map/edge_rows/pallas_call | solution.py:136
  53.8 3.7 %collective-permute-start = (bf16[48,144]{1,0:T(8,128)(2,1)}, bf16[48,144]{1,0:T(8,128)(2,1)S(1)}, u32[]{:S(2)}, u32[]{:S(2)}) collective-permute-start(bf16[48,144]{1,0:T(8,128)(2,1)} %get-tuple-element.19), channel_id=1, source_target_pairs={{0,1},{1,2},{2,3},{3,4},{4,5},{5,6},{6,7},{8,9},{9,10},{10,11},{11... | collective-permute-start | bytes 41480 | tf_op jit(solution)/shard_map/ppermute | solution.py:632
  57.5 1.5 %collective-permute-start.1 = (bf16[48,144]{1,0:T(8,128)(2,1)}, bf16[48,144]{1,0:T(8,128)(2,1)S(1)}, u32[]{:S(2)}, u32[]{:S(2)}) collective-permute-start(bf16[48,144]{1,0:T(8,128)(2,1)} %get-tuple-element.20), channel_id=1, source_target_pairs={{1,0},{2,1},{3,2},{4,3},{5,4},{6,5},{7,6},{9,8},{10,9},{11,10},{12... | collective-permute-start | bytes 41480 | tf_op jit(solution)/shard_map/ppermute | solution.py:631
  59.0 0.7 pad_add_fusion.ends_ref
  59.7 3.8 %collective-permute-done.1.below_ref = bf16[48,144]{1,0:T(8,128)(2,1)S(1)} collective-permute-done((bf16[48,144]{1,0:T(8,128)(2,1)}, bf16[48,144]{1,0:T(8,128)(2,1)S(1)}, u32[]{:S(2)}, u32[]{:S(2)}) %collective-permute-start.1) | collective-permute-done | bytes 13856 | tf_op jit(solution)/shard_map/ppermute | solution.py:631
  63.5 0.6 copy-done.8
  64.0 6.2 %rec_taps.1 = (bf16[16,32,768]{2,1,0:T(8,128)(2,1)}, f32[32,128]{1,0:T(8,128)}) custom-call(s32[2]{0:T(128)} %pad_add_fusion.ends_ref, f32[48,896]{1,0:T(8,128)} %get-tuple-element.17.own_ref, f32[48,768]{1,0:T(8,128)} %get-tuple-element.18.wanted_ref, bf16[48,144]{1,0:T(8,128)(2,1)} %copy-done.7, bf16[48,144]{1,0:T(8,128)(2,1)} %copy-done.8, ...), custom_call_target="tpu_custom_call" | custom-call | flops 84934656 | bytes 3145728 | tf_op jit(solution)/shard_map/rec_taps/pallas_call | solution.py:522
  70.2 41.6 %psum.7.rec_sum = f32[32,128]{1,0:T(8,128)} all-reduce(f32[32,128]{1,0:T(8,128)} %get-tuple-element.24), channel_id=1, replica_groups=mesh['clip'=4,'row'=8] {'clip','row'}, use_global_device_ids=true, to_apply=%region_0.1 | all-reduce | flops 4096 | bytes 32768 | tf_op jit(solution)/shard_map/psum | solution.py:643
  112.0 0.2 reshape.76
  112.2 0.7 copy.42
  112.9 0.7 copy-done
  113.6 5.2 %feature_pull.1 = (bf16[12288,128]{1,0:T(8,128)(2,1)}, f32[3,3,3,128]{3,2,1,0:T(4,128)}, f32[1,1]{1,0:T(1,128)}) custom-call(bf16[16,32,768]{2,1,0:T(8,128)(2,1)} %get-tuple-element.21.rec_hbm, bf16[16,32,768]{2,1,0:T(8,128)(2,1)} %get-tuple-element.23.gan_hbm, f32[32,128]{1,0:T(8,128)} %psum.7.rec_sum, bf16[32,32,128]{2,1,0:T(8,128)(2,1)} %copy-done, ...), custom_call_target="tpu_custom_call" | custom-call | flops 201326592 | bytes 6291456 | tf_op jit(solution)/shard_map/feature_pull/pallas_call | solution.py:586
  (26 shorter events, 0.3 us)
Async XLA Ops:
  0.6 13.6 %copy-start.10 = (bf16[4,4,3,64]{3,1,2,0:T(4,128)(2,1)S(1)}, bf16[4,4,3,64]{3,1,2,0:T(4,128)(2,1)}, u32[]{:S(2)}) copy-start(bf16[4,4,3,64]{3,1,2,0:T(4,128)(2,1)} %param.17) | copy-start | bytes 18436
  6.7 8.2 %copy-start.3 = (pred[48,1664]{1,0:T(8,128)(4,1)S(1)}, pred[48,1664]{1,0:T(8,128)(4,1)}, u32[]{:S(2)}) copy-start(pred[48,1664]{1,0:T(8,128)(4,1)} %constant.28.clone) | copy-start | bytes 239620
  6.7 8.2 %copy-start.4 = (pred[48,1664]{1,0:T(8,128)(4,1)S(1)}, pred[48,1664]{1,0:T(8,128)(4,1)}, u32[]{:S(2)}) copy-start(pred[48,1664]{1,0:T(8,128)(4,1)} %constant.29.clone) | copy-start | bytes 239620
  6.7 8.2 %copy-start.5 = (pred[48,1664]{1,0:T(8,128)(4,1)S(1)}, pred[48,1664]{1,0:T(8,128)(4,1)}, u32[]{:S(2)}) copy-start(pred[48,1664]{1,0:T(8,128)(4,1)} %constant.30.clone) | copy-start | bytes 239620
  6.7 8.2 %copy-start.6 = (pred[48,1664]{1,0:T(8,128)(4,1)S(1)}, pred[48,1664]{1,0:T(8,128)(4,1)}, u32[]{:S(2)}) copy-start(pred[48,1664]{1,0:T(8,128)(4,1)} %constant.31.clone) | copy-start | bytes 239620
  6.8 14.7 %all-to-all-start = ((bf16[8,8,896]{2,1,0:T(8,128)(2,1)}), bf16[8,8,896]{2,1,0:T(8,128)(2,1)S(1)}, u32[]{:S(2)}, u32[]{:S(2)}) async-start(bf16[8,8,896]{2,1,0:T(8,128)(2,1)} %bitcast.44), calls=%async_computation | async-start | bytes 229376 | tf_op jit(solution)/shard_map/all_to_all | solution.py:624
  14.5 3.0 %copy-start.9 = (bf16[4,4,512,1]{2,1,3,0:T(4,128)(2,1)S(1)}, bf16[4,4,512,1]{2,1,3,0:T(4,128)(2,1)}, u32[]{:S(2)}) copy-start(bf16[4,4,512,1]{2,1,3,0:T(4,128)(2,1)} %param.21) | copy-start | bytes 49156
  21.4 0.7 copy-start.2
  49.2 63.7 %all-to-all-start.2 = ((bf16[32,32,128]{2,1,0:T(8,128)(2,1)}), bf16[32,32,128]{2,1,0:T(8,128)(2,1)S(1)}, u32[]{:S(2)}, u32[]{:S(2)}) async-start(bf16[32,32,128]{2,1,0:T(8,128)(2,1)} %get-tuple-element.25), calls=%async_computation.2 | async-start | bytes 524288 | tf_op jit(solution)/shard_map/all_to_all | solution.py:652
  53.8 58.0 %copy-start.1 = (bf16[8,8,896]{2,1,0:T(8,128)(2,1)S(1)}, bf16[8,8,896]{2,1,0:T(8,128)(2,1)}, u32[]{:S(2)}) copy-start(bf16[8,8,896]{2,1,0:T(8,128)(2,1)} %all_to_all.15) | copy-start | bytes 344068
  53.8 5.8 %collective-permute-start = (bf16[48,144]{1,0:T(8,128)(2,1)}, bf16[48,144]{1,0:T(8,128)(2,1)S(1)}, u32[]{:S(2)}, u32[]{:S(2)}) collective-permute-start(bf16[48,144]{1,0:T(8,128)(2,1)} %get-tuple-element.19), channel_id=1, source_target_pairs={{0,1},{1,2},{2,3},{3,4},{4,5},{5,6},{6,7},{8,9},{9,10},{10,11},{11... | collective-permute-start | bytes 41480 | tf_op jit(solution)/shard_map/ppermute | solution.py:632
  57.5 5.9 %collective-permute-start.1 = (bf16[48,144]{1,0:T(8,128)(2,1)}, bf16[48,144]{1,0:T(8,128)(2,1)S(1)}, u32[]{:S(2)}, u32[]{:S(2)}) collective-permute-start(bf16[48,144]{1,0:T(8,128)(2,1)} %get-tuple-element.20), channel_id=1, source_target_pairs={{1,0},{2,1},{3,2},{4,3},{5,4},{6,5},{7,6},{9,8},{10,9},{11,10},{12... | collective-permute-start | bytes 41480 | tf_op jit(solution)/shard_map/ppermute | solution.py:631
  59.7 3.8 %copy-start.7 = (bf16[48,144]{1,0:T(8,128)(2,1)}, bf16[48,144]{1,0:T(8,128)(2,1)S(1)}, u32[]{:S(2)}) copy-start(bf16[48,144]{1,0:T(8,128)(2,1)S(1)} %collective-permute-done.above_ref) | copy-start | bytes 41476
  63.4 0.6 copy-start.8
  112.9 0.7 copy-start

commit v3 on v2

--- a/solution.py
+++ b/solution.py
@@ -19,6 +19,7 @@
 VM = pl.BlockSpec(memory_space=pltpu.VMEM)
 HBM = pl.BlockSpec(memory_space=pl.ANY)
 WHOLE = pltpu.CompilerParams(vmem_limit_bytes=60 * 2**20)
+PART = pltpu.CompilerParams(vmem_limit_bytes=24 * 2**20)
 
 
 def up_to(value, step):
@@ -34,21 +35,12 @@
 
 
 def forward_kernel(
-    feat_hbm, weight_ref, pay_ref, own_ref, flat_ref, feat_ref, weight_scr, taps_ref, out_ref, sems,
-    *, frames, devices, group, cols, lanes,
+    feat_ref, weight_ref, pay_ref, own_ref, flat_ref, weight_scr, taps_ref, out_ref, *, frames, devices, group, cols, lanes
 ):
     pixels = feat_ref.shape[0] // frames
     pieces = pixels // LANES
     pitch = out_ref.shape[1] // devices
     taps = flat_ref.shape[0]
-    copies = [
-        pltpu.make_async_copy(
-            feat_hbm.at[pl.ds(frame * pixels, pixels), :], feat_ref.at[pl.ds(frame * pixels, pixels), :], sems.at[frame]
-        )
-        for frame in range(frames)
-    ]
-    for copy in copies:
-        copy.start()
     weight_scr[...] = jnp.zeros_like(weight_scr)
     for a in range(3):
         for b in range(3):
@@ -58,7 +50,6 @@
     flat_ref[...] = weight
     out_ref[...] = jnp.zeros_like(out_ref)
     for frame in range(frames):
-        copies[frame].wait()
         product = mat(weight, feat_ref[frame * pixels : (frame + 1) * pixels, :], NT)
         slot = slot_of(frame, devices, group)
         for k in range(pieces):
@@ -98,16 +89,14 @@
             jax.ShapeDtypeStruct((3 * frames, lanes), F32),
             jax.ShapeDtypeStruct((32, channels), BF16),
         ),
-        in_specs=[pl.BlockSpec(memory_space=pl.ANY), VM],
+        in_specs=[VM, VM],
         out_specs=(VM,) * 3,
         scratch_shapes=[
-            pltpu.VMEM(features.shape, BF16),
             pltpu.VMEM((32, channels), F32),
             pltpu.VMEM((pixels // LANES, 32 * frames, LANES), F32),
             pltpu.VMEM((lanes // LANES, devices * pitch, LANES), F32),
-            pltpu.SemaphoreType.DMA((frames,)),
         ],
-        compiler_params=WHOLE,
+        compiler_params=PART,
         cost_estimate=pl.CostEstimate(flops=2 * features.size * 27, bytes_accessed=2 * features.size, transcendentals=0),
         name="forward_taps",
     )(features, weight)
@@ -145,7 +134,7 @@
         in_specs=[VM, VM],
         out_specs=(VM,) * 3,
         scratch_shapes=[pltpu.VMEM((frames * 3 * block_rows, LANES), F32)],
-        compiler_params=WHOLE,
+        compiler_params=PART,
         cost_estimate=pl.CostEstimate(flops=10**9, bytes_accessed=10**7, transcendentals=0),
         name="edge_rows",
     )(own, target)
@@ -165,8 +154,8 @@
 
 
 def disc_kernel(
-    pay_ref, gather_ref, scatter_ref, band_hbm, second_hbm, third_hbm, fourth_hbm, head_ref, out_ref,
-    zin, band, second, third, fourth, rows_in, act_one, slope_one, cols_two, act_two, slope_two, act_three, cols_four,
+    pay_ref, gather_ref, window_ref, band_ref, second_hbm, third_hbm, fourth_hbm, head_ref, unwindow_hbm, scatter_hbm, out_ref,
+    zin, second, third, fourth, unwindow, scatter, rows_in, act_one, slope_one, cols_two, act_two, slope_two, act_three, cols_four,
     pull_four, pull_three, pull_two, zout, sems, *, devices, group, cols, block_rows, period,
 ):
     lanes = pay_ref.shape[1]
@@ -181,7 +170,13 @@
     copies = [
         pltpu.make_async_copy(source, target, sems.at[i])
         for i, (source, target) in enumerate(
-            ((band_hbm, band), (second_hbm, second), (third_hbm, third), (fourth_hbm, fourth))
+            (
+                (second_hbm, second),
+                (third_hbm, third),
+                (fourth_hbm, fourth),
+                (unwindow_hbm, unwindow),
+                (scatter_hbm, scatter),
+            )
         )
     ]
     for copy in copies:
@@ -196,26 +191,35 @@
         for i in range(span):
             row = jnp.concatenate([plane[:, i * cols : (i + 1) * cols] for plane in planes], axis=1)
             rows_in[pl.ds((i * group + part) * devices, devices), :] = row
-    image = mat(gather_ref[...], rows_in[...].astype(BF16)).astype(BF16).astype(F32)
-    ext = [image[r * unit : (r + 1) * unit] for r in range(8)]
+    image = mat(gather_ref[...], rows_in[...].astype(BF16)).astype(BF16)
+    wins = mat(image, window_ref[...])
+    ext = [wins[r * unit : (r + 1) * unit] for r in range(8)]
     ext = [shift_rows(ext[7], 1, period)] + ext + [shift_rows(ext[0], -1, period)]
-    ext = [piece.astype(BF16) for piece in ext]
-    copies[0].wait()
-    left = [jnp.concatenate([ext[a + 2 * p] for p in range(4)], axis=0) for a in range(4)]
     width_one = act_one.shape[1]
-    step = 256
-    for start in range(0, width_one, step):
-        end = min(start + step, width_one)
-        pre = mat(left[0], band[0:wide, start:end])
-        for a in range(1, 4):
-            pre = pre + mat(left[a], band[a * wide : (a + 1) * wide, start:end])
-        act, slope = gate_of(pre)
+    strip = 8 * d1
+    band = band_ref[...]
+    for k in range(-(-width_one // strip)):
+        low, high = slice(2 * k * LANES, (2 * k + 1) * LANES), slice((2 * k + 1) * LANES, (2 * k + 2) * LANES)
+        left = jnp.concatenate(
+            [
+                jnp.concatenate([ext[2 * p + h][:, low] + ext[2 * p + h + 1][:, high] for p in range(4)], axis=0)
+                for h in (0, 2)
+            ],
+            axis=1,
+        ).astype(BF16)
+        start, end = k * strip, min((k + 1) * strip, width_one)
+        act, slope = gate_of(mat(left, band[:, : end - start]))
+        if k == 0 or end == width_one:
+            lane = start + lax.broadcasted_iota(jnp.int32, slope.shape, 1)
+            inside = (lane >= d1) & (lane < width_one - d1)
+            slope = jnp.where(inside, slope, 0.0)
+            act = jnp.where(inside, act.astype(F32), 0.0).astype(BF16)
         slope_one[:, start:end] = slope
         act_one[unit : 5 * unit, start:end] = act
         actual = act.astype(F32)
         act_one[0:unit, start:end] = shift_rows(actual[3 * unit :], 1, period).astype(BF16)
         act_one[5 * unit :, start:end] = shift_rows(actual[:unit], -1, period).astype(BF16)
-    copies[1].wait()
+    copies[0].wait()
     for x in range(x2):
         for a in range(4):
             for p in range(2):
@@ -234,7 +238,7 @@
         act_two[unit : 3 * unit, at] = block
         act_two[0:unit, at] = shift_rows(actual[unit:], 1, period).astype(BF16)
         act_two[3 * unit :, at] = shift_rows(actual[:unit], -1, period).astype(BF16)
-    copies[2].wait()
+    copies[1].wait()
     left = jnp.concatenate(
         [
             jnp.concatenate([act_two[a * unit : (a + 1) * unit, 2 * x * d2 : (2 * x + 4) * d2] for a in range(4)], axis=1)
@@ -257,7 +261,7 @@
             cols_four[x * unit : (x + 1) * unit, a * 4 * d3 : (a + 1) * 4 * d3] = act_three[
                 a * unit : (a + 1) * unit, x * d3 : (x + 4) * d3
             ]
-    copies[3].wait()
+    copies[2].wait()
     pre = mat(cols_four[...], fourth[...])
     _, slope = gate_of(pre)
     row = lax.broadcasted_iota(jnp.int32, (unit, d4), 0) % period
@@ -328,18 +332,31 @@
         )
         strips.append((both * slope_one[:, 2 * k * d1 : (2 * k + 2) * d1]).astype(BF16))
     cot = jnp.concatenate(strips, axis=1)
-    pulls = [mat(cot, band[a * wide : (a + 1) * wide, :], NT) for a in range(4)]
-    part = lambda p, a: pulls[a][p * unit : (p + 1) * unit]
-    phases = []
-    for r in range(8):
-        terms = [part(p, a) for p in range(4) for a in range(4) if 2 * p + a - 1 == r]
-        if r == 0:
-            terms.append(shift_rows(part(3, 3), 1, period))
-        if r == 7:
-            terms.append(shift_rows(part(0, 0), -1, period))
-        phases.append(functools.reduce(lambda u, v: u + v, terms))
+    copies[3].wait()
+    copies[4].wait()
+    sums = []
+    for k in range(-(-width_one // strip)):
+        start, end = k * strip, min((k + 1) * strip, width_one)
+        pulls = mat(cot[:, start:end], band[:, : end - start], NT)
+        groups = []
+        for m in range(5):
+            terms = [
+                pulls[p * unit : (p + 1) * unit, (m - p) * LANES : (m - p + 1) * LANES] for p in range(4) if 0 <= m - p < 2
+            ]
+            groups.append(functools.reduce(lambda u, v: u + v, terms))
+        sums.append(jnp.concatenate(groups, axis=0))
+    sums = jnp.concatenate(sums, axis=1)
+    upper = sums.astype(BF16)
+    lower = (sums - upper.astype(F32)).astype(BF16)
+    both = mat(upper, unwindow[...]) + mat(lower, unwindow[...])
+    half = both.shape[1] // 2
+    odd = [both[m * unit : (m + 1) * unit, 0:wide] for m in range(5)]
+    even = [both[m * unit : (m + 1) * unit, half : half + wide] for m in range(5)]
+    phases = [even[r // 2] if r % 2 == 0 else odd[(r + 1) // 2] for r in range(8)]
+    phases[0] = phases[0] + shift_rows(even[4], 1, period)
+    phases[7] = phases[7] + shift_rows(odd[0], -1, period)
     image = jnp.concatenate(phases, axis=0).astype(BF16)
-    rows = mat(scatter_ref[...], image)
+    rows = mat(scatter[...], image)
     zout[...] = jnp.zeros_like(zout)
     for part_at in range(group):
         picked = [rows[(i * group + part_at) * devices : (i * group + part_at + 1) * devices] for i in range(span)]
@@ -367,18 +384,33 @@
     return gather
 
 
-def band_of(first, cols):
+def windows_of(cols, d1):
+    wide = 3 * cols
+    count = -(-(cols // 2 + 2) // 8)
+    half = up_to(wide, LANES)
+    window = np.zeros((wide, count * 2 * LANES), np.float32)
+    unwindow = np.zeros((count * LANES, 2 * half), np.float32)
+    for k in range(count):
+        for c in range(3):
+            for j in range(18):
+                x = 16 * k - 3 + j
+                if 0 <= x < cols:
+                    for e in range(2):
+                        at = e * LANES // 2 + c * 18 + j
+                        window[c * cols + x, (2 * k + e) * LANES + at] = 1.0
+                        unwindow[k * LANES + at, e * half + c * cols + x] = 1.0
+    return window, unwindow
+
+
+def band_of(first):
     d1 = first.shape[-1]
-    width = (cols // 2 + 2) * d1
-    x = np.arange(cols)[:, None]
-    out_x = np.arange(width)[None, :] // d1 - 1
-    tap = x - 2 * out_x + 1
-    inside = (out_x >= 0) & (out_x < cols // 2)
-    tiled = jnp.tile(first, (1, 1, 1, cols // 2 + 2))
-    band = jnp.zeros((4, 3, cols, width), BF16)
+    tap = np.arange(18)[:, None] - 2 * (np.arange(8 * d1)[None, :] // d1)
+    tiled = jnp.tile(first, (1, 1, 1, 8))
+    band = jnp.zeros((4, 3, 18, 8 * d1), BF16)
     for b in range(4):
-        band = jnp.where(jnp.asarray((tap == b) & inside), tiled[:, b, :, None, :], band)
-    return band.reshape(4 * 3 * cols, width)
+        band = jnp.where(jnp.asarray(tap == b), tiled[:, b, :, None, :], band)
+    band = jnp.pad(band.reshape(4, 54, 8 * d1), ((0, 0), (0, LANES // 2 - 54), (0, 0)))
+    return band.reshape(2 * LANES, 8 * d1)
 
 
 def disc_call(payload, first, second, third, fourth, head, devices, group, cols, block_rows):
@@ -388,16 +420,19 @@
     x2, x3 = cols // 4, cols // 8
     x4 = x3 - 1
     gather = row_maps(devices, group, block_rows)
-    band = band_of(first, cols)
+    window, unwindow = windows_of(cols, d1)
+    width_one = (cols // 2 + 2) * d1
     args = (
         payload,
         jnp.asarray(gather, BF16),
-        jnp.asarray(gather.T, BF16),
-        band,
+        jnp.asarray(window, BF16),
+        band_of(first),
         second.reshape(16 * d1, d2),
         third.reshape(16 * d2, d3),
         fourth.reshape(16 * d3, d4),
         head.reshape(16, d4),
+        jnp.asarray(unwindow, BF16),
+        jnp.asarray(gather.T, BF16),
     )
     lanes = payload.shape[1]
     return pl.pallas_call(
@@ -405,17 +440,18 @@
             disc_kernel, devices=devices, group=group, cols=cols, block_rows=block_rows, period=period
         ),
         out_shape=jax.ShapeDtypeStruct(payload.shape, BF16),
-        in_specs=[VM, VM, VM, HBM, HBM, HBM, HBM, VM],
+        in_specs=[VM, VM, VM, VM, HBM, HBM, HBM, VM, HBM, HBM],
         out_specs=VM,
         scratch_shapes=[
             pltpu.VMEM((lanes // LANES, payload.shape[0], LANES), F32),
-            pltpu.VMEM(band.shape, BF16),
             pltpu.VMEM((16 * d1, d2), BF16),
             pltpu.VMEM((16 * d2, d3), BF16),
             pltpu.VMEM((16 * d3, d4), BF16),
+            pltpu.VMEM(unwindow.shape, BF16),
+            pltpu.VMEM(gather.T.shape, BF16),
             pltpu.VMEM((gather.shape[1], 3 * cols), F32),
-            pltpu.VMEM((6 * unit, band.shape[1]), BF16),
-            pltpu.VMEM((4 * unit, band.shape[1]), F32),
+            pltpu.VMEM((6 * unit, width_one), BF16),
+            pltpu.VMEM((4 * unit, width_one), F32),
             pltpu.VMEM((x2 * 2 * unit, 16 * d1), BF16),
             pltpu.VMEM((4 * unit, (x2 + 2) * d2), BF16),
             pltpu.VMEM((x2 * 2 * unit, d2), F32),
@@ -425,7 +461,7 @@
             pltpu.VMEM((x3 * unit, 16 * d2), F32),
             pltpu.VMEM((x2 * 2 * unit, 16 * d1), F32),
             pltpu.VMEM((lanes // LANES, payload.shape[0], LANES), F32),
-            pltpu.SemaphoreType.DMA((4,)),
+            pltpu.SemaphoreType.DMA((5,)),
         ],
         compiler_params=WHOLE,
         cost_estimate=pl.CostEstimate(flops=4 * 10**9, bytes_accessed=8 * 10**6, transcendentals=10**6),
@@ -450,36 +486,20 @@
         taps_ref[k, pl.ds(27 * frames, (padded - 27) * frames), :] = jnp.zeros(((padded - 27) * frames, LANES), F32)
 
 
-def weigh(taps_ref, taps_out, feat_ref, copies, frames, devices, group, pieces, padded):
+def weigh(taps_ref, feat_ref, frames, devices, group, pieces, padded):
     pixels = pieces * LANES
     total = jnp.zeros((padded, feat_ref.shape[1]), F32)
     for frame in range(frames):
         rows = pl.ds(slot_of(frame, devices, group), padded, stride=frames)
         taps = jnp.concatenate([taps_ref[k, rows, :] for k in range(pieces)], axis=1).astype(BF16)
-        taps_out[frame] = taps
-        copies[frame].wait()
         total = total + mat(taps, feat_ref[frame * pixels : (frame + 1) * pixels, :])
     return total
 
 
-def fetch(feat_hbm, feat_ref, sems, frames):
-    pixels = feat_ref.shape[0] // frames
-    copies = [
-        pltpu.make_async_copy(
-            feat_hbm.at[pl.ds(frame * pixels, pixels), :], feat_ref.at[pl.ds(frame * pixels, pixels), :], sems.at[frame]
-        )
-        for frame in range(frames)
-    ]
-    for copy in copies:
-        copy.start()
-    return copies
-
-
 def rec_kernel(
-    ends_ref, own_ref, wanted_ref, above_ref, below_ref, feat_hbm, taps_out, part_ref, feat_ref, taps_ref, sems,
+    ends_ref, own_ref, wanted_ref, above_ref, below_ref, feat_ref, part_ref, plane_ref, taps_ref,
     *, frames, devices, group, cols, block_rows,
 ):
-    copies = fetch(feat_hbm, feat_ref, sems, frames)
     lanes = own_ref.shape[1]
     pieces = block_rows * cols // LANES
     none = lambda count: jnp.zeros((3 * frames, count), F32)
@@ -492,16 +512,13 @@
     lane = lax.broadcasted_iota(jnp.int32, (3 * frames, lanes), 1)
     plane = loss_scale * (own_ref[...] + added - asked)
     plane = jnp.where((lane >= ends_ref[0]) & (lane < ends_ref[1]), plane, 0.0)
-    put_taps(plane, taps_ref, frames, cols, pieces, taps_out.shape[1])
-    part_ref[...] = weigh(taps_ref, taps_out, feat_ref, copies, frames, devices, group, pieces, taps_out.shape[1])
-
-
-def gan_kernel(
-    plane_ref, feat_hbm, taps_out, part_ref, feat_ref, taps_ref, zin, sems, *, frames, devices, group, cols, block_rows
-):
-    copies = fetch(feat_hbm, feat_ref, sems, frames)
+    plane_ref[...] = plane
+    put_taps(plane, taps_ref, frames, cols, pieces, 32)
+    part_ref[...] = weigh(taps_ref, feat_ref, frames, devices, group, pieces, 32).astype(BF16)
+
+
+def unpack(plane_ref, zin, devices, group):
     lanes = plane_ref.shape[1]
-    pieces = block_rows * cols // LANES
     pitch = plane_ref.shape[0] // devices
     for k in range(lanes // LANES):
         zin[k] = plane_ref[:, k * LANES : (k + 1) * LANES].astype(F32)
@@ -510,50 +527,57 @@
         for part in range(group):
             row = pl.ds(o * group + part, devices, stride=pitch)
             blocks.append(jnp.concatenate([zin[k, row, :] for k in range(lanes // LANES)], axis=1))
-    plane = jnp.concatenate(blocks, axis=0)
-    put_taps(plane, taps_ref, frames, cols, pieces, taps_out.shape[1])
-    total = weigh(taps_ref, taps_out, feat_ref, copies, frames, devices, group, pieces, taps_out.shape[1])
-    total = total.astype(BF16)
+    return jnp.concatenate(blocks, axis=0)
+
+
+def gan_kernel(plane_ref, feat_ref, part_ref, taps_ref, zin, *, frames, devices, group, cols, block_rows):
+    pieces = block_rows * cols // LANES
+    put_taps(unpack(plane_ref, zin, devices, group), taps_ref, frames, cols, pieces, 32)
+    total = weigh(taps_ref, feat_ref, frames, devices, group, pieces, 32).astype(BF16)
     for i in range(part_ref.shape[0]):
         part_ref[i] = total
 
 
-def taps_call(kernel, specs, operands, features, part, extra, frames, devices, group, cols, block_rows, name):
+def turn_kernel(
+    rec_ref, plane_ref, out_ref, rec_taps, gan_taps, zin, *, frames, devices, group, cols, block_rows
+):
+    pieces = block_rows * cols // LANES
+    pixels = pieces * LANES
+    put_taps(rec_ref[...], rec_taps, frames, cols, pieces, 32)
+    put_taps(unpack(plane_ref, zin, devices, group), gan_taps, frames, cols, pieces, 32)
+    for pair in range(frames // 2):
+        for k in range(pieces):
+            parts = []
+            for frame in (2 * pair, 2 * pair + 1):
+                rows = pl.ds(slot_of(frame, devices, group), 32, stride=frames)
+                parts += [rec_taps[k, rows, :], gan_taps[k, rows, :]]
+            at = pair * pixels + k * LANES
+            out_ref[at : at + LANES, :] = jnp.concatenate(parts, axis=0).T.astype(BF16)
+
+
+def taps_call(kernel, specs, operands, out, scratch, frames, devices, group, cols, block_rows, flops, name):
     return pl.pallas_call(
         functools.partial(kernel, frames=frames, devices=devices, group=group, cols=cols, block_rows=block_rows),
-        out_shape=(jax.ShapeDtypeStruct((frames, 32, block_rows * cols), BF16), part),
-        in_specs=specs + [HBM],
-        out_specs=(VM, VM),
-        scratch_shapes=[
-            pltpu.VMEM(features.shape, BF16),
-            pltpu.VMEM((block_rows * cols // LANES, 32 * frames, LANES), F32),
-            *extra,
-            pltpu.SemaphoreType.DMA((frames,)),
-        ],
-        compiler_params=WHOLE,
-        cost_estimate=pl.CostEstimate(
-            flops=2 * features.size * 27, bytes_accessed=2 * features.size, transcendentals=0
-        ),
+        out_shape=out,
+        in_specs=specs,
+        out_specs=jax.tree.map(lambda _: VM, out),
+        scratch_shapes=scratch,
+        compiler_params=PART,
+        cost_estimate=pl.CostEstimate(flops=flops, bytes_accessed=4 * 10**6, transcendentals=0),
         name=name,
-    )(*operands, features)
+    )(*operands)
 
 
 def final_kernel(
-    rec_hbm, gan_hbm, rec_sum, gan_sums, weight_ref, out_hbm, grad_ref, adapt_ref, rec_ref, gan_ref, both_ref, out_ref,
-    in_sems, out_sems, *, pixels, chunk,
+    taps_ref, rec_sums, gan_sums, weight_ref, out_hbm, grad_ref, adapt_ref, both_ref, out_ref, sems, *, pixels, chunk
 ):
-    frames, padded, block = rec_ref.shape
-    loads = []
-    for at in range(0, frames, chunk):
-        part = pl.ds(at, chunk)
-        loads.append(pltpu.make_async_copy(rec_hbm.at[part], rec_ref.at[part], in_sems.at[0, at // chunk]))
-        loads.append(pltpu.make_async_copy(gan_hbm.at[part], gan_ref.at[part], in_sems.at[1, at // chunk]))
-    for copy in loads:
-        copy.start()
-    gan = gan_sums[0].astype(F32)
-    for i in range(1, gan_sums.shape[0]):
-        gan = gan + gan_sums[i].astype(F32)
-    rec = rec_sum[...]
+    total = []
+    for ref in (rec_sums, gan_sums):
+        value = ref[0].astype(F32)
+        for i in range(1, ref.shape[0]):
+            value = value + ref[i].astype(F32)
+        total.append(value)
+    rec, gan = total
     norm = lambda values: jnp.sqrt(jnp.sum(jnp.sum(values * values, axis=1, keepdims=True), axis=0, keepdims=True))
     adaptive = norm(rec) / (norm(gan) + epsilon)
     grad = (rec + adaptive * gan) / pixels
@@ -563,49 +587,47 @@
             grad_ref[a, b] = grad[at : at + 3, :]
     adapt_ref[...] = adaptive
     weight = weight_ref[...]
-    both_ref[:padded] = weight
-    both_ref[padded:] = (adaptive * weight.astype(F32)).astype(BF16)
+    padded, channels = weight.shape
+    scaled = (adaptive * weight.astype(F32)).astype(BF16)
+    both_ref[...] = jnp.zeros_like(both_ref)
+    both_ref[0:padded, 0:channels] = weight
+    both_ref[padded : 2 * padded, 0:channels] = scaled
+    both_ref[2 * padded : 3 * padded, channels:] = weight
+    both_ref[3 * padded :, channels:] = scaled
+    pairs = taps_ref.shape[0] // chunk
     stores = []
-    for frame in range(frames):
-        if frame % chunk == 0:
-            loads[frame // chunk * 2].wait()
-            loads[frame // chunk * 2 + 1].wait()
-        left = jnp.concatenate([rec_ref[frame], gan_ref[frame]], axis=0)
-        out_ref[frame * block : (frame + 1) * block] = mat(left, both_ref[...], TN).astype(BF16)
-        rows = pl.ds(frame * block, block)
-        stores.append(pltpu.make_async_copy(out_ref.at[rows], out_hbm.at[rows], out_sems.at[frame]))
+    for pair in range(pairs):
+        product = mat(taps_ref[pair * chunk : (pair + 1) * chunk], both_ref[...]).astype(BF16)
+        rows = pl.ds(2 * pair * chunk, 2 * chunk)
+        out_ref[2 * pair * chunk : (2 * pair + 1) * chunk] = product[:, :channels]
+        out_ref[(2 * pair + 1) * chunk : (2 * pair + 2) * chunk] = product[:, channels:]
+        stores.append(pltpu.make_async_copy(out_ref.at[rows], out_hbm.at[rows], sems.at[pair]))
         stores[-1].start()
     for copy in stores:
         copy.wait()
 
 
-def final_call(rec_taps, gan_taps, rec_sum, gan_sums, weight, pixels):
-    frames, padded, block = rec_taps.shape
-    channels = weight.shape[1]
-    chunk = 4
+def final_call(taps, rec_sums, gan_sums, weight, pixels, chunk):
+    padded, channels = weight.shape
+    rows = 2 * taps.shape[0]
     return pl.pallas_call(
         functools.partial(final_kernel, pixels=pixels, chunk=chunk),
         out_shape=(
-            jax.ShapeDtypeStruct((frames * block, channels), BF16),
+            jax.ShapeDtypeStruct((rows, channels), BF16),
             jax.ShapeDtypeStruct((3, 3, 3, channels), F32),
             jax.ShapeDtypeStruct((1, 1), F32),
         ),
-        in_specs=[HBM, HBM, VM, VM, VM],
+        in_specs=[VM] * 4,
         out_specs=(HBM, VM, VM),
         scratch_shapes=[
-            pltpu.VMEM(rec_taps.shape, BF16),
-            pltpu.VMEM(gan_taps.shape, BF16),
-            pltpu.VMEM((2 * padded, channels), BF16),
-            pltpu.VMEM((frames * block, channels), BF16),
-            pltpu.SemaphoreType.DMA((2, frames // chunk)),
-            pltpu.SemaphoreType.DMA((frames,)),
+            pltpu.VMEM((4 * padded, 2 * channels), BF16),
+            pltpu.VMEM((rows, channels), BF16),
+            pltpu.SemaphoreType.DMA((rows // (2 * chunk),)),
         ],
-        compiler_params=WHOLE,
-        cost_estimate=pl.CostEstimate(
-            flops=4 * frames * block * channels * padded, bytes_accessed=4 * frames * block * channels, transcendentals=0
-        ),
+        compiler_params=PART,
+        cost_estimate=pl.CostEstimate(flops=4 * rows * channels * padded, bytes_accessed=4 * rows * channels, transcendentals=0),
         name="feature_pull",
-    )(rec_taps, gan_taps, rec_sum, gan_sums, weight)
+    )(taps, rec_sums, gan_sums, weight)
 
 
 def per_device(
@@ -619,6 +641,7 @@
     lanes = up_to((block_rows + 2) * cols, LANES)
     pitch = up_to(3 * group, 8)
     edge = lax.axis_index("row")
+    sizes = (frames, devices, group, cols, block_rows)
     feats = features.reshape(frames * block_rows * cols, channels)
     payload, own, weight = forward_call(feats, conv_weight, frames, devices, group, cols, lanes, pitch)
     trade = lambda values: lax.all_to_all(
@@ -628,6 +651,7 @@
     wanted, upward, downward = edge_call(
         own, target[0].transpose(0, 2, 1, 3), frames, devices, group, block_rows, cols
     )
+    arrived, upward, downward = lax.optimization_barrier((arrived, upward, downward))
     below = lax.ppermute(upward, "row", [(i + 1, i) for i in range(devices - 1)])
     above = lax.ppermute(downward, "row", [(i, i + 1) for i in range(devices - 1)])
     ends = jnp.stack(
@@ -636,24 +660,33 @@
             jnp.where(edge == devices - 1, (block_rows + 1) * cols, (block_rows + 2) * cols),
         ]
     ).astype(jnp.int32)
-    rec_taps, rec_part = taps_call(
-        rec_kernel, [pl.BlockSpec(memory_space=pltpu.SMEM), VM, VM, VM, VM], (ends, own, wanted, above, below), feats,
-        jax.ShapeDtypeStruct((32, channels), F32), [], frames, devices, group, cols, block_rows, "rec_taps",
-    )
-    rec_sum = lax.psum(rec_part, ("clip", "row"))
+    taps_scratch = pltpu.VMEM((block_rows * cols // LANES, 32 * frames, LANES), F32)
+    plane_scratch = pltpu.VMEM((lanes // LANES, devices * pitch, LANES), F32)
+    flops = 2 * features.size * 27
+    rec_part, rec_plane = taps_call(
+        rec_kernel, [pl.BlockSpec(memory_space=pltpu.SMEM)] + [VM] * 5, (ends, own, wanted, above, below, feats),
+        (jax.ShapeDtypeStruct((32, channels), BF16), jax.ShapeDtypeStruct(own.shape, F32)),
+        [taps_scratch], *sizes, flops, "rec_taps",
+    )
+    rec_sums = lax.all_gather(rec_part, ("clip", "row"))
     sent = disc_call(
         arrived, disc_first, disc_second, disc_third, disc_fourth, disc_head, devices, group, cols, block_rows
     )
     returned = trade(sent)
-    gan_taps, gan_part = taps_call(
-        gan_kernel, [VM], (returned,), feats, jax.ShapeDtypeStruct((clips * devices, 32, channels), BF16),
-        [pltpu.VMEM((lanes // LANES, devices * pitch, LANES), F32)], frames, devices, group, cols, block_rows, "gan_taps",
+    returned, rec_plane = lax.optimization_barrier((returned, rec_plane))
+    gan_part = taps_call(
+        gan_kernel, [VM, VM], (returned, feats), jax.ShapeDtypeStruct((clips * devices, 32, channels), BF16),
+        [taps_scratch, plane_scratch], *sizes, flops, "gan_taps",
     )
     gan_sums = lax.all_to_all(gan_part, ("clip", "row"), split_axis=0, concat_axis=0, tiled=True)
+    taps = taps_call(
+        turn_kernel, [VM, VM], (rec_plane, returned), jax.ShapeDtypeStruct((feats.shape[0] // 2, LANES), BF16),
+        [taps_scratch, taps_scratch, plane_scratch], *sizes, flops, "turn_taps",
+    )
     image_back = returned.reshape(devices, pitch, lanes)[:, : 3 * group, cols : (block_rows + 1) * cols]
     image_back = image_back.reshape(devices, 3, group, block_rows, cols).transpose(0, 2, 3, 1, 4)
     image_back = image_back.reshape(1, frames, block_rows, 3, cols)
-    feature_grad, weight_grad, adaptive = final_call(rec_taps, gan_taps, rec_sum, gan_sums, weight, pixels)
+    feature_grad, weight_grad, adaptive = final_call(taps, rec_sums, gan_sums, weight, pixels, block_rows * cols)
     return (feature_grad.reshape(features.shape), image_back, weight_grad, adaptive[0, 0])
 
 

time: 120 us -> 131 us (1.092)
  blocking collectives: 52.8 us -> 70.1 us
  Pallas kernels: 35.4 us -> 20.2 us
  starting transfers between devices: 15.2 us -> 21.3 us
  local copies, waits for them, and re-layouts: 4.27 us -> 8.53 us
  other arithmetic: 3.24 us -> 0.61 us
    all_gather x0 -> x1, blocking collectives: none -> 70.1 us  [per_device(): rec_sums = lax.all_gather(rec_part, ('clip', 'row'))]
    psum x1 -> x0, blocking collectives: 41.6 us -> none  [per_device(): rec_sum = lax.psum(rec_part, ('clip', 'row'))]
    all_to_all x1 -> x0, blocking collectives: 11.2 us -> none  [per_device(): lax.all_to_all(values.reshape(devices, pitch, lanes), 'row', split_axis=0...]
    pallas_call x2 -> x3, Pallas kernels: 12.3 us -> 5.53 us  [taps_call(): pl.pallas_call(functools.partial(kernel, frames=frames, devices=devices,...]
    unnamed x22 -> x32, local copies, waits for them, and re-layouts: 1.99 us -> 5.81 us
    pallas_call x1, Pallas kernels: 6.06 us -> 2.34 us  [forward_call(): pl.pallas_call(functools.partial(forward_kernel, frames=frames, devices=d...]
    all_to_all x1 -> x2, starting transfers between devices: 7.42 us -> 10.7 us  [per_device(): lax.all_to_all(values.reshape(devices, pitch, lanes), 'row', split_axis=0...]
    all_to_all x1, starting transfers between devices: 2.6 us -> 5.5 us  [per_device(): lax.all_to_all(gan_part, ('clip', 'row'), split_axis=0, concat_axis=0, ti...]
  transfers between devices with their start and end apart: 4 -> 5, of which waited for: 2 -> 3; matrix products, arithmetic and copies ran while one was open for 5% -> 3% of each run, Pallas kernels for 7% -> 3%
where the time goes in v3:
time: 131 us; the launch traced here: 130 us
  blocking collectives  70.1 us (54%)
  starting transfers between devices  21.3 us (16%)
  Pallas kernels  20.2 us (15%)
  local copies, waits for them, and re-layouts  8.53 us (7%)
  waiting for transfers between devices  8.14 us (6%)
    all_gather x1, blocking collectives, per_device(): rec_sums = lax.all_gather(rec_part, ('clip', 'row'))  70.1 us
    all_to_all x2, starting transfers between devices, per_device(): lax.all_to_all(values.reshape(devices, pitch, lanes), 'row', split_axis=0...  10.7 us
    pallas_call x1, Pallas kernels, disc_call(): pl.pallas_call(functools.partial(disc_kernel, devices=devices, group=grou...  9.15 us
    unnamed x32, local copies, waits for them, and re-layouts  5.81 us
    pallas_call x3, Pallas kernels, taps_call(): pl.pallas_call(functools.partial(kernel, frames=frames, devices=devices,...  5.53 us
    all_to_all x1, starting transfers between devices, per_device(): lax.all_to_all(gan_part, ('clip', 'row'), split_axis=0, concat_axis=0, ti...  5.5 us
    ppermute x1, waiting for transfers between devices, per_device(): lax.ppermute(upward, 'row', [(i + 1, i) for i in range(devices - 1)])  4.22 us
    ppermute x1, starting transfers between devices, per_device(): lax.ppermute(downward, 'row', [(i, i + 1) for i in range(devices - 1)])  3.8 us
  transfers between devices with their start and end apart: 5, of which 3 were waited for; matrix products, arithmetic and copies ran while one was open for 3% of the time, Pallas kernels for 3%

profile of v3, /device:TPU:0, one launch (start us, length us, event | category | flops | bytes accessed | tf_op | source)
XLA Modules:
  0.0 130.0 jit_solution(10245813946956520102)
XLA Ops:
  0.7 1.9 %copy-done = bf16[1,16,16,48,128]{4,3,2,1,0:T(8,128)(2,1)S(1)} copy-done((bf16[1,16,16,48,128]{4,3,2,1,0:T(8,128)(2,1)S(1)}, bf16[1,16,16,48,128]{4,3,2,1,0:T(8,128)(2,1)}, u32[]{:S(2)}) %copy-start) | copy-done | bytes 3145752
  2.6 0.7 copy-done.6
  3.3 2.3 %forward_taps.1 = (bf16[64,896]{1,0:T(8,128)(2,1)}, f32[48,896]{1,0:T(8,128)S(1)}, bf16[32,128]{1,0:T(8,128)(2,1)S(1)}) custom-call(bf16[12288,128]{1,0:T(8,128)(2,1)S(1)} %bitcast.50, bf16[3,3,3,128]{3,2,1,0:T(4,128)(2,1)S(1)} %copy-done.6), custom_call_target="tpu_custom_call" | custom-call | flops 84934656 | bytes 3145728 | tf_op jit(solution)/shard_map/forward_taps/pallas_call | solution.py:85
  5.6 7.3 %all-to-all-start = ((bf16[8,8,896]{2,1,0:T(8,128)(2,1)}), bf16[8,8,896]{2,1,0:T(8,128)(2,1)S(1)}, u32[]{:S(2)}, u32[]{:S(2)}) async-start(bf16[8,8,896]{2,1,0:T(8,128)(2,1)} %bitcast.1), calls=%async_computation | async-start | bytes 229376 | tf_op jit(solution)/shard_map/all_to_all | solution.py:647
  13.4 0.5 fusion.2
  14.0 0.6 reshape.74.head_ref
  14.6 0.7 pad.4.clone
  15.7 0.7 copy-done.4
  16.3 3.8 %all-to-all-done = bf16[8,8,896]{2,1,0:T(8,128)(2,1)S(1)} async-done(((bf16[8,8,896]{2,1,0:T(8,128)(2,1)}), bf16[8,8,896]{2,1,0:T(8,128)(2,1)S(1)}, u32[]{:S(2)}, u32[]{:S(2)}) %all-to-all-start) | async-done | bytes 114720 | tf_op jit(solution)/shard_map/all_to_all | solution.py:647
  20.1 0.6 copy-done.8
  20.8 9.2 %disc_rows.1 = bf16[64,896]{1,0:T(8,128)(2,1)} custom-call(bf16[64,896]{1,0:T(8,128)(2,1)} %bitcast.60, bf16[256,288]{1,0:T(8,128)(2,1)} %constant.33.clone.gather_ref, bf16[144,1024]{1,0:T(8,128)(2,1)} %constant.34.clone.window_ref, bf16[256,512]{1,0:T(8,128)(2,1)} %bitcast.58, bf16[1024,128]{1,0:T(8,128)(2,1)} %bitcast.65, bf16[2048,256]{1,0:T(8,128)(2,1)} %bitcast.64, ...), custom_call_target="tpu_custom_call" | custom-call | flops 4000000000 | bytes 8000000 | tf_op jit(solution)/shard_map/disc_rows/pallas_call | solution.py:438
  29.9 3.4 %all-to-all-start.1 = ((bf16[8,8,896]{2,1,0:T(8,128)(2,1)}), bf16[8,8,896]{2,1,0:T(8,128)(2,1)S(1)}, u32[]{:S(2)}, u32[]{:S(2)}) async-start(bf16[8,8,896]{2,1,0:T(8,128)(2,1)} %bitcast.61), calls=%async_computation.1 | async-start | bytes 229376 | tf_op jit(solution)/shard_map/all_to_all | solution.py:647
  33.3 3.8 %collective-permute-start = (bf16[48,144]{1,0:T(8,128)(2,1)S(1)}, bf16[48,144]{1,0:T(8,128)(2,1)S(1)}, u32[]{:S(2)}, u32[]{:S(2)}) collective-permute-start(bf16[48,144]{1,0:T(8,128)(2,1)S(1)} %get-tuple-element.26), channel_id=1, source_target_pairs={{0,1},{1,2},{2,3},{3,4},{4,5},{5,6},{6,7},{8,9},{9,10},{10,11},{11... | collective-permute-start | bytes 41480 | tf_op jit(solution)/shard_map/ppermute | solution.py:656
  37.2 1.3 collective-permute-start.1
  38.7 4.2 %collective-permute-done.1.below_ref = bf16[48,144]{1,0:T(8,128)(2,1)S(1)} collective-permute-done((bf16[48,144]{1,0:T(8,128)(2,1)S(1)}, bf16[48,144]{1,0:T(8,128)(2,1)S(1)}, u32[]{:S(2)}, u32[]{:S(2)}) %collective-permute-start.1) | collective-permute-done | bytes 13856 | tf_op jit(solution)/shard_map/ppermute | solution.py:655
  42.9 0.9 copy-done.3
  43.8 0.9 copy-done.5
  44.7 1.8 %rec_taps.1 = (bf16[32,128]{1,0:T(8,128)(2,1)S(1)}, f32[48,896]{1,0:T(8,128)S(1)}) custom-call(s32[2]{0:T(128)S(1)} %pad_add_fusion.ends_ref, f32[48,896]{1,0:T(8,128)S(1)} %copy-done.3, f32[48,768]{1,0:T(8,128)S(1)} %copy-done.5, bf16[48,144]{1,0:T(8,128)(2,1)S(1)} %collective-permute-done.above_ref, bf16[48,144]{1,0:T(8,128)(2,1)S(1)} %collective-permute-done.1.below_ref, ...), custom_call_target="tpu_custom_call" | custom-call | flops 84934656 | bytes 4000000 | tf_op jit(solution)/shard_map/rec_taps/pallas_call | solution.py:559
  46.5 1.9 %gan_taps.1 = bf16[32,32,128]{2,1,0:T(8,128)(2,1)} custom-call(bf16[64,896]{1,0:T(8,128)(2,1)S(1)} %bitcast.53, bf16[12288,128]{1,0:T(8,128)(2,1)S(1)} %bitcast.52), custom_call_target="tpu_custom_call" | custom-call | flops 84934656 | bytes 4000000 | tf_op jit(solution)/shard_map/gan_taps/pallas_call | solution.py:559
  48.4 5.5 %all-to-all-start.2 = ((bf16[32,32,128]{2,1,0:T(8,128)(2,1)}), bf16[32,32,128]{2,1,0:T(8,128)(2,1)S(1)}, u32[]{:S(2)}, u32[]{:S(2)}) async-start(bf16[32,32,128]{2,1,0:T(8,128)(2,1)} %gan_taps.1), calls=%async_computation.2 | async-start | bytes 524288 | tf_op jit(solution)/shard_map/all_to_all | solution.py:681
  53.9 70.1 %all-gather = bf16[1024,128]{1,0:T(8,128)(2,1)S(1)} all-gather(bf16[32,128]{1,0:T(8,128)(2,1)S(1)} %get-tuple-element.31), channel_id=2, replica_groups=mesh['clip'=4,'row'=8] {'clip','row'}, dimensions={0}, use_global_device_ids=true | all-gather | bytes 270336 | tf_op jit(solution)/shard_map/all_gather | solution.py:671
  124.4 0.7 copy.34
  125.1 1.9 %turn_taps.1.taps_ref = bf16[6144,128]{1,0:T(8,128)(2,1)S(1)} custom-call(f32[48,896]{1,0:T(8,128)S(1)} %get-tuple-element.29.rec_ref, bf16[64,896]{1,0:T(8,128)(2,1)S(1)} %bitcast.54), custom_call_target="tpu_custom_call" | custom-call | flops 84934656 | bytes 4000000 | tf_op jit(solution)/shard_map/turn_taps/pallas_call | solution.py:559
  126.9 2.9 %feature_pull.1 = (bf16[12288,128]{1,0:T(8,128)(2,1)}, f32[3,3,3,128]{3,2,1,0:T(4,128)}, f32[1,1]{1,0:T(1,128)}) custom-call(bf16[6144,128]{1,0:T(8,128)(2,1)S(1)} %turn_taps.1.taps_ref, bf16[32,32,128]{2,1,0:T(8,128)(2,1)S(1)} %bitcast.55, bf16[32,32,128]{2,1,0:T(8,128)(2,1)S(1)} %all-to-all-done.2.gan_sums, bf16[32,128]{1,0:T(8,128)(2,1)S(1)} %get-tuple-element.32.weight_ref), custom_call_target="tpu_custom_call" | custom-call | flops 201326592 | bytes 6291456 | tf_op jit(solution)/shard_map/feature_pull/pallas_call | solution.py:613
  (46 shorter events, 1.3 us)
Async XLA Ops:
  0.6 12.5 %copy-start.12 = (pred[18,512]{1,0:T(8,128)(4,1)S(1)}, pred[18,512]{1,0:T(8,128)(4,1)}, u32[]{:S(2)}) copy-start(pred[18,512]{1,0:T(8,128)(4,1)} %constant.38.clone) | copy-start | bytes 27652
  0.6 12.7 %copy-start.11 = (pred[18,512]{1,0:T(8,128)(4,1)S(1)}, pred[18,512]{1,0:T(8,128)(4,1)}, u32[]{:S(2)}) copy-start(pred[18,512]{1,0:T(8,128)(4,1)} %constant.35.clone) | copy-start | bytes 27652
  0.7 1.9 %copy-start = (bf16[1,16,16,48,128]{4,3,2,1,0:T(8,128)(2,1)S(1)}, bf16[1,16,16,48,128]{4,3,2,1,0:T(8,128)(2,1)}, u32[]{:S(2)}) copy-start(bf16[1,16,16,48,128]{4,3,2,1,0:T(8,128)(2,1)} %param.16) | copy-start | bytes 9437188
  2.6 0.7 copy-start.6
  3.3 9.6 %copy-start.10 = (bf16[4,4,3,64]{3,1,2,0:T(4,128)(2,1)S(1)}, bf16[4,4,3,64]{3,1,2,0:T(4,128)(2,1)}, u32[]{:S(2)}) copy-start(bf16[4,4,3,64]{3,1,2,0:T(4,128)(2,1)} %param.19) | copy-start | bytes 18436
  3.3 10.0 %copy-start.14 = (pred[18,512]{1,0:T(8,128)(4,1)S(1)}, pred[18,512]{1,0:T(8,128)(4,1)}, u32[]{:S(2)}) copy-start(pred[18,512]{1,0:T(8,128)(4,1)} %constant.37.clone) | copy-start | bytes 27652
  3.3 10.0 %copy-start.13 = (pred[18,512]{1,0:T(8,128)(4,1)S(1)}, pred[18,512]{1,0:T(8,128)(4,1)}, u32[]{:S(2)}) copy-start(pred[18,512]{1,0:T(8,128)(4,1)} %constant.36.clone) | copy-start | bytes 27652
  3.3 10.8 %copy-start.9 = (bf16[4,4,512,1]{2,1,3,0:T(4,128)(2,1)S(1)}, bf16[4,4,512,1]{2,1,3,0:T(4,128)(2,1)}, u32[]{:S(2)}) copy-start(bf16[4,4,512,1]{2,1,3,0:T(4,128)(2,1)} %param.23) | copy-start | bytes 49156
  3.3 12.1 %copy-start.7 = (bf16[1,16,16,3,48]{4,2,3,1,0:T(8,128)(2,1)S(1)}, bf16[1,16,16,3,48]{4,2,3,1,0:T(8,128)(2,1)}, u32[]{:S(2)}) copy-start(bf16[1,16,16,3,48]{4,2,3,1,0:T(8,128)(2,1)} %param.17) | copy-start | bytes 221188
  5.6 10.1 %copy-start.2 = (f32[48,896]{1,0:T(8,128)}, f32[48,896]{1,0:T(8,128)S(1)}, u32[]{:S(2)}) copy-start(f32[48,896]{1,0:T(8,128)S(1)} %get-tuple-element.21.own_ref) | copy-start | bytes 516100
  5.6 14.5 %all-to-all-start = ((bf16[8,8,896]{2,1,0:T(8,128)(2,1)}), bf16[8,8,896]{2,1,0:T(8,128)(2,1)S(1)}, u32[]{:S(2)}, u32[]{:S(2)}) async-start(bf16[8,8,896]{2,1,0:T(8,128)(2,1)} %bitcast.1), calls=%async_computation | async-start | bytes 229376 | tf_op jit(solution)/shard_map/all_to_all | solution.py:647
  15.7 0.7 copy-start.4
  20.1 0.6 copy-start.8
  20.8 22.1 %copy-start.1 = (bf16[1,16,16,48,128]{4,3,2,1,0:T(8,128)(2,1)S(1)}, bf16[1,16,16,48,128]{4,3,2,1,0:T(8,128)(2,1)}, u32[]{:S(2)}) copy-start(bf16[1,16,16,48,128]{4,3,2,1,0:T(8,128)(2,1)} %param.16) | copy-start | bytes 9437188
  29.9 16.5 %all-to-all-start.1 = ((bf16[8,8,896]{2,1,0:T(8,128)(2,1)}), bf16[8,8,896]{2,1,0:T(8,128)(2,1)S(1)}, u32[]{:S(2)}, u32[]{:S(2)}) async-start(bf16[8,8,896]{2,1,0:T(8,128)(2,1)} %bitcast.61), calls=%async_computation.1 | async-start | bytes 229376 | tf_op jit(solution)/shard_map/all_to_all | solution.py:647
  33.3 5.3 %collective-permute-start = (bf16[48,144]{1,0:T(8,128)(2,1)S(1)}, bf16[48,144]{1,0:T(8,128)(2,1)S(1)}, u32[]{:S(2)}, u32[]{:S(2)}) collective-permute-start(bf16[48,144]{1,0:T(8,128)(2,1)S(1)} %get-tuple-element.26), channel_id=1, source_target_pairs={{0,1},{1,2},{2,3},{3,4},{4,5},{5,6},{6,7},{8,9},{9,10},{10,11},{11... | collective-permute-start | bytes 41480 | tf_op jit(solution)/shard_map/ppermute | solution.py:656
  37.2 5.7 %collective-permute-start.1 = (bf16[48,144]{1,0:T(8,128)(2,1)S(1)}, bf16[48,144]{1,0:T(8,128)(2,1)S(1)}, u32[]{:S(2)}, u32[]{:S(2)}) collective-permute-start(bf16[48,144]{1,0:T(8,128)(2,1)S(1)} %get-tuple-element.27), channel_id=1, source_target_pairs={{1,0},{2,1},{3,2},{4,3},{5,4},{6,5},{7,6},{9,8},{10,9},{11,10},{12... | collective-permute-start | bytes 41480 | tf_op jit(solution)/shard_map/ppermute | solution.py:655
  42.9 0.9 copy-start.3
  43.8 0.9 copy-start.5
  48.4 78.5 %all-to-all-start.2 = ((bf16[32,32,128]{2,1,0:T(8,128)(2,1)}), bf16[32,32,128]{2,1,0:T(8,128)(2,1)S(1)}, u32[]{:S(2)}, u32[]{:S(2)}) async-start(bf16[32,32,128]{2,1,0:T(8,128)(2,1)} %gan_taps.1), calls=%async_computation.2 | async-start | bytes 524288 | tf_op jit(solution)/shard_map/all_to_all | solution.py:681

commit v4 on v3

--- a/solution.py
+++ b/solution.py
@@ -35,21 +35,48 @@
 
 
 def forward_kernel(
-    feat_ref, weight_ref, pay_ref, own_ref, flat_ref, weight_scr, taps_ref, out_ref, *, frames, devices, group, cols, lanes
+    feat_hbm, target_hbm, weight_hbm, pay_ref, own_ref, flat_ref, feat_ref, target_ref, weight_ref, weight_scr, target_scr,
+    taps_ref, out_ref, sems, *, frames, devices, group, cols, lanes, chunks,
 ):
     pixels = feat_ref.shape[0] // frames
     pieces = pixels // LANES
     pitch = out_ref.shape[1] // devices
     taps = flat_ref.shape[0]
+    block_rows = pixels // cols
+    size = feat_ref.shape[0] // chunks
+    copies = [
+        pltpu.make_async_copy(weight_hbm, weight_ref, sems.at[chunks]),
+        pltpu.make_async_copy(target_hbm, target_ref, sems.at[chunks + 1]),
+    ] + [
+        pltpu.make_async_copy(feat_hbm.at[pl.ds(i * size, size), :], feat_ref.at[pl.ds(i * size, size), :], sems.at[i])
+        for i in range(chunks)
+    ]
+    for copy in copies:
+        copy.start()
     weight_scr[...] = jnp.zeros_like(weight_scr)
+    out_ref[...] = jnp.zeros_like(out_ref)
+    copies[0].wait()
+    copies[1].wait()
     for a in range(3):
         for b in range(3):
             at = (a * 3 + b) * 3
             weight_scr[at : at + 3, :] = weight_ref[a, b].astype(F32)
     weight = weight_scr[...].astype(BF16)
     flat_ref[...] = weight
-    out_ref[...] = jnp.zeros_like(out_ref)
+    target_scr[:, 0:cols] = target_ref[...].reshape(target_scr.shape[0], cols).astype(F32)
+    edges = []
+    for y in (0, block_rows - 1):
+        for o in range(3):
+            for part in range(group):
+                rows = pl.ds((part * 3 + o) * block_rows + y, devices, stride=group * 3 * block_rows)
+                edges.append(target_scr[rows, :][:, 0:cols])
+    edges.append(jnp.zeros((devices, lanes - len(edges) * cols), F32))
+    edges = jnp.concatenate(edges, axis=1)
+    for k in range(lanes // LANES):
+        out_ref[k, pl.ds(3 * group, devices, stride=pitch), :] = edges[:, k * LANES : (k + 1) * LANES]
     for frame in range(frames):
+        if frame % (frames // chunks) == 0:
+            copies[2 + frame // (frames // chunks)].wait()
         product = mat(weight, feat_ref[frame * pixels : (frame + 1) * pixels, :], NT)
         slot = slot_of(frame, devices, group)
         for k in range(pieces):
@@ -79,64 +106,69 @@
         pay_ref[:, k * LANES : (k + 1) * LANES] = out_ref[k].astype(BF16)
 
 
-def forward_call(features, weight, frames, devices, group, cols, lanes, pitch):
+def forward_call(features, target, weight, frames, devices, group, cols, lanes, pitch):
     pixels = features.shape[0] // frames
     channels = features.shape[1]
+    chunks = 4
     return pl.pallas_call(
-        functools.partial(forward_kernel, frames=frames, devices=devices, group=group, cols=cols, lanes=lanes),
+        functools.partial(
+            forward_kernel, frames=frames, devices=devices, group=group, cols=cols, lanes=lanes, chunks=chunks
+        ),
         out_shape=(
             jax.ShapeDtypeStruct((devices * pitch, lanes), BF16),
             jax.ShapeDtypeStruct((3 * frames, lanes), F32),
             jax.ShapeDtypeStruct((32, channels), BF16),
         ),
-        in_specs=[VM, VM],
+        in_specs=[HBM, HBM, HBM],
         out_specs=(VM,) * 3,
         scratch_shapes=[
+            pltpu.VMEM(features.shape, BF16),
+            pltpu.VMEM(target.shape, BF16),
+            pltpu.VMEM(weight.shape, BF16),
             pltpu.VMEM((32, channels), F32),
+            pltpu.VMEM((3 * pixels // cols * frames, LANES), F32),
             pltpu.VMEM((pixels // LANES, 32 * frames, LANES), F32),
             pltpu.VMEM((lanes // LANES, devices * pitch, LANES), F32),
+            pltpu.SemaphoreType.DMA((chunks + 2,)),
         ],
-        compiler_params=PART,
+        compiler_params=WHOLE,
         cost_estimate=pl.CostEstimate(flops=2 * features.size * 27, bytes_accessed=2 * features.size, transcendentals=0),
         name="forward_taps",
-    )(features, weight)
-
-
-def edge_kernel(own_ref, target_ref, wanted_ref, up_ref, down_ref, scr, *, frames, devices, group, block_rows, cols):
+    )(features, target, weight)
+
+
+def inner_kernel(own_ref, target_ref, inner_ref, scr, *, frames, devices, group, block_rows, cols):
     scr[:, 0:cols] = target_ref[...].reshape(scr.shape[0], cols).astype(F32)
     stride = group * 3 * block_rows
+    lanes = own_ref.shape[1]
     for o in range(3):
         for part in range(group):
             at = o * frames + part * devices
-            rows = [
+            rows = [jnp.zeros((devices, cols), F32)]
+            rows += [
                 scr[pl.ds((part * 3 + o) * block_rows + y, devices, stride=stride), :][:, 0:cols]
                 for y in range(block_rows)
             ]
-            wanted_ref[at : at + devices, :] = jnp.concatenate(rows, axis=1)
-    own = own_ref[...]
-    wanted = wanted_ref[...]
-    up_ref[...] = jnp.concatenate([own[:, 0 : 2 * cols], wanted[:, 0:cols]], axis=1).astype(BF16)
-    down_ref[...] = jnp.concatenate(
-        [own[:, block_rows * cols : (block_rows + 2) * cols], wanted[:, (block_rows - 1) * cols :]], axis=1
-    ).astype(BF16)
-
-
-def edge_call(own, target, frames, devices, group, block_rows, cols):
+            rows.append(jnp.zeros((devices, lanes - (block_rows + 1) * cols), F32))
+            wanted = jnp.concatenate(rows, axis=1)
+            lane = lax.broadcasted_iota(jnp.int32, wanted.shape, 1)
+            inside = (lane >= 2 * cols) & (lane < block_rows * cols)
+            own = jnp.where(inside, own_ref[at : at + devices, :], 0.0)
+            inner_ref[at : at + devices, :] = loss_scale * (own - wanted)
+
+
+def inner_call(own, target, frames, devices, group, block_rows, cols):
     return pl.pallas_call(
         functools.partial(
-            edge_kernel, frames=frames, devices=devices, group=group, block_rows=block_rows, cols=cols
+            inner_kernel, frames=frames, devices=devices, group=group, block_rows=block_rows, cols=cols
         ),
-        out_shape=(
-            jax.ShapeDtypeStruct((3 * frames, block_rows * cols), F32),
-            jax.ShapeDtypeStruct((3 * frames, 3 * cols), BF16),
-            jax.ShapeDtypeStruct((3 * frames, 3 * cols), BF16),
-        ),
+        out_shape=jax.ShapeDtypeStruct(own.shape, F32),
         in_specs=[VM, VM],
-        out_specs=(VM,) * 3,
+        out_specs=VM,
         scratch_shapes=[pltpu.VMEM((frames * 3 * block_rows, LANES), F32)],
         compiler_params=PART,
-        cost_estimate=pl.CostEstimate(flops=10**9, bytes_accessed=10**7, transcendentals=0),
-        name="edge_rows",
+        cost_estimate=pl.CostEstimate(flops=10**8, bytes_accessed=10**6, transcendentals=0),
+        name="inner_rows",
     )(own, target)
 
 
@@ -151,6 +183,29 @@
 def gate_of(values):
     logistic = 1.0 / (1.0 + jnp.exp(-values))
     return (values * logistic).astype(BF16), logistic * (1.0 + values * (1.0 - logistic))
+
+
+def edge_planes(zin, zout, image, scatter, devices, group, cols, span, lanes, pitch):
+    zout[...] = jnp.zeros_like(zout)
+    step = group * devices
+    first = mat(scatter[0 : 2 * step], image)
+    last = mat(scatter[(span - 2) * step :], image)
+    row = pl.ds(3 * group, devices, stride=pitch)
+    target = jnp.concatenate([zin[k, row, :] for k in range(lanes // LANES)], axis=1)
+    outer, inner = [], []
+    for e, rows, out_at, in_at, move in ((0, first, 0, 1, 1), (1, last, 1, 0, -1)):
+        for o in range(3):
+            for part in range(group):
+                pick = lambda i: rows[i * step + part * devices : i * step + (part + 1) * devices, o * cols : (o + 1) * cols]
+                at = ((1 - e) * 3 * group + o * group + part) * cols
+                wanted = shift_rows(target[:, at : at + cols], move, devices)
+                outer.append(loss_scale * (pick(out_at) - wanted))
+                inner.append(pick(in_at))
+    for i, pieces in enumerate((outer, inner)):
+        pieces.append(jnp.zeros((devices, lanes - 6 * group * cols), F32))
+        plane = jnp.concatenate(pieces, axis=1)
+        for k in range(lanes // LANES):
+            zout[k, pl.ds(3 * group + i, devices, stride=pitch), :] = plane[:, k * LANES : (k + 1) * LANES]
 
 
 def disc_kernel(
@@ -179,8 +234,8 @@
             )
         )
     ]
-    for copy in copies:
-        copy.start()
+    for i in (4, 0, 1, 2, 3):
+        copies[i].start()
     for k in range(lanes // LANES):
         zin[k] = pay_ref[:, k * LANES : (k + 1) * LANES].astype(F32)
     for part in range(group):
@@ -193,6 +248,8 @@
             rows_in[pl.ds((i * group + part) * devices, devices), :] = row
     image = mat(gather_ref[...], rows_in[...].astype(BF16)).astype(BF16)
     wins = mat(image, window_ref[...])
+    copies[4].wait()
+    edge_planes(zin, zout, image, scatter, devices, group, cols, span, lanes, pitch)
     ext = [wins[r * unit : (r + 1) * unit] for r in range(8)]
     ext = [shift_rows(ext[7], 1, period)] + ext + [shift_rows(ext[0], -1, period)]
     width_one = act_one.shape[1]
@@ -333,7 +390,6 @@
         strips.append((both * slope_one[:, 2 * k * d1 : (2 * k + 2) * d1]).astype(BF16))
     cot = jnp.concatenate(strips, axis=1)
     copies[3].wait()
-    copies[4].wait()
     sums = []
     for k in range(-(-width_one // strip)):
         start, end = k * strip, min((k + 1) * strip, width_one)
@@ -357,7 +413,6 @@
     phases[7] = phases[7] + shift_rows(odd[0], -1, period)
     image = jnp.concatenate(phases, axis=0).astype(BF16)
     rows = mat(scatter[...], image)
-    zout[...] = jnp.zeros_like(zout)
     for part_at in range(group):
         picked = [rows[(i * group + part_at) * devices : (i * group + part_at + 1) * devices] for i in range(span)]
         for o in range(3):
@@ -486,37 +541,6 @@
         taps_ref[k, pl.ds(27 * frames, (padded - 27) * frames), :] = jnp.zeros(((padded - 27) * frames, LANES), F32)
 
 
-def weigh(taps_ref, feat_ref, frames, devices, group, pieces, padded):
-    pixels = pieces * LANES
-    total = jnp.zeros((padded, feat_ref.shape[1]), F32)
-    for frame in range(frames):
-        rows = pl.ds(slot_of(frame, devices, group), padded, stride=frames)
-        taps = jnp.concatenate([taps_ref[k, rows, :] for k in range(pieces)], axis=1).astype(BF16)
-        total = total + mat(taps, feat_ref[frame * pixels : (frame + 1) * pixels, :])
-    return total
-
-
-def rec_kernel(
-    ends_ref, own_ref, wanted_ref, above_ref, below_ref, feat_ref, part_ref, plane_ref, taps_ref,
-    *, frames, devices, group, cols, block_rows,
-):
-    lanes = own_ref.shape[1]
-    pieces = block_rows * cols // LANES
-    none = lambda count: jnp.zeros((3 * frames, count), F32)
-    rest = none(lanes - (block_rows + 2) * cols)
-    above, below = above_ref[...].astype(F32), below_ref[...].astype(F32)
-    added = jnp.concatenate(
-        [above[:, : 2 * cols], none((block_rows - 2) * cols), below[:, : 2 * cols], rest], axis=1
-    )
-    asked = jnp.concatenate([above[:, 2 * cols :], wanted_ref[...], below[:, 2 * cols :], rest], axis=1)
-    lane = lax.broadcasted_iota(jnp.int32, (3 * frames, lanes), 1)
-    plane = loss_scale * (own_ref[...] + added - asked)
-    plane = jnp.where((lane >= ends_ref[0]) & (lane < ends_ref[1]), plane, 0.0)
-    plane_ref[...] = plane
-    put_taps(plane, taps_ref, frames, cols, pieces, 32)
-    part_ref[...] = weigh(taps_ref, feat_ref, frames, devices, group, pieces, 32).astype(BF16)
-
-
 def unpack(plane_ref, zin, devices, group):
     lanes = plane_ref.shape[1]
     pitch = plane_ref.shape[0] // devices
@@ -530,12 +554,49 @@
     return jnp.concatenate(blocks, axis=0)
 
 
-def gan_kernel(plane_ref, feat_ref, part_ref, taps_ref, zin, *, frames, devices, group, cols, block_rows):
+def rec_rows(inner_ref, zin, devices, group, cols, block_rows):
+    lanes = inner_ref.shape[1]
+    pitch = zin.shape[1] // devices
+    edges = []
+    for i in range(2):
+        row = pl.ds(3 * group + i, devices, stride=pitch)
+        edges.append(jnp.concatenate([zin[k, row, :] for k in range(lanes // LANES)], axis=1))
+    blocks = []
+    for i, e in ((0, 0), (1, 0), (1, 1), (0, 1)):
+        pieces = [
+            edges[i][:, (e * 3 * group + at) * cols : (e * 3 * group + at + 1) * cols] for at in range(3 * group)
+        ]
+        blocks.append(jnp.concatenate(pieces, axis=0))
+    none = lambda count: jnp.zeros((blocks[0].shape[0], count), F32)
+    above, first, last, below = blocks
+    rest = lanes - (block_rows + 2) * cols
+    return inner_ref[...], jnp.concatenate(
+        [above, first * loss_scale, none((block_rows - 2) * cols), last * loss_scale, below, none(rest)], axis=1
+    )
+
+
+def both_kernel(
+    inner_ref, plane_ref, feat_ref, part_ref, rec_ref, rec_taps, gan_taps, zin, *, frames, devices, group, cols, block_rows
+):
     pieces = block_rows * cols // LANES
-    put_taps(unpack(plane_ref, zin, devices, group), taps_ref, frames, cols, pieces, 32)
-    total = weigh(taps_ref, feat_ref, frames, devices, group, pieces, 32).astype(BF16)
-    for i in range(part_ref.shape[0]):
-        part_ref[i] = total
+    put_taps(unpack(plane_ref, zin, devices, group), gan_taps, frames, cols, pieces, 32)
+    inner, edges = rec_rows(inner_ref, zin, devices, group, cols, block_rows)
+    rec = inner + edges
+    rec_ref[...] = rec
+    put_taps(rec, rec_taps, frames, cols, pieces, 32)
+    pixels = pieces * LANES
+    total = jnp.zeros(part_ref.shape, F32)
+    for frame in range(frames):
+        rows = pl.ds(slot_of(frame, devices, group), 32, stride=frames)
+        taps = jnp.concatenate(
+            [
+                jnp.concatenate([taps_ref[k, rows, :] for k in range(pieces)], axis=1)
+                for taps_ref in (rec_taps, gan_taps)
+            ],
+            axis=0,
+        )
+        total = total + mat(taps.astype(BF16), feat_ref[frame * pixels : (frame + 1) * pixels, :])
+    part_ref[...] = total
 
 
 def turn_kernel(
@@ -568,16 +629,9 @@
     )(*operands)
 
 
-def final_kernel(
-    taps_ref, rec_sums, gan_sums, weight_ref, out_hbm, grad_ref, adapt_ref, both_ref, out_ref, sems, *, pixels, chunk
-):
-    total = []
-    for ref in (rec_sums, gan_sums):
-        value = ref[0].astype(F32)
-        for i in range(1, ref.shape[0]):
-            value = value + ref[i].astype(F32)
-        total.append(value)
-    rec, gan = total
+def final_kernel(taps_ref, sums_ref, weight_ref, out_hbm, grad_ref, adapt_ref, both_ref, out_ref, sems, *, pixels, chunk):
+    half = weight_ref.shape[0]
+    rec, gan = sums_ref[0:half, :], sums_ref[half:, :]
     norm = lambda values: jnp.sqrt(jnp.sum(jnp.sum(values * values, axis=1, keepdims=True), axis=0, keepdims=True))
     adaptive = norm(rec) / (norm(gan) + epsilon)
     grad = (rec + adaptive * gan) / pixels
@@ -607,7 +661,7 @@
         copy.wait()
 
 
-def final_call(taps, rec_sums, gan_sums, weight, pixels, chunk):
+def final_call(taps, sums, weight, pixels, chunk):
     padded, channels = weight.shape
     rows = 2 * taps.shape[0]
     return pl.pallas_call(
@@ -617,7 +671,7 @@
             jax.ShapeDtypeStruct((3, 3, 3, channels), F32),
             jax.ShapeDtypeStruct((1, 1), F32),
         ),
-        in_specs=[VM] * 4,
+        in_specs=[VM] * 3,
         out_specs=(HBM, VM, VM),
         scratch_shapes=[
             pltpu.VMEM((4 * padded, 2 * channels), BF16),
@@ -627,7 +681,7 @@
         compiler_params=PART,
         cost_estimate=pl.CostEstimate(flops=4 * rows * channels * padded, bytes_accessed=4 * rows * channels, transcendentals=0),
         name="feature_pull",
-    )(taps, rec_sums, gan_sums, weight)
+    )(taps, sums, weight)
 
 
 def per_device(
@@ -639,46 +693,35 @@
     group = frames // devices
     pixels = clips * devices * frames * block_rows * cols
     lanes = up_to((block_rows + 2) * cols, LANES)
-    pitch = up_to(3 * group, 8)
-    edge = lax.axis_index("row")
+    pitch = up_to(3 * group + 2, 8)
     sizes = (frames, devices, group, cols, block_rows)
     feats = features.reshape(frames * block_rows * cols, channels)
-    payload, own, weight = forward_call(feats, conv_weight, frames, devices, group, cols, lanes, pitch)
+    wanted = target[0].transpose(0, 2, 1, 3)
+    payload, own, weight = forward_call(feats, wanted, conv_weight, frames, devices, group, cols, lanes, pitch)
     trade = lambda values: lax.all_to_all(
         values.reshape(devices, pitch, lanes), "row", split_axis=0, concat_axis=0, tiled=True
     ).reshape(devices * pitch, lanes)
     arrived = trade(payload)
-    wanted, upward, downward = edge_call(
-        own, target[0].transpose(0, 2, 1, 3), frames, devices, group, block_rows, cols
-    )
-    arrived, upward, downward = lax.optimization_barrier((arrived, upward, downward))
-    below = lax.ppermute(upward, "row", [(i + 1, i) for i in range(devices - 1)])
-    above = lax.ppermute(downward, "row", [(i, i + 1) for i in range(devices - 1)])
-    ends = jnp.stack(
-        [
-            jnp.where(edge == 0, cols, 0),
-            jnp.where(edge == devices - 1, (block_rows + 1) * cols, (block_rows + 2) * cols),
-        ]
-    ).astype(jnp.int32)
-    taps_scratch = pltpu.VMEM((block_rows * cols // LANES, 32 * frames, LANES), F32)
-    plane_scratch = pltpu.VMEM((lanes // LANES, devices * pitch, LANES), F32)
-    flops = 2 * features.size * 27
-    rec_part, rec_plane = taps_call(
-        rec_kernel, [pl.BlockSpec(memory_space=pltpu.SMEM)] + [VM] * 5, (ends, own, wanted, above, below, feats),
-        (jax.ShapeDtypeStruct((32, channels), BF16), jax.ShapeDtypeStruct(own.shape, F32)),
-        [taps_scratch], *sizes, flops, "rec_taps",
-    )
-    rec_sums = lax.all_gather(rec_part, ("clip", "row"))
+    inner = inner_call(own, wanted, frames, devices, group, block_rows, cols)
+    arrived, inner = lax.optimization_barrier((arrived, inner))
     sent = disc_call(
         arrived, disc_first, disc_second, disc_third, disc_fourth, disc_head, devices, group, cols, block_rows
     )
     returned = trade(sent)
-    returned, rec_plane = lax.optimization_barrier((returned, rec_plane))
-    gan_part = taps_call(
-        gan_kernel, [VM, VM], (returned, feats), jax.ShapeDtypeStruct((clips * devices, 32, channels), BF16),
-        [taps_scratch, plane_scratch], *sizes, flops, "gan_taps",
+    taps_scratch = pltpu.VMEM((block_rows * cols // LANES, 32 * frames, LANES), F32)
+    plane_scratch = pltpu.VMEM((lanes // LANES, devices * pitch, LANES), F32)
+    flops = 4 * features.size * 27
+    part, rec_plane = taps_call(
+        both_kernel, [VM, VM, VM], (inner, returned, feats),
+        (jax.ShapeDtypeStruct((64, channels), F32), jax.ShapeDtypeStruct(own.shape, F32)),
+        [taps_scratch, taps_scratch, plane_scratch], *sizes, flops, "both_taps",
     )
-    gan_sums = lax.all_to_all(gan_part, ("clip", "row"), split_axis=0, concat_axis=0, tiled=True)
+    everyone = clips * devices
+    slices = up_to(part.size, everyone * LANES) // everyone // LANES
+    part = jnp.pad(part, ((0, everyone * slices - part.shape[0]), (0, 0))).reshape(everyone, slices, LANES)
+    share = lambda values: lax.all_to_all(values, ("clip", "row"), split_axis=0, concat_axis=0, tiled=True)
+    mine = jnp.sum(share(part), axis=0)
+    sums = share(jnp.broadcast_to(mine[None], part.shape)).reshape(everyone * slices, LANES)[:64]
     taps = taps_call(
         turn_kernel, [VM, VM], (rec_plane, returned), jax.ShapeDtypeStruct((feats.shape[0] // 2, LANES), BF16),
         [taps_scratch, taps_scratch, plane_scratch], *sizes, flops, "turn_taps",
@@ -686,7 +729,7 @@
     image_back = returned.reshape(devices, pitch, lanes)[:, : 3 * group, cols : (block_rows + 1) * cols]
     image_back = image_back.reshape(devices, 3, group, block_rows, cols).transpose(0, 2, 3, 1, 4)
     image_back = image_back.reshape(1, frames, block_rows, 3, cols)
-    feature_grad, weight_grad, adaptive = final_call(taps, rec_sums, gan_sums, weight, pixels, block_rows * cols)
+    feature_grad, weight_grad, adaptive = final_call(taps, sums, weight, pixels, block_rows * cols)
     return (feature_grad.reshape(features.shape), image_back, weight_grad, adaptive[0, 0])
 
 

time: 131 us -> 65.4 us (0.50)
  blocking collectives: 70.1 us -> 19.8 us
  starting transfers between devices: 21.3 us -> 10 us
  local copies, waits for them, and re-layouts: 8.53 us -> 5.01 us
    all_gather x1 -> x0, blocking collectives: 70.1 us -> none  [per_device(): rec_sums = lax.all_gather(rec_part, ('clip', 'row'))]
    all_to_all x0 -> x2, blocking collectives: none -> 19.8 us  [the longest x1 10.5 us: per_device(): lax.all_to_all(values.reshape(devices, pitch, lanes), 'row', split_axis=0...]
    ppermute x2 -> x0, starting transfers between devices: 5.09 us -> none  [the longest x1 3.8 us: per_device(): lax.ppermute(downward, 'row', [(i, i + 1) for i in range(devices - 1)])]
    ppermute x2 -> x0, waiting for transfers between devices: 4.34 us -> none  [the longest x1 4.22 us: per_device(): lax.ppermute(upward, 'row', [(i + 1, i) for i in range(devices - 1)])]
    unnamed x32 -> x23, local copies, waits for them, and re-layouts: 5.81 us -> 1.65 us
    all_to_all x1, waiting for transfers between devices: 0.01 us -> 4.1 us  [per_device(): lax.all_to_all(values, ('clip', 'row'), split_axis=0, concat_axis=0, tile...]
    all_to_all x2 -> x1, starting transfers between devices: 10.7 us -> 7.29 us  [per_device(): lax.all_to_all(values.reshape(devices, pitch, lanes), 'row', split_axis=0...]
    all_to_all x1, starting transfers between devices: 5.5 us -> 2.75 us  [per_device(): lax.all_to_all(values, ('clip', 'row'), split_axis=0, concat_axis=0, tile...]
  transfers between devices with their start and end apart: 5 -> 2, of which waited for: 3 -> 2; matrix products, arithmetic and copies ran while one was open for 3% -> 5% of each run, Pallas kernels for 3% -> 3%
where the time goes in v4:
time: 65.4 us; the launch traced here: 65 us
  Pallas kernels  20.8 us (32%)
  blocking collectives  19.8 us (30%)
  starting transfers between devices  10 us (15%)
  waiting for transfers between devices  7.65 us (12%)
  local copies, waits for them, and re-layouts  5.01 us (8%)
  between operations  1.07 us (2%)
    all_to_all x1, blocking collectives, per_device(): lax.all_to_all(values.reshape(devices, pitch, lanes), 'row', split_axis=0...  10.5 us
    pallas_call x1, Pallas kernels, disc_call(): pl.pallas_call(functools.partial(disc_kernel, devices=devices, group=grou...  9.57 us
    all_to_all x1, blocking collectives, per_device(): lax.all_to_all(values, ('clip', 'row'), split_axis=0, concat_axis=0, tile...  9.29 us
    all_to_all x1, starting transfers between devices, per_device(): lax.all_to_all(values.reshape(devices, pitch, lanes), 'row', split_axis=0...  7.29 us
    pallas_call x2, Pallas kernels, taps_call(): pl.pallas_call(functools.partial(kernel, frames=frames, devices=devices,...  4.15 us
    all_to_all x1, waiting for transfers between devices, per_device(): lax.all_to_all(values, ('clip', 'row'), split_axis=0, concat_axis=0, tile...  4.1 us
    pallas_call x1, Pallas kernels, forward_call(): pl.pallas_call(functools.partial(forward_kernel, frames=frames, devices=d...  3.99 us
    all_to_all x1, waiting for transfers between devices, per_device(): lax.all_to_all(values.reshape(devices, pitch, lanes), 'row', split_axis=0...  3.55 us
  transfers between devices with their start and end apart: 2, of which 2 were waited for; matrix products, arithmetic and copies ran while one was open for 5% of the time, Pallas kernels for 3%

profile of v4, /device:TPU:0, one launch (start us, length us, event | category | flops | bytes accessed | tf_op | source)
XLA Modules:
  0.0 65.0 jit_solution(12248254910154130897)
XLA Ops:
  0.6 0.0 copy-start.8
  0.7 4.0 %forward_taps.1 = (bf16[64,896]{1,0:T(8,128)(2,1)}, f32[48,896]{1,0:T(8,128)}, bf16[32,128]{1,0:T(8,128)(2,1)}) custom-call(bf16[12288,128]{1,0:T(8,128)(2,1)} %bitcast.48, bf16[16,3,16,48]{3,2,1,0:T(8,128)(2,1)} %bitcast.52, bf16[3,3,3,128]{3,2,1,0:T(4,128)(2,1)} %weight_hbm.1), custom_call_target="tpu_custom_call" | custom-call | flops 84934656 | bytes 3145728 | tf_op jit(solution)/shard_map/forward_taps/pallas_call | solution.py:113
  4.7 7.3 %all-to-all-start = ((bf16[8,8,896]{2,1,0:T(8,128)(2,1)}), bf16[8,8,896]{2,1,0:T(8,128)(2,1)S(1)}, u32[]{:S(2)}, u32[]{:S(2)}) async-start(bf16[8,8,896]{2,1,0:T(8,128)(2,1)} %bitcast.60), calls=%async_computation | async-start | bytes 229376 | tf_op jit(solution)/shard_map/all_to_all | solution.py:701
  12.0 0.1 tile.10
  12.1 0.1 fusion.3
  12.5 0.5 fusion.2
  13.1 0.6 reshape.78.head_ref
  13.7 0.7 %pad.4.clone = bf16[4,64,512]{2,1,0:T(8,128)(2,1)} pad(bf16[4,54,512]{2,1,0:T(8,128)(2,1)S(1)} %copy.44, bf16[]{:T(256)} %constant.10.clone.1), padding=0_0x0_10x0_0 | pad | bytes 483330 | tf_op jit(solution)/shard_map/jit(_pad)/pad | solution.py:467
  14.5 0.9 %copy-done.2 = f32[48,896]{1,0:T(8,128)S(1)} copy-done((f32[48,896]{1,0:T(8,128)S(1)}, f32[48,896]{1,0:T(8,128)}, u32[]{:S(2)}) %copy-start.2) | copy-done | bytes 172056
  15.4 0.3 inner_rows.1.inner_ref
  15.7 3.6 %all-to-all-done = bf16[8,8,896]{2,1,0:T(8,128)(2,1)S(1)} async-done(((bf16[8,8,896]{2,1,0:T(8,128)(2,1)}), bf16[8,8,896]{2,1,0:T(8,128)(2,1)S(1)}, u32[]{:S(2)}, u32[]{:S(2)}) %all-to-all-start) | async-done | bytes 114720 | tf_op jit(solution)/shard_map/all_to_all | solution.py:701
  19.2 0.6 copy-done.4
  19.9 9.6 %disc_rows.1 = bf16[64,896]{1,0:T(8,128)(2,1)} custom-call(bf16[64,896]{1,0:T(8,128)(2,1)} %bitcast.59, bf16[256,288]{1,0:T(8,128)(2,1)} %constant.22.clone.gather_ref, bf16[144,1024]{1,0:T(8,128)(2,1)} %constant.23.clone.window_ref, bf16[256,512]{1,0:T(8,128)(2,1)} %bitcast.57, bf16[1024,128]{1,0:T(8,128)(2,1)} %bitcast.65, bf16[2048,256]{1,0:T(8,128)(2,1)} %bitcast.64, ...), custom_call_target="tpu_custom_call" | custom-call | flops 4000000000 | bytes 8000000 | tf_op jit(solution)/shard_map/disc_rows/pallas_call | solution.py:493
  29.5 10.5 %all_to_all.20 = bf16[8,8,896]{2,1,0:T(8,128)(2,1)S(1)} all-to-all(bf16[8,8,896]{2,1,0:T(8,128)(2,1)} %bitcast.61), channel_id=1, replica_groups=mesh['clip'=4,'row'=8] {'row'}, dimensions={0} | all-to-all | bytes 229376 | tf_op jit(solution)/shard_map/all_to_all | solution.py:701
  40.0 2.3 %both_taps.1 = (f32[64,128]{1,0:T(8,128)S(1)}, f32[48,896]{1,0:T(8,128)S(1)}) custom-call(f32[48,896]{1,0:T(8,128)S(1)} %inner_rows.1.inner_ref, bf16[64,896]{1,0:T(8,128)(2,1)S(1)} %bitcast.50, bf16[12288,128]{1,0:T(8,128)(2,1)S(1)} %bitcast.49), custom_call_target="tpu_custom_call" | custom-call | flops 169869312 | bytes 4000000 | tf_op jit(solution)/shard_map/both_taps/pallas_call | solution.py:620
  42.3 9.3 %all_to_all.21 = f32[32,2,128]{2,1,0:T(2,128)S(1)} all-to-all(f32[32,2,128]{2,1,0:T(2,128)S(1)} %bitcast.55), channel_id=1, replica_groups=mesh['clip'=4,'row'=8] {'clip','row'}, dimensions={0} | all-to-all | bytes 65536 | tf_op jit(solution)/shard_map/all_to_all | solution.py:722
  51.6 0.6 broadcast_in_dim.102
  52.2 2.7 %all-to-all-start.3 = ((f32[32,2,128]{2,1,0:T(2,128)}), f32[32,2,128]{2,1,0:T(2,128)S(1)}, u32[]{:S(2)}, u32[]{:S(2)}) async-start(f32[32,2,128]{2,1,0:T(2,128)} %broadcast_in_dim.102), calls=%async_computation.3 | async-start | bytes 65536 | tf_op jit(solution)/shard_map/all_to_all | solution.py:722
  55.0 0.1 slice.24
  55.1 0.2 reshape.84
  55.3 0.7 %copy.43 = bf16[8,2,16,3,48]{4,2,3,1,0:T(8,128)(2,1)} copy(bf16[8,2,16,3,48]{4,2,0,1,3:T(8,128)(2,1)S(1)} %bitcast.56) | data formatting | bytes 147456 | tf_op jit(solution)/shard_map/transpose | solution.py:730
  56.0 1.9 %turn_taps.1.taps_ref = bf16[6144,128]{1,0:T(8,128)(2,1)S(1)} custom-call(f32[48,896]{1,0:T(8,128)S(1)} %get-tuple-element.18.rec_ref, bf16[64,896]{1,0:T(8,128)(2,1)S(1)} %bitcast.51), custom_call_target="tpu_custom_call" | custom-call | flops 169869312 | bytes 4000000 | tf_op jit(solution)/shard_map/turn_taps/pallas_call | solution.py:620
  57.9 4.1 %all-to-all-done.3 = f32[32,2,128]{2,1,0:T(2,128)S(1)} async-done(((f32[32,2,128]{2,1,0:T(2,128)}), f32[32,2,128]{2,1,0:T(2,128)S(1)}, u32[]{:S(2)}, u32[]{:S(2)}) %all-to-all-start.3) | async-done | bytes 32800 | tf_op jit(solution)/shard_map/all_to_all | solution.py:722
  62.0 2.8 %feature_pull.1 = (bf16[12288,128]{1,0:T(8,128)(2,1)}, f32[3,3,3,128]{3,2,1,0:T(4,128)}, f32[1,1]{1,0:T(1,128)}) custom-call(bf16[6144,128]{1,0:T(8,128)(2,1)S(1)} %turn_taps.1.taps_ref, f32[64,128]{1,0:T(8,128)S(1)} %bitcast.54, bf16[32,128]{1,0:T(8,128)(2,1)S(1)} %copy-done.3), custom_call_target="tpu_custom_call" | custom-call | flops 201326592 | bytes 6291456 | tf_op jit(solution)/shard_map/feature_pull/pallas_call | solution.py:667
  (33 shorter events, 0.3 us)
Async XLA Ops:
  0.6 11.6 %copy-start.8 = (pred[18,512]{1,0:T(8,128)(4,1)S(1)}, pred[18,512]{1,0:T(8,128)(4,1)}, u32[]{:S(2)}) copy-start(pred[18,512]{1,0:T(8,128)(4,1)} %constant.27.clone) | copy-start | bytes 27652
  0.6 11.7 %copy-start.10 = (pred[18,512]{1,0:T(8,128)(4,1)S(1)}, pred[18,512]{1,0:T(8,128)(4,1)}, u32[]{:S(2)}) copy-start(pred[18,512]{1,0:T(8,128)(4,1)} %constant.26.clone) | copy-start | bytes 27652
  0.7 11.7 %copy-start.9 = (pred[18,512]{1,0:T(8,128)(4,1)S(1)}, pred[18,512]{1,0:T(8,128)(4,1)}, u32[]{:S(2)}) copy-start(pred[18,512]{1,0:T(8,128)(4,1)} %constant.25.clone) | copy-start | bytes 27652
  0.7 11.8 %copy-start.7 = (pred[18,512]{1,0:T(8,128)(4,1)S(1)}, pred[18,512]{1,0:T(8,128)(4,1)}, u32[]{:S(2)}) copy-start(pred[18,512]{1,0:T(8,128)(4,1)} %constant.24.clone) | copy-start | bytes 27652
  0.7 13.8 %copy-start.1 = (bf16[1,16,16,3,48]{4,2,3,1,0:T(8,128)(2,1)S(1)}, bf16[1,16,16,3,48]{4,2,3,1,0:T(8,128)(2,1)}, u32[]{:S(2)}) copy-start(bf16[1,16,16,3,48]{4,2,3,1,0:T(8,128)(2,1)} %param.17) | copy-start | bytes 221188
  0.7 11.3 %copy-start.6 = (bf16[4,4,3,64]{3,1,2,0:T(4,128)(2,1)S(1)}, bf16[4,4,3,64]{3,1,2,0:T(4,128)(2,1)}, u32[]{:S(2)}) copy-start(bf16[4,4,3,64]{3,1,2,0:T(4,128)(2,1)} %param.19) | copy-start | bytes 18436
  0.7 12.4 %copy-start.5 = (bf16[4,4,512,1]{2,1,3,0:T(4,128)(2,1)S(1)}, bf16[4,4,512,1]{2,1,3,0:T(4,128)(2,1)}, u32[]{:S(2)}) copy-start(bf16[4,4,512,1]{2,1,3,0:T(4,128)(2,1)} %param.23) | copy-start | bytes 49156
  4.7 14.5 %all-to-all-start = ((bf16[8,8,896]{2,1,0:T(8,128)(2,1)}), bf16[8,8,896]{2,1,0:T(8,128)(2,1)S(1)}, u32[]{:S(2)}, u32[]{:S(2)}) async-start(bf16[8,8,896]{2,1,0:T(8,128)(2,1)} %bitcast.60), calls=%async_computation | async-start | bytes 229376 | tf_op jit(solution)/shard_map/all_to_all | solution.py:701
  14.5 0.9 %copy-start.2 = (f32[48,896]{1,0:T(8,128)S(1)}, f32[48,896]{1,0:T(8,128)}, u32[]{:S(2)}) copy-start(f32[48,896]{1,0:T(8,128)} %get-tuple-element.15.own_ref) | copy-start | bytes 516100
  19.2 0.6 copy-start.4
  19.9 20.1 %copy-start = (bf16[1,16,16,48,128]{4,3,2,1,0:T(8,128)(2,1)S(1)}, bf16[1,16,16,48,128]{4,3,2,1,0:T(8,128)(2,1)}, u32[]{:S(2)}) copy-start(bf16[1,16,16,48,128]{4,3,2,1,0:T(8,128)(2,1)} %param.16) | copy-start | bytes 9437188
  40.0 22.0 %copy-start.3 = (bf16[32,128]{1,0:T(8,128)(2,1)S(1)}, bf16[32,128]{1,0:T(8,128)(2,1)}, u32[]{:S(2)}) copy-start(bf16[32,128]{1,0:T(8,128)(2,1)} %get-tuple-element.20.weight_ref) | copy-start | bytes 24580
  52.2 9.8 %all-to-all-start.3 = ((f32[32,2,128]{2,1,0:T(2,128)}), f32[32,2,128]{2,1,0:T(2,128)S(1)}, u32[]{:S(2)}, u32[]{:S(2)}) async-start(f32[32,2,128]{2,1,0:T(2,128)} %broadcast_in_dim.102), calls=%async_computation.3 | async-start | bytes 65536 | tf_op jit(solution)/shard_map/all_to_all | solution.py:722

commit v5 on v4

--- a/solution.py
+++ b/solution.py
@@ -19,6 +19,7 @@
 VM = pl.BlockSpec(memory_space=pltpu.VMEM)
 HBM = pl.BlockSpec(memory_space=pl.ANY)
 WHOLE = pltpu.CompilerParams(vmem_limit_bytes=60 * 2**20)
+MOST = pltpu.CompilerParams(vmem_limit_bytes=119 * 2**19)
 PART = pltpu.CompilerParams(vmem_limit_bytes=24 * 2**20)
 
 
@@ -43,14 +44,13 @@
     pitch = out_ref.shape[1] // devices
     taps = flat_ref.shape[0]
     block_rows = pixels // cols
-    size = feat_ref.shape[0] // chunks
     copies = [
-        pltpu.make_async_copy(weight_hbm, weight_ref, sems.at[chunks]),
-        pltpu.make_async_copy(target_hbm, target_ref, sems.at[chunks + 1]),
-    ] + [
-        pltpu.make_async_copy(feat_hbm.at[pl.ds(i * size, size), :], feat_ref.at[pl.ds(i * size, size), :], sems.at[i])
-        for i in range(chunks)
+        pltpu.make_async_copy(weight_hbm, weight_ref, sems.at[frames]),
+        pltpu.make_async_copy(target_hbm, target_ref, sems.at[frames + 1]),
     ]
+    for slot in range(frames):
+        rows = pl.ds((slot % devices * group + slot // devices) * pixels, pixels)
+        copies.append(pltpu.make_async_copy(feat_hbm.at[rows, :], feat_ref.at[rows, :], sems.at[slot]))
     for copy in copies:
         copy.start()
     weight_scr[...] = jnp.zeros_like(weight_scr)
@@ -74,34 +74,42 @@
     edges = jnp.concatenate(edges, axis=1)
     for k in range(lanes // LANES):
         out_ref[k, pl.ds(3 * group, devices, stride=pitch), :] = edges[:, k * LANES : (k + 1) * LANES]
-    for frame in range(frames):
-        if frame % (frames // chunks) == 0:
-            copies[2 + frame // (frames // chunks)].wait()
-        product = mat(weight, feat_ref[frame * pixels : (frame + 1) * pixels, :], NT)
-        slot = slot_of(frame, devices, group)
-        for k in range(pieces):
-            taps_ref[k, pl.ds(slot, taps, stride=frames), :] = product[:, k * LANES : (k + 1) * LANES]
-    column = lax.broadcasted_iota(jnp.int32, (frames, pixels), 1) % cols
-
-    def tap(a, b, o):
-        rows = pl.ds(((a * 3 + b) * 3 + o) * frames, frames)
-        return jnp.concatenate([taps_ref[k, rows, :] for k in range(pieces)], axis=1)
-
-    for o in range(3):
-        total = None
-        for a in range(3):
-            part = tap(a, 1, o)
-            part = part + jnp.where(column == 0, 0.0, pltpu.roll(tap(a, 0, o), 1, 1))
-            part = part + jnp.where(column == cols - 1, 0.0, pltpu.roll(tap(a, 2, o), pixels - 1, 1))
-            part = jnp.concatenate([part, jnp.zeros((frames, lanes - pixels), F32)], axis=1)
-            if a < 2:
-                part = pltpu.roll(part, (2 - a) * cols, 1)
-            total = part if total is None else total + part
-        own_ref[o * frames : (o + 1) * frames, :] = total
-        for part in range(group):
-            rows = total[part * devices : (part + 1) * devices, :]
+    column = lax.broadcasted_iota(jnp.int32, (devices, pixels), 1) % cols
+
+    def finish(part):
+        def tap(a, b, o):
+            rows = pl.ds(((a * 3 + b) * 3 + o) * frames + part * devices, devices)
+            return jnp.concatenate([taps_ref[k, rows, :] for k in range(pieces)], axis=1)
+
+        for o in range(3):
+            total = None
+            for a in range(3):
+                term = tap(a, 1, o)
+                term = term + jnp.where(column == 0, 0.0, pltpu.roll(tap(a, 0, o), 1, 1))
+                term = term + jnp.where(column == cols - 1, 0.0, pltpu.roll(tap(a, 2, o), pixels - 1, 1))
+                term = jnp.concatenate([term, jnp.zeros((devices, lanes - pixels), F32)], axis=1)
+                if a < 2:
+                    term = pltpu.roll(term, (2 - a) * cols, 1)
+                total = term if total is None else total + term
+            at = o * frames + part * devices
+            own_ref[at : at + devices, :] = total
             for k in range(lanes // LANES):
-                out_ref[k, pl.ds(o * group + part, devices, stride=pitch), :] = rows[:, k * LANES : (k + 1) * LANES]
+                rows = pl.ds(o * group + part, devices, stride=pitch)
+                out_ref[k, rows, :] = total[:, k * LANES : (k + 1) * LANES]
+
+    step = frames // chunks
+    done = 0
+    for chunk in range(chunks):
+        for slot in range(chunk * step, (chunk + 1) * step):
+            copies[2 + slot].wait()
+        for slot in range(chunk * step, (chunk + 1) * step):
+            frame = slot % devices * group + slot // devices
+            product = mat(weight, feat_ref[frame * pixels : (frame + 1) * pixels, :], NT)
+            for k in range(pieces):
+                taps_ref[k, pl.ds(slot, taps, stride=frames), :] = product[:, k * LANES : (k + 1) * LANES]
+        while (done + 1) * devices <= chunk * step or (chunk == chunks - 1 and done < group):
+            finish(done)
+            done += 1
     for k in range(lanes // LANES):
         pay_ref[:, k * LANES : (k + 1) * LANES] = out_ref[k].astype(BF16)
 
@@ -129,7 +137,7 @@
             pltpu.VMEM((3 * pixels // cols * frames, LANES), F32),
             pltpu.VMEM((pixels // LANES, 32 * frames, LANES), F32),
             pltpu.VMEM((lanes // LANES, devices * pitch, LANES), F32),
-            pltpu.SemaphoreType.DMA((chunks + 2,)),
+            pltpu.SemaphoreType.DMA((frames + 2,)),
         ],
         compiler_params=WHOLE,
         cost_estimate=pl.CostEstimate(flops=2 * features.size * 27, bytes_accessed=2 * features.size, transcendentals=0),
@@ -518,7 +526,7 @@
             pltpu.VMEM((lanes // LANES, payload.shape[0], LANES), F32),
             pltpu.SemaphoreType.DMA((5,)),
         ],
-        compiler_params=WHOLE,
+        compiler_params=MOST,
         cost_estimate=pl.CostEstimate(flops=4 * 10**9, bytes_accessed=8 * 10**6, transcendentals=10**6),
         name="disc_rows",
     )(*args)
@@ -585,7 +593,7 @@
     rec_ref[...] = rec
     put_taps(rec, rec_taps, frames, cols, pieces, 32)
     pixels = pieces * LANES
-    total = jnp.zeros(part_ref.shape, F32)
+    total = jnp.zeros((64, feat_ref.shape[1]), F32)
     for frame in range(frames):
         rows = pl.ds(slot_of(frame, devices, group), 32, stride=frames)
         taps = jnp.concatenate(
@@ -596,7 +604,10 @@
             axis=0,
         )
         total = total + mat(taps.astype(BF16), feat_ref[frame * pixels : (frame + 1) * pixels, :])
-    part_ref[...] = total
+    blank = jnp.zeros((part_ref.shape[1] - 54, total.shape[1]), F32)
+    total = jnp.concatenate([total[0:27], total[32:59], blank], axis=0).astype(BF16)
+    for i in range(part_ref.shape[0]):
+        part_ref[i] = total
 
 
 def turn_kernel(
@@ -630,8 +641,10 @@
 
 
 def final_kernel(taps_ref, sums_ref, weight_ref, out_hbm, grad_ref, adapt_ref, both_ref, out_ref, sems, *, pixels, chunk):
-    half = weight_ref.shape[0]
-    rec, gan = sums_ref[0:half, :], sums_ref[half:, :]
+    total = sums_ref[0].astype(F32)
+    for i in range(1, sums_ref.shape[0]):
+        total = total + sums_ref[i].astype(F32)
+    rec, gan = total[0:27], total[27:54]
     norm = lambda values: jnp.sqrt(jnp.sum(jnp.sum(values * values, axis=1, keepdims=True), axis=0, keepdims=True))
     adaptive = norm(rec) / (norm(gan) + epsilon)
     grad = (rec + adaptive * gan) / pixels
@@ -713,15 +726,10 @@
     flops = 4 * features.size * 27
     part, rec_plane = taps_call(
         both_kernel, [VM, VM, VM], (inner, returned, feats),
-        (jax.ShapeDtypeStruct((64, channels), F32), jax.ShapeDtypeStruct(own.shape, F32)),
+        (jax.ShapeDtypeStruct((clips * devices, 56, channels), BF16), jax.ShapeDtypeStruct(own.shape, F32)),
         [taps_scratch, taps_scratch, plane_scratch], *sizes, flops, "both_taps",
     )
-    everyone = clips * devices
-    slices = up_to(part.size, everyone * LANES) // everyone // LANES
-    part = jnp.pad(part, ((0, everyone * slices - part.shape[0]), (0, 0))).reshape(everyone, slices, LANES)
-    share = lambda values: lax.all_to_all(values, ("clip", "row"), split_axis=0, concat_axis=0, tiled=True)
-    mine = jnp.sum(share(part), axis=0)
-    sums = share(jnp.broadcast_to(mine[None], part.shape)).reshape(everyone * slices, LANES)[:64]
+    sums = lax.all_to_all(part, ("clip", "row"), split_axis=0, concat_axis=0, tiled=True)
     taps = taps_call(
         turn_kernel, [VM, VM], (rec_plane, returned), jax.ShapeDtypeStruct((feats.shape[0] // 2, LANES), BF16),
         [taps_scratch, taps_scratch, plane_scratch], *sizes, flops, "turn_taps",

time: 65.4 us -> 64.1 us (0.980)
  blocking collectives: 19.8 us -> 10.5 us
  waiting for transfers between devices: 7.65 us -> 15.4 us
  Pallas kernels: 20.8 us -> 21.6 us
    all_to_all x1 -> x0, blocking collectives: 9.29 us -> none  [per_device(): lax.all_to_all(values, ('clip', 'row'), split_axis=0, concat_axis=0, tile...]
    all_to_all x1, waiting for transfers between devices: 4.1 us -> 11.9 us  [per_device(): lax.all_to_all(part, ('clip', 'row'), split_axis=0, concat_axis=0, tiled=...]
    pallas_call x2, Pallas kernels: 4.15 us -> 4.84 us  [taps_call(): pl.pallas_call(functools.partial(kernel, frames=frames, devices=devices,...]
where the time goes in v5:
time: 64.1 us; the launch traced here: 63.6 us
  Pallas kernels  21.6 us (34%)
  waiting for transfers between devices  15.4 us (24%)
  blocking collectives  10.5 us (16%)
  starting transfers between devices  10.1 us (16%)
  local copies, waits for them, and re-layouts  4.38 us (7%)
  between operations  1.06 us (2%)
    all_to_all x1, waiting for transfers between devices, per_device(): lax.all_to_all(part, ('clip', 'row'), split_axis=0, concat_axis=0, tiled=...  11.9 us
    all_to_all x1, blocking collectives, per_device(): lax.all_to_all(values.reshape(devices, pitch, lanes), 'row', split_axis=0...  10.5 us
    pallas_call x1, Pallas kernels, disc_call(): pl.pallas_call(functools.partial(disc_kernel, devices=devices, group=grou...  9.56 us
    all_to_all x1, starting transfers between devices, per_device(): lax.all_to_all(values.reshape(devices, pitch, lanes), 'row', split_axis=0...  7.29 us
    pallas_call x2, Pallas kernels, taps_call(): pl.pallas_call(functools.partial(kernel, frames=frames, devices=devices,...  4.84 us
    pallas_call x1, Pallas kernels, forward_call(): pl.pallas_call(functools.partial(forward_kernel, frames=frames, devices=d...  4.08 us
    all_to_all x1, waiting for transfers between devices, per_device(): lax.all_to_all(values.reshape(devices, pitch, lanes), 'row', split_axis=0...  3.55 us
    pallas_call x1, Pallas kernels, final_call(): pl.pallas_call(functools.partial(final_kernel, pixels=pixels, chunk=chunk...  2.87 us
  transfers between devices with their start and end apart: 2, of which 2 were waited for; matrix products, arithmetic and copies ran while one was open for 5% of the time, Pallas kernels for 3%

profile of v5, /device:TPU:0, one launch (start us, length us, event | category | flops | bytes accessed | tf_op | source)
XLA Modules:
  0.0 63.6 jit_solution(5656890812105866425)
XLA Ops:
  0.6 0.0 copy-start.8
  0.6 0.0 copy-start.10
  0.7 0.0 copy-start.9
  0.7 4.1 %forward_taps.1 = (bf16[64,896]{1,0:T(8,128)(2,1)}, f32[48,896]{1,0:T(8,128)}, bf16[32,128]{1,0:T(8,128)(2,1)}) custom-call(bf16[12288,128]{1,0:T(8,128)(2,1)} %bitcast.46, bf16[16,3,16,48]{3,2,1,0:T(8,128)(2,1)} %bitcast.50, bf16[3,3,3,128]{3,2,1,0:T(4,128)(2,1)} %weight_hbm.1), custom_call_target="tpu_custom_call" | custom-call | flops 84934656 | bytes 3145728 | tf_op jit(solution)/shard_map/forward_taps/pallas_call | solution.py:121
  4.8 7.3 %all-to-all-start = ((bf16[8,8,896]{2,1,0:T(8,128)(2,1)}), bf16[8,8,896]{2,1,0:T(8,128)(2,1)S(1)}, u32[]{:S(2)}, u32[]{:S(2)}) async-start(bf16[8,8,896]{2,1,0:T(8,128)(2,1)} %bitcast.56), calls=%async_computation | async-start | bytes 229376 | tf_op jit(solution)/shard_map/all_to_all | solution.py:714
  12.1 0.1 tile.10
  12.2 0.1 fusion.3
  12.6 0.5 fusion.2
  13.2 0.6 reshape.71.head_ref
  13.8 0.7 %pad.4.clone = bf16[4,64,512]{2,1,0:T(8,128)(2,1)} pad(bf16[4,54,512]{2,1,0:T(8,128)(2,1)S(1)} %copy.44, bf16[]{:T(256)} %constant.9.clone.1), padding=0_0x0_10x0_0 | pad | bytes 483330 | tf_op jit(solution)/shard_map/jit(_pad)/pad | solution.py:475
  14.5 0.9 %copy-done.2 = f32[48,896]{1,0:T(8,128)S(1)} copy-done((f32[48,896]{1,0:T(8,128)S(1)}, f32[48,896]{1,0:T(8,128)}, u32[]{:S(2)}) %copy-start.2) | copy-done | bytes 172056
  15.5 0.3 inner_rows.1.inner_ref
  15.8 3.6 %all-to-all-done = bf16[8,8,896]{2,1,0:T(8,128)(2,1)S(1)} async-done(((bf16[8,8,896]{2,1,0:T(8,128)(2,1)}), bf16[8,8,896]{2,1,0:T(8,128)(2,1)S(1)}, u32[]{:S(2)}, u32[]{:S(2)}) %all-to-all-start) | async-done | bytes 114720 | tf_op jit(solution)/shard_map/all_to_all | solution.py:714
  19.3 0.6 %copy-done.4 = bf16[8,8,896]{2,1,0:T(8,128)(2,1)} copy-done((bf16[8,8,896]{2,1,0:T(8,128)(2,1)}, bf16[8,8,896]{2,1,0:T(8,128)(2,1)S(1)}, u32[]{:S(2)}) %copy-start.4) | copy-done | bytes 114712
  20.0 9.6 %disc_rows.1 = bf16[64,896]{1,0:T(8,128)(2,1)} custom-call(bf16[64,896]{1,0:T(8,128)(2,1)} %bitcast.55, bf16[256,288]{1,0:T(8,128)(2,1)} %constant.20.clone.gather_ref, bf16[144,1024]{1,0:T(8,128)(2,1)} %constant.21.clone.window_ref, bf16[256,512]{1,0:T(8,128)(2,1)} %bitcast.53, bf16[1024,128]{1,0:T(8,128)(2,1)} %bitcast.61, bf16[2048,256]{1,0:T(8,128)(2,1)} %bitcast.60, ...), custom_call_target="tpu_custom_call" | custom-call | flops 4000000000 | bytes 8000000 | tf_op jit(solution)/shard_map/disc_rows/pallas_call | solution.py:501
  29.5 10.5 %all_to_all.15 = bf16[8,8,896]{2,1,0:T(8,128)(2,1)S(1)} all-to-all(bf16[8,8,896]{2,1,0:T(8,128)(2,1)} %bitcast.57), channel_id=1, replica_groups=mesh['clip'=4,'row'=8] {'row'}, dimensions={0} | all-to-all | bytes 229376 | tf_op jit(solution)/shard_map/all_to_all | solution.py:714
  40.1 3.0 %both_taps.1 = (bf16[32,56,128]{2,1,0:T(8,128)(2,1)}, f32[48,896]{1,0:T(8,128)S(1)}) custom-call(f32[48,896]{1,0:T(8,128)S(1)} %inner_rows.1.inner_ref, bf16[64,896]{1,0:T(8,128)(2,1)S(1)} %bitcast.48, bf16[12288,128]{1,0:T(8,128)(2,1)S(1)} %bitcast.47), custom_call_target="tpu_custom_call" | custom-call | flops 169869312 | bytes 4000000 | tf_op jit(solution)/shard_map/both_taps/pallas_call | solution.py:631
  43.0 2.8 %all-to-all-start.2 = ((bf16[32,56,128]{2,1,0:T(8,128)(2,1)}), bf16[32,56,128]{2,1,0:T(8,128)(2,1)S(1)}, u32[]{:S(2)}, u32[]{:S(2)}) async-start(bf16[32,56,128]{2,1,0:T(8,128)(2,1)} %get-tuple-element.19), calls=%async_computation.2 | async-start | bytes 917504 | tf_op jit(solution)/shard_map/all_to_all | solution.py:732
  45.8 0.1 slice.24
  45.9 0.2 reshape.75
  46.2 0.7 %copy.43 = bf16[8,2,16,3,48]{4,2,3,1,0:T(8,128)(2,1)} copy(bf16[8,2,16,3,48]{4,2,0,1,3:T(8,128)(2,1)S(1)} %bitcast.52) | data formatting | bytes 147456 | tf_op jit(solution)/shard_map/transpose | solution.py:738
  46.8 1.9 %turn_taps.1.taps_ref = bf16[6144,128]{1,0:T(8,128)(2,1)S(1)} custom-call(f32[48,896]{1,0:T(8,128)S(1)} %get-tuple-element.18.rec_ref, bf16[64,896]{1,0:T(8,128)(2,1)S(1)} %bitcast.49), custom_call_target="tpu_custom_call" | custom-call | flops 169869312 | bytes 4000000 | tf_op jit(solution)/shard_map/turn_taps/pallas_call | solution.py:631
  48.7 11.9 %all-to-all-done.2.sums_ref = bf16[32,56,128]{2,1,0:T(8,128)(2,1)S(1)} async-done(((bf16[32,56,128]{2,1,0:T(8,128)(2,1)}), bf16[32,56,128]{2,1,0:T(8,128)(2,1)S(1)}, u32[]{:S(2)}, u32[]{:S(2)}) %all-to-all-start.2) | async-done | bytes 458784 | tf_op jit(solution)/shard_map/all_to_all | solution.py:732
  60.6 2.9 %feature_pull.1 = (bf16[12288,128]{1,0:T(8,128)(2,1)}, f32[3,3,3,128]{3,2,1,0:T(4,128)}, f32[1,1]{1,0:T(1,128)}) custom-call(bf16[6144,128]{1,0:T(8,128)(2,1)S(1)} %turn_taps.1.taps_ref, bf16[32,56,128]{2,1,0:T(8,128)(2,1)S(1)} %all-to-all-done.2.sums_ref, bf16[32,128]{1,0:T(8,128)(2,1)S(1)} %copy-done.3), custom_call_target="tpu_custom_call" | custom-call | flops 201326592 | bytes 6291456 | tf_op jit(solution)/shard_map/feature_pull/pallas_call | solution.py:680
  (30 shorter events, 0.3 us)
Async XLA Ops:
  0.6 11.7 %copy-start.8 = (pred[18,512]{1,0:T(8,128)(4,1)S(1)}, pred[18,512]{1,0:T(8,128)(4,1)}, u32[]{:S(2)}) copy-start(pred[18,512]{1,0:T(8,128)(4,1)} %constant.25.clone) | copy-start | bytes 27652
  0.6 11.7 %copy-start.10 = (pred[18,512]{1,0:T(8,128)(4,1)S(1)}, pred[18,512]{1,0:T(8,128)(4,1)}, u32[]{:S(2)}) copy-start(pred[18,512]{1,0:T(8,128)(4,1)} %constant.24.clone) | copy-start | bytes 27652
  0.7 11.8 %copy-start.9 = (pred[18,512]{1,0:T(8,128)(4,1)S(1)}, pred[18,512]{1,0:T(8,128)(4,1)}, u32[]{:S(2)}) copy-start(pred[18,512]{1,0:T(8,128)(4,1)} %constant.23.clone) | copy-start | bytes 27652
  0.7 11.8 %copy-start.7 = (pred[18,512]{1,0:T(8,128)(4,1)S(1)}, pred[18,512]{1,0:T(8,128)(4,1)}, u32[]{:S(2)}) copy-start(pred[18,512]{1,0:T(8,128)(4,1)} %constant.22.clone) | copy-start | bytes 27652
  0.7 13.9 %copy-start.1 = (bf16[1,16,16,3,48]{4,2,3,1,0:T(8,128)(2,1)S(1)}, bf16[1,16,16,3,48]{4,2,3,1,0:T(8,128)(2,1)}, u32[]{:S(2)}) copy-start(bf16[1,16,16,3,48]{4,2,3,1,0:T(8,128)(2,1)} %param.17) | copy-start | bytes 221188
  0.7 11.4 %copy-start.6 = (bf16[4,4,3,64]{3,1,2,0:T(4,128)(2,1)S(1)}, bf16[4,4,3,64]{3,1,2,0:T(4,128)(2,1)}, u32[]{:S(2)}) copy-start(bf16[4,4,3,64]{3,1,2,0:T(4,128)(2,1)} %param.19) | copy-start | bytes 18436
  0.7 12.5 %copy-start.5 = (bf16[4,4,512,1]{2,1,3,0:T(4,128)(2,1)S(1)}, bf16[4,4,512,1]{2,1,3,0:T(4,128)(2,1)}, u32[]{:S(2)}) copy-start(bf16[4,4,512,1]{2,1,3,0:T(4,128)(2,1)} %param.23) | copy-start | bytes 49156
  4.8 14.5 %all-to-all-start = ((bf16[8,8,896]{2,1,0:T(8,128)(2,1)}), bf16[8,8,896]{2,1,0:T(8,128)(2,1)S(1)}, u32[]{:S(2)}, u32[]{:S(2)}) async-start(bf16[8,8,896]{2,1,0:T(8,128)(2,1)} %bitcast.56), calls=%async_computation | async-start | bytes 229376 | tf_op jit(solution)/shard_map/all_to_all | solution.py:714
  14.5 0.9 %copy-start.2 = (f32[48,896]{1,0:T(8,128)S(1)}, f32[48,896]{1,0:T(8,128)}, u32[]{:S(2)}) copy-start(f32[48,896]{1,0:T(8,128)} %get-tuple-element.15.own_ref) | copy-start | bytes 516100
  19.3 0.6 %copy-start.4 = (bf16[8,8,896]{2,1,0:T(8,128)(2,1)}, bf16[8,8,896]{2,1,0:T(8,128)(2,1)S(1)}, u32[]{:S(2)}) copy-start(bf16[8,8,896]{2,1,0:T(8,128)(2,1)S(1)} %all-to-all-done) | copy-start | bytes 344068
  20.0 20.1 %copy-start = (bf16[1,16,16,48,128]{4,3,2,1,0:T(8,128)(2,1)S(1)}, bf16[1,16,16,48,128]{4,3,2,1,0:T(8,128)(2,1)}, u32[]{:S(2)}) copy-start(bf16[1,16,16,48,128]{4,3,2,1,0:T(8,128)(2,1)} %param.16) | copy-start | bytes 9437188
  40.1 20.5 %copy-start.3 = (bf16[32,128]{1,0:T(8,128)(2,1)S(1)}, bf16[32,128]{1,0:T(8,128)(2,1)}, u32[]{:S(2)}) copy-start(bf16[32,128]{1,0:T(8,128)(2,1)} %get-tuple-element.20.weight_ref) | copy-start | bytes 24580
  43.0 17.6 %all-to-all-start.2 = ((bf16[32,56,128]{2,1,0:T(8,128)(2,1)}), bf16[32,56,128]{2,1,0:T(8,128)(2,1)S(1)}, u32[]{:S(2)}, u32[]{:S(2)}) async-start(bf16[32,56,128]{2,1,0:T(8,128)(2,1)} %get-tuple-element.19), calls=%async_computation.2 | async-start | bytes 917504 | tf_op jit(solution)/shard_map/all_to_all | solution.py:732

commit v6 on v5

--- a/solution.py
+++ b/solution.py
@@ -51,8 +51,8 @@
     for slot in range(frames):
         rows = pl.ds((slot % devices * group + slot // devices) * pixels, pixels)
         copies.append(pltpu.make_async_copy(feat_hbm.at[rows, :], feat_ref.at[rows, :], sems.at[slot]))
-    for copy in copies:
-        copy.start()
+    for i, copy in enumerate(copies):
+        copy.start(priority=i % 2)
     weight_scr[...] = jnp.zeros_like(weight_scr)
     out_ref[...] = jnp.zeros_like(out_ref)
     copies[0].wait()
@@ -193,22 +193,17 @@
     return (values * logistic).astype(BF16), logistic * (1.0 + values * (1.0 - logistic))
 
 
-def edge_planes(zin, zout, image, scatter, devices, group, cols, span, lanes, pitch):
-    zout[...] = jnp.zeros_like(zout)
-    step = group * devices
-    first = mat(scatter[0 : 2 * step], image)
-    last = mat(scatter[(span - 2) * step :], image)
+def edge_planes(zin, zout, first, last, devices, group, cols, lanes, pitch):
     row = pl.ds(3 * group, devices, stride=pitch)
     target = jnp.concatenate([zin[k, row, :] for k in range(lanes // LANES)], axis=1)
     outer, inner = [], []
-    for e, rows, out_at, in_at, move in ((0, first, 0, 1, 1), (1, last, 1, 0, -1)):
+    for e, rows, other, move in ((0, first, last, 1), (1, last, first, -1)):
         for o in range(3):
             for part in range(group):
-                pick = lambda i: rows[i * step + part * devices : i * step + (part + 1) * devices, o * cols : (o + 1) * cols]
                 at = ((1 - e) * 3 * group + o * group + part) * cols
-                wanted = shift_rows(target[:, at : at + cols], move, devices)
-                outer.append(loss_scale * (pick(out_at) - wanted))
-                inner.append(pick(in_at))
+                near = other[part][:, o * cols : (o + 1) * cols] - target[:, at : at + cols]
+                outer.append(shift_rows(loss_scale * near, move, devices))
+                inner.append(rows[part][:, o * cols : (o + 1) * cols])
     for i, pieces in enumerate((outer, inner)):
         pieces.append(jnp.zeros((devices, lanes - 6 * group * cols), F32))
         plane = jnp.concatenate(pieces, axis=1)
@@ -217,8 +212,8 @@
 
 
 def disc_kernel(
-    pay_ref, gather_ref, window_ref, band_ref, second_hbm, third_hbm, fourth_hbm, head_ref, unwindow_hbm, scatter_hbm, out_ref,
-    zin, second, third, fourth, unwindow, scatter, rows_in, act_one, slope_one, cols_two, act_two, slope_two, act_three, cols_four,
+    pay_ref, head_ref, window_hbm, band_hbm, second_hbm, third_hbm, fourth_hbm, unwindow_hbm, out_ref,
+    zin, window, band_ref, second, third, fourth, unwindow, rows_in, act_one, slope_one, cols_two, act_two, slope_two, act_three, cols_four,
     pull_four, pull_three, pull_two, zout, sems, *, devices, group, cols, block_rows, period,
 ):
     lanes = pay_ref.shape[1]
@@ -230,34 +225,47 @@
     d2, d3, d4 = second.shape[1], third.shape[1], fourth.shape[1]
     x1, x2, x3 = cols // 2, cols // 4, cols // 8
     x4 = x3 - 1
-    copies = [
-        pltpu.make_async_copy(source, target, sems.at[i])
-        for i, (source, target) in enumerate(
-            (
-                (second_hbm, second),
-                (third_hbm, third),
-                (fourth_hbm, fourth),
-                (unwindow_hbm, unwindow),
-                (scatter_hbm, scatter),
-            )
-        )
-    ]
-    for i in (4, 0, 1, 2, 3):
-        copies[i].start()
+    pairs = (
+        (window_hbm, window),
+        (band_hbm, band_ref),
+        (second_hbm, second),
+        (third_hbm, third),
+        (fourth_hbm, fourth),
+        (unwindow_hbm, unwindow),
+    )
+    copies = [pltpu.make_async_copy(source, target, sems.at[i]) for i, (source, target) in enumerate(pairs)]
+    for i, copy in enumerate(copies):
+        copy.start(priority=i % 2)
+    cells = block_rows // 8
+    spot = lambda y, part: pl.ds((y % 8 * group + part) * period + y // 8, devices, stride=cells)
     for k in range(lanes // LANES):
         zin[k] = pay_ref[:, k * LANES : (k + 1) * LANES].astype(F32)
+    zout[...] = jnp.zeros_like(zout)
+    firsts, lasts = [], []
     for part in range(group):
         planes = []
         for o in range(3):
             pieces = [zin[k, pl.ds(o * group + part, devices, stride=pitch), :] for k in range(lanes // LANES)]
             planes.append(jnp.concatenate(pieces, axis=1))
-        for i in range(span):
-            row = jnp.concatenate([plane[:, i * cols : (i + 1) * cols] for plane in planes], axis=1)
-            rows_in[pl.ds((i * group + part) * devices, devices), :] = row
-    image = mat(gather_ref[...], rows_in[...].astype(BF16)).astype(BF16)
-    wins = mat(image, window_ref[...])
-    copies[4].wait()
-    edge_planes(zin, zout, image, scatter, devices, group, cols, span, lanes, pitch)
+        lines = [
+            jnp.concatenate(
+                [plane[:, i * cols : (i + 1) * cols] for plane in planes]
+                + [jnp.zeros((devices, 2 * LANES - wide), F32)],
+                axis=1,
+            )
+            for i in range(span)
+        ]
+        lines[1] = lines[1] + shift_rows(lines[span - 1], 1, devices)
+        lines[block_rows] = lines[block_rows] + shift_rows(lines[0], -1, devices)
+        for y in range(block_rows):
+            for k in range(2):
+                rows_in[k, spot(y, part), :] = lines[y + 1][:, k * LANES : (k + 1) * LANES]
+        firsts.append(lines[1])
+        lasts.append(lines[block_rows])
+    image = jnp.concatenate([rows_in[0], rows_in[1]], axis=1)[:, :wide].astype(BF16)
+    copies[0].wait()
+    copies[1].wait()
+    wins = mat(image, window[...])
     ext = [wins[r * unit : (r + 1) * unit] for r in range(8)]
     ext = [shift_rows(ext[7], 1, period)] + ext + [shift_rows(ext[0], -1, period)]
     width_one = act_one.shape[1]
@@ -284,7 +292,7 @@
         actual = act.astype(F32)
         act_one[0:unit, start:end] = shift_rows(actual[3 * unit :], 1, period).astype(BF16)
         act_one[5 * unit :, start:end] = shift_rows(actual[:unit], -1, period).astype(BF16)
-    copies[0].wait()
+    copies[2].wait()
     for x in range(x2):
         for a in range(4):
             for p in range(2):
@@ -303,7 +311,7 @@
         act_two[unit : 3 * unit, at] = block
         act_two[0:unit, at] = shift_rows(actual[unit:], 1, period).astype(BF16)
         act_two[3 * unit :, at] = shift_rows(actual[:unit], -1, period).astype(BF16)
-    copies[1].wait()
+    copies[3].wait()
     left = jnp.concatenate(
         [
             jnp.concatenate([act_two[a * unit : (a + 1) * unit, 2 * x * d2 : (2 * x + 4) * d2] for a in range(4)], axis=1)
@@ -326,8 +334,9 @@
             cols_four[x * unit : (x + 1) * unit, a * 4 * d3 : (a + 1) * 4 * d3] = act_three[
                 a * unit : (a + 1) * unit, x * d3 : (x + 4) * d3
             ]
-    copies[2].wait()
+    copies[4].wait()
     pre = mat(cols_four[...], fourth[...])
+    edge_planes(zin, zout, firsts, lasts, devices, group, cols, lanes, pitch)
     _, slope = gate_of(pre)
     row = lax.broadcasted_iota(jnp.int32, (unit, d4), 0) % period
     head = head_ref[...].astype(F32) * -loss_scale
@@ -397,7 +406,7 @@
         )
         strips.append((both * slope_one[:, 2 * k * d1 : (2 * k + 2) * d1]).astype(BF16))
     cot = jnp.concatenate(strips, axis=1)
-    copies[3].wait()
+    copies[5].wait()
     sums = []
     for k in range(-(-width_one // strip)):
         start, end = k * strip, min((k + 1) * strip, width_one)
@@ -419,32 +428,24 @@
     phases = [even[r // 2] if r % 2 == 0 else odd[(r + 1) // 2] for r in range(8)]
     phases[0] = phases[0] + shift_rows(even[4], 1, period)
     phases[7] = phases[7] + shift_rows(odd[0], -1, period)
-    image = jnp.concatenate(phases, axis=0).astype(BF16)
-    rows = mat(scatter[...], image)
-    for part_at in range(group):
-        picked = [rows[(i * group + part_at) * devices : (i * group + part_at + 1) * devices] for i in range(span)]
+    image = jnp.concatenate(phases, axis=0)
+    image = jnp.concatenate([image, jnp.zeros((image.shape[0], 2 * LANES - wide), F32)], axis=1)
+    for k in range(2):
+        rows_in[k] = image[:, k * LANES : (k + 1) * LANES]
+    for part in range(group):
+        lines = [
+            jnp.concatenate([rows_in[k, spot(y, part), :] for k in range(2)], axis=1)[:, :wide]
+            for y in range(block_rows)
+        ]
+        lines = [shift_rows(lines[-1], 1, devices)] + lines + [shift_rows(lines[0], -1, devices)]
         for o in range(3):
-            plane = [piece[:, o * cols : (o + 1) * cols] for piece in picked]
+            plane = [line[:, o * cols : (o + 1) * cols] for line in lines]
             plane.append(jnp.zeros((devices, lanes - span * cols), F32))
             plane = jnp.concatenate(plane, axis=1)
             for k in range(lanes // LANES):
-                zout[k, pl.ds(o * group + part_at, devices, stride=pitch), :] = plane[:, k * LANES : (k + 1) * LANES]
+                zout[k, pl.ds(o * group + part, devices, stride=pitch), :] = plane[:, k * LANES : (k + 1) * LANES]
     for k in range(lanes // LANES):
         out_ref[:, k * LANES : (k + 1) * LANES] = zout[k].astype(BF16)
-
-
-def row_maps(devices, group, block_rows):
-    height = devices * block_rows
-    period = height // 8
-    span = block_rows + 2
-    gather = np.zeros((8 * group * period, span * group * devices), np.float32)
-    for device in range(devices):
-        for i in range(span):
-            y = device * block_rows + i - 1
-            if 0 <= y < height:
-                for part in range(group):
-                    gather[((y % 8) * group + part) * period + y // 8, (i * group + part) * devices + device] = 1.0
-    return gather
 
 
 def windows_of(cols, d1):
@@ -482,20 +483,17 @@
     d1, d2, d3, d4 = first.shape[-1], second.shape[-1], third.shape[-1], fourth.shape[-1]
     x2, x3 = cols // 4, cols // 8
     x4 = x3 - 1
-    gather = row_maps(devices, group, block_rows)
     window, unwindow = windows_of(cols, d1)
     width_one = (cols // 2 + 2) * d1
     args = (
         payload,
-        jnp.asarray(gather, BF16),
+        head.reshape(16, d4),
         jnp.asarray(window, BF16),
         band_of(first),
         second.reshape(16 * d1, d2),
         third.reshape(16 * d2, d3),
         fourth.reshape(16 * d3, d4),
-        head.reshape(16, d4),
         jnp.asarray(unwindow, BF16),
-        jnp.asarray(gather.T, BF16),
     )
     lanes = payload.shape[1]
     return pl.pallas_call(
@@ -503,16 +501,17 @@
             disc_kernel, devices=devices, group=group, cols=cols, block_rows=block_rows, period=period
         ),
         out_shape=jax.ShapeDtypeStruct(payload.shape, BF16),
-        in_specs=[VM, VM, VM, VM, HBM, HBM, HBM, VM, HBM, HBM],
+        in_specs=[VM, VM] + [HBM] * 6,
         out_specs=VM,
         scratch_shapes=[
             pltpu.VMEM((lanes // LANES, payload.shape[0], LANES), F32),
+            pltpu.VMEM(window.shape, BF16),
+            pltpu.VMEM((2 * LANES, 8 * d1), BF16),
             pltpu.VMEM((16 * d1, d2), BF16),
             pltpu.VMEM((16 * d2, d3), BF16),
             pltpu.VMEM((16 * d3, d4), BF16),
             pltpu.VMEM(unwindow.shape, BF16),
-            pltpu.VMEM(gather.T.shape, BF16),
-            pltpu.VMEM((gather.shape[1], 3 * cols), F32),
+            pltpu.VMEM((2, 8 * unit, LANES), F32),
             pltpu.VMEM((6 * unit, width_one), BF16),
             pltpu.VMEM((4 * unit, width_one), F32),
             pltpu.VMEM((x2 * 2 * unit, 16 * d1), BF16),
@@ -524,7 +523,7 @@
             pltpu.VMEM((x3 * unit, 16 * d2), F32),
             pltpu.VMEM((x2 * 2 * unit, 16 * d1), F32),
             pltpu.VMEM((lanes // LANES, payload.shape[0], LANES), F32),
-            pltpu.SemaphoreType.DMA((5,)),
+            pltpu.SemaphoreType.DMA((6,)),
         ],
         compiler_params=MOST,
         cost_estimate=pl.CostEstimate(flops=4 * 10**9, bytes_accessed=8 * 10**6, transcendentals=10**6),
@@ -669,7 +668,7 @@
         out_ref[2 * pair * chunk : (2 * pair + 1) * chunk] = product[:, :channels]
         out_ref[(2 * pair + 1) * chunk : (2 * pair + 2) * chunk] = product[:, channels:]
         stores.append(pltpu.make_async_copy(out_ref.at[rows], out_hbm.at[rows], sems.at[pair]))
-        stores[-1].start()
+        stores[-1].start(priority=pair % 2)
     for copy in stores:
         copy.wait()
 
@@ -700,7 +699,8 @@
 def per_device(
     features, target, conv_weight, disc_first, disc_second, disc_third, disc_fourth, disc_head
 ):
-    devices = lax.axis_size("row")
+    row = ("far", "near")
+    devices = lax.axis_size(row)
     clips = lax.axis_size("clip")
     _, frames, block_rows, cols, channels = features.shape
     group = frames // devices
@@ -712,7 +712,7 @@
     wanted = target[0].transpose(0, 2, 1, 3)
     payload, own, weight = forward_call(feats, wanted, conv_weight, frames, devices, group, cols, lanes, pitch)
     trade = lambda values: lax.all_to_all(
-        values.reshape(devices, pitch, lanes), "row", split_axis=0, concat_axis=0, tiled=True
+        values.reshape(devices, pitch, lanes), row, split_axis=0, concat_axis=0, tiled=True
     ).reshape(devices * pitch, lanes)
     arrived = trade(payload)
     inner = inner_call(own, wanted, frames, devices, group, block_rows, cols)
@@ -726,10 +726,11 @@
     flops = 4 * features.size * 27
     part, rec_plane = taps_call(
         both_kernel, [VM, VM, VM], (inner, returned, feats),
-        (jax.ShapeDtypeStruct((clips * devices, 56, channels), BF16), jax.ShapeDtypeStruct(own.shape, F32)),
+        (jax.ShapeDtypeStruct((clips * lax.axis_size("near"), 56, channels), BF16), jax.ShapeDtypeStruct(own.shape, F32)),
         [taps_scratch, taps_scratch, plane_scratch], *sizes, flops, "both_taps",
     )
-    sums = lax.all_to_all(part, ("clip", "row"), split_axis=0, concat_axis=0, tiled=True)
+    share = lambda values, axes: lax.all_to_all(values, axes, split_axis=0, concat_axis=0, tiled=True)
+    sums = share(sum_call(share(part, ("clip", "near")), lax.axis_size("far")), "far")
     taps = taps_call(
         turn_kernel, [VM, VM], (rec_plane, returned), jax.ShapeDtypeStruct((feats.shape[0] // 2, LANES), BF16),
         [taps_scratch, taps_scratch, plane_scratch], *sizes, flops, "turn_taps",
@@ -741,11 +742,34 @@
     return (feature_grad.reshape(features.shape), image_back, weight_grad, adaptive[0, 0])
 
 
+def sum_kernel(parts_ref, out_ref):
+    total = parts_ref[0].astype(F32)
+    for i in range(1, parts_ref.shape[0]):
+        total = total + parts_ref[i].astype(F32)
+    total = total.astype(BF16)
+    for i in range(out_ref.shape[0]):
+        out_ref[i] = total
+
+
+def sum_call(parts, copies):
+    return pl.pallas_call(
+        sum_kernel,
+        out_shape=jax.ShapeDtypeStruct((copies,) + parts.shape[1:], BF16),
+        in_specs=[VM],
+        out_specs=VM,
+        compiler_params=PART,
+        name="sum_parts",
+    )(parts)
+
+
 def solution(mesh):
-    rows = P("clip", None, "row", None, None)
+    clips, devices = mesh.shape["clip"], mesh.shape["row"]
+    near = 2 if devices % 2 == 0 else 1
+    split = jax.sharding.Mesh(mesh.devices.reshape(clips, devices // near, near), ("clip", "far", "near"))
+    rows = P("clip", None, ("far", "near"), None, None)
     return jax.shard_map(
         per_device,
-        mesh=mesh,
+        mesh=split,
         in_specs=(rows, rows, P(), P(), P(), P(), P(), P()),
         out_specs=(rows, rows, P(), P()),
         check_vma=False,

time: 64.1 us -> 64.5 us (level)
  waiting for transfers between devices: 15.4 us -> 6.16 us
  blocking collectives: 10.5 us -> 18 us
  Pallas kernels: 21.6 us -> 23.1 us
  starting transfers between devices: 10.1 us -> 10.8 us
    all_to_all x2, waiting for transfers between devices: 15.4 us -> 6.16 us  [the longest x1 3.55 us: per_device(): lax.all_to_all(values.reshape(devices, pitch, lanes), row, split_axis=0,...]
    all_to_all x1 -> x2, blocking collectives: 10.5 us -> 18 us  [the longest x1 10.5 us: per_device(): lax.all_to_all(values.reshape(devices, pitch, lanes), row, split_axis=0,...]
    pallas_call x1, Pallas kernels: 9.56 us -> 10.7 us  [disc_call(): pl.pallas_call(functools.partial(disc_kernel, devices=devices, group=grou...]
    pallas_call x2, Pallas kernels: 4.84 us -> 4.15 us  [taps_call(): pl.pallas_call(functools.partial(kernel, frames=frames, devices=devices,...]
    all_to_all x2, starting transfers between devices: 10.1 us -> 10.8 us  [the longest x1 7.29 us: per_device(): lax.all_to_all(values.reshape(devices, pitch, lanes), row, split_axis=0,...]
where the time goes in v6:
time: 64.5 us; the launch traced here: 64 us
  Pallas kernels  23.1 us (36%)
  blocking collectives  18 us (28%)
  starting transfers between devices  10.8 us (17%)
  waiting for transfers between devices  6.16 us (10%)
  local copies, waits for them, and re-layouts  4.38 us (7%)
  between operations  1.07 us (2%)
    pallas_call x1, Pallas kernels, disc_call(): pl.pallas_call(functools.partial(disc_kernel, devices=devices, group=grou...  10.7 us
    all_to_all x1, blocking collectives, per_device(): lax.all_to_all(values.reshape(devices, pitch, lanes), row, split_axis=0,...  10.5 us
    all_to_all x1, blocking collectives, per_device(): lax.all_to_all(values, axes, split_axis=0, concat_axis=0, tiled=True)  7.47 us
    all_to_all x1, starting transfers between devices, per_device(): lax.all_to_all(values.reshape(devices, pitch, lanes), row, split_axis=0,...  7.29 us
    pallas_call x1, Pallas kernels, forward_call(): pl.pallas_call(functools.partial(forward_kernel, frames=frames, devices=d...  4.5 us
    pallas_call x2, Pallas kernels, taps_call(): pl.pallas_call(functools.partial(kernel, frames=frames, devices=devices,...  4.15 us
    all_to_all x1, waiting for transfers between devices, per_device(): lax.all_to_all(values.reshape(devices, pitch, lanes), row, split_axis=0,...  3.55 us
    all_to_all x1, starting transfers between devices, per_device(): lax.all_to_all(values, axes, split_axis=0, concat_axis=0, tiled=True)  3.46 us
  transfers between devices with their start and end apart: 2, of which 2 were waited for; matrix products, arithmetic and copies ran while one was open for 5% of the time, Pallas kernels for 3%

profile of v6, /device:TPU:0, one launch (start us, length us, event | category | flops | bytes accessed | tf_op | source)
XLA Modules:
  0.0 64.0 jit_solution(13533981714420151403)
XLA Ops:
  0.6 0.0 copy-start.8
  0.7 4.5 %forward_taps.1 = (bf16[64,896]{1,0:T(8,128)(2,1)}, f32[48,896]{1,0:T(8,128)}, bf16[32,128]{1,0:T(8,128)(2,1)}) custom-call(bf16[12288,128]{1,0:T(8,128)(2,1)} %bitcast.46, bf16[16,3,16,48]{3,2,1,0:T(8,128)(2,1)} %bitcast.50, bf16[3,3,3,128]{3,2,1,0:T(4,128)(2,1)} %weight_hbm.1), custom_call_target="tpu_custom_call" | custom-call | flops 84934656 | bytes 3145728 | tf_op jit(solution)/shard_map/forward_taps/pallas_call | solution.py:121
  5.2 7.3 %all-to-all-start = ((bf16[8,8,896]{2,1,0:T(8,128)(2,1)}), bf16[8,8,896]{2,1,0:T(8,128)(2,1)S(1)}, u32[]{:S(2)}, u32[]{:S(2)}) async-start(bf16[8,8,896]{2,1,0:T(8,128)(2,1)} %bitcast.56), calls=%async_computation | async-start | bytes 229376 | tf_op jit(solution)/shard_map/all_to_all | solution.py:714
  12.5 0.1 tile.10
  12.7 0.1 fusion.3
  13.0 0.5 fusion.2
  13.6 0.6 reshape.67.head_ref
  14.2 0.7 %pad.4.clone = bf16[4,64,512]{2,1,0:T(8,128)(2,1)} pad(bf16[4,54,512]{2,1,0:T(8,128)(2,1)S(1)} %copy.42, bf16[]{:T(256)} %constant.7.clone.1), padding=0_0x0_10x0_0 | pad | bytes 483330 | tf_op jit(solution)/shard_map/jit(_pad)/pad | solution.py:476
  15.0 0.9 %copy-done.2 = f32[48,896]{1,0:T(8,128)S(1)} copy-done((f32[48,896]{1,0:T(8,128)S(1)}, f32[48,896]{1,0:T(8,128)}, u32[]{:S(2)}) %copy-start.2) | copy-done | bytes 172056
  15.9 0.3 inner_rows.1.inner_ref
  16.2 3.6 %all-to-all-done = bf16[8,8,896]{2,1,0:T(8,128)(2,1)S(1)} async-done(((bf16[8,8,896]{2,1,0:T(8,128)(2,1)}), bf16[8,8,896]{2,1,0:T(8,128)(2,1)S(1)}, u32[]{:S(2)}, u32[]{:S(2)}) %all-to-all-start) | async-done | bytes 114720 | tf_op jit(solution)/shard_map/all_to_all | solution.py:714
  19.7 0.6 %copy-done.4 = bf16[8,8,896]{2,1,0:T(8,128)(2,1)} copy-done((bf16[8,8,896]{2,1,0:T(8,128)(2,1)}, bf16[8,8,896]{2,1,0:T(8,128)(2,1)S(1)}, u32[]{:S(2)}) %copy-start.4) | copy-done | bytes 114712
  20.4 10.7 %disc_rows.1 = bf16[64,896]{1,0:T(8,128)(2,1)} custom-call(bf16[64,896]{1,0:T(8,128)(2,1)} %bitcast.55, bf16[16,512]{1,0:T(8,128)(2,1)} %reshape.67.head_ref, bf16[144,1024]{1,0:T(8,128)(2,1)} %constant.16.clone.window_hbm, bf16[256,512]{1,0:T(8,128)(2,1)} %bitcast.53, bf16[1024,128]{1,0:T(8,128)(2,1)} %bitcast.61, bf16[2048,256]{1,0:T(8,128)(2,1)} %bitcast.60, ...), custom_call_target="tpu_custom_call" | custom-call | flops 4000000000 | bytes 8000000 | tf_op jit(solution)/shard_map/disc_rows/pallas_call | solution.py:499
  31.1 10.5 %all_to_all.20 = bf16[8,8,896]{2,1,0:T(8,128)(2,1)S(1)} all-to-all(bf16[8,8,896]{2,1,0:T(8,128)(2,1)} %bitcast.57), channel_id=1, replica_groups=mesh['clip'=4,'far'=4,'near'=2] {'far','near'}, dimensions={0} | all-to-all | bytes 229376 | tf_op jit(solution)/shard_map/all_to_all | solution.py:714
  41.6 2.3 %both_taps.1 = (bf16[8,56,128]{2,1,0:T(8,128)(2,1)S(1)}, f32[48,896]{1,0:T(8,128)S(1)}) custom-call(f32[48,896]{1,0:T(8,128)S(1)} %inner_rows.1.inner_ref, bf16[64,896]{1,0:T(8,128)(2,1)S(1)} %bitcast.48, bf16[12288,128]{1,0:T(8,128)(2,1)S(1)} %bitcast.47), custom_call_target="tpu_custom_call" | custom-call | flops 169869312 | bytes 4000000 | tf_op jit(solution)/shard_map/both_taps/pallas_call | solution.py:630
  43.9 7.5 %all_to_all.21.parts_ref = bf16[8,56,128]{2,1,0:T(8,128)(2,1)S(1)} all-to-all(bf16[8,56,128]{2,1,0:T(8,128)(2,1)S(1)} %get-tuple-element.19), channel_id=1, replica_groups=mesh['clip'=4,'far'=4,'near'=2] {'clip','near'}, dimensions={0} | all-to-all | bytes 229376 | tf_op jit(solution)/shard_map/all_to_all | solution.py:732
  51.4 0.6 %sum_parts.1 = bf16[4,56,128]{2,1,0:T(8,128)(2,1)} custom-call(bf16[8,56,128]{2,1,0:T(8,128)(2,1)S(1)} %all_to_all.21.parts_ref), custom_call_target="tpu_custom_call" | custom-call | tf_op jit(solution)/shard_map/sum_parts/pallas_call | solution.py:755
  52.0 3.5 %all-to-all-start.3 = ((bf16[4,56,128]{2,1,0:T(8,128)(2,1)}), bf16[4,56,128]{2,1,0:T(8,128)(2,1)S(1)}, u32[]{:S(2)}, u32[]{:S(2)}) async-start(bf16[4,56,128]{2,1,0:T(8,128)(2,1)} %sum_parts.1), calls=%async_computation.3 | async-start | bytes 114688 | tf_op jit(solution)/shard_map/all_to_all | solution.py:732
  55.5 0.1 slice.24
  55.6 0.2 reshape.75
  55.8 0.7 %copy.41 = bf16[8,2,16,3,48]{4,2,3,1,0:T(8,128)(2,1)} copy(bf16[8,2,16,3,48]{4,2,0,1,3:T(8,128)(2,1)S(1)} %bitcast.52) | data formatting | bytes 147456 | tf_op jit(solution)/shard_map/transpose | solution.py:739
  56.5 1.9 %turn_taps.1.taps_ref = bf16[6144,128]{1,0:T(8,128)(2,1)S(1)} custom-call(f32[48,896]{1,0:T(8,128)S(1)} %get-tuple-element.18.rec_ref, bf16[64,896]{1,0:T(8,128)(2,1)S(1)} %bitcast.49), custom_call_target="tpu_custom_call" | custom-call | flops 169869312 | bytes 4000000 | tf_op jit(solution)/shard_map/turn_taps/pallas_call | solution.py:630
  58.4 2.6 %all-to-all-done.3.sums_ref = bf16[4,56,128]{2,1,0:T(8,128)(2,1)S(1)} async-done(((bf16[4,56,128]{2,1,0:T(8,128)(2,1)}), bf16[4,56,128]{2,1,0:T(8,128)(2,1)S(1)}, u32[]{:S(2)}, u32[]{:S(2)}) %all-to-all-start.3) | async-done | bytes 57376 | tf_op jit(solution)/shard_map/all_to_all | solution.py:732
  61.0 2.8 %feature_pull.1 = (bf16[12288,128]{1,0:T(8,128)(2,1)}, f32[3,3,3,128]{3,2,1,0:T(4,128)}, f32[1,1]{1,0:T(1,128)}) custom-call(bf16[6144,128]{1,0:T(8,128)(2,1)S(1)} %turn_taps.1.taps_ref, bf16[4,56,128]{2,1,0:T(8,128)(2,1)S(1)} %all-to-all-done.3.sums_ref, bf16[32,128]{1,0:T(8,128)(2,1)S(1)} %copy-done.3), custom_call_target="tpu_custom_call" | custom-call | flops 201326592 | bytes 6291456 | tf_op jit(solution)/shard_map/feature_pull/pallas_call | solution.py:679
  (32 shorter events, 0.3 us)
Async XLA Ops:
  0.6 12.1 %copy-start.8 = (pred[18,512]{1,0:T(8,128)(4,1)S(1)}, pred[18,512]{1,0:T(8,128)(4,1)}, u32[]{:S(2)}) copy-start(pred[18,512]{1,0:T(8,128)(4,1)} %constant.20.clone) | copy-start | bytes 27652
  0.6 12.2 %copy-start.10 = (pred[18,512]{1,0:T(8,128)(4,1)S(1)}, pred[18,512]{1,0:T(8,128)(4,1)}, u32[]{:S(2)}) copy-start(pred[18,512]{1,0:T(8,128)(4,1)} %constant.19.clone) | copy-start | bytes 27652
  0.7 12.2 %copy-start.9 = (pred[18,512]{1,0:T(8,128)(4,1)S(1)}, pred[18,512]{1,0:T(8,128)(4,1)}, u32[]{:S(2)}) copy-start(pred[18,512]{1,0:T(8,128)(4,1)} %constant.18.clone) | copy-start | bytes 27652
  0.7 12.3 %copy-start.7 = (pred[18,512]{1,0:T(8,128)(4,1)S(1)}, pred[18,512]{1,0:T(8,128)(4,1)}, u32[]{:S(2)}) copy-start(pred[18,512]{1,0:T(8,128)(4,1)} %constant.17.clone) | copy-start | bytes 27652
  0.7 14.3 %copy-start.1 = (bf16[1,16,16,3,48]{4,2,3,1,0:T(8,128)(2,1)S(1)}, bf16[1,16,16,3,48]{4,2,3,1,0:T(8,128)(2,1)}, u32[]{:S(2)}) copy-start(bf16[1,16,16,3,48]{4,2,3,1,0:T(8,128)(2,1)} %param.15) | copy-start | bytes 221188
  0.7 11.8 %copy-start.6 = (bf16[4,4,3,64]{3,1,2,0:T(4,128)(2,1)S(1)}, bf16[4,4,3,64]{3,1,2,0:T(4,128)(2,1)}, u32[]{:S(2)}) copy-start(bf16[4,4,3,64]{3,1,2,0:T(4,128)(2,1)} %param.17) | copy-start | bytes 18436
  0.7 12.9 %copy-start.5 = (bf16[4,4,512,1]{2,1,3,0:T(4,128)(2,1)S(1)}, bf16[4,4,512,1]{2,1,3,0:T(4,128)(2,1)}, u32[]{:S(2)}) copy-start(bf16[4,4,512,1]{2,1,3,0:T(4,128)(2,1)} %param.21) | copy-start | bytes 49156
  5.2 14.5 %all-to-all-start = ((bf16[8,8,896]{2,1,0:T(8,128)(2,1)}), bf16[8,8,896]{2,1,0:T(8,128)(2,1)S(1)}, u32[]{:S(2)}, u32[]{:S(2)}) async-start(bf16[8,8,896]{2,1,0:T(8,128)(2,1)} %bitcast.56), calls=%async_computation | async-start | bytes 229376 | tf_op jit(solution)/shard_map/all_to_all | solution.py:714
  15.0 0.9 %copy-start.2 = (f32[48,896]{1,0:T(8,128)S(1)}, f32[48,896]{1,0:T(8,128)}, u32[]{:S(2)}) copy-start(f32[48,896]{1,0:T(8,128)} %get-tuple-element.15.own_ref) | copy-start | bytes 516100
  19.7 0.6 %copy-start.4 = (bf16[8,8,896]{2,1,0:T(8,128)(2,1)}, bf16[8,8,896]{2,1,0:T(8,128)(2,1)S(1)}, u32[]{:S(2)}) copy-start(bf16[8,8,896]{2,1,0:T(8,128)(2,1)S(1)} %all-to-all-done) | copy-start | bytes 344068
  20.4 21.2 %copy-start = (bf16[1,16,16,48,128]{4,3,2,1,0:T(8,128)(2,1)S(1)}, bf16[1,16,16,48,128]{4,3,2,1,0:T(8,128)(2,1)}, u32[]{:S(2)}) copy-start(bf16[1,16,16,48,128]{4,3,2,1,0:T(8,128)(2,1)} %param.14) | copy-start | bytes 9437188
  41.6 19.4 %copy-start.3 = (bf16[32,128]{1,0:T(8,128)(2,1)S(1)}, bf16[32,128]{1,0:T(8,128)(2,1)}, u32[]{:S(2)}) copy-start(bf16[32,128]{1,0:T(8,128)(2,1)} %get-tuple-element.20.weight_ref) | copy-start | bytes 24580
  52.0 9.0 %all-to-all-start.3 = ((bf16[4,56,128]{2,1,0:T(8,128)(2,1)}), bf16[4,56,128]{2,1,0:T(8,128)(2,1)S(1)}, u32[]{:S(2)}, u32[]{:S(2)}) async-start(bf16[4,56,128]{2,1,0:T(8,128)(2,1)} %sum_parts.1), calls=%async_computation.3 | async-start | bytes 114688 | tf_op jit(solution)/shard_map/all_to_all | solution.py:732

commit v7 on v6

--- a/solution.py
+++ b/solution.py
@@ -36,13 +36,13 @@
 
 
 def forward_kernel(
-    feat_hbm, target_hbm, weight_hbm, pay_ref, own_ref, flat_ref, feat_ref, target_ref, weight_ref, weight_scr, target_scr,
+    feat_hbm, target_hbm, weight_hbm, pay_ref, feat_ref, target_ref, weight_ref, weight_scr, target_scr,
     taps_ref, out_ref, sems, *, frames, devices, group, cols, lanes, chunks,
 ):
     pixels = feat_ref.shape[0] // frames
     pieces = pixels // LANES
     pitch = out_ref.shape[1] // devices
-    taps = flat_ref.shape[0]
+    taps = weight_scr.shape[0]
     block_rows = pixels // cols
     copies = [
         pltpu.make_async_copy(weight_hbm, weight_ref, sems.at[frames]),
@@ -51,8 +51,8 @@
     for slot in range(frames):
         rows = pl.ds((slot % devices * group + slot // devices) * pixels, pixels)
         copies.append(pltpu.make_async_copy(feat_hbm.at[rows, :], feat_ref.at[rows, :], sems.at[slot]))
-    for i, copy in enumerate(copies):
-        copy.start(priority=i % 2)
+    for copy in copies:
+        copy.start()
     weight_scr[...] = jnp.zeros_like(weight_scr)
     out_ref[...] = jnp.zeros_like(out_ref)
     copies[0].wait()
@@ -62,7 +62,6 @@
             at = (a * 3 + b) * 3
             weight_scr[at : at + 3, :] = weight_ref[a, b].astype(F32)
     weight = weight_scr[...].astype(BF16)
-    flat_ref[...] = weight
     target_scr[:, 0:cols] = target_ref[...].reshape(target_scr.shape[0], cols).astype(F32)
     edges = []
     for y in (0, block_rows - 1):
@@ -91,8 +90,6 @@
                 if a < 2:
                     term = pltpu.roll(term, (2 - a) * cols, 1)
                 total = term if total is None else total + term
-            at = o * frames + part * devices
-            own_ref[at : at + devices, :] = total
             for k in range(lanes // LANES):
                 rows = pl.ds(o * group + part, devices, stride=pitch)
                 out_ref[k, rows, :] = total[:, k * LANES : (k + 1) * LANES]
@@ -117,18 +114,14 @@
 def forward_call(features, target, weight, frames, devices, group, cols, lanes, pitch):
     pixels = features.shape[0] // frames
     channels = features.shape[1]
-    chunks = 4
+    chunks = 2
     return pl.pallas_call(
         functools.partial(
             forward_kernel, frames=frames, devices=devices, group=group, cols=cols, lanes=lanes, chunks=chunks
         ),
-        out_shape=(
-            jax.ShapeDtypeStruct((devices * pitch, lanes), BF16),
-            jax.ShapeDtypeStruct((3 * frames, lanes), F32),
-            jax.ShapeDtypeStruct((32, channels), BF16),
-        ),
+        out_shape=jax.ShapeDtypeStruct((devices * pitch, lanes), BF16),
         in_specs=[HBM, HBM, HBM],
-        out_specs=(VM,) * 3,
+        out_specs=VM,
         scratch_shapes=[
             pltpu.VMEM(features.shape, BF16),
             pltpu.VMEM(target.shape, BF16),
@@ -145,10 +138,13 @@
     )(features, target, weight)
 
 
-def inner_kernel(own_ref, target_ref, inner_ref, scr, *, frames, devices, group, block_rows, cols):
+def inner_kernel(pay_ref, target_ref, inner_ref, scr, zin, *, frames, devices, group, block_rows, cols):
     scr[:, 0:cols] = target_ref[...].reshape(scr.shape[0], cols).astype(F32)
     stride = group * 3 * block_rows
-    lanes = own_ref.shape[1]
+    lanes = pay_ref.shape[1]
+    pitch = pay_ref.shape[0] // devices
+    for k in range(lanes // LANES):
+        zin[k] = pay_ref[:, k * LANES : (k + 1) * LANES].astype(F32)
     for o in range(3):
         for part in range(group):
             at = o * frames + part * devices
@@ -161,23 +157,28 @@
             wanted = jnp.concatenate(rows, axis=1)
             lane = lax.broadcasted_iota(jnp.int32, wanted.shape, 1)
             inside = (lane >= 2 * cols) & (lane < block_rows * cols)
-            own = jnp.where(inside, own_ref[at : at + devices, :], 0.0)
-            inner_ref[at : at + devices, :] = loss_scale * (own - wanted)
-
-
-def inner_call(own, target, frames, devices, group, block_rows, cols):
+            row = pl.ds(o * group + part, devices, stride=pitch)
+            own = jnp.concatenate([zin[k, row, :] for k in range(lanes // LANES)], axis=1)
+            inner_ref[at : at + devices, :] = loss_scale * (jnp.where(inside, own, 0.0) - wanted)
+
+
+def inner_call(payload, target, frames, devices, group, block_rows, cols):
+    lanes = payload.shape[1]
     return pl.pallas_call(
         functools.partial(
             inner_kernel, frames=frames, devices=devices, group=group, block_rows=block_rows, cols=cols
         ),
-        out_shape=jax.ShapeDtypeStruct(own.shape, F32),
+        out_shape=jax.ShapeDtypeStruct((3 * frames, lanes), F32),
         in_specs=[VM, VM],
         out_specs=VM,
-        scratch_shapes=[pltpu.VMEM((frames * 3 * block_rows, LANES), F32)],
+        scratch_shapes=[
+            pltpu.VMEM((frames * 3 * block_rows, LANES), F32),
+            pltpu.VMEM((lanes // LANES, payload.shape[0], LANES), F32),
+        ],
         compiler_params=PART,
         cost_estimate=pl.CostEstimate(flops=10**8, bytes_accessed=10**6, transcendentals=0),
         name="inner_rows",
-    )(own, target)
+    )(payload, target)
 
 
 def shift_rows(values, step, period):
@@ -189,7 +190,7 @@
 
 
 def gate_of(values):
-    logistic = 1.0 / (1.0 + jnp.exp(-values))
+    logistic = 0.5 + 0.5 * jnp.tanh(0.5 * values)
     return (values * logistic).astype(BF16), logistic * (1.0 + values * (1.0 - logistic))
 
 
@@ -234,8 +235,8 @@
         (unwindow_hbm, unwindow),
     )
     copies = [pltpu.make_async_copy(source, target, sems.at[i]) for i, (source, target) in enumerate(pairs)]
-    for i, copy in enumerate(copies):
-        copy.start(priority=i % 2)
+    for copy in copies:
+        copy.start()
     cells = block_rows // 8
     spot = lambda y, part: pl.ds((y % 8 * group + part) * period + y // 8, devices, stride=cells)
     for k in range(lanes // LANES):
@@ -639,7 +640,14 @@
     )(*operands)
 
 
-def final_kernel(taps_ref, sums_ref, weight_ref, out_hbm, grad_ref, adapt_ref, both_ref, out_ref, sems, *, pixels, chunk):
+def final_kernel(
+    taps_ref, sums_ref, weight_ref, out_hbm, grad_ref, adapt_ref, weight_scr, both_ref, out_ref, sems, *, pixels, chunk
+):
+    weight_scr[...] = jnp.zeros_like(weight_scr)
+    for a in range(3):
+        for b in range(3):
+            at = (a * 3 + b) * 3
+            weight_scr[at : at + 3, :] = weight_ref[a, b].astype(F32)
     total = sums_ref[0].astype(F32)
     for i in range(1, sums_ref.shape[0]):
         total = total + sums_ref[i].astype(F32)
@@ -652,7 +660,7 @@
             at = (a * 3 + b) * 3
             grad_ref[a, b] = grad[at : at + 3, :]
     adapt_ref[...] = adaptive
-    weight = weight_ref[...]
+    weight = weight_scr[...].astype(BF16)
     padded, channels = weight.shape
     scaled = (adaptive * weight.astype(F32)).astype(BF16)
     both_ref[...] = jnp.zeros_like(both_ref)
@@ -668,13 +676,13 @@
         out_ref[2 * pair * chunk : (2 * pair + 1) * chunk] = product[:, :channels]
         out_ref[(2 * pair + 1) * chunk : (2 * pair + 2) * chunk] = product[:, channels:]
         stores.append(pltpu.make_async_copy(out_ref.at[rows], out_hbm.at[rows], sems.at[pair]))
-        stores[-1].start(priority=pair % 2)
+        stores[-1].start()
     for copy in stores:
         copy.wait()
 
 
 def final_call(taps, sums, weight, pixels, chunk):
-    padded, channels = weight.shape
+    padded, channels = 32, weight.shape[-1]
     rows = 2 * taps.shape[0]
     return pl.pallas_call(
         functools.partial(final_kernel, pixels=pixels, chunk=chunk),
@@ -686,6 +694,7 @@
         in_specs=[VM] * 3,
         out_specs=(HBM, VM, VM),
         scratch_shapes=[
+            pltpu.VMEM((padded, channels), F32),
             pltpu.VMEM((4 * padded, 2 * channels), BF16),
             pltpu.VMEM((rows, channels), BF16),
             pltpu.SemaphoreType.DMA((rows // (2 * chunk),)),
@@ -710,12 +719,12 @@
     sizes = (frames, devices, group, cols, block_rows)
     feats = features.reshape(frames * block_rows * cols, channels)
     wanted = target[0].transpose(0, 2, 1, 3)
-    payload, own, weight = forward_call(feats, wanted, conv_weight, frames, devices, group, cols, lanes, pitch)
+    payload = forward_call(feats, wanted, conv_weight, frames, devices, group, cols, lanes, pitch)
     trade = lambda values: lax.all_to_all(
         values.reshape(devices, pitch, lanes), row, split_axis=0, concat_axis=0, tiled=True
     ).reshape(devices * pitch, lanes)
     arrived = trade(payload)
-    inner = inner_call(own, wanted, frames, devices, group, block_rows, cols)
+    inner = inner_call(payload, wanted, frames, devices, group, block_rows, cols)
     arrived, inner = lax.optimization_barrier((arrived, inner))
     sent = disc_call(
         arrived, disc_first, disc_second, disc_third, disc_fourth, disc_head, devices, group, cols, block_rows
@@ -726,7 +735,7 @@
     flops = 4 * features.size * 27
     part, rec_plane = taps_call(
         both_kernel, [VM, VM, VM], (inner, returned, feats),
-        (jax.ShapeDtypeStruct((clips * lax.axis_size("near"), 56, channels), BF16), jax.ShapeDtypeStruct(own.shape, F32)),
+        (jax.ShapeDtypeStruct((clips * lax.axis_size("near"), 56, channels), BF16), jax.ShapeDtypeStruct(inner.shape, F32)),
         [taps_scratch, taps_scratch, plane_scratch], *sizes, flops, "both_taps",
     )
     share = lambda values, axes: lax.all_to_all(values, axes, split_axis=0, concat_axis=0, tiled=True)
@@ -738,7 +747,7 @@
     image_back = returned.reshape(devices, pitch, lanes)[:, : 3 * group, cols : (block_rows + 1) * cols]
     image_back = image_back.reshape(devices, 3, group, block_rows, cols).transpose(0, 2, 3, 1, 4)
     image_back = image_back.reshape(1, frames, block_rows, 3, cols)
-    feature_grad, weight_grad, adaptive = final_call(taps, sums, weight, pixels, block_rows * cols)
+    feature_grad, weight_grad, adaptive = final_call(taps, sums, conv_weight, pixels, block_rows * cols)
     return (feature_grad.reshape(features.shape), image_back, weight_grad, adaptive[0, 0])
 
 

time: 64.5 us -> 63.3 us (0.981)
  Pallas kernels: 23.1 us -> 21.2 us
  local copies, waits for them, and re-layouts: 4.38 us -> 5.94 us
  waiting for transfers between devices: 6.16 us -> 5.24 us
    unnamed x23 -> x27, local copies, waits for them, and re-layouts: 1.65 us -> 3.21 us
    pallas_call x1, Pallas kernels: 10.7 us -> 9.26 us  [disc_call(): pl.pallas_call(functools.partial(disc_kernel, devices=devices, group=grou...]
    all_to_all x1, waiting for transfers between devices: 2.6 us -> 1.68 us  [per_device(): lax.all_to_all(values, axes, split_axis=0, concat_axis=0, tiled=True)]
where the time goes in v7:
time: 63.3 us; the launch traced here: 62.7 us
  Pallas kernels  21.2 us (33%)
  blocking collectives  18 us (28%)
  starting transfers between devices  10.7 us (17%)
  local copies, waits for them, and re-layouts  5.94 us (9%)
  waiting for transfers between devices  5.24 us (8%)
  between operations  1.08 us (2%)
    all_to_all x1, blocking collectives, per_device(): lax.all_to_all(values.reshape(devices, pitch, lanes), row, split_axis=0,...  10.5 us
    pallas_call x1, Pallas kernels, disc_call(): pl.pallas_call(functools.partial(disc_kernel, devices=devices, group=grou...  9.26 us
    all_to_all x1, blocking collectives, per_device(): lax.all_to_all(values, axes, split_axis=0, concat_axis=0, tiled=True)  7.45 us
    all_to_all x1, starting transfers between devices, per_device(): lax.all_to_all(values.reshape(devices, pitch, lanes), row, split_axis=0,...  7.29 us
    pallas_call x2, Pallas kernels, taps_call(): pl.pallas_call(functools.partial(kernel, frames=frames, devices=devices,...  4.15 us
    pallas_call x1, Pallas kernels, forward_call(): pl.pallas_call(functools.partial(forward_kernel, frames=frames, devices=d...  4.06 us
    all_to_all x1, waiting for transfers between devices, per_device(): lax.all_to_all(values.reshape(devices, pitch, lanes), row, split_axis=0,...  3.56 us
    all_to_all x1, starting transfers between devices, per_device(): lax.all_to_all(values, axes, split_axis=0, concat_axis=0, tiled=True)  3.46 us
  transfers between devices with their start and end apart: 2, of which 2 were waited for; matrix products, arithmetic and copies ran while one was open for 5% of the time, Pallas kernels for 3%

profile of v7, /device:TPU:0, one launch (start us, length us, event | category | flops | bytes accessed | tf_op | source)
XLA Modules:
  0.0 62.7 jit_solution(8069176495805061758)
XLA Ops:
  0.7 4.1 %forward_taps.1.pay_ref = bf16[64,896]{1,0:T(8,128)(2,1)} custom-call(bf16[12288,128]{1,0:T(8,128)(2,1)} %bitcast.46, bf16[16,3,16,48]{3,2,1,0:T(8,128)(2,1)} %bitcast.51, bf16[3,3,3,128]{3,2,1,0:T(4,128)(2,1)} %weight_ref.1), custom_call_target="tpu_custom_call" | custom-call | flops 84934656 | bytes 3145728 | tf_op jit(solution)/shard_map/forward_taps/pallas_call | solution.py:118
  4.8 7.3 %all-to-all-start = ((bf16[8,8,896]{2,1,0:T(8,128)(2,1)}), bf16[8,8,896]{2,1,0:T(8,128)(2,1)S(1)}, u32[]{:S(2)}, u32[]{:S(2)}) async-start(bf16[8,8,896]{2,1,0:T(8,128)(2,1)} %bitcast.50), calls=%async_computation | async-start | bytes 229376 | tf_op jit(solution)/shard_map/all_to_all | solution.py:723
  12.1 0.1 tile.10
  12.6 0.5 fusion.2
  13.2 0.6 reshape.67.head_ref
  13.8 0.7 %pad.4.clone = bf16[4,64,512]{2,1,0:T(8,128)(2,1)} pad(bf16[4,54,512]{2,1,0:T(8,128)(2,1)S(1)} %copy.42, bf16[]{:T(256)} %constant.7.clone.1), padding=0_0x0_10x0_0 | pad | bytes 483330 | tf_op jit(solution)/shard_map/jit(_pad)/pad | solution.py:477
  14.5 0.9 %copy-done.1 = bf16[64,896]{1,0:T(8,128)(2,1)S(1)} copy-done((bf16[64,896]{1,0:T(8,128)(2,1)S(1)}, bf16[64,896]{1,0:T(8,128)(2,1)}, u32[]{:S(2)}) %copy-start.1) | copy-done | bytes 114712
  15.4 0.3 inner_rows.1.inner_ref
  15.7 3.6 %all-to-all-done = bf16[8,8,896]{2,1,0:T(8,128)(2,1)S(1)} async-done(((bf16[8,8,896]{2,1,0:T(8,128)(2,1)}), bf16[8,8,896]{2,1,0:T(8,128)(2,1)S(1)}, u32[]{:S(2)}, u32[]{:S(2)}) %all-to-all-start) | async-done | bytes 114720 | tf_op jit(solution)/shard_map/all_to_all | solution.py:723
  19.3 0.6 %copy-done.6 = bf16[8,8,896]{2,1,0:T(8,128)(2,1)} copy-done((bf16[8,8,896]{2,1,0:T(8,128)(2,1)}, bf16[8,8,896]{2,1,0:T(8,128)(2,1)S(1)}, u32[]{:S(2)}) %copy-start.6) | copy-done | bytes 114712
  20.0 9.3 %disc_rows.1 = bf16[64,896]{1,0:T(8,128)(2,1)} custom-call(bf16[64,896]{1,0:T(8,128)(2,1)} %bitcast.56, bf16[16,512]{1,0:T(8,128)(2,1)} %reshape.67.head_ref, bf16[144,1024]{1,0:T(8,128)(2,1)} %constant.16.clone.window_hbm, bf16[256,512]{1,0:T(8,128)(2,1)} %bitcast.54, bf16[1024,128]{1,0:T(8,128)(2,1)} %bitcast.61, bf16[2048,256]{1,0:T(8,128)(2,1)} %bitcast.60, ...), custom_call_target="tpu_custom_call" | custom-call | flops 4000000000 | bytes 8000000 | tf_op jit(solution)/shard_map/disc_rows/pallas_call | solution.py:500
  29.2 10.5 %all_to_all.20 = bf16[8,8,896]{2,1,0:T(8,128)(2,1)S(1)} all-to-all(bf16[8,8,896]{2,1,0:T(8,128)(2,1)} %bitcast.57), channel_id=1, replica_groups=mesh['clip'=4,'far'=4,'near'=2] {'far','near'}, dimensions={0} | all-to-all | bytes 229376 | tf_op jit(solution)/shard_map/all_to_all | solution.py:723
  39.7 2.3 %both_taps.1 = (bf16[8,56,128]{2,1,0:T(8,128)(2,1)S(1)}, f32[48,896]{1,0:T(8,128)S(1)}) custom-call(f32[48,896]{1,0:T(8,128)S(1)} %inner_rows.1.inner_ref, bf16[64,896]{1,0:T(8,128)(2,1)S(1)} %bitcast.48, bf16[12288,128]{1,0:T(8,128)(2,1)S(1)} %bitcast.47), custom_call_target="tpu_custom_call" | custom-call | flops 169869312 | bytes 4000000 | tf_op jit(solution)/shard_map/both_taps/pallas_call | solution.py:631
  42.0 0.7 %copy-done.3 = f32[48,896]{1,0:T(8,128)} copy-done((f32[48,896]{1,0:T(8,128)}, f32[48,896]{1,0:T(8,128)S(1)}, u32[]{:S(2)}) %copy-start.3) | copy-done | bytes 172056
  42.7 7.5 %all_to_all.21.parts_ref = bf16[8,56,128]{2,1,0:T(8,128)(2,1)S(1)} all-to-all(bf16[8,56,128]{2,1,0:T(8,128)(2,1)S(1)} %get-tuple-element.14), channel_id=1, replica_groups=mesh['clip'=4,'far'=4,'near'=2] {'clip','near'}, dimensions={0} | all-to-all | bytes 229376 | tf_op jit(solution)/shard_map/all_to_all | solution.py:741
  50.2 0.6 %sum_parts.1 = bf16[4,56,128]{2,1,0:T(8,128)(2,1)} custom-call(bf16[8,56,128]{2,1,0:T(8,128)(2,1)S(1)} %all_to_all.21.parts_ref), custom_call_target="tpu_custom_call" | custom-call | tf_op jit(solution)/shard_map/sum_parts/pallas_call | solution.py:764
  50.8 3.5 %all-to-all-start.3 = ((bf16[4,56,128]{2,1,0:T(8,128)(2,1)}), bf16[4,56,128]{2,1,0:T(8,128)(2,1)S(1)}, u32[]{:S(2)}, u32[]{:S(2)}) async-start(bf16[4,56,128]{2,1,0:T(8,128)(2,1)} %sum_parts.1), calls=%async_computation.3 | async-start | bytes 114688 | tf_op jit(solution)/shard_map/all_to_all | solution.py:741
  54.3 0.1 slice.24
  54.4 0.2 reshape.75
  54.6 0.7 %copy.41 = bf16[8,2,16,3,48]{4,2,3,1,0:T(8,128)(2,1)} copy(bf16[8,2,16,3,48]{4,2,0,1,3:T(8,128)(2,1)S(1)} %bitcast.53) | data formatting | bytes 147456 | tf_op jit(solution)/shard_map/transpose | solution.py:748
  55.3 0.9 %copy-done.4 = f32[48,896]{1,0:T(8,128)S(1)} copy-done((f32[48,896]{1,0:T(8,128)S(1)}, f32[48,896]{1,0:T(8,128)}, u32[]{:S(2)}) %copy-start.4) | copy-done | bytes 172056
  56.2 1.9 %turn_taps.1.taps_ref = bf16[6144,128]{1,0:T(8,128)(2,1)S(1)} custom-call(f32[48,896]{1,0:T(8,128)S(1)} %copy-done.4, bf16[64,896]{1,0:T(8,128)(2,1)S(1)} %bitcast.49), custom_call_target="tpu_custom_call" | custom-call | flops 169869312 | bytes 4000000 | tf_op jit(solution)/shard_map/turn_taps/pallas_call | solution.py:631
  58.1 1.7 %all-to-all-done.3.sums_ref = bf16[4,56,128]{2,1,0:T(8,128)(2,1)S(1)} async-done(((bf16[4,56,128]{2,1,0:T(8,128)(2,1)}), bf16[4,56,128]{2,1,0:T(8,128)(2,1)S(1)}, u32[]{:S(2)}, u32[]{:S(2)}) %all-to-all-start.3) | async-done | bytes 57376 | tf_op jit(solution)/shard_map/all_to_all | solution.py:741
  59.8 2.8 %feature_pull.1 = (bf16[12288,128]{1,0:T(8,128)(2,1)}, f32[3,3,3,128]{3,2,1,0:T(4,128)}, f32[1,1]{1,0:T(1,128)}) custom-call(bf16[6144,128]{1,0:T(8,128)(2,1)S(1)} %turn_taps.1.taps_ref, bf16[4,56,128]{2,1,0:T(8,128)(2,1)S(1)} %all-to-all-done.3.sums_ref, bf16[3,3,3,128]{3,2,1,0:T(4,128)(2,1)S(1)} %copy-done.5), custom_call_target="tpu_custom_call" | custom-call | flops 201326592 | bytes 6291456 | tf_op jit(solution)/shard_map/feature_pull/pallas_call | solution.py:687
  (36 shorter events, 0.4 us)
Async XLA Ops:
  0.6 11.7 %copy-start.10 = (pred[18,512]{1,0:T(8,128)(4,1)S(1)}, pred[18,512]{1,0:T(8,128)(4,1)}, u32[]{:S(2)}) copy-start(pred[18,512]{1,0:T(8,128)(4,1)} %constant.20.clone) | copy-start | bytes 27652
  0.6 11.7 %copy-start.12 = (pred[18,512]{1,0:T(8,128)(4,1)S(1)}, pred[18,512]{1,0:T(8,128)(4,1)}, u32[]{:S(2)}) copy-start(pred[18,512]{1,0:T(8,128)(4,1)} %constant.19.clone) | copy-start | bytes 27652
  0.7 11.8 %copy-start.11 = (pred[18,512]{1,0:T(8,128)(4,1)S(1)}, pred[18,512]{1,0:T(8,128)(4,1)}, u32[]{:S(2)}) copy-start(pred[18,512]{1,0:T(8,128)(4,1)} %constant.18.clone) | copy-start | bytes 27652
  0.7 11.8 %copy-start.9 = (pred[18,512]{1,0:T(8,128)(4,1)S(1)}, pred[18,512]{1,0:T(8,128)(4,1)}, u32[]{:S(2)}) copy-start(pred[18,512]{1,0:T(8,128)(4,1)} %constant.17.clone) | copy-start | bytes 27652
  0.7 13.8 %copy-start.2 = (bf16[1,16,16,3,48]{4,2,3,1,0:T(8,128)(2,1)S(1)}, bf16[1,16,16,3,48]{4,2,3,1,0:T(8,128)(2,1)}, u32[]{:S(2)}) copy-start(bf16[1,16,16,3,48]{4,2,3,1,0:T(8,128)(2,1)} %param.15) | copy-start | bytes 221188
  0.7 11.4 %copy-start.8 = (bf16[4,4,3,64]{3,1,2,0:T(4,128)(2,1)S(1)}, bf16[4,4,3,64]{3,1,2,0:T(4,128)(2,1)}, u32[]{:S(2)}) copy-start(bf16[4,4,3,64]{3,1,2,0:T(4,128)(2,1)} %param.17) | copy-start | bytes 18436
  0.7 12.5 %copy-start.7 = (bf16[4,4,512,1]{2,1,3,0:T(4,128)(2,1)S(1)}, bf16[4,4,512,1]{2,1,3,0:T(4,128)(2,1)}, u32[]{:S(2)}) copy-start(bf16[4,4,512,1]{2,1,3,0:T(4,128)(2,1)} %param.21) | copy-start | bytes 49156
  4.8 14.5 %all-to-all-start = ((bf16[8,8,896]{2,1,0:T(8,128)(2,1)}), bf16[8,8,896]{2,1,0:T(8,128)(2,1)S(1)}, u32[]{:S(2)}, u32[]{:S(2)}) async-start(bf16[8,8,896]{2,1,0:T(8,128)(2,1)} %bitcast.50), calls=%async_computation | async-start | bytes 229376 | tf_op jit(solution)/shard_map/all_to_all | solution.py:723
  14.5 0.9 %copy-start.1 = (bf16[64,896]{1,0:T(8,128)(2,1)S(1)}, bf16[64,896]{1,0:T(8,128)(2,1)}, u32[]{:S(2)}) copy-start(bf16[64,896]{1,0:T(8,128)(2,1)} %forward_taps.1.pay_ref) | copy-start | bytes 344068
  19.3 0.6 %copy-start.6 = (bf16[8,8,896]{2,1,0:T(8,128)(2,1)}, bf16[8,8,896]{2,1,0:T(8,128)(2,1)S(1)}, u32[]{:S(2)}) copy-start(bf16[8,8,896]{2,1,0:T(8,128)(2,1)S(1)} %all-to-all-done) | copy-start | bytes 344068
  20.0 19.8 %copy-start = (bf16[1,16,16,48,128]{4,3,2,1,0:T(8,128)(2,1)S(1)}, bf16[1,16,16,48,128]{4,3,2,1,0:T(8,128)(2,1)}, u32[]{:S(2)}) copy-start(bf16[1,16,16,48,128]{4,3,2,1,0:T(8,128)(2,1)} %param.14) | copy-start | bytes 9437188
  39.7 20.0 %copy-start.5 = (bf16[3,3,3,128]{3,2,1,0:T(4,128)(2,1)S(1)}, bf16[3,3,3,128]{3,2,1,0:T(4,128)(2,1)}, u32[]{:S(2)}) copy-start(bf16[3,3,3,128]{3,2,1,0:T(4,128)(2,1)} %weight_ref.1) | copy-start | bytes 20740
  42.0 0.7 %copy-start.3 = (f32[48,896]{1,0:T(8,128)}, f32[48,896]{1,0:T(8,128)S(1)}, u32[]{:S(2)}) copy-start(f32[48,896]{1,0:T(8,128)S(1)} %get-tuple-element.13.rec_ref) | copy-start | bytes 516100
  50.8 9.0 %all-to-all-start.3 = ((bf16[4,56,128]{2,1,0:T(8,128)(2,1)}), bf16[4,56,128]{2,1,0:T(8,128)(2,1)S(1)}, u32[]{:S(2)}, u32[]{:S(2)}) async-start(bf16[4,56,128]{2,1,0:T(8,128)(2,1)} %sum_parts.1), calls=%async_computation.3 | async-start | bytes 114688 | tf_op jit(solution)/shard_map/all_to_all | solution.py:741
  55.3 0.9 %copy-start.4 = (f32[48,896]{1,0:T(8,128)S(1)}, f32[48,896]{1,0:T(8,128)}, u32[]{:S(2)}) copy-start(f32[48,896]{1,0:T(8,128)} %copy-done.3) | copy-start | bytes 516100

commit v8 on v7

--- a/solution.py
+++ b/solution.py
@@ -19,7 +19,7 @@
 VM = pl.BlockSpec(memory_space=pltpu.VMEM)
 HBM = pl.BlockSpec(memory_space=pl.ANY)
 WHOLE = pltpu.CompilerParams(vmem_limit_bytes=60 * 2**20)
-MOST = pltpu.CompilerParams(vmem_limit_bytes=119 * 2**19)
+MOST = pltpu.CompilerParams(vmem_limit_bytes=115 * 2**19)
 PART = pltpu.CompilerParams(vmem_limit_bytes=24 * 2**20)
 
 
@@ -56,23 +56,11 @@
     weight_scr[...] = jnp.zeros_like(weight_scr)
     out_ref[...] = jnp.zeros_like(out_ref)
     copies[0].wait()
-    copies[1].wait()
     for a in range(3):
         for b in range(3):
             at = (a * 3 + b) * 3
             weight_scr[at : at + 3, :] = weight_ref[a, b].astype(F32)
     weight = weight_scr[...].astype(BF16)
-    target_scr[:, 0:cols] = target_ref[...].reshape(target_scr.shape[0], cols).astype(F32)
-    edges = []
-    for y in (0, block_rows - 1):
-        for o in range(3):
-            for part in range(group):
-                rows = pl.ds((part * 3 + o) * block_rows + y, devices, stride=group * 3 * block_rows)
-                edges.append(target_scr[rows, :][:, 0:cols])
-    edges.append(jnp.zeros((devices, lanes - len(edges) * cols), F32))
-    edges = jnp.concatenate(edges, axis=1)
-    for k in range(lanes // LANES):
-        out_ref[k, pl.ds(3 * group, devices, stride=pitch), :] = edges[:, k * LANES : (k + 1) * LANES]
     column = lax.broadcasted_iota(jnp.int32, (devices, pixels), 1) % cols
 
     def finish(part):
@@ -94,6 +82,19 @@
                 rows = pl.ds(o * group + part, devices, stride=pitch)
                 out_ref[k, rows, :] = total[:, k * LANES : (k + 1) * LANES]
 
+    def edge_rows():
+        target_scr[:, 0:cols] = target_ref[...].reshape(target_scr.shape[0], cols).astype(F32)
+        edges = []
+        for y in (0, block_rows - 1):
+            for o in range(3):
+                for part in range(group):
+                    rows = pl.ds((part * 3 + o) * block_rows + y, devices, stride=group * 3 * block_rows)
+                    edges.append(target_scr[rows, :][:, 0:cols])
+        edges.append(jnp.zeros((devices, lanes - len(edges) * cols), F32))
+        edges = jnp.concatenate(edges, axis=1)
+        for k in range(lanes // LANES):
+            out_ref[k, pl.ds(3 * group, devices, stride=pitch), :] = edges[:, k * LANES : (k + 1) * LANES]
+
     step = frames // chunks
     done = 0
     for chunk in range(chunks):
@@ -104,6 +105,9 @@
             product = mat(weight, feat_ref[frame * pixels : (frame + 1) * pixels, :], NT)
             for k in range(pieces):
                 taps_ref[k, pl.ds(slot, taps, stride=frames), :] = product[:, k * LANES : (k + 1) * LANES]
+        if chunk == 0:
+            copies[1].wait()
+            edge_rows()
         while (done + 1) * devices <= chunk * step or (chunk == chunks - 1 and done < group):
             finish(done)
             done += 1
@@ -213,8 +217,8 @@
 
 
 def disc_kernel(
-    pay_ref, head_ref, window_hbm, band_hbm, second_hbm, third_hbm, fourth_hbm, unwindow_hbm, out_ref,
-    zin, window, band_ref, second, third, fourth, unwindow, rows_in, act_one, slope_one, cols_two, act_two, slope_two, act_three, cols_four,
+    pay_ref, head_ref, window, band_ref, second, third, unwindow, fourth_hbm, out_ref,
+    zin, fourth, rows_in, act_one, slope_one, cols_two, act_two, slope_two, act_three, cols_four,
     pull_four, pull_three, pull_two, zout, sems, *, devices, group, cols, block_rows, period,
 ):
     lanes = pay_ref.shape[1]
@@ -226,15 +230,13 @@
     d2, d3, d4 = second.shape[1], third.shape[1], fourth.shape[1]
     x1, x2, x3 = cols // 2, cols // 4, cols // 8
     x4 = x3 - 1
-    pairs = (
-        (window_hbm, window),
-        (band_hbm, band_ref),
-        (second_hbm, second),
-        (third_hbm, third),
-        (fourth_hbm, fourth),
-        (unwindow_hbm, unwindow),
-    )
-    copies = [pltpu.make_async_copy(source, target, sems.at[i]) for i, (source, target) in enumerate(pairs)]
+    quarter = fourth.shape[0] // 4
+    copies = [
+        pltpu.make_async_copy(
+            fourth_hbm.at[pl.ds(a * quarter, quarter), :], fourth.at[pl.ds(a * quarter, quarter), :], sems.at[a]
+        )
+        for a in range(4)
+    ]
     for copy in copies:
         copy.start()
     cells = block_rows // 8
@@ -264,8 +266,6 @@
         firsts.append(lines[1])
         lasts.append(lines[block_rows])
     image = jnp.concatenate([rows_in[0], rows_in[1]], axis=1)[:, :wide].astype(BF16)
-    copies[0].wait()
-    copies[1].wait()
     wins = mat(image, window[...])
     ext = [wins[r * unit : (r + 1) * unit] for r in range(8)]
     ext = [shift_rows(ext[7], 1, period)] + ext + [shift_rows(ext[0], -1, period)]
@@ -293,7 +293,6 @@
         actual = act.astype(F32)
         act_one[0:unit, start:end] = shift_rows(actual[3 * unit :], 1, period).astype(BF16)
         act_one[5 * unit :, start:end] = shift_rows(actual[:unit], -1, period).astype(BF16)
-    copies[2].wait()
     for x in range(x2):
         for a in range(4):
             for p in range(2):
@@ -312,7 +311,6 @@
         act_two[unit : 3 * unit, at] = block
         act_two[0:unit, at] = shift_rows(actual[unit:], 1, period).astype(BF16)
         act_two[3 * unit :, at] = shift_rows(actual[:unit], -1, period).astype(BF16)
-    copies[3].wait()
     left = jnp.concatenate(
         [
             jnp.concatenate([act_two[a * unit : (a + 1) * unit, 2 * x * d2 : (2 * x + 4) * d2] for a in range(4)], axis=1)
@@ -335,9 +333,12 @@
             cols_four[x * unit : (x + 1) * unit, a * 4 * d3 : (a + 1) * 4 * d3] = act_three[
                 a * unit : (a + 1) * unit, x * d3 : (x + 4) * d3
             ]
-    copies[4].wait()
-    pre = mat(cols_four[...], fourth[...])
     edge_planes(zin, zout, firsts, lasts, devices, group, cols, lanes, pitch)
+    pre = None
+    for a in range(4):
+        copies[a].wait()
+        term = mat(cols_four[:, a * quarter : (a + 1) * quarter], fourth[a * quarter : (a + 1) * quarter, :])
+        pre = term if pre is None else pre + term
     _, slope = gate_of(pre)
     row = lax.broadcasted_iota(jnp.int32, (unit, d4), 0) % period
     head = head_ref[...].astype(F32) * -loss_scale
@@ -407,7 +408,6 @@
         )
         strips.append((both * slope_one[:, 2 * k * d1 : (2 * k + 2) * d1]).astype(BF16))
     cot = jnp.concatenate(strips, axis=1)
-    copies[5].wait()
     sums = []
     for k in range(-(-width_one // strip)):
         start, end = k * strip, min((k + 1) * strip, width_one)
@@ -422,10 +422,15 @@
     sums = jnp.concatenate(sums, axis=1)
     upper = sums.astype(BF16)
     lower = (sums - upper.astype(F32)).astype(BF16)
-    both = mat(upper, unwindow[...]) + mat(lower, unwindow[...])
-    half = both.shape[1] // 2
-    odd = [both[m * unit : (m + 1) * unit, 0:wide] for m in range(5)]
-    even = [both[m * unit : (m + 1) * unit, half : half + wide] for m in range(5)]
+    low = lax.broadcasted_iota(jnp.int32, upper.shape, 1) % LANES < LANES // 2
+    blank = jnp.zeros_like(upper)
+    split = [jnp.where(low, upper, blank), jnp.where(low, lower, blank), jnp.where(low, blank, upper), jnp.where(low, blank, lower)]
+    both = mat(jnp.concatenate(split, axis=0), unwindow[...])
+    size = 5 * unit
+    odd = both[:size] + both[size : 2 * size]
+    even = both[2 * size : 3 * size] + both[3 * size :]
+    odd = [odd[m * unit : (m + 1) * unit, :] for m in range(5)]
+    even = [even[m * unit : (m + 1) * unit, :] for m in range(5)]
     phases = [even[r // 2] if r % 2 == 0 else odd[(r + 1) // 2] for r in range(8)]
     phases[0] = phases[0] + shift_rows(even[4], 1, period)
     phases[7] = phases[7] + shift_rows(odd[0], -1, period)
@@ -452,9 +457,8 @@
 def windows_of(cols, d1):
     wide = 3 * cols
     count = -(-(cols // 2 + 2) // 8)
-    half = up_to(wide, LANES)
     window = np.zeros((wide, count * 2 * LANES), np.float32)
-    unwindow = np.zeros((count * LANES, 2 * half), np.float32)
+    unwindow = np.zeros((count * LANES, wide), np.float32)
     for k in range(count):
         for c in range(3):
             for j in range(18):
@@ -463,38 +467,75 @@
                     for e in range(2):
                         at = e * LANES // 2 + c * 18 + j
                         window[c * cols + x, (2 * k + e) * LANES + at] = 1.0
-                        unwindow[k * LANES + at, e * half + c * cols + x] = 1.0
+                        unwindow[k * LANES + at, c * cols + x] = 1.0
     return window, unwindow
 
 
-def band_of(first):
-    d1 = first.shape[-1]
-    tap = np.arange(18)[:, None] - 2 * (np.arange(8 * d1)[None, :] // d1)
-    tiled = jnp.tile(first, (1, 1, 1, 8))
-    band = jnp.zeros((4, 3, 18, 8 * d1), BF16)
-    for b in range(4):
-        band = jnp.where(jnp.asarray(tap == b), tiled[:, b, :, None, :], band)
-    band = jnp.pad(band.reshape(4, 54, 8 * d1), ((0, 0), (0, LANES // 2 - 54), (0, 0)))
-    return band.reshape(2 * LANES, 8 * d1)
-
-
-def disc_call(payload, first, second, third, fourth, head, devices, group, cols, block_rows):
+def stage_kernel(
+    first_ref, window_hbm, unwindow_hbm, second_hbm, third_hbm, window, unwindow, second, third, band, scr, sems
+):
+    pairs = ((window_hbm, window), (second_hbm, second), (third_hbm, third), (unwindow_hbm, unwindow))
+    copies = [pltpu.make_async_copy(source, target, sems.at[i]) for i, (source, target) in enumerate(pairs)]
+    for copy in copies:
+        copy.start()
+    d1 = first_ref.shape[-1]
+    scr[...] = jnp.zeros_like(scr)
+    row = lax.broadcasted_iota(jnp.int32, (18, 8 * d1), 0)
+    tap = row - 2 * (lax.broadcasted_iota(jnp.int32, (18, 8 * d1), 1) // d1)
+    for a in range(4):
+        lines = [first_ref[a, b].astype(F32) for b in range(4)]
+        for c in range(3):
+            block = jnp.zeros((18, 8 * d1), F32)
+            for b in range(4):
+                line = jnp.concatenate([lines[b][c : c + 1, :]] * 8, axis=1)
+                block = jnp.where(tap == b, jnp.broadcast_to(line, block.shape), block)
+            at = a * LANES // 2 + c * 18
+            scr[at : at + 18, :] = block
+    band[...] = scr[...].astype(BF16)
+    for copy in copies:
+        copy.wait()
+
+
+def stage_call(first, second, third, cols):
+    d1, d2, d3 = first.shape[-1], second.shape[-1], third.shape[-1]
+    window, unwindow = windows_of(cols, d1)
+    operands = (
+        first,
+        jnp.asarray(window, BF16),
+        jnp.asarray(unwindow, BF16),
+        second.reshape(16 * d1, d2),
+        third.reshape(16 * d2, d3),
+    )
+    shapes = [value.shape for value in operands[1:]] + [(2 * LANES, 8 * d1)]
+    return pl.pallas_call(
+        stage_kernel,
+        out_shape=tuple(jax.ShapeDtypeStruct(shape, BF16) for shape in shapes),
+        in_specs=[VM] + [HBM] * 4,
+        out_specs=(VM,) * 5,
+        scratch_shapes=[pltpu.VMEM((2 * LANES, 8 * d1), F32), pltpu.SemaphoreType.DMA((4,))],
+        compiler_params=PART,
+        cost_estimate=pl.CostEstimate(flops=10**8, bytes_accessed=4 * 10**6, transcendentals=0),
+        name="stage_weights",
+    )(*operands)
+
+
+def disc_call(payload, staged, fourth, head, devices, group, cols, block_rows):
     period = devices * block_rows // 8
     unit = group * period
-    d1, d2, d3, d4 = first.shape[-1], second.shape[-1], third.shape[-1], fourth.shape[-1]
+    window, unwindow, second, third, band = staged
+    d1, d2, d3, d4 = band.shape[1] // 8, second.shape[1], third.shape[1], fourth.shape[-1]
     x2, x3 = cols // 4, cols // 8
     x4 = x3 - 1
-    window, unwindow = windows_of(cols, d1)
     width_one = (cols // 2 + 2) * d1
     args = (
         payload,
         head.reshape(16, d4),
-        jnp.asarray(window, BF16),
-        band_of(first),
-        second.reshape(16 * d1, d2),
-        third.reshape(16 * d2, d3),
+        window,
+        band,
+        second,
+        third,
+        unwindow,
         fourth.reshape(16 * d3, d4),
-        jnp.asarray(unwindow, BF16),
     )
     lanes = payload.shape[1]
     return pl.pallas_call(
@@ -502,16 +543,11 @@
             disc_kernel, devices=devices, group=group, cols=cols, block_rows=block_rows, period=period
         ),
         out_shape=jax.ShapeDtypeStruct(payload.shape, BF16),
-        in_specs=[VM, VM] + [HBM] * 6,
+        in_specs=[VM] * 7 + [HBM],
         out_specs=VM,
         scratch_shapes=[
             pltpu.VMEM((lanes // LANES, payload.shape[0], LANES), F32),
-            pltpu.VMEM(window.shape, BF16),
-            pltpu.VMEM((2 * LANES, 8 * d1), BF16),
-            pltpu.VMEM((16 * d1, d2), BF16),
-            pltpu.VMEM((16 * d2, d3), BF16),
             pltpu.VMEM((16 * d3, d4), BF16),
-            pltpu.VMEM(unwindow.shape, BF16),
             pltpu.VMEM((2, 8 * unit, LANES), F32),
             pltpu.VMEM((6 * unit, width_one), BF16),
             pltpu.VMEM((4 * unit, width_one), F32),
@@ -524,7 +560,7 @@
             pltpu.VMEM((x3 * unit, 16 * d2), F32),
             pltpu.VMEM((x2 * 2 * unit, 16 * d1), F32),
             pltpu.VMEM((lanes // LANES, payload.shape[0], LANES), F32),
-            pltpu.SemaphoreType.DMA((6,)),
+            pltpu.SemaphoreType.DMA((4,)),
         ],
         compiler_params=MOST,
         cost_estimate=pl.CostEstimate(flops=4 * 10**9, bytes_accessed=8 * 10**6, transcendentals=10**6),
@@ -584,14 +620,12 @@
 
 
 def both_kernel(
-    inner_ref, plane_ref, feat_ref, part_ref, rec_ref, rec_taps, gan_taps, zin, *, frames, devices, group, cols, block_rows
+    inner_ref, plane_ref, feat_ref, part_ref, rec_taps, gan_taps, zin, *, frames, devices, group, cols, block_rows
 ):
     pieces = block_rows * cols // LANES
     put_taps(unpack(plane_ref, zin, devices, group), gan_taps, frames, cols, pieces, 32)
     inner, edges = rec_rows(inner_ref, zin, devices, group, cols, block_rows)
-    rec = inner + edges
-    rec_ref[...] = rec
-    put_taps(rec, rec_taps, frames, cols, pieces, 32)
+    put_taps(inner + edges, rec_taps, frames, cols, pieces, 32)
     pixels = pieces * LANES
     total = jnp.zeros((64, feat_ref.shape[1]), F32)
     for frame in range(frames):
@@ -611,12 +645,13 @@
 
 
 def turn_kernel(
-    rec_ref, plane_ref, out_ref, rec_taps, gan_taps, zin, *, frames, devices, group, cols, block_rows
+    inner_ref, plane_ref, out_ref, rec_taps, gan_taps, zin, *, frames, devices, group, cols, block_rows
 ):
     pieces = block_rows * cols // LANES
     pixels = pieces * LANES
-    put_taps(rec_ref[...], rec_taps, frames, cols, pieces, 32)
     put_taps(unpack(plane_ref, zin, devices, group), gan_taps, frames, cols, pieces, 32)
+    inner, edges = rec_rows(inner_ref, zin, devices, group, cols, block_rows)
+    put_taps(inner + edges, rec_taps, frames, cols, pieces, 32)
     for pair in range(frames // 2):
         for k in range(pieces):
             parts = []
@@ -725,23 +760,23 @@
     ).reshape(devices * pitch, lanes)
     arrived = trade(payload)
     inner = inner_call(payload, wanted, frames, devices, group, block_rows, cols)
+    _, disc_first = lax.optimization_barrier((payload, disc_first))
+    staged = stage_call(disc_first, disc_second, disc_third, cols)
     arrived, inner = lax.optimization_barrier((arrived, inner))
-    sent = disc_call(
-        arrived, disc_first, disc_second, disc_third, disc_fourth, disc_head, devices, group, cols, block_rows
-    )
+    sent = disc_call(arrived, staged, disc_fourth, disc_head, devices, group, cols, block_rows)
     returned = trade(sent)
     taps_scratch = pltpu.VMEM((block_rows * cols // LANES, 32 * frames, LANES), F32)
     plane_scratch = pltpu.VMEM((lanes // LANES, devices * pitch, LANES), F32)
     flops = 4 * features.size * 27
-    part, rec_plane = taps_call(
+    part = taps_call(
         both_kernel, [VM, VM, VM], (inner, returned, feats),
-        (jax.ShapeDtypeStruct((clips * lax.axis_size("near"), 56, channels), BF16), jax.ShapeDtypeStruct(inner.shape, F32)),
+        jax.ShapeDtypeStruct((clips * lax.axis_size("near"), 56, channels), BF16),
         [taps_scratch, taps_scratch, plane_scratch], *sizes, flops, "both_taps",
     )
     share = lambda values, axes: lax.all_to_all(values, axes, split_axis=0, concat_axis=0, tiled=True)
     sums = share(sum_call(share(part, ("clip", "near")), lax.axis_size("far")), "far")
     taps = taps_call(
-        turn_kernel, [VM, VM], (rec_plane, returned), jax.ShapeDtypeStruct((feats.shape[0] // 2, LANES), BF16),
+        turn_kernel, [VM, VM], (inner, returned), jax.ShapeDtypeStruct((feats.shape[0] // 2, LANES), BF16),
         [taps_scratch, taps_scratch, plane_scratch], *sizes, flops, "turn_taps",
     )
     image_back = returned.reshape(devices, pitch, lanes)[:, : 3 * group, cols : (block_rows + 1) * cols]

time: 63.3 us -> 64.8 us (1.024)
  waiting for transfers between devices: 5.24 us -> 3.53 us
  blocking collectives: 18 us -> 19.6 us
  Pallas kernels: 21.2 us -> 22.3 us
  local copies, waits for them, and re-layouts: 5.94 us -> 6.99 us
    all_to_all x1, waiting for transfers between devices: 3.56 us -> 1.06 us  [per_device(): lax.all_to_all(values.reshape(devices, pitch, lanes), row, split_axis=0,...]
    unnamed x27 -> x32, local copies, waits for them, and re-layouts: 3.21 us -> 5.35 us
    all_to_all x1, blocking collectives: 10.5 us -> 12.2 us  [per_device(): lax.all_to_all(values.reshape(devices, pitch, lanes), row, split_axis=0,...]
    all_to_all x1, waiting for transfers between devices: 1.68 us -> 2.47 us  [per_device(): lax.all_to_all(values, axes, split_axis=0, concat_axis=0, tiled=True)]
    pad x1 -> x0, local copies, waits for them, and re-layouts: 0.72 us -> none  [band_of(): jnp.pad(band.reshape(4, 54, 8 * d1), ((0, 0), (0, LANES // 2 - 54), (0, 0)))]
  transfers between devices with their start and end apart: 2 -> 2, of which waited for: 2 -> 2; matrix products, arithmetic and copies ran while one was open for 5% -> 3% of each run, Pallas kernels for 3% -> 4%
where the time goes in v8:
time: 64.8 us; the launch traced here: 64.2 us
  Pallas kernels  22.3 us (34%)
  blocking collectives  19.6 us (30%)
  starting transfers between devices  10.8 us (17%)
  local copies, waits for them, and re-layouts  6.99 us (11%)
  waiting for transfers between devices  3.53 us (5%)
  between operations  0.99 us (2%)
    all_to_all x1, blocking collectives, per_device(): lax.all_to_all(values.reshape(devices, pitch, lanes), row, split_axis=0,...  12.2 us
    pallas_call x1, Pallas kernels, disc_call(): pl.pallas_call(functools.partial(disc_kernel, devices=devices, group=grou...  9.55 us
    all_to_all x1, blocking collectives, per_device(): lax.all_to_all(values, axes, split_axis=0, concat_axis=0, tiled=True)  7.46 us
    all_to_all x1, starting transfers between devices, per_device(): lax.all_to_all(values.reshape(devices, pitch, lanes), row, split_axis=0,...  7.29 us
    unnamed x32, local copies, waits for them, and re-layouts  5.35 us
    pallas_call x1, Pallas kernels, forward_call(): pl.pallas_call(functools.partial(forward_kernel, frames=frames, devices=d...  4.28 us
    pallas_call x2, Pallas kernels, taps_call(): pl.pallas_call(functools.partial(kernel, frames=frames, devices=devices,...  4.28 us
    all_to_all x1, starting transfers between devices, per_device(): lax.all_to_all(values, axes, split_axis=0, concat_axis=0, tiled=True)  3.46 us
  transfers between devices with their start and end apart: 2, of which 2 were waited for; matrix products, arithmetic and copies ran while one was open for 3% of the time, Pallas kernels for 4%

profile of v8, /device:TPU:0, one launch (start us, length us, event | category | flops | bytes accessed | tf_op | source)
XLA Modules:
  0.0 64.2 jit_solution(6689101634011657833)
XLA Ops:
  0.7 4.3 %forward_taps.1.pay_ref = bf16[64,896]{1,0:T(8,128)(2,1)} custom-call(bf16[12288,128]{1,0:T(8,128)(2,1)} %bitcast.19, bf16[16,3,16,48]{3,2,1,0:T(8,128)(2,1)} %bitcast.25, bf16[3,3,3,128]{3,2,1,0:T(4,128)(2,1)} %weight_ref.1), custom_call_target="tpu_custom_call" | custom-call | flops 84934656 | bytes 3145728 | tf_op jit(solution)/shard_map/forward_taps/pallas_call | solution.py:122
  5.0 7.3 %all-to-all-start = ((bf16[8,8,896]{2,1,0:T(8,128)(2,1)}), bf16[8,8,896]{2,1,0:T(8,128)(2,1)S(1)}, u32[]{:S(2)}, u32[]{:S(2)}) async-start(bf16[8,8,896]{2,1,0:T(8,128)(2,1)} %bitcast.24), calls=%async_computation | async-start | bytes 229376 | tf_op jit(solution)/shard_map/all_to_all | solution.py:758
  12.3 0.6 reshape.47.head_ref
  12.9 0.9 %copy-done.2 = bf16[64,896]{1,0:T(8,128)(2,1)S(1)} copy-done((bf16[64,896]{1,0:T(8,128)(2,1)S(1)}, bf16[64,896]{1,0:T(8,128)(2,1)}, u32[]{:S(2)}) %copy-start.2) | copy-done | bytes 114712
  13.8 0.3 inner_rows.1.inner_ref
  14.2 0.5 stage_weights.1
  14.7 1.0 %copy-done.8 = bf16[2048,256]{1,0:T(8,128)(2,1)} copy-done((bf16[2048,256]{1,0:T(8,128)(2,1)}, bf16[2048,256]{1,0:T(8,128)(2,1)S(1)}, u32[]{:S(2)}) %copy-start.8) | copy-done | bytes 1048600
  15.7 0.7 %copy-done.9 = bf16[144,1024]{1,0:T(8,128)(2,1)} copy-done((bf16[144,1024]{1,0:T(8,128)(2,1)}, bf16[144,1024]{1,0:T(8,128)(2,1)S(1)}, u32[]{:S(2)}) %copy-start.9) | copy-done | bytes 294936
  16.4 0.7 %copy-done.10 = bf16[512,144]{1,0:T(8,128)(2,1)} copy-done((bf16[512,144]{1,0:T(8,128)(2,1)}, bf16[512,144]{1,0:T(8,128)(2,1)S(1)}, u32[]{:S(2)}) %copy-start.10) | copy-done | bytes 147480
  17.1 0.7 %copy-done.11 = bf16[1024,128]{1,0:T(8,128)(2,1)} copy-done((bf16[1024,128]{1,0:T(8,128)(2,1)}, bf16[1024,128]{1,0:T(8,128)(2,1)S(1)}, u32[]{:S(2)}) %copy-start.11) | copy-done | bytes 262168
  17.8 0.7 %copy-done.12 = bf16[256,512]{1,0:T(8,128)(2,1)} copy-done((bf16[256,512]{1,0:T(8,128)(2,1)}, bf16[256,512]{1,0:T(8,128)(2,1)S(1)}, u32[]{:S(2)}) %copy-start.12) | copy-done | bytes 262168
  18.5 1.1 %all-to-all-done = bf16[8,8,896]{2,1,0:T(8,128)(2,1)S(1)} async-done(((bf16[8,8,896]{2,1,0:T(8,128)(2,1)}), bf16[8,8,896]{2,1,0:T(8,128)(2,1)S(1)}, u32[]{:S(2)}, u32[]{:S(2)}) %all-to-all-start) | async-done | bytes 114720 | tf_op jit(solution)/shard_map/all_to_all | solution.py:758
  19.5 0.6 %copy-done.13 = bf16[8,8,896]{2,1,0:T(8,128)(2,1)} copy-done((bf16[8,8,896]{2,1,0:T(8,128)(2,1)}, bf16[8,8,896]{2,1,0:T(8,128)(2,1)S(1)}, u32[]{:S(2)}) %copy-start.13) | copy-done | bytes 114712
  20.2 9.5 %disc_rows.1 = bf16[64,896]{1,0:T(8,128)(2,1)} custom-call(bf16[64,896]{1,0:T(8,128)(2,1)} %bitcast.30, bf16[16,512]{1,0:T(8,128)(2,1)} %reshape.47.head_ref, bf16[144,1024]{1,0:T(8,128)(2,1)} %copy-done.9, bf16[256,512]{1,0:T(8,128)(2,1)} %copy-done.12, bf16[1024,128]{1,0:T(8,128)(2,1)} %copy-done.11, bf16[2048,256]{1,0:T(8,128)(2,1)} %copy-done.8, ...), custom_call_target="tpu_custom_call" | custom-call | flops 4000000000 | bytes 8000000 | tf_op jit(solution)/shard_map/disc_rows/pallas_call | solution.py:541
  29.7 12.2 %all_to_all.20 = bf16[8,8,896]{2,1,0:T(8,128)(2,1)S(1)} all-to-all(bf16[8,8,896]{2,1,0:T(8,128)(2,1)} %bitcast.31), channel_id=1, replica_groups=mesh['clip'=4,'far'=4,'near'=2] {'far','near'}, dimensions={0} | all-to-all | bytes 229376 | tf_op jit(solution)/shard_map/all_to_all | solution.py:758
  41.9 2.3 %both_taps.1 = bf16[8,56,128]{2,1,0:T(8,128)(2,1)S(1)} custom-call(f32[48,896]{1,0:T(8,128)S(1)} %inner_rows.1.inner_ref, bf16[64,896]{1,0:T(8,128)(2,1)S(1)} %bitcast.21, bf16[12288,128]{1,0:T(8,128)(2,1)S(1)} %bitcast.20), custom_call_target="tpu_custom_call" | custom-call | flops 169869312 | bytes 4000000 | tf_op jit(solution)/shard_map/both_taps/pallas_call | solution.py:666
  44.2 7.5 %all_to_all.21.parts_ref = bf16[8,56,128]{2,1,0:T(8,128)(2,1)S(1)} all-to-all(bf16[8,56,128]{2,1,0:T(8,128)(2,1)S(1)} %both_taps.1), channel_id=1, replica_groups=mesh['clip'=4,'far'=4,'near'=2] {'clip','near'}, dimensions={0} | all-to-all | bytes 229376 | tf_op jit(solution)/shard_map/all_to_all | solution.py:776
  51.6 0.6 %sum_parts.1 = bf16[4,56,128]{2,1,0:T(8,128)(2,1)} custom-call(bf16[8,56,128]{2,1,0:T(8,128)(2,1)S(1)} %all_to_all.21.parts_ref), custom_call_target="tpu_custom_call" | custom-call | tf_op jit(solution)/shard_map/sum_parts/pallas_call | solution.py:799
  52.3 3.5 %all-to-all-start.3 = ((bf16[4,56,128]{2,1,0:T(8,128)(2,1)}), bf16[4,56,128]{2,1,0:T(8,128)(2,1)S(1)}, u32[]{:S(2)}, u32[]{:S(2)}) async-start(bf16[4,56,128]{2,1,0:T(8,128)(2,1)} %sum_parts.1), calls=%async_computation.3 | async-start | bytes 114688 | tf_op jit(solution)/shard_map/all_to_all | solution.py:776
  55.9 0.2 reshape.54
  56.1 0.7 %copy.25 = bf16[8,2,16,3,48]{4,2,3,1,0:T(8,128)(2,1)} copy(bf16[8,2,16,3,48]{4,2,0,1,3:T(8,128)(2,1)S(1)} %bitcast.28) | data formatting | bytes 147456 | tf_op jit(solution)/shard_map/transpose | solution.py:783
  56.8 2.0 %turn_taps.1.taps_ref = bf16[6144,128]{1,0:T(8,128)(2,1)S(1)} custom-call(f32[48,896]{1,0:T(8,128)S(1)} %inner_rows.1.inner_ref, bf16[64,896]{1,0:T(8,128)(2,1)S(1)} %bitcast.22), custom_call_target="tpu_custom_call" | custom-call | flops 169869312 | bytes 4000000 | tf_op jit(solution)/shard_map/turn_taps/pallas_call | solution.py:666
  58.8 2.5 %all-to-all-done.3.sums_ref = bf16[4,56,128]{2,1,0:T(8,128)(2,1)S(1)} async-done(((bf16[4,56,128]{2,1,0:T(8,128)(2,1)}), bf16[4,56,128]{2,1,0:T(8,128)(2,1)S(1)}, u32[]{:S(2)}, u32[]{:S(2)}) %all-to-all-start.3) | async-done | bytes 57376 | tf_op jit(solution)/shard_map/all_to_all | solution.py:776
  61.3 2.8 %feature_pull.1 = (bf16[12288,128]{1,0:T(8,128)(2,1)}, f32[3,3,3,128]{3,2,1,0:T(4,128)}, f32[1,1]{1,0:T(1,128)}) custom-call(bf16[6144,128]{1,0:T(8,128)(2,1)S(1)} %turn_taps.1.taps_ref, bf16[4,56,128]{2,1,0:T(8,128)(2,1)S(1)} %all-to-all-done.3.sums_ref, bf16[3,3,3,128]{3,2,1,0:T(4,128)(2,1)S(1)} %copy-done.7), custom_call_target="tpu_custom_call" | custom-call | flops 201326592 | bytes 6291456 | tf_op jit(solution)/shard_map/feature_pull/pallas_call | solution.py:722
  (28 shorter events, 0.2 us)
Async XLA Ops:
  0.6 13.5 %copy-start.4 = (bf16[144,1024]{1,0:T(8,128)(2,1)S(1)}, bf16[144,1024]{1,0:T(8,128)(2,1)}, u32[]{:S(2)}) copy-start(bf16[144,1024]{1,0:T(8,128)(2,1)} %constant.4.clone.window_hbm) | copy-start | bytes 884740
  0.6 13.5 %copy-start.6 = (bf16[512,144]{1,0:T(8,128)(2,1)S(1)}, bf16[512,144]{1,0:T(8,128)(2,1)}, u32[]{:S(2)}) copy-start(bf16[512,144]{1,0:T(8,128)(2,1)} %constant.5.clone.unwindow_hbm) | copy-start | bytes 442372
  0.7 12.3 %copy-start.3 = (bf16[1,16,16,3,48]{4,2,3,1,0:T(8,128)(2,1)S(1)}, bf16[1,16,16,3,48]{4,2,3,1,0:T(8,128)(2,1)}, u32[]{:S(2)}) copy-start(bf16[1,16,16,3,48]{4,2,3,1,0:T(8,128)(2,1)} %param.11) | copy-start | bytes 221188
  0.7 11.6 %copy-start.15 = (bf16[4,4,3,64]{3,1,2,0:T(4,128)(2,1)S(1)}, bf16[4,4,3,64]{3,1,2,0:T(4,128)(2,1)}, u32[]{:S(2)}) copy-start(bf16[4,4,3,64]{3,1,2,0:T(4,128)(2,1)} %param.13) | copy-start | bytes 18436
  0.7 11.6 %copy-start.14 = (bf16[4,4,512,1]{2,1,3,0:T(4,128)(2,1)S(1)}, bf16[4,4,512,1]{2,1,3,0:T(4,128)(2,1)}, u32[]{:S(2)}) copy-start(bf16[4,4,512,1]{2,1,3,0:T(4,128)(2,1)} %param.17) | copy-start | bytes 49156
  0.7 13.5 %copy-start.5 = (bf16[4,4,64,128]{3,2,1,0:T(8,128)(2,1)S(1)}, bf16[4,4,64,128]{3,2,1,0:T(8,128)(2,1)}, u32[]{:S(2)}) copy-start(bf16[4,4,64,128]{3,2,1,0:T(8,128)(2,1)} %param.14) | copy-start | bytes 786436
  0.7 13.5 %copy-start.1 = (bf16[4,4,128,256]{3,2,1,0:T(8,128)(2,1)S(1)}, bf16[4,4,128,256]{3,2,1,0:T(8,128)(2,1)}, u32[]{:S(2)}) copy-start(bf16[4,4,128,256]{3,2,1,0:T(8,128)(2,1)} %param.15) | copy-start | bytes 3145732
  5.0 14.5 %all-to-all-start = ((bf16[8,8,896]{2,1,0:T(8,128)(2,1)}), bf16[8,8,896]{2,1,0:T(8,128)(2,1)S(1)}, u32[]{:S(2)}, u32[]{:S(2)}) async-start(bf16[8,8,896]{2,1,0:T(8,128)(2,1)} %bitcast.24), calls=%async_computation | async-start | bytes 229376 | tf_op jit(solution)/shard_map/all_to_all | solution.py:758
  12.9 0.9 %copy-start.2 = (bf16[64,896]{1,0:T(8,128)(2,1)S(1)}, bf16[64,896]{1,0:T(8,128)(2,1)}, u32[]{:S(2)}) copy-start(bf16[64,896]{1,0:T(8,128)(2,1)} %forward_taps.1.pay_ref) | copy-start | bytes 344068
  14.7 1.0 %copy-start.8 = (bf16[2048,256]{1,0:T(8,128)(2,1)}, bf16[2048,256]{1,0:T(8,128)(2,1)S(1)}, u32[]{:S(2)}) copy-start(bf16[2048,256]{1,0:T(8,128)(2,1)S(1)} %get-tuple-element.21.third) | copy-start | bytes 3145732
  15.7 0.7 %copy-start.9 = (bf16[144,1024]{1,0:T(8,128)(2,1)}, bf16[144,1024]{1,0:T(8,128)(2,1)S(1)}, u32[]{:S(2)}) copy-start(bf16[144,1024]{1,0:T(8,128)(2,1)S(1)} %get-tuple-element.18.window) | copy-start | bytes 884740
  16.4 0.7 %copy-start.10 = (bf16[512,144]{1,0:T(8,128)(2,1)}, bf16[512,144]{1,0:T(8,128)(2,1)S(1)}, u32[]{:S(2)}) copy-start(bf16[512,144]{1,0:T(8,128)(2,1)S(1)} %get-tuple-element.22.unwindow) | copy-start | bytes 442372
  17.1 0.7 %copy-start.11 = (bf16[1024,128]{1,0:T(8,128)(2,1)}, bf16[1024,128]{1,0:T(8,128)(2,1)S(1)}, u32[]{:S(2)}) copy-start(bf16[1024,128]{1,0:T(8,128)(2,1)S(1)} %get-tuple-element.20.second) | copy-start | bytes 786436
  17.8 0.7 %copy-start.12 = (bf16[256,512]{1,0:T(8,128)(2,1)}, bf16[256,512]{1,0:T(8,128)(2,1)S(1)}, u32[]{:S(2)}) copy-start(bf16[256,512]{1,0:T(8,128)(2,1)S(1)} %get-tuple-element.19.band_ref) | copy-start | bytes 786436
  19.5 0.6 %copy-start.13 = (bf16[8,8,896]{2,1,0:T(8,128)(2,1)}, bf16[8,8,896]{2,1,0:T(8,128)(2,1)S(1)}, u32[]{:S(2)}) copy-start(bf16[8,8,896]{2,1,0:T(8,128)(2,1)S(1)} %all-to-all-done) | copy-start | bytes 344068
  20.2 21.7 %copy-start = (bf16[1,16,16,48,128]{4,3,2,1,0:T(8,128)(2,1)S(1)}, bf16[1,16,16,48,128]{4,3,2,1,0:T(8,128)(2,1)}, u32[]{:S(2)}) copy-start(bf16[1,16,16,48,128]{4,3,2,1,0:T(8,128)(2,1)} %param.10) | copy-start | bytes 9437188
  41.9 19.4 %copy-start.7 = (bf16[3,3,3,128]{3,2,1,0:T(4,128)(2,1)S(1)}, bf16[3,3,3,128]{3,2,1,0:T(4,128)(2,1)}, u32[]{:S(2)}) copy-start(bf16[3,3,3,128]{3,2,1,0:T(4,128)(2,1)} %weight_ref.1) | copy-start | bytes 20740
  52.3 9.0 %all-to-all-start.3 = ((bf16[4,56,128]{2,1,0:T(8,128)(2,1)}), bf16[4,56,128]{2,1,0:T(8,128)(2,1)S(1)}, u32[]{:S(2)}, u32[]{:S(2)}) async-start(bf16[4,56,128]{2,1,0:T(8,128)(2,1)} %sum_parts.1), calls=%async_computation.3 | async-start | bytes 114688 | tf_op jit(solution)/shard_map/all_to_all | solution.py:776

commit v9 on v8

--- a/solution.py
+++ b/solution.py
@@ -19,7 +19,7 @@
 VM = pl.BlockSpec(memory_space=pltpu.VMEM)
 HBM = pl.BlockSpec(memory_space=pl.ANY)
 WHOLE = pltpu.CompilerParams(vmem_limit_bytes=60 * 2**20)
-MOST = pltpu.CompilerParams(vmem_limit_bytes=115 * 2**19)
+MOST = pltpu.CompilerParams(vmem_limit_bytes=48 * 2**20)
 PART = pltpu.CompilerParams(vmem_limit_bytes=24 * 2**20)
 
 
@@ -95,6 +95,8 @@
         for k in range(lanes // LANES):
             out_ref[k, pl.ds(3 * group, devices, stride=pitch), :] = edges[:, k * LANES : (k + 1) * LANES]
 
+    copies[1].wait()
+    edge_rows()
     step = frames // chunks
     done = 0
     for chunk in range(chunks):
@@ -105,9 +107,6 @@
             product = mat(weight, feat_ref[frame * pixels : (frame + 1) * pixels, :], NT)
             for k in range(pieces):
                 taps_ref[k, pl.ds(slot, taps, stride=frames), :] = product[:, k * LANES : (k + 1) * LANES]
-        if chunk == 0:
-            copies[1].wait()
-            edge_rows()
         while (done + 1) * devices <= chunk * step or (chunk == chunks - 1 and done < group):
             finish(done)
             done += 1

time: 64.8 us -> 63.6 us (0.981)
  Pallas kernels: 22.3 us -> 19.8 us
  blocking collectives: 19.6 us -> 17.9 us
  local copies, waits for them, and re-layouts: 6.99 us -> 8.58 us
  waiting for transfers between devices: 3.53 us -> 5.08 us
    pallas_call x1, Pallas kernels: 9.55 us -> 7.16 us  [disc_call(): pl.pallas_call(functools.partial(disc_kernel, devices=devices, group=grou...]
    unnamed x32 -> x36, local copies, waits for them, and re-layouts: 5.35 us -> 7.55 us
    all_to_all x1, blocking collectives: 12.2 us -> 10.4 us  [per_device(): lax.all_to_all(values.reshape(devices, pitch, lanes), row, split_axis=0,...]
    all_to_all x1, waiting for transfers between devices: 1.06 us -> 2.61 us  [per_device(): lax.all_to_all(values.reshape(devices, pitch, lanes), row, split_axis=0,...]
  transfers between devices with their start and end apart: 2 -> 2, of which waited for: 2 -> 2; matrix products, arithmetic and copies ran while one was open for 3% -> 2% of each run, Pallas kernels for 4% -> 4%
where the time goes in v9:
time: 63.6 us; the launch traced here: 63.1 us
  Pallas kernels  19.8 us (31%)
  blocking collectives  17.9 us (28%)
  starting transfers between devices  10.8 us (17%)
  local copies, waits for them, and re-layouts  8.58 us (13%)
  waiting for transfers between devices  5.08 us (8%)
  between operations  1.01 us (2%)
    all_to_all x1, blocking collectives, per_device(): lax.all_to_all(values.reshape(devices, pitch, lanes), row, split_axis=0,...  10.4 us
    unnamed x36, local copies, waits for them, and re-layouts  7.55 us
    all_to_all x1, blocking collectives, per_device(): lax.all_to_all(values, axes, split_axis=0, concat_axis=0, tiled=True)  7.46 us
    all_to_all x1, starting transfers between devices, per_device(): lax.all_to_all(values.reshape(devices, pitch, lanes), row, split_axis=0,...  7.29 us
    pallas_call x1, Pallas kernels, disc_call(): pl.pallas_call(functools.partial(disc_kernel, devices=devices, group=grou...  7.16 us
    pallas_call x2, Pallas kernels, taps_call(): pl.pallas_call(functools.partial(kernel, frames=frames, devices=devices,...  4.28 us
    pallas_call x1, Pallas kernels, forward_call(): pl.pallas_call(functools.partial(forward_kernel, frames=frames, devices=d...  4.16 us
    all_to_all x1, starting transfers between devices, per_device(): lax.all_to_all(values, axes, split_axis=0, concat_axis=0, tiled=True)  3.46 us
  transfers between devices with their start and end apart: 2, of which 2 were waited for; matrix products, arithmetic and copies ran while one was open for 2% of the time, Pallas kernels for 4%

profile of v9, /device:TPU:0, one launch (start us, length us, event | category | flops | bytes accessed | tf_op | source)
XLA Modules:
  0.0 63.1 jit_solution(478920598064372690)
XLA Ops:
  0.7 4.2 %forward_taps.1.pay_ref = bf16[64,896]{1,0:T(8,128)(2,1)} custom-call(bf16[12288,128]{1,0:T(8,128)(2,1)} %bitcast.19, bf16[16,3,16,48]{3,2,1,0:T(8,128)(2,1)} %bitcast.25, bf16[3,3,3,128]{3,2,1,0:T(4,128)(2,1)} %weight_ref.1), custom_call_target="tpu_custom_call" | custom-call | flops 84934656 | bytes 3145728 | tf_op jit(solution)/shard_map/forward_taps/pallas_call | solution.py:121
  4.9 7.3 %all-to-all-start = ((bf16[8,8,896]{2,1,0:T(8,128)(2,1)}), bf16[8,8,896]{2,1,0:T(8,128)(2,1)S(1)}, u32[]{:S(2)}, u32[]{:S(2)}) async-start(bf16[8,8,896]{2,1,0:T(8,128)(2,1)} %bitcast.24), calls=%async_computation | async-start | bytes 229376 | tf_op jit(solution)/shard_map/all_to_all | solution.py:757
  12.2 0.9 %copy-done.2 = bf16[64,896]{1,0:T(8,128)(2,1)S(1)} copy-done((bf16[64,896]{1,0:T(8,128)(2,1)S(1)}, bf16[64,896]{1,0:T(8,128)(2,1)}, u32[]{:S(2)}) %copy-start.2) | copy-done | bytes 114712
  13.1 0.3 inner_rows.1.inner_ref
  13.5 0.5 stage_weights.1
  14.0 0.7 %copy-done.8 = bf16[144,1024]{1,0:T(8,128)(2,1)} copy-done((bf16[144,1024]{1,0:T(8,128)(2,1)}, bf16[144,1024]{1,0:T(8,128)(2,1)S(1)}, u32[]{:S(2)}) %copy-start.8) | copy-done | bytes 294936
  14.7 0.7 %copy-done.10 = bf16[512,144]{1,0:T(8,128)(2,1)} copy-done((bf16[512,144]{1,0:T(8,128)(2,1)}, bf16[512,144]{1,0:T(8,128)(2,1)S(1)}, u32[]{:S(2)}) %copy-start.10) | copy-done | bytes 147480
  15.4 0.7 %copy-done.12 = bf16[1024,128]{1,0:T(8,128)(2,1)} copy-done((bf16[1024,128]{1,0:T(8,128)(2,1)}, bf16[1024,128]{1,0:T(8,128)(2,1)S(1)}, u32[]{:S(2)}) %copy-start.12) | copy-done | bytes 262168
  16.1 0.7 %copy-done.14 = bf16[256,512]{1,0:T(8,128)(2,1)} copy-done((bf16[256,512]{1,0:T(8,128)(2,1)}, bf16[256,512]{1,0:T(8,128)(2,1)S(1)}, u32[]{:S(2)}) %copy-start.14) | copy-done | bytes 262168
  16.8 2.6 %all-to-all-done = bf16[8,8,896]{2,1,0:T(8,128)(2,1)S(1)} async-done(((bf16[8,8,896]{2,1,0:T(8,128)(2,1)}), bf16[8,8,896]{2,1,0:T(8,128)(2,1)S(1)}, u32[]{:S(2)}, u32[]{:S(2)}) %all-to-all-start) | async-done | bytes 114720 | tf_op jit(solution)/shard_map/all_to_all | solution.py:757
  19.4 1.0 %copy-done.9 = bf16[144,1024]{1,0:T(8,128)(2,1)S(1)} copy-done((bf16[144,1024]{1,0:T(8,128)(2,1)S(1)}, bf16[144,1024]{1,0:T(8,128)(2,1)}, u32[]{:S(2)}) %copy-start.9) | copy-done | bytes 294936
  20.4 0.9 %copy-done.11 = bf16[512,144]{1,0:T(8,128)(2,1)S(1)} copy-done((bf16[512,144]{1,0:T(8,128)(2,1)S(1)}, bf16[512,144]{1,0:T(8,128)(2,1)}, u32[]{:S(2)}) %copy-start.11) | copy-done | bytes 147480
  21.3 0.9 %copy-done.13 = bf16[1024,128]{1,0:T(8,128)(2,1)S(1)} copy-done((bf16[1024,128]{1,0:T(8,128)(2,1)S(1)}, bf16[1024,128]{1,0:T(8,128)(2,1)}, u32[]{:S(2)}) %copy-start.13) | copy-done | bytes 262168
  22.3 0.9 %copy-done.15 = bf16[256,512]{1,0:T(8,128)(2,1)S(1)} copy-done((bf16[256,512]{1,0:T(8,128)(2,1)S(1)}, bf16[256,512]{1,0:T(8,128)(2,1)}, u32[]{:S(2)}) %copy-start.15) | copy-done | bytes 262168
  23.2 7.2 %disc_rows.1 = bf16[64,896]{1,0:T(8,128)(2,1)S(1)} custom-call(bf16[64,896]{1,0:T(8,128)(2,1)S(1)} %bitcast.28, bf16[16,512]{1,0:T(8,128)(2,1)S(1)} %reshape.47.head_ref, bf16[144,1024]{1,0:T(8,128)(2,1)S(1)} %copy-done.9, bf16[256,512]{1,0:T(8,128)(2,1)S(1)} %copy-done.15, bf16[1024,128]{1,0:T(8,128)(2,1)S(1)} %copy-done.13, ...), custom_call_target="tpu_custom_call" | custom-call | flops 4000000000 | bytes 8000000 | tf_op jit(solution)/shard_map/disc_rows/pallas_call | solution.py:540
  30.4 10.4 %all_to_all.20 = bf16[8,8,896]{2,1,0:T(8,128)(2,1)S(1)} all-to-all(bf16[8,8,896]{2,1,0:T(8,128)(2,1)S(1)} %bitcast.29), channel_id=1, replica_groups=mesh['clip'=4,'far'=4,'near'=2] {'far','near'}, dimensions={0} | all-to-all | bytes 229376 | tf_op jit(solution)/shard_map/all_to_all | solution.py:757
  40.8 2.3 %both_taps.1 = bf16[8,56,128]{2,1,0:T(8,128)(2,1)S(1)} custom-call(f32[48,896]{1,0:T(8,128)S(1)} %inner_rows.1.inner_ref, bf16[64,896]{1,0:T(8,128)(2,1)S(1)} %bitcast.21, bf16[12288,128]{1,0:T(8,128)(2,1)S(1)} %bitcast.20), custom_call_target="tpu_custom_call" | custom-call | flops 169869312 | bytes 4000000 | tf_op jit(solution)/shard_map/both_taps/pallas_call | solution.py:665
  43.1 7.5 %all_to_all.21.parts_ref = bf16[8,56,128]{2,1,0:T(8,128)(2,1)S(1)} all-to-all(bf16[8,56,128]{2,1,0:T(8,128)(2,1)S(1)} %both_taps.1), channel_id=1, replica_groups=mesh['clip'=4,'far'=4,'near'=2] {'clip','near'}, dimensions={0} | all-to-all | bytes 229376 | tf_op jit(solution)/shard_map/all_to_all | solution.py:775
  50.5 0.6 %sum_parts.1 = bf16[4,56,128]{2,1,0:T(8,128)(2,1)} custom-call(bf16[8,56,128]{2,1,0:T(8,128)(2,1)S(1)} %all_to_all.21.parts_ref), custom_call_target="tpu_custom_call" | custom-call | tf_op jit(solution)/shard_map/sum_parts/pallas_call | solution.py:798
  51.2 3.5 %all-to-all-start.3 = ((bf16[4,56,128]{2,1,0:T(8,128)(2,1)}), bf16[4,56,128]{2,1,0:T(8,128)(2,1)S(1)}, u32[]{:S(2)}, u32[]{:S(2)}) async-start(bf16[4,56,128]{2,1,0:T(8,128)(2,1)} %sum_parts.1), calls=%async_computation.3 | async-start | bytes 114688 | tf_op jit(solution)/shard_map/all_to_all | solution.py:775
  55.0 0.7 %copy.25 = bf16[8,2,16,3,48]{4,2,3,1,0:T(8,128)(2,1)} copy(bf16[8,2,16,3,48]{4,2,0,1,3:T(8,128)(2,1)S(1)} %bitcast.30) | data formatting | bytes 147456 | tf_op jit(solution)/shard_map/transpose | solution.py:782
  55.7 2.0 %turn_taps.1.taps_ref = bf16[6144,128]{1,0:T(8,128)(2,1)S(1)} custom-call(f32[48,896]{1,0:T(8,128)S(1)} %inner_rows.1.inner_ref, bf16[64,896]{1,0:T(8,128)(2,1)S(1)} %bitcast.22), custom_call_target="tpu_custom_call" | custom-call | flops 169869312 | bytes 4000000 | tf_op jit(solution)/shard_map/turn_taps/pallas_call | solution.py:665
  57.7 2.5 %all-to-all-done.3.sums_ref = bf16[4,56,128]{2,1,0:T(8,128)(2,1)S(1)} async-done(((bf16[4,56,128]{2,1,0:T(8,128)(2,1)}), bf16[4,56,128]{2,1,0:T(8,128)(2,1)S(1)}, u32[]{:S(2)}, u32[]{:S(2)}) %all-to-all-start.3) | async-done | bytes 57376 | tf_op jit(solution)/shard_map/all_to_all | solution.py:775
  60.2 2.8 %feature_pull.1 = (bf16[12288,128]{1,0:T(8,128)(2,1)}, f32[3,3,3,128]{3,2,1,0:T(4,128)}, f32[1,1]{1,0:T(1,128)}) custom-call(bf16[6144,128]{1,0:T(8,128)(2,1)S(1)} %turn_taps.1.taps_ref, bf16[4,56,128]{2,1,0:T(8,128)(2,1)S(1)} %all-to-all-done.3.sums_ref, bf16[3,3,3,128]{3,2,1,0:T(4,128)(2,1)S(1)} %copy-done.7), custom_call_target="tpu_custom_call" | custom-call | flops 201326592 | bytes 6291456 | tf_op jit(solution)/shard_map/feature_pull/pallas_call | solution.py:721
  (32 shorter events, 0.4 us)
Async XLA Ops:
  0.6 12.8 %copy-start.4 = (bf16[144,1024]{1,0:T(8,128)(2,1)S(1)}, bf16[144,1024]{1,0:T(8,128)(2,1)}, u32[]{:S(2)}) copy-start(bf16[144,1024]{1,0:T(8,128)(2,1)} %constant.4.clone.window_hbm) | copy-start | bytes 884740
  0.6 12.8 %copy-start.6 = (bf16[512,144]{1,0:T(8,128)(2,1)S(1)}, bf16[512,144]{1,0:T(8,128)(2,1)}, u32[]{:S(2)}) copy-start(bf16[512,144]{1,0:T(8,128)(2,1)} %constant.5.clone.unwindow_hbm) | copy-start | bytes 442372
  0.7 11.6 %copy-start.3 = (bf16[1,16,16,3,48]{4,2,3,1,0:T(8,128)(2,1)S(1)}, bf16[1,16,16,3,48]{4,2,3,1,0:T(8,128)(2,1)}, u32[]{:S(2)}) copy-start(bf16[1,16,16,3,48]{4,2,3,1,0:T(8,128)(2,1)} %param.11) | copy-start | bytes 221188
  0.7 11.5 %copy-start.17 = (bf16[4,4,3,64]{3,1,2,0:T(4,128)(2,1)S(1)}, bf16[4,4,3,64]{3,1,2,0:T(4,128)(2,1)}, u32[]{:S(2)}) copy-start(bf16[4,4,3,64]{3,1,2,0:T(4,128)(2,1)} %param.13) | copy-start | bytes 18436
  0.7 11.5 %copy-start.16 = (bf16[4,4,512,1]{2,1,3,0:T(4,128)(2,1)S(1)}, bf16[4,4,512,1]{2,1,3,0:T(4,128)(2,1)}, u32[]{:S(2)}) copy-start(bf16[4,4,512,1]{2,1,3,0:T(4,128)(2,1)} %param.17) | copy-start | bytes 49156
  0.7 12.8 %copy-start.5 = (bf16[4,4,64,128]{3,2,1,0:T(8,128)(2,1)S(1)}, bf16[4,4,64,128]{3,2,1,0:T(8,128)(2,1)}, u32[]{:S(2)}) copy-start(bf16[4,4,64,128]{3,2,1,0:T(8,128)(2,1)} %param.14) | copy-start | bytes 786436
  0.7 12.8 %copy-start.1 = (bf16[4,4,128,256]{3,2,1,0:T(8,128)(2,1)S(1)}, bf16[4,4,128,256]{3,2,1,0:T(8,128)(2,1)}, u32[]{:S(2)}) copy-start(bf16[4,4,128,256]{3,2,1,0:T(8,128)(2,1)} %param.15) | copy-start | bytes 3145732
  4.9 14.5 %all-to-all-start = ((bf16[8,8,896]{2,1,0:T(8,128)(2,1)}), bf16[8,8,896]{2,1,0:T(8,128)(2,1)S(1)}, u32[]{:S(2)}, u32[]{:S(2)}) async-start(bf16[8,8,896]{2,1,0:T(8,128)(2,1)} %bitcast.24), calls=%async_computation | async-start | bytes 229376 | tf_op jit(solution)/shard_map/all_to_all | solution.py:757
  12.2 0.9 %copy-start.2 = (bf16[64,896]{1,0:T(8,128)(2,1)S(1)}, bf16[64,896]{1,0:T(8,128)(2,1)}, u32[]{:S(2)}) copy-start(bf16[64,896]{1,0:T(8,128)(2,1)} %forward_taps.1.pay_ref) | copy-start | bytes 344068
  14.0 0.7 %copy-start.8 = (bf16[144,1024]{1,0:T(8,128)(2,1)}, bf16[144,1024]{1,0:T(8,128)(2,1)S(1)}, u32[]{:S(2)}) copy-start(bf16[144,1024]{1,0:T(8,128)(2,1)S(1)} %get-tuple-element.18.window) | copy-start | bytes 884740
  14.7 0.7 %copy-start.10 = (bf16[512,144]{1,0:T(8,128)(2,1)}, bf16[512,144]{1,0:T(8,128)(2,1)S(1)}, u32[]{:S(2)}) copy-start(bf16[512,144]{1,0:T(8,128)(2,1)S(1)} %get-tuple-element.22.unwindow) | copy-start | bytes 442372
  15.4 0.7 %copy-start.12 = (bf16[1024,128]{1,0:T(8,128)(2,1)}, bf16[1024,128]{1,0:T(8,128)(2,1)S(1)}, u32[]{:S(2)}) copy-start(bf16[1024,128]{1,0:T(8,128)(2,1)S(1)} %get-tuple-element.20.second) | copy-start | bytes 786436
  16.1 0.7 %copy-start.14 = (bf16[256,512]{1,0:T(8,128)(2,1)}, bf16[256,512]{1,0:T(8,128)(2,1)S(1)}, u32[]{:S(2)}) copy-start(bf16[256,512]{1,0:T(8,128)(2,1)S(1)} %get-tuple-element.19.band_ref) | copy-start | bytes 786436
  19.4 1.0 %copy-start.9 = (bf16[144,1024]{1,0:T(8,128)(2,1)S(1)}, bf16[144,1024]{1,0:T(8,128)(2,1)}, u32[]{:S(2)}) copy-start(bf16[144,1024]{1,0:T(8,128)(2,1)} %copy-done.8) | copy-start | bytes 884740
  20.4 0.9 %copy-start.11 = (bf16[512,144]{1,0:T(8,128)(2,1)S(1)}, bf16[512,144]{1,0:T(8,128)(2,1)}, u32[]{:S(2)}) copy-start(bf16[512,144]{1,0:T(8,128)(2,1)} %copy-done.10) | copy-start | bytes 442372
  21.3 0.9 %copy-start.13 = (bf16[1024,128]{1,0:T(8,128)(2,1)S(1)}, bf16[1024,128]{1,0:T(8,128)(2,1)}, u32[]{:S(2)}) copy-start(bf16[1024,128]{1,0:T(8,128)(2,1)} %copy-done.12) | copy-start | bytes 786436
  22.3 0.9 %copy-start.15 = (bf16[256,512]{1,0:T(8,128)(2,1)S(1)}, bf16[256,512]{1,0:T(8,128)(2,1)}, u32[]{:S(2)}) copy-start(bf16[256,512]{1,0:T(8,128)(2,1)} %copy-done.14) | copy-start | bytes 786436
  23.2 17.6 %copy-start = (bf16[1,16,16,48,128]{4,3,2,1,0:T(8,128)(2,1)S(1)}, bf16[1,16,16,48,128]{4,3,2,1,0:T(8,128)(2,1)}, u32[]{:S(2)}) copy-start(bf16[1,16,16,48,128]{4,3,2,1,0:T(8,128)(2,1)} %param.10) | copy-start | bytes 9437188
  40.8 19.4 %copy-start.7 = (bf16[3,3,3,128]{3,2,1,0:T(4,128)(2,1)S(1)}, bf16[3,3,3,128]{3,2,1,0:T(4,128)(2,1)}, u32[]{:S(2)}) copy-start(bf16[3,3,3,128]{3,2,1,0:T(4,128)(2,1)} %weight_ref.1) | copy-start | bytes 20740
  51.2 9.0 %all-to-all-start.3 = ((bf16[4,56,128]{2,1,0:T(8,128)(2,1)}), bf16[4,56,128]{2,1,0:T(8,128)(2,1)S(1)}, u32[]{:S(2)}, u32[]{:S(2)}) async-start(bf16[4,56,128]{2,1,0:T(8,128)(2,1)} %sum_parts.1), calls=%async_computation.3 | async-start | bytes 114688 | tf_op jit(solution)/shard_map/all_to_all | solution.py:775

commit v10 on v9

--- a/solution.py
+++ b/solution.py
@@ -216,8 +216,8 @@
 
 
 def disc_kernel(
-    pay_ref, head_ref, window, band_ref, second, third, unwindow, fourth_hbm, out_ref,
-    zin, fourth, rows_in, act_one, slope_one, cols_two, act_two, slope_two, act_three, cols_four,
+    pay_ref, head_ref, window, band_ref, second, unwindow, third_hbm, fourth_hbm, out_ref,
+    zin, third, fourth, rows_in, act_one, slope_one, cols_two, act_two, slope_two, act_three, cols_four,
     pull_four, pull_three, pull_two, zout, sems, *, devices, group, cols, block_rows, period,
 ):
     lanes = pay_ref.shape[1]
@@ -236,8 +236,9 @@
         )
         for a in range(4)
     ]
-    for copy in copies:
-        copy.start()
+    copies.append(pltpu.make_async_copy(third_hbm, third, sems.at[4]))
+    for i in (4, 0, 1, 2, 3):
+        copies[i].start()
     cells = block_rows // 8
     spot = lambda y, part: pl.ds((y % 8 * group + part) * period + y // 8, devices, stride=cells)
     for k in range(lanes // LANES):
@@ -317,6 +318,7 @@
         ],
         axis=0,
     )
+    copies[4].wait()
     act, slope_three = gate_of(mat(left, third[...]))
     act_three[:, 0:d3] = jnp.zeros((4 * unit, d3), BF16)
     act_three[:, (x3 + 1) * d3 :] = jnp.zeros((4 * unit, d3), BF16)
@@ -453,30 +455,25 @@
         out_ref[:, k * LANES : (k + 1) * LANES] = zout[k].astype(BF16)
 
 
-def windows_of(cols, d1):
-    wide = 3 * cols
-    count = -(-(cols // 2 + 2) // 8)
-    window = np.zeros((wide, count * 2 * LANES), np.float32)
-    unwindow = np.zeros((count * LANES, wide), np.float32)
-    for k in range(count):
-        for c in range(3):
-            for j in range(18):
-                x = 16 * k - 3 + j
-                if 0 <= x < cols:
-                    for e in range(2):
-                        at = e * LANES // 2 + c * 18 + j
-                        window[c * cols + x, (2 * k + e) * LANES + at] = 1.0
-                        unwindow[k * LANES + at, c * cols + x] = 1.0
-    return window, unwindow
-
-
-def stage_kernel(
-    first_ref, window_hbm, unwindow_hbm, second_hbm, third_hbm, window, unwindow, second, third, band, scr, sems
-):
-    pairs = ((window_hbm, window), (second_hbm, second), (third_hbm, third), (unwindow_hbm, unwindow))
-    copies = [pltpu.make_async_copy(source, target, sems.at[i]) for i, (source, target) in enumerate(pairs)]
-    for copy in copies:
-        copy.start()
+def window_of(at, cols):
+    k, rest = at // LANES, at % LANES
+    inner = rest % (LANES // 2)
+    colour = jnp.where(inner >= 18, 1, 0) + jnp.where(inner >= 36, 1, 0)
+    x = 16 * k - 3 + inner - 18 * colour
+    inside = (inner < 54) & (x >= 0) & (x < cols)
+    return jnp.where(inside, colour * cols + x, -1), rest // (LANES // 2)
+
+
+def stage_kernel(first_ref, second_hbm, window, unwindow, second, band, scr, sem, *, cols):
+    copy = pltpu.make_async_copy(second_hbm, second, sem.at[0])
+    copy.start()
+    row = lax.broadcasted_iota(jnp.int32, window.shape, 0)
+    lane = lax.broadcasted_iota(jnp.int32, window.shape, 1)
+    place, half = window_of(lane // (2 * LANES) * LANES + lane % LANES, cols)
+    window[...] = jnp.where((place == row) & (half == lane // LANES % 2), 1.0, 0.0).astype(BF16)
+    place, _ = window_of(lax.broadcasted_iota(jnp.int32, unwindow.shape, 0), cols)
+    column = lax.broadcasted_iota(jnp.int32, unwindow.shape, 1)
+    unwindow[...] = jnp.where(place == column, 1.0, 0.0).astype(BF16)
     d1 = first_ref.shape[-1]
     scr[...] = jnp.zeros_like(scr)
     row = lax.broadcasted_iota(jnp.int32, (18, 8 * d1), 0)
@@ -491,38 +488,30 @@
             at = a * LANES // 2 + c * 18
             scr[at : at + 18, :] = block
     band[...] = scr[...].astype(BF16)
-    for copy in copies:
-        copy.wait()
-
-
-def stage_call(first, second, third, cols):
-    d1, d2, d3 = first.shape[-1], second.shape[-1], third.shape[-1]
-    window, unwindow = windows_of(cols, d1)
-    operands = (
-        first,
-        jnp.asarray(window, BF16),
-        jnp.asarray(unwindow, BF16),
-        second.reshape(16 * d1, d2),
-        third.reshape(16 * d2, d3),
-    )
-    shapes = [value.shape for value in operands[1:]] + [(2 * LANES, 8 * d1)]
+    copy.wait()
+
+
+def stage_call(first, second, cols):
+    d1, d2 = first.shape[-1], second.shape[-1]
+    count = -(-(cols // 2 + 2) // 8)
+    shapes = [(3 * cols, count * 2 * LANES), (count * LANES, 3 * cols), (16 * d1, d2), (2 * LANES, 8 * d1)]
     return pl.pallas_call(
-        stage_kernel,
+        functools.partial(stage_kernel, cols=cols),
         out_shape=tuple(jax.ShapeDtypeStruct(shape, BF16) for shape in shapes),
-        in_specs=[VM] + [HBM] * 4,
-        out_specs=(VM,) * 5,
-        scratch_shapes=[pltpu.VMEM((2 * LANES, 8 * d1), F32), pltpu.SemaphoreType.DMA((4,))],
+        in_specs=[VM, HBM],
+        out_specs=(VM,) * 4,
+        scratch_shapes=[pltpu.VMEM((2 * LANES, 8 * d1), F32), pltpu.SemaphoreType.DMA((1,))],
         compiler_params=PART,
         cost_estimate=pl.CostEstimate(flops=10**8, bytes_accessed=4 * 10**6, transcendentals=0),
         name="stage_weights",
-    )(*operands)
-
-
-def disc_call(payload, staged, fourth, head, devices, group, cols, block_rows):
+    )(first, second.reshape(16 * d1, d2))
+
+
+def disc_call(payload, staged, third, fourth, head, devices, group, cols, block_rows):
     period = devices * block_rows // 8
     unit = group * period
-    window, unwindow, second, third, band = staged
-    d1, d2, d3, d4 = band.shape[1] // 8, second.shape[1], third.shape[1], fourth.shape[-1]
+    window, unwindow, second, band = staged
+    d1, d2, d3, d4 = band.shape[1] // 8, second.shape[1], third.shape[-1], fourth.shape[-1]
     x2, x3 = cols // 4, cols // 8
     x4 = x3 - 1
     width_one = (cols // 2 + 2) * d1
@@ -532,8 +521,8 @@
         window,
         band,
         second,
-        third,
         unwindow,
+        third.reshape(16 * d2, d3),
         fourth.reshape(16 * d3, d4),
     )
     lanes = payload.shape[1]
@@ -542,10 +531,11 @@
             disc_kernel, devices=devices, group=group, cols=cols, block_rows=block_rows, period=period
         ),
         out_shape=jax.ShapeDtypeStruct(payload.shape, BF16),
-        in_specs=[VM] * 7 + [HBM],
+        in_specs=[VM] * 6 + [HBM] * 2,
         out_specs=VM,
         scratch_shapes=[
             pltpu.VMEM((lanes // LANES, payload.shape[0], LANES), F32),
+            pltpu.VMEM((16 * d2, d3), BF16),
             pltpu.VMEM((16 * d3, d4), BF16),
             pltpu.VMEM((2, 8 * unit, LANES), F32),
             pltpu.VMEM((6 * unit, width_one), BF16),
@@ -559,7 +549,7 @@
             pltpu.VMEM((x3 * unit, 16 * d2), F32),
             pltpu.VMEM((x2 * 2 * unit, 16 * d1), F32),
             pltpu.VMEM((lanes // LANES, payload.shape[0], LANES), F32),
-            pltpu.SemaphoreType.DMA((4,)),
+            pltpu.SemaphoreType.DMA((5,)),
         ],
         compiler_params=MOST,
         cost_estimate=pl.CostEstimate(flops=4 * 10**9, bytes_accessed=8 * 10**6, transcendentals=10**6),
@@ -760,9 +750,9 @@
     arrived = trade(payload)
     inner = inner_call(payload, wanted, frames, devices, group, block_rows, cols)
     _, disc_first = lax.optimization_barrier((payload, disc_first))
-    staged = stage_call(disc_first, disc_second, disc_third, cols)
+    staged = stage_call(disc_first, disc_second, cols)
     arrived, inner = lax.optimization_barrier((arrived, inner))
-    sent = disc_call(arrived, staged, disc_fourth, disc_head, devices, group, cols, block_rows)
+    sent = disc_call(arrived, staged, disc_third, disc_fourth, disc_head, devices, group, cols, block_rows)
     returned = trade(sent)
     taps_scratch = pltpu.VMEM((block_rows * cols // LANES, 32 * frames, LANES), F32)
     plane_scratch = pltpu.VMEM((lanes // LANES, devices * pitch, LANES), F32)

time: 63.6 us -> 59.2 us (0.931)
  local copies, waits for them, and re-layouts: 8.58 us -> 1.97 us
  waiting for transfers between devices: 5.08 us -> 7.71 us
  blocking collectives: 17.9 us -> 17.1 us
    unnamed x36 -> x16, local copies, waits for them, and re-layouts: 7.55 us -> 0.93 us
    all_to_all x1, waiting for transfers between devices: 2.61 us -> 5.24 us  [per_device(): lax.all_to_all(values.reshape(devices, pitch, lanes), row, split_axis=0,...]
    all_to_all x1, blocking collectives: 10.4 us -> 9.62 us  [per_device(): lax.all_to_all(values.reshape(devices, pitch, lanes), row, split_axis=0,...]
  transfers between devices with their start and end apart: 2 -> 2, of which waited for: 2 -> 2; matrix products, arithmetic and copies ran while one was open for 2% -> 2% of each run, Pallas kernels for 4% -> 5%
where the time goes in v10:
time: 59.2 us; the launch traced here: 58.7 us
  Pallas kernels  20.3 us (34%)
  blocking collectives  17.1 us (29%)
  starting transfers between devices  10.7 us (18%)
  waiting for transfers between devices  7.71 us (13%)
  local copies, waits for them, and re-layouts  1.97 us (3%)
  between operations  0.95 us (2%)
    all_to_all x1, blocking collectives, per_device(): lax.all_to_all(values.reshape(devices, pitch, lanes), row, split_axis=0,...  9.62 us
    all_to_all x1, blocking collectives, per_device(): lax.all_to_all(values, axes, split_axis=0, concat_axis=0, tiled=True)  7.44 us
    pallas_call x1, Pallas kernels, disc_call(): pl.pallas_call(functools.partial(disc_kernel, devices=devices, group=grou...  7.42 us
    all_to_all x1, starting transfers between devices, per_device(): lax.all_to_all(values.reshape(devices, pitch, lanes), row, split_axis=0,...  7.29 us
    all_to_all x1, waiting for transfers between devices, per_device(): lax.all_to_all(values.reshape(devices, pitch, lanes), row, split_axis=0,...  5.24 us
    pallas_call x2, Pallas kernels, taps_call(): pl.pallas_call(functools.partial(kernel, frames=frames, devices=devices,...  4.28 us
    pallas_call x1, Pallas kernels, forward_call(): pl.pallas_call(functools.partial(forward_kernel, frames=frames, devices=d...  4.13 us
    all_to_all x1, starting transfers between devices, per_device(): lax.all_to_all(values, axes, split_axis=0, concat_axis=0, tiled=True)  3.46 us
  transfers between devices with their start and end apart: 2, of which 2 were waited for; matrix products, arithmetic and copies ran while one was open for 2% of the time, Pallas kernels for 5%

profile of v10, /device:TPU:0, one launch (start us, length us, event | category | flops | bytes accessed | tf_op | source)
XLA Modules:
  0.0 58.7 jit_solution(13268363231684557290)
XLA Ops:
  0.6 0.0 copy-start.2
  0.6 0.0 copy-start.7
  0.7 0.0 copy-start.6
  0.7 0.0 copy-start.5
  0.7 0.0 copy-start.4
  0.7 4.1 %forward_taps.1.pay_ref = bf16[64,896]{1,0:T(8,128)(2,1)} custom-call(bf16[12288,128]{1,0:T(8,128)(2,1)} %bitcast.19, bf16[16,3,16,48]{3,2,1,0:T(8,128)(2,1)} %bitcast.24, bf16[3,3,3,128]{3,2,1,0:T(4,128)(2,1)} %weight_ref.1), custom_call_target="tpu_custom_call" | custom-call | flops 84934656 | bytes 3145728 | tf_op jit(solution)/shard_map/forward_taps/pallas_call | solution.py:121
  4.8 7.3 %all-to-all-start = ((bf16[8,8,896]{2,1,0:T(8,128)(2,1)}), bf16[8,8,896]{2,1,0:T(8,128)(2,1)S(1)}, u32[]{:S(2)}, u32[]{:S(2)}) async-start(bf16[8,8,896]{2,1,0:T(8,128)(2,1)} %bitcast.23), calls=%async_computation | async-start | bytes 229376 | tf_op jit(solution)/shard_map/all_to_all | solution.py:747
  12.2 0.0 copy-start.1
  12.2 0.9 %copy-done.1 = bf16[64,896]{1,0:T(8,128)(2,1)S(1)} copy-done((bf16[64,896]{1,0:T(8,128)(2,1)S(1)}, bf16[64,896]{1,0:T(8,128)(2,1)}, u32[]{:S(2)}) %copy-start.1) | copy-done | bytes 114712
  13.1 0.3 inner_rows.1.inner_ref
  13.4 0.7 %stage_weights.1 = (bf16[144,1024]{1,0:T(8,128)(2,1)S(1)}, bf16[512,144]{1,0:T(8,128)(2,1)S(1)}, bf16[1024,128]{1,0:T(8,128)(2,1)S(1)}, bf16[256,512]{1,0:T(8,128)(2,1)S(1)}) custom-call(bf16[4,4,3,64]{3,2,1,0:T(4,128)(2,1)S(1)} %copy.21.first_ref, bf16[1024,128]{1,0:T(8,128)(2,1)S(1)} %bitcast.29), custom_call_target="tpu_custom_call" | custom-call | flops 100000000 | bytes 4000000 | tf_op jit(solution)/shard_map/stage_weights/pallas_call | solution.py:498
  14.1 5.2 %all-to-all-done = bf16[8,8,896]{2,1,0:T(8,128)(2,1)S(1)} async-done(((bf16[8,8,896]{2,1,0:T(8,128)(2,1)}), bf16[8,8,896]{2,1,0:T(8,128)(2,1)S(1)}, u32[]{:S(2)}, u32[]{:S(2)}) %all-to-all-start) | async-done | bytes 114720 | tf_op jit(solution)/shard_map/all_to_all | solution.py:747
  19.4 7.4 %disc_rows.1 = bf16[64,896]{1,0:T(8,128)(2,1)S(1)} custom-call(bf16[64,896]{1,0:T(8,128)(2,1)S(1)} %bitcast.26, bf16[16,512]{1,0:T(8,128)(2,1)S(1)} %reshape.47.head_ref, bf16[144,1024]{1,0:T(8,128)(2,1)S(1)} %get-tuple-element.17.window, bf16[256,512]{1,0:T(8,128)(2,1)S(1)} %get-tuple-element.18.band_ref, bf16[1024,128]{1,0:T(8,128)(2,1)S(1)} %get-tuple-element.19.second, ...), custom_call_target="tpu_custom_call" | custom-call | flops 4000000000 | bytes 8000000 | tf_op jit(solution)/shard_map/disc_rows/pallas_call | solution.py:529
  26.8 9.6 %all_to_all.20 = bf16[8,8,896]{2,1,0:T(8,128)(2,1)S(1)} all-to-all(bf16[8,8,896]{2,1,0:T(8,128)(2,1)S(1)} %bitcast.27), channel_id=1, replica_groups=mesh['clip'=4,'far'=4,'near'=2] {'far','near'}, dimensions={0} | all-to-all | bytes 229376 | tf_op jit(solution)/shard_map/all_to_all | solution.py:747
  36.4 2.3 %both_taps.1 = bf16[8,56,128]{2,1,0:T(8,128)(2,1)S(1)} custom-call(f32[48,896]{1,0:T(8,128)S(1)} %inner_rows.1.inner_ref, bf16[64,896]{1,0:T(8,128)(2,1)S(1)} %bitcast.21, bf16[12288,128]{1,0:T(8,128)(2,1)S(1)} %bitcast.20), custom_call_target="tpu_custom_call" | custom-call | flops 169869312 | bytes 4000000 | tf_op jit(solution)/shard_map/both_taps/pallas_call | solution.py:655
  38.7 7.4 %all_to_all.21.parts_ref = bf16[8,56,128]{2,1,0:T(8,128)(2,1)S(1)} all-to-all(bf16[8,56,128]{2,1,0:T(8,128)(2,1)S(1)} %both_taps.1), channel_id=1, replica_groups=mesh['clip'=4,'far'=4,'near'=2] {'clip','near'}, dimensions={0} | all-to-all | bytes 229376 | tf_op jit(solution)/shard_map/all_to_all | solution.py:765
  46.1 0.6 %sum_parts.1 = bf16[4,56,128]{2,1,0:T(8,128)(2,1)} custom-call(bf16[8,56,128]{2,1,0:T(8,128)(2,1)S(1)} %all_to_all.21.parts_ref), custom_call_target="tpu_custom_call" | custom-call | tf_op jit(solution)/shard_map/sum_parts/pallas_call | solution.py:788
  46.8 3.5 %all-to-all-start.3 = ((bf16[4,56,128]{2,1,0:T(8,128)(2,1)}), bf16[4,56,128]{2,1,0:T(8,128)(2,1)S(1)}, u32[]{:S(2)}, u32[]{:S(2)}) async-start(bf16[4,56,128]{2,1,0:T(8,128)(2,1)} %sum_parts.1), calls=%async_computation.3 | async-start | bytes 114688 | tf_op jit(solution)/shard_map/all_to_all | solution.py:765
  50.2 0.1 slice.4
  50.4 0.2 reshape.54
  50.6 0.7 %copy.23 = bf16[8,2,16,3,48]{4,2,3,1,0:T(8,128)(2,1)} copy(bf16[8,2,16,3,48]{4,2,0,1,3:T(8,128)(2,1)S(1)} %bitcast.30) | data formatting | bytes 147456 | tf_op jit(solution)/shard_map/transpose | solution.py:772
  51.3 2.0 %turn_taps.1.taps_ref = bf16[6144,128]{1,0:T(8,128)(2,1)S(1)} custom-call(f32[48,896]{1,0:T(8,128)S(1)} %inner_rows.1.inner_ref, bf16[64,896]{1,0:T(8,128)(2,1)S(1)} %bitcast.22), custom_call_target="tpu_custom_call" | custom-call | flops 169869312 | bytes 4000000 | tf_op jit(solution)/shard_map/turn_taps/pallas_call | solution.py:655
  53.3 2.5 %all-to-all-done.3.sums_ref = bf16[4,56,128]{2,1,0:T(8,128)(2,1)S(1)} async-done(((bf16[4,56,128]{2,1,0:T(8,128)(2,1)}), bf16[4,56,128]{2,1,0:T(8,128)(2,1)S(1)}, u32[]{:S(2)}, u32[]{:S(2)}) %all-to-all-start.3) | async-done | bytes 57376 | tf_op jit(solution)/shard_map/all_to_all | solution.py:765
  55.8 2.8 %feature_pull.1 = (bf16[12288,128]{1,0:T(8,128)(2,1)}, f32[3,3,3,128]{3,2,1,0:T(4,128)}, f32[1,1]{1,0:T(1,128)}) custom-call(bf16[6144,128]{1,0:T(8,128)(2,1)S(1)} %turn_taps.1.taps_ref, bf16[4,56,128]{2,1,0:T(8,128)(2,1)S(1)} %all-to-all-done.3.sums_ref, bf16[3,3,3,128]{3,2,1,0:T(4,128)(2,1)S(1)} %copy-done.3), custom_call_target="tpu_custom_call" | custom-call | flops 201326592 | bytes 6291456 | tf_op jit(solution)/shard_map/feature_pull/pallas_call | solution.py:711
  (12 shorter events, 0.1 us)
Async XLA Ops:
  0.6 11.5 %copy-start.2 = (bf16[1,16,16,3,48]{4,2,3,1,0:T(8,128)(2,1)S(1)}, bf16[1,16,16,3,48]{4,2,3,1,0:T(8,128)(2,1)}, u32[]{:S(2)}) copy-start(bf16[1,16,16,3,48]{4,2,3,1,0:T(8,128)(2,1)} %param.9) | copy-start | bytes 221188
  0.6 11.5 %copy-start.7 = (bf16[4,4,3,64]{3,1,2,0:T(4,128)(2,1)S(1)}, bf16[4,4,3,64]{3,1,2,0:T(4,128)(2,1)}, u32[]{:S(2)}) copy-start(bf16[4,4,3,64]{3,1,2,0:T(4,128)(2,1)} %param.11) | copy-start | bytes 18436
  0.7 11.5 %copy-start.6 = (bf16[4,4,512,1]{2,1,3,0:T(4,128)(2,1)S(1)}, bf16[4,4,512,1]{2,1,3,0:T(4,128)(2,1)}, u32[]{:S(2)}) copy-start(bf16[4,4,512,1]{2,1,3,0:T(4,128)(2,1)} %param.15) | copy-start | bytes 49156
  0.7 12.7 %copy-start.5 = (bf16[4,4,64,128]{3,2,1,0:T(8,128)(2,1)S(1)}, bf16[4,4,64,128]{3,2,1,0:T(8,128)(2,1)}, u32[]{:S(2)}) copy-start(bf16[4,4,64,128]{3,2,1,0:T(8,128)(2,1)} %param.12) | copy-start | bytes 786436
  0.7 18.7 %copy-start.4 = (bf16[4,4,128,256]{3,2,1,0:T(8,128)(2,1)S(1)}, bf16[4,4,128,256]{3,2,1,0:T(8,128)(2,1)}, u32[]{:S(2)}) copy-start(bf16[4,4,128,256]{3,2,1,0:T(8,128)(2,1)} %param.13) | copy-start | bytes 3145732
  4.8 14.5 %all-to-all-start = ((bf16[8,8,896]{2,1,0:T(8,128)(2,1)}), bf16[8,8,896]{2,1,0:T(8,128)(2,1)S(1)}, u32[]{:S(2)}, u32[]{:S(2)}) async-start(bf16[8,8,896]{2,1,0:T(8,128)(2,1)} %bitcast.23), calls=%async_computation | async-start | bytes 229376 | tf_op jit(solution)/shard_map/all_to_all | solution.py:747
  12.2 0.9 %copy-start.1 = (bf16[64,896]{1,0:T(8,128)(2,1)S(1)}, bf16[64,896]{1,0:T(8,128)(2,1)}, u32[]{:S(2)}) copy-start(bf16[64,896]{1,0:T(8,128)(2,1)} %forward_taps.1.pay_ref) | copy-start | bytes 344068
  19.3 17.1 %copy-start = (bf16[1,16,16,48,128]{4,3,2,1,0:T(8,128)(2,1)S(1)}, bf16[1,16,16,48,128]{4,3,2,1,0:T(8,128)(2,1)}, u32[]{:S(2)}) copy-start(bf16[1,16,16,48,128]{4,3,2,1,0:T(8,128)(2,1)} %param.8) | copy-start | bytes 9437188
  36.4 19.3 %copy-start.3 = (bf16[3,3,3,128]{3,2,1,0:T(4,128)(2,1)S(1)}, bf16[3,3,3,128]{3,2,1,0:T(4,128)(2,1)}, u32[]{:S(2)}) copy-start(bf16[3,3,3,128]{3,2,1,0:T(4,128)(2,1)} %weight_ref.1) | copy-start | bytes 20740
  46.8 9.0 %all-to-all-start.3 = ((bf16[4,56,128]{2,1,0:T(8,128)(2,1)}), bf16[4,56,128]{2,1,0:T(8,128)(2,1)S(1)}, u32[]{:S(2)}, u32[]{:S(2)}) async-start(bf16[4,56,128]{2,1,0:T(8,128)(2,1)} %sum_parts.1), calls=%async_computation.3 | async-start | bytes 114688 | tf_op jit(solution)/shard_map/all_to_all | solution.py:765

commit v11 on v10

--- a/solution.py
+++ b/solution.py
@@ -37,7 +37,7 @@
 
 def forward_kernel(
     feat_hbm, target_hbm, weight_hbm, pay_ref, feat_ref, target_ref, weight_ref, weight_scr, target_scr,
-    taps_ref, out_ref, sems, *, frames, devices, group, cols, lanes, chunks,
+    out_ref, sems, *taps_refs, frames, devices, group, cols, lanes, chunks,
 ):
     pixels = feat_ref.shape[0] // frames
     pieces = pixels // LANES
@@ -65,8 +65,8 @@
 
     def finish(part):
         def tap(a, b, o):
-            rows = pl.ds(((a * 3 + b) * 3 + o) * frames + part * devices, devices)
-            return jnp.concatenate([taps_ref[k, rows, :] for k in range(pieces)], axis=1)
+            rows = pl.ds(((a * 3 + b) * 3 + o) * devices, devices)
+            return jnp.concatenate([taps_refs[part][k, rows, :] for k in range(pieces)], axis=1)
 
         for o in range(3):
             total = None
@@ -106,7 +106,8 @@
             frame = slot % devices * group + slot // devices
             product = mat(weight, feat_ref[frame * pixels : (frame + 1) * pixels, :], NT)
             for k in range(pieces):
-                taps_ref[k, pl.ds(slot, taps, stride=frames), :] = product[:, k * LANES : (k + 1) * LANES]
+                rows = pl.ds(slot % devices, taps, stride=devices)
+                taps_refs[slot // devices][k, rows, :] = product[:, k * LANES : (k + 1) * LANES]
         while (done + 1) * devices <= chunk * step or (chunk == chunks - 1 and done < group):
             finish(done)
             done += 1
@@ -131,10 +132,10 @@
             pltpu.VMEM(weight.shape, BF16),
             pltpu.VMEM((32, channels), F32),
             pltpu.VMEM((3 * pixels // cols * frames, LANES), F32),
-            pltpu.VMEM((pixels // LANES, 32 * frames, LANES), F32),
             pltpu.VMEM((lanes // LANES, devices * pitch, LANES), F32),
             pltpu.SemaphoreType.DMA((frames + 2,)),
-        ],
+        ]
+        + [pltpu.VMEM((pixels // LANES, 32 * devices, LANES), F32)] * group,
         compiler_params=WHOLE,
         cost_estimate=pl.CostEstimate(flops=2 * features.size * 27, bytes_accessed=2 * features.size, transcendentals=0),
         name="forward_taps",
@@ -335,12 +336,6 @@
                 a * unit : (a + 1) * unit, x * d3 : (x + 4) * d3
             ]
     edge_planes(zin, zout, firsts, lasts, devices, group, cols, lanes, pitch)
-    pre = None
-    for a in range(4):
-        copies[a].wait()
-        term = mat(cols_four[:, a * quarter : (a + 1) * quarter], fourth[a * quarter : (a + 1) * quarter, :])
-        pre = term if pre is None else pre + term
-    _, slope = gate_of(pre)
     row = lax.broadcasted_iota(jnp.int32, (unit, d4), 0) % period
     head = head_ref[...].astype(F32) * -loss_scale
     heads = []
@@ -353,6 +348,12 @@
             term = jnp.where(inside, jnp.broadcast_to(tap, (unit, d4)), 0.0)
             total = term if total is None else total + term
         heads.append(total)
+    pre = None
+    for a in range(4):
+        copies[a].wait()
+        term = mat(cols_four[:, a * quarter : (a + 1) * quarter], fourth[a * quarter : (a + 1) * quarter, :])
+        pre = term if pre is None else pre + term
+    _, slope = gate_of(pre)
     cot = (jnp.concatenate(heads, axis=0) * slope).astype(BF16)
     pull_four[...] = mat(cot, fourth[...], NT)
     cots = []

time: 59.2 us -> 59.1 us (level)
  no operation moved by 1% of the time
where the time goes in v11:
time: 59.1 us; the launch traced here: 58.6 us
  Pallas kernels  20.2 us (34%)
  blocking collectives  17.1 us (29%)
  starting transfers between devices  10.8 us (18%)
  waiting for transfers between devices  7.71 us (13%)
  local copies, waits for them, and re-layouts  1.97 us (3%)
  between operations  0.95 us (2%)
    all_to_all x1, blocking collectives, per_device(): lax.all_to_all(values.reshape(devices, pitch, lanes), row, split_axis=0,...  9.62 us
    all_to_all x1, blocking collectives, per_device(): lax.all_to_all(values, axes, split_axis=0, concat_axis=0, tiled=True)  7.46 us
    pallas_call x1, Pallas kernels, disc_call(): pl.pallas_call(functools.partial(disc_kernel, devices=devices, group=grou...  7.41 us
    all_to_all x1, starting transfers between devices, per_device(): lax.all_to_all(values.reshape(devices, pitch, lanes), row, split_axis=0,...  7.29 us
    all_to_all x1, waiting for transfers between devices, per_device(): lax.all_to_all(values.reshape(devices, pitch, lanes), row, split_axis=0,...  5.24 us
    pallas_call x2, Pallas kernels, taps_call(): pl.pallas_call(functools.partial(kernel, frames=frames, devices=devices,...  4.28 us
    pallas_call x1, Pallas kernels, forward_call(): pl.pallas_call(functools.partial(forward_kernel, frames=frames, devices=d...  4.02 us
    all_to_all x1, starting transfers between devices, per_device(): lax.all_to_all(values, axes, split_axis=0, concat_axis=0, tiled=True)  3.46 us
  transfers between devices with their start and end apart: 2, of which 2 were waited for; matrix products, arithmetic and copies ran while one was open for 2% of the time, Pallas kernels for 5%

profile of v11, /device:TPU:0, one launch (start us, length us, event | category | flops | bytes accessed | tf_op | source)
XLA Modules:
  0.0 58.6 jit_solution(9372162236229357608)
XLA Ops:
  0.6 0.0 copy-start.2
  0.6 0.0 copy-start.7
  0.7 0.0 copy-start.6
  0.7 0.0 copy-start.5
  0.7 0.0 copy-start.4
  0.7 4.0 %forward_taps.1.pay_ref = bf16[64,896]{1,0:T(8,128)(2,1)} custom-call(bf16[12288,128]{1,0:T(8,128)(2,1)} %bitcast.19, bf16[16,3,16,48]{3,2,1,0:T(8,128)(2,1)} %bitcast.24, bf16[3,3,3,128]{3,2,1,0:T(4,128)(2,1)} %weight_ref.1), custom_call_target="tpu_custom_call" | custom-call | flops 84934656 | bytes 3145728 | tf_op jit(solution)/shard_map/forward_taps/pallas_call | solution.py:122
  4.7 7.3 %all-to-all-start = ((bf16[8,8,896]{2,1,0:T(8,128)(2,1)}), bf16[8,8,896]{2,1,0:T(8,128)(2,1)S(1)}, u32[]{:S(2)}, u32[]{:S(2)}) async-start(bf16[8,8,896]{2,1,0:T(8,128)(2,1)} %bitcast.23), calls=%async_computation | async-start | bytes 229376 | tf_op jit(solution)/shard_map/all_to_all | solution.py:748
  12.1 0.0 copy-start.1
  12.1 0.9 %copy-done.1 = bf16[64,896]{1,0:T(8,128)(2,1)S(1)} copy-done((bf16[64,896]{1,0:T(8,128)(2,1)S(1)}, bf16[64,896]{1,0:T(8,128)(2,1)}, u32[]{:S(2)}) %copy-start.1) | copy-done | bytes 114712
  13.0 0.3 inner_rows.1.inner_ref
  13.3 0.7 %stage_weights.1 = (bf16[144,1024]{1,0:T(8,128)(2,1)S(1)}, bf16[512,144]{1,0:T(8,128)(2,1)S(1)}, bf16[1024,128]{1,0:T(8,128)(2,1)S(1)}, bf16[256,512]{1,0:T(8,128)(2,1)S(1)}) custom-call(bf16[4,4,3,64]{3,2,1,0:T(4,128)(2,1)S(1)} %copy.21.first_ref, bf16[1024,128]{1,0:T(8,128)(2,1)S(1)} %bitcast.29), custom_call_target="tpu_custom_call" | custom-call | flops 100000000 | bytes 4000000 | tf_op jit(solution)/shard_map/stage_weights/pallas_call | solution.py:499
  14.0 5.2 %all-to-all-done = bf16[8,8,896]{2,1,0:T(8,128)(2,1)S(1)} async-done(((bf16[8,8,896]{2,1,0:T(8,128)(2,1)}), bf16[8,8,896]{2,1,0:T(8,128)(2,1)S(1)}, u32[]{:S(2)}, u32[]{:S(2)}) %all-to-all-start) | async-done | bytes 114720 | tf_op jit(solution)/shard_map/all_to_all | solution.py:748
  19.2 7.4 %disc_rows.1 = bf16[64,896]{1,0:T(8,128)(2,1)S(1)} custom-call(bf16[64,896]{1,0:T(8,128)(2,1)S(1)} %bitcast.26, bf16[16,512]{1,0:T(8,128)(2,1)S(1)} %reshape.47.head_ref, bf16[144,1024]{1,0:T(8,128)(2,1)S(1)} %get-tuple-element.17.window, bf16[256,512]{1,0:T(8,128)(2,1)S(1)} %get-tuple-element.18.band_ref, bf16[1024,128]{1,0:T(8,128)(2,1)S(1)} %get-tuple-element.19.second, ...), custom_call_target="tpu_custom_call" | custom-call | flops 4000000000 | bytes 8000000 | tf_op jit(solution)/shard_map/disc_rows/pallas_call | solution.py:530
  26.7 9.6 %all_to_all.20 = bf16[8,8,896]{2,1,0:T(8,128)(2,1)S(1)} all-to-all(bf16[8,8,896]{2,1,0:T(8,128)(2,1)S(1)} %bitcast.27), channel_id=1, replica_groups=mesh['clip'=4,'far'=4,'near'=2] {'far','near'}, dimensions={0} | all-to-all | bytes 229376 | tf_op jit(solution)/shard_map/all_to_all | solution.py:748
  36.3 2.3 %both_taps.1 = bf16[8,56,128]{2,1,0:T(8,128)(2,1)S(1)} custom-call(f32[48,896]{1,0:T(8,128)S(1)} %inner_rows.1.inner_ref, bf16[64,896]{1,0:T(8,128)(2,1)S(1)} %bitcast.21, bf16[12288,128]{1,0:T(8,128)(2,1)S(1)} %bitcast.20), custom_call_target="tpu_custom_call" | custom-call | flops 169869312 | bytes 4000000 | tf_op jit(solution)/shard_map/both_taps/pallas_call | solution.py:656
  38.6 7.5 %all_to_all.21.parts_ref = bf16[8,56,128]{2,1,0:T(8,128)(2,1)S(1)} all-to-all(bf16[8,56,128]{2,1,0:T(8,128)(2,1)S(1)} %both_taps.1), channel_id=1, replica_groups=mesh['clip'=4,'far'=4,'near'=2] {'clip','near'}, dimensions={0} | all-to-all | bytes 229376 | tf_op jit(solution)/shard_map/all_to_all | solution.py:766
  46.0 0.6 %sum_parts.1 = bf16[4,56,128]{2,1,0:T(8,128)(2,1)} custom-call(bf16[8,56,128]{2,1,0:T(8,128)(2,1)S(1)} %all_to_all.21.parts_ref), custom_call_target="tpu_custom_call" | custom-call | tf_op jit(solution)/shard_map/sum_parts/pallas_call | solution.py:789
  46.7 3.5 %all-to-all-start.3 = ((bf16[4,56,128]{2,1,0:T(8,128)(2,1)}), bf16[4,56,128]{2,1,0:T(8,128)(2,1)S(1)}, u32[]{:S(2)}, u32[]{:S(2)}) async-start(bf16[4,56,128]{2,1,0:T(8,128)(2,1)} %sum_parts.1), calls=%async_computation.3 | async-start | bytes 114688 | tf_op jit(solution)/shard_map/all_to_all | solution.py:766
  50.1 0.1 slice.4
  50.3 0.2 reshape.54
  50.5 0.7 %copy.23 = bf16[8,2,16,3,48]{4,2,3,1,0:T(8,128)(2,1)} copy(bf16[8,2,16,3,48]{4,2,0,1,3:T(8,128)(2,1)S(1)} %bitcast.30) | data formatting | bytes 147456 | tf_op jit(solution)/shard_map/transpose | solution.py:773
  51.2 2.0 %turn_taps.1.taps_ref = bf16[6144,128]{1,0:T(8,128)(2,1)S(1)} custom-call(f32[48,896]{1,0:T(8,128)S(1)} %inner_rows.1.inner_ref, bf16[64,896]{1,0:T(8,128)(2,1)S(1)} %bitcast.22), custom_call_target="tpu_custom_call" | custom-call | flops 169869312 | bytes 4000000 | tf_op jit(solution)/shard_map/turn_taps/pallas_call | solution.py:656
  53.2 2.5 %all-to-all-done.3.sums_ref = bf16[4,56,128]{2,1,0:T(8,128)(2,1)S(1)} async-done(((bf16[4,56,128]{2,1,0:T(8,128)(2,1)}), bf16[4,56,128]{2,1,0:T(8,128)(2,1)S(1)}, u32[]{:S(2)}, u32[]{:S(2)}) %all-to-all-start.3) | async-done | bytes 57376 | tf_op jit(solution)/shard_map/all_to_all | solution.py:766
  55.7 2.8 %feature_pull.1 = (bf16[12288,128]{1,0:T(8,128)(2,1)}, f32[3,3,3,128]{3,2,1,0:T(4,128)}, f32[1,1]{1,0:T(1,128)}) custom-call(bf16[6144,128]{1,0:T(8,128)(2,1)S(1)} %turn_taps.1.taps_ref, bf16[4,56,128]{2,1,0:T(8,128)(2,1)S(1)} %all-to-all-done.3.sums_ref, bf16[3,3,3,128]{3,2,1,0:T(4,128)(2,1)S(1)} %copy-done.3), custom_call_target="tpu_custom_call" | custom-call | flops 201326592 | bytes 6291456 | tf_op jit(solution)/shard_map/feature_pull/pallas_call | solution.py:712
  (12 shorter events, 0.1 us)
Async XLA Ops:
  0.6 11.4 %copy-start.2 = (bf16[1,16,16,3,48]{4,2,3,1,0:T(8,128)(2,1)S(1)}, bf16[1,16,16,3,48]{4,2,3,1,0:T(8,128)(2,1)}, u32[]{:S(2)}) copy-start(bf16[1,16,16,3,48]{4,2,3,1,0:T(8,128)(2,1)} %param.9) | copy-start | bytes 221188
  0.6 11.4 %copy-start.7 = (bf16[4,4,3,64]{3,1,2,0:T(4,128)(2,1)S(1)}, bf16[4,4,3,64]{3,1,2,0:T(4,128)(2,1)}, u32[]{:S(2)}) copy-start(bf16[4,4,3,64]{3,1,2,0:T(4,128)(2,1)} %param.11) | copy-start | bytes 18436
  0.7 11.4 %copy-start.6 = (bf16[4,4,512,1]{2,1,3,0:T(4,128)(2,1)S(1)}, bf16[4,4,512,1]{2,1,3,0:T(4,128)(2,1)}, u32[]{:S(2)}) copy-start(bf16[4,4,512,1]{2,1,3,0:T(4,128)(2,1)} %param.15) | copy-start | bytes 49156
  0.7 12.6 %copy-start.5 = (bf16[4,4,64,128]{3,2,1,0:T(8,128)(2,1)S(1)}, bf16[4,4,64,128]{3,2,1,0:T(8,128)(2,1)}, u32[]{:S(2)}) copy-start(bf16[4,4,64,128]{3,2,1,0:T(8,128)(2,1)} %param.12) | copy-start | bytes 786436
  0.7 18.6 %copy-start.4 = (bf16[4,4,128,256]{3,2,1,0:T(8,128)(2,1)S(1)}, bf16[4,4,128,256]{3,2,1,0:T(8,128)(2,1)}, u32[]{:S(2)}) copy-start(bf16[4,4,128,256]{3,2,1,0:T(8,128)(2,1)} %param.13) | copy-start | bytes 3145732
  4.7 14.5 %all-to-all-start = ((bf16[8,8,896]{2,1,0:T(8,128)(2,1)}), bf16[8,8,896]{2,1,0:T(8,128)(2,1)S(1)}, u32[]{:S(2)}, u32[]{:S(2)}) async-start(bf16[8,8,896]{2,1,0:T(8,128)(2,1)} %bitcast.23), calls=%async_computation | async-start | bytes 229376 | tf_op jit(solution)/shard_map/all_to_all | solution.py:748
  12.1 0.9 %copy-start.1 = (bf16[64,896]{1,0:T(8,128)(2,1)S(1)}, bf16[64,896]{1,0:T(8,128)(2,1)}, u32[]{:S(2)}) copy-start(bf16[64,896]{1,0:T(8,128)(2,1)} %forward_taps.1.pay_ref) | copy-start | bytes 344068
  19.2 17.0 %copy-start = (bf16[1,16,16,48,128]{4,3,2,1,0:T(8,128)(2,1)S(1)}, bf16[1,16,16,48,128]{4,3,2,1,0:T(8,128)(2,1)}, u32[]{:S(2)}) copy-start(bf16[1,16,16,48,128]{4,3,2,1,0:T(8,128)(2,1)} %param.8) | copy-start | bytes 9437188
  36.3 19.4 %copy-start.3 = (bf16[3,3,3,128]{3,2,1,0:T(4,128)(2,1)S(1)}, bf16[3,3,3,128]{3,2,1,0:T(4,128)(2,1)}, u32[]{:S(2)}) copy-start(bf16[3,3,3,128]{3,2,1,0:T(4,128)(2,1)} %weight_ref.1) | copy-start | bytes 20740
  46.7 9.0 %all-to-all-start.3 = ((bf16[4,56,128]{2,1,0:T(8,128)(2,1)}), bf16[4,56,128]{2,1,0:T(8,128)(2,1)S(1)}, u32[]{:S(2)}, u32[]{:S(2)}) async-start(bf16[4,56,128]{2,1,0:T(8,128)(2,1)} %sum_parts.1), calls=%async_computation.3 | async-start | bytes 114688 | tf_op jit(solution)/shard_map/all_to_all | solution.py:766

commit v12 on v11

--- a/solution.py
+++ b/solution.py
@@ -51,7 +51,7 @@
     for slot in range(frames):
         rows = pl.ds((slot % devices * group + slot // devices) * pixels, pixels)
         copies.append(pltpu.make_async_copy(feat_hbm.at[rows, :], feat_ref.at[rows, :], sems.at[slot]))
-    for copy in copies:
+    for copy in copies[:1] + copies[2:] + copies[1:2]:
         copy.start()
     weight_scr[...] = jnp.zeros_like(weight_scr)
     out_ref[...] = jnp.zeros_like(out_ref)
@@ -95,19 +95,21 @@
         for k in range(lanes // LANES):
             out_ref[k, pl.ds(3 * group, devices, stride=pitch), :] = edges[:, k * LANES : (k + 1) * LANES]
 
-    copies[1].wait()
-    edge_rows()
     step = frames // chunks
     done = 0
     for chunk in range(chunks):
         for slot in range(chunk * step, (chunk + 1) * step):
             copies[2 + slot].wait()
+        if chunk == chunks - 1:
+            copies[1].wait()
         for slot in range(chunk * step, (chunk + 1) * step):
             frame = slot % devices * group + slot // devices
             product = mat(weight, feat_ref[frame * pixels : (frame + 1) * pixels, :], NT)
             for k in range(pieces):
                 rows = pl.ds(slot % devices, taps, stride=devices)
                 taps_refs[slot // devices][k, rows, :] = product[:, k * LANES : (k + 1) * LANES]
+        if chunk == chunks - 1:
+            edge_rows()
         while (done + 1) * devices <= chunk * step or (chunk == chunks - 1 and done < group):
             finish(done)
             done += 1
@@ -697,11 +699,12 @@
     stores = []
     for pair in range(pairs):
         product = mat(taps_ref[pair * chunk : (pair + 1) * chunk], both_ref[...]).astype(BF16)
-        rows = pl.ds(2 * pair * chunk, 2 * chunk)
-        out_ref[2 * pair * chunk : (2 * pair + 1) * chunk] = product[:, :channels]
-        out_ref[(2 * pair + 1) * chunk : (2 * pair + 2) * chunk] = product[:, channels:]
-        stores.append(pltpu.make_async_copy(out_ref.at[rows], out_hbm.at[rows], sems.at[pair]))
-        stores[-1].start()
+        for i in range(2):
+            at = (2 * pair + i) * chunk
+            out_ref[at : at + chunk] = product[:, i * channels : (i + 1) * channels]
+            rows = pl.ds(at, chunk)
+            stores.append(pltpu.make_async_copy(out_ref.at[rows], out_hbm.at[rows], sems.at[2 * pair + i]))
+            stores[-1].start()
     for copy in stores:
         copy.wait()
 
@@ -722,7 +725,7 @@
             pltpu.VMEM((padded, channels), F32),
             pltpu.VMEM((4 * padded, 2 * channels), BF16),
             pltpu.VMEM((rows, channels), BF16),
-            pltpu.SemaphoreType.DMA((rows // (2 * chunk),)),
+            pltpu.SemaphoreType.DMA((rows // chunk,)),
         ],
         compiler_params=PART,
         cost_estimate=pl.CostEstimate(flops=4 * rows * channels * padded, bytes_accessed=4 * rows * channels, transcendentals=0),

time: 59.1 us -> 59.1 us (level)
  no operation moved by 1% of the time
where the time goes in v12:
time: 59.1 us; the launch traced here: 58.7 us
  Pallas kernels  20.2 us (34%)
  blocking collectives  17.1 us (29%)
  starting transfers between devices  10.8 us (18%)
  waiting for transfers between devices  7.71 us (13%)
  local copies, waits for them, and re-layouts  1.97 us (3%)
  between operations  0.95 us (2%)
    all_to_all x1, blocking collectives, per_device(): lax.all_to_all(values.reshape(devices, pitch, lanes), row, split_axis=0,...  9.62 us
    all_to_all x1, blocking collectives, per_device(): lax.all_to_all(values, axes, split_axis=0, concat_axis=0, tiled=True)  7.46 us
    pallas_call x1, Pallas kernels, disc_call(): pl.pallas_call(functools.partial(disc_kernel, devices=devices, group=grou...  7.41 us
    all_to_all x1, starting transfers between devices, per_device(): lax.all_to_all(values.reshape(devices, pitch, lanes), row, split_axis=0,...  7.29 us
    all_to_all x1, waiting for transfers between devices, per_device(): lax.all_to_all(values.reshape(devices, pitch, lanes), row, split_axis=0,...  5.24 us
    pallas_call x2, Pallas kernels, taps_call(): pl.pallas_call(functools.partial(kernel, frames=frames, devices=devices,...  4.28 us
    pallas_call x1, Pallas kernels, forward_call(): pl.pallas_call(functools.partial(forward_kernel, frames=frames, devices=d...  4.01 us
    all_to_all x1, starting transfers between devices, per_device(): lax.all_to_all(values, axes, split_axis=0, concat_axis=0, tiled=True)  3.46 us
  transfers between devices with their start and end apart: 2, of which 2 were waited for; matrix products, arithmetic and copies ran while one was open for 2% of the time, Pallas kernels for 5%

profile of v12, /device:TPU:0, one launch (start us, length us, event | category | flops | bytes accessed | tf_op | source)
XLA Modules:
  0.0 58.7 jit_solution(15216544999725172492)
XLA Ops:
  0.6 0.0 copy-start.2
  0.6 0.0 copy-start.7
  0.7 0.0 copy-start.6
  0.7 0.0 copy-start.5
  0.7 0.0 copy-start.4
  0.7 4.0 %forward_taps.1.pay_ref = bf16[64,896]{1,0:T(8,128)(2,1)} custom-call(bf16[12288,128]{1,0:T(8,128)(2,1)} %bitcast.19, bf16[16,3,16,48]{3,2,1,0:T(8,128)(2,1)} %bitcast.24, bf16[3,3,3,128]{3,2,1,0:T(4,128)(2,1)} %weight_ref.1), custom_call_target="tpu_custom_call" | custom-call | flops 84934656 | bytes 3145728 | tf_op jit(solution)/shard_map/forward_taps/pallas_call | solution.py:124
  4.7 7.3 %all-to-all-start = ((bf16[8,8,896]{2,1,0:T(8,128)(2,1)}), bf16[8,8,896]{2,1,0:T(8,128)(2,1)S(1)}, u32[]{:S(2)}, u32[]{:S(2)}) async-start(bf16[8,8,896]{2,1,0:T(8,128)(2,1)} %bitcast.23), calls=%async_computation | async-start | bytes 229376 | tf_op jit(solution)/shard_map/all_to_all | solution.py:751
  12.1 0.0 copy-start.1
  12.1 0.9 %copy-done.1 = bf16[64,896]{1,0:T(8,128)(2,1)S(1)} copy-done((bf16[64,896]{1,0:T(8,128)(2,1)S(1)}, bf16[64,896]{1,0:T(8,128)(2,1)}, u32[]{:S(2)}) %copy-start.1) | copy-done | bytes 114712
  13.0 0.3 inner_rows.1.inner_ref
  13.3 0.7 %stage_weights.1 = (bf16[144,1024]{1,0:T(8,128)(2,1)S(1)}, bf16[512,144]{1,0:T(8,128)(2,1)S(1)}, bf16[1024,128]{1,0:T(8,128)(2,1)S(1)}, bf16[256,512]{1,0:T(8,128)(2,1)S(1)}) custom-call(bf16[4,4,3,64]{3,2,1,0:T(4,128)(2,1)S(1)} %copy.21.first_ref, bf16[1024,128]{1,0:T(8,128)(2,1)S(1)} %bitcast.29), custom_call_target="tpu_custom_call" | custom-call | flops 100000000 | bytes 4000000 | tf_op jit(solution)/shard_map/stage_weights/pallas_call | solution.py:501
  14.0 5.2 %all-to-all-done = bf16[8,8,896]{2,1,0:T(8,128)(2,1)S(1)} async-done(((bf16[8,8,896]{2,1,0:T(8,128)(2,1)}), bf16[8,8,896]{2,1,0:T(8,128)(2,1)S(1)}, u32[]{:S(2)}, u32[]{:S(2)}) %all-to-all-start) | async-done | bytes 114720 | tf_op jit(solution)/shard_map/all_to_all | solution.py:751
  19.2 7.4 %disc_rows.1 = bf16[64,896]{1,0:T(8,128)(2,1)S(1)} custom-call(bf16[64,896]{1,0:T(8,128)(2,1)S(1)} %bitcast.26, bf16[16,512]{1,0:T(8,128)(2,1)S(1)} %reshape.47.head_ref, bf16[144,1024]{1,0:T(8,128)(2,1)S(1)} %get-tuple-element.17.window, bf16[256,512]{1,0:T(8,128)(2,1)S(1)} %get-tuple-element.18.band_ref, bf16[1024,128]{1,0:T(8,128)(2,1)S(1)} %get-tuple-element.19.second, ...), custom_call_target="tpu_custom_call" | custom-call | flops 4000000000 | bytes 8000000 | tf_op jit(solution)/shard_map/disc_rows/pallas_call | solution.py:532
  26.7 9.6 %all_to_all.20 = bf16[8,8,896]{2,1,0:T(8,128)(2,1)S(1)} all-to-all(bf16[8,8,896]{2,1,0:T(8,128)(2,1)S(1)} %bitcast.27), channel_id=1, replica_groups=mesh['clip'=4,'far'=4,'near'=2] {'far','near'}, dimensions={0} | all-to-all | bytes 229376 | tf_op jit(solution)/shard_map/all_to_all | solution.py:751
  36.3 2.3 %both_taps.1 = bf16[8,56,128]{2,1,0:T(8,128)(2,1)S(1)} custom-call(f32[48,896]{1,0:T(8,128)S(1)} %inner_rows.1.inner_ref, bf16[64,896]{1,0:T(8,128)(2,1)S(1)} %bitcast.21, bf16[12288,128]{1,0:T(8,128)(2,1)S(1)} %bitcast.20), custom_call_target="tpu_custom_call" | custom-call | flops 169869312 | bytes 4000000 | tf_op jit(solution)/shard_map/both_taps/pallas_call | solution.py:658
  38.6 7.5 %all_to_all.21.parts_ref = bf16[8,56,128]{2,1,0:T(8,128)(2,1)S(1)} all-to-all(bf16[8,56,128]{2,1,0:T(8,128)(2,1)S(1)} %both_taps.1), channel_id=1, replica_groups=mesh['clip'=4,'far'=4,'near'=2] {'clip','near'}, dimensions={0} | all-to-all | bytes 229376 | tf_op jit(solution)/shard_map/all_to_all | solution.py:769
  46.0 0.6 %sum_parts.1 = bf16[4,56,128]{2,1,0:T(8,128)(2,1)} custom-call(bf16[8,56,128]{2,1,0:T(8,128)(2,1)S(1)} %all_to_all.21.parts_ref), custom_call_target="tpu_custom_call" | custom-call | tf_op jit(solution)/shard_map/sum_parts/pallas_call | solution.py:792
  46.7 3.5 %all-to-all-start.3 = ((bf16[4,56,128]{2,1,0:T(8,128)(2,1)}), bf16[4,56,128]{2,1,0:T(8,128)(2,1)S(1)}, u32[]{:S(2)}, u32[]{:S(2)}) async-start(bf16[4,56,128]{2,1,0:T(8,128)(2,1)} %sum_parts.1), calls=%async_computation.3 | async-start | bytes 114688 | tf_op jit(solution)/shard_map/all_to_all | solution.py:769
  50.1 0.1 slice.4
  50.3 0.2 reshape.54
  50.5 0.7 %copy.23 = bf16[8,2,16,3,48]{4,2,3,1,0:T(8,128)(2,1)} copy(bf16[8,2,16,3,48]{4,2,0,1,3:T(8,128)(2,1)S(1)} %bitcast.30) | data formatting | bytes 147456 | tf_op jit(solution)/shard_map/transpose | solution.py:776
  51.2 2.0 %turn_taps.1.taps_ref = bf16[6144,128]{1,0:T(8,128)(2,1)S(1)} custom-call(f32[48,896]{1,0:T(8,128)S(1)} %inner_rows.1.inner_ref, bf16[64,896]{1,0:T(8,128)(2,1)S(1)} %bitcast.22), custom_call_target="tpu_custom_call" | custom-call | flops 169869312 | bytes 4000000 | tf_op jit(solution)/shard_map/turn_taps/pallas_call | solution.py:658
  53.2 2.5 %all-to-all-done.3.sums_ref = bf16[4,56,128]{2,1,0:T(8,128)(2,1)S(1)} async-done(((bf16[4,56,128]{2,1,0:T(8,128)(2,1)}), bf16[4,56,128]{2,1,0:T(8,128)(2,1)S(1)}, u32[]{:S(2)}, u32[]{:S(2)}) %all-to-all-start.3) | async-done | bytes 57376 | tf_op jit(solution)/shard_map/all_to_all | solution.py:769
  55.6 2.9 %feature_pull.1 = (bf16[12288,128]{1,0:T(8,128)(2,1)}, f32[3,3,3,128]{3,2,1,0:T(4,128)}, f32[1,1]{1,0:T(1,128)}) custom-call(bf16[6144,128]{1,0:T(8,128)(2,1)S(1)} %turn_taps.1.taps_ref, bf16[4,56,128]{2,1,0:T(8,128)(2,1)S(1)} %all-to-all-done.3.sums_ref, bf16[3,3,3,128]{3,2,1,0:T(4,128)(2,1)S(1)} %copy-done.3), custom_call_target="tpu_custom_call" | custom-call | flops 201326592 | bytes 6291456 | tf_op jit(solution)/shard_map/feature_pull/pallas_call | solution.py:715
  (12 shorter events, 0.1 us)
Async XLA Ops:
  0.6 11.4 %copy-start.2 = (bf16[1,16,16,3,48]{4,2,3,1,0:T(8,128)(2,1)S(1)}, bf16[1,16,16,3,48]{4,2,3,1,0:T(8,128)(2,1)}, u32[]{:S(2)}) copy-start(bf16[1,16,16,3,48]{4,2,3,1,0:T(8,128)(2,1)} %param.9) | copy-start | bytes 221188
  0.6 11.4 %copy-start.7 = (bf16[4,4,3,64]{3,1,2,0:T(4,128)(2,1)S(1)}, bf16[4,4,3,64]{3,1,2,0:T(4,128)(2,1)}, u32[]{:S(2)}) copy-start(bf16[4,4,3,64]{3,1,2,0:T(4,128)(2,1)} %param.11) | copy-start | bytes 18436
  0.7 11.4 %copy-start.6 = (bf16[4,4,512,1]{2,1,3,0:T(4,128)(2,1)S(1)}, bf16[4,4,512,1]{2,1,3,0:T(4,128)(2,1)}, u32[]{:S(2)}) copy-start(bf16[4,4,512,1]{2,1,3,0:T(4,128)(2,1)} %param.15) | copy-start | bytes 49156
  0.7 12.6 %copy-start.5 = (bf16[4,4,64,128]{3,2,1,0:T(8,128)(2,1)S(1)}, bf16[4,4,64,128]{3,2,1,0:T(8,128)(2,1)}, u32[]{:S(2)}) copy-start(bf16[4,4,64,128]{3,2,1,0:T(8,128)(2,1)} %param.12) | copy-start | bytes 786436
  0.7 18.6 %copy-start.4 = (bf16[4,4,128,256]{3,2,1,0:T(8,128)(2,1)S(1)}, bf16[4,4,128,256]{3,2,1,0:T(8,128)(2,1)}, u32[]{:S(2)}) copy-start(bf16[4,4,128,256]{3,2,1,0:T(8,128)(2,1)} %param.13) | copy-start | bytes 3145732
  4.7 14.5 %all-to-all-start = ((bf16[8,8,896]{2,1,0:T(8,128)(2,1)}), bf16[8,8,896]{2,1,0:T(8,128)(2,1)S(1)}, u32[]{:S(2)}, u32[]{:S(2)}) async-start(bf16[8,8,896]{2,1,0:T(8,128)(2,1)} %bitcast.23), calls=%async_computation | async-start | bytes 229376 | tf_op jit(solution)/shard_map/all_to_all | solution.py:751
  12.1 0.9 %copy-start.1 = (bf16[64,896]{1,0:T(8,128)(2,1)S(1)}, bf16[64,896]{1,0:T(8,128)(2,1)}, u32[]{:S(2)}) copy-start(bf16[64,896]{1,0:T(8,128)(2,1)} %forward_taps.1.pay_ref) | copy-start | bytes 344068
  19.2 17.0 %copy-start = (bf16[1,16,16,48,128]{4,3,2,1,0:T(8,128)(2,1)S(1)}, bf16[1,16,16,48,128]{4,3,2,1,0:T(8,128)(2,1)}, u32[]{:S(2)}) copy-start(bf16[1,16,16,48,128]{4,3,2,1,0:T(8,128)(2,1)} %param.8) | copy-start | bytes 9437188
  36.3 19.4 %copy-start.3 = (bf16[3,3,3,128]{3,2,1,0:T(4,128)(2,1)S(1)}, bf16[3,3,3,128]{3,2,1,0:T(4,128)(2,1)}, u32[]{:S(2)}) copy-start(bf16[3,3,3,128]{3,2,1,0:T(4,128)(2,1)} %weight_ref.1) | copy-start | bytes 20740
  46.7 9.0 %all-to-all-start.3 = ((bf16[4,56,128]{2,1,0:T(8,128)(2,1)}), bf16[4,56,128]{2,1,0:T(8,128)(2,1)S(1)}, u32[]{:S(2)}, u32[]{:S(2)}) async-start(bf16[4,56,128]{2,1,0:T(8,128)(2,1)} %sum_parts.1), calls=%async_computation.3 | async-start | bytes 114688 | tf_op jit(solution)/shard_map/all_to_all | solution.py:769

commit v13 on v11

--- a/solution.py
+++ b/solution.py
@@ -51,7 +51,7 @@
     for slot in range(frames):
         rows = pl.ds((slot % devices * group + slot // devices) * pixels, pixels)
         copies.append(pltpu.make_async_copy(feat_hbm.at[rows, :], feat_ref.at[rows, :], sems.at[slot]))
-    for copy in copies:
+    for copy in copies[:1] + copies[2:] + copies[1:2]:
         copy.start()
     weight_scr[...] = jnp.zeros_like(weight_scr)
     out_ref[...] = jnp.zeros_like(out_ref)
@@ -95,19 +95,21 @@
         for k in range(lanes // LANES):
             out_ref[k, pl.ds(3 * group, devices, stride=pitch), :] = edges[:, k * LANES : (k + 1) * LANES]
 
-    copies[1].wait()
-    edge_rows()
     step = frames // chunks
     done = 0
     for chunk in range(chunks):
         for slot in range(chunk * step, (chunk + 1) * step):
             copies[2 + slot].wait()
+        if chunk == chunks - 1:
+            copies[1].wait()
         for slot in range(chunk * step, (chunk + 1) * step):
             frame = slot % devices * group + slot // devices
             product = mat(weight, feat_ref[frame * pixels : (frame + 1) * pixels, :], NT)
             for k in range(pieces):
                 rows = pl.ds(slot % devices, taps, stride=devices)
                 taps_refs[slot // devices][k, rows, :] = product[:, k * LANES : (k + 1) * LANES]
+        if chunk == chunks - 1:
+            edge_rows()
         while (done + 1) * devices <= chunk * step or (chunk == chunks - 1 and done < group):
             finish(done)
             done += 1
@@ -588,8 +590,7 @@
     return jnp.concatenate(blocks, axis=0)
 
 
-def rec_rows(inner_ref, zin, devices, group, cols, block_rows):
-    lanes = inner_ref.shape[1]
+def edge_blocks(zin, lanes, devices, group, cols):
     pitch = zin.shape[1] // devices
     edges = []
     for i in range(2):
@@ -601,35 +602,62 @@
             edges[i][:, (e * 3 * group + at) * cols : (e * 3 * group + at + 1) * cols] for at in range(3 * group)
         ]
         blocks.append(jnp.concatenate(pieces, axis=0))
-    none = lambda count: jnp.zeros((blocks[0].shape[0], count), F32)
     above, first, last, below = blocks
-    rest = lanes - (block_rows + 2) * cols
-    return inner_ref[...], jnp.concatenate(
-        [above, first * loss_scale, none((block_rows - 2) * cols), last * loss_scale, below, none(rest)], axis=1
-    )
-
-
-def both_kernel(
-    inner_ref, plane_ref, feat_ref, part_ref, rec_taps, gan_taps, zin, *, frames, devices, group, cols, block_rows
-):
-    pieces = block_rows * cols // LANES
-    put_taps(unpack(plane_ref, zin, devices, group), gan_taps, frames, cols, pieces, 32)
-    inner, edges = rec_rows(inner_ref, zin, devices, group, cols, block_rows)
-    put_taps(inner + edges, rec_taps, frames, cols, pieces, 32)
-    pixels = pieces * LANES
-    total = jnp.zeros((64, feat_ref.shape[1]), F32)
+    return above, first * loss_scale, last * loss_scale, below
+
+
+def weigh(taps_ref, feat_ref, frames, devices, group, pieces, choose):
+    total = jnp.zeros((32, feat_ref.shape[1]), F32)
     for frame in range(frames):
         rows = pl.ds(slot_of(frame, devices, group), 32, stride=frames)
-        taps = jnp.concatenate(
-            [
-                jnp.concatenate([taps_ref[k, rows, :] for k in range(pieces)], axis=1)
-                for taps_ref in (rec_taps, gan_taps)
-            ],
-            axis=0,
-        )
-        total = total + mat(taps.astype(BF16), feat_ref[frame * pixels : (frame + 1) * pixels, :])
-    blank = jnp.zeros((part_ref.shape[1] - 54, total.shape[1]), F32)
-    total = jnp.concatenate([total[0:27], total[32:59], blank], axis=0).astype(BF16)
+        taps = jnp.concatenate([taps_ref[k, rows, :] for k in range(pieces)], axis=1).astype(BF16)
+        total = total + mat(taps, choose(frame))
+    return total
+
+
+def rec_kernel(inner_ref, feat_ref, part_ref, taps_ref, *, frames, devices, group, cols, block_rows):
+    pixels = block_rows * cols
+    put_taps(inner_ref[...], taps_ref, frames, cols, pixels // LANES, 32)
+    whole = lambda frame: feat_ref[frame * pixels : (frame + 1) * pixels, :]
+    part_ref[...] = weigh(taps_ref, feat_ref, frames, devices, group, pixels // LANES, whole)
+
+
+def both_kernel(
+    rec_ref, plane_ref, feat_ref, part_ref, gan_taps, edge_taps, zin, *, frames, devices, group, cols, block_rows
+):
+    lanes = plane_ref.shape[1]
+    pixels = block_rows * cols
+    put_taps(unpack(plane_ref, zin, devices, group), gan_taps, frames, cols, pixels // LANES, 32)
+    above, first, last, below = edge_blocks(zin, lanes, devices, group, cols)
+    none = jnp.zeros((above.shape[0], 4 * cols), F32)
+    plane = jnp.concatenate([above, first, none, last, below], axis=1)
+    size = 8 * cols
+    lane = lax.broadcasted_iota(jnp.int32, plane.shape, 1)
+    for b in range(3):
+        moved = plane
+        if b == 0:
+            moved = jnp.where(lane % cols == cols - 1, 0.0, pltpu.roll(plane, size - 1, 1))
+        if b == 2:
+            moved = jnp.where(lane % cols == 0, 0.0, pltpu.roll(plane, 1, 1))
+        for a in range(3):
+            turned = moved if a == 2 else pltpu.roll(moved, size - (2 - a) * cols, 1)
+            turned = jnp.where(lane % (4 * cols) < 2 * cols, turned, 0.0)
+            for k in range(size // LANES):
+                rows = pl.ds((a * 3 + b) * 3 * frames, 3 * frames)
+                edge_taps[k, rows, :] = turned[:, k * LANES : (k + 1) * LANES]
+    for k in range(size // LANES):
+        edge_taps[k, pl.ds(27 * frames, 5 * frames), :] = jnp.zeros((5 * frames, LANES), F32)
+    whole = lambda frame: feat_ref[frame * pixels : (frame + 1) * pixels, :]
+    gan = weigh(gan_taps, feat_ref, frames, devices, group, pixels // LANES, whole)
+
+    def ends(frame):
+        start, end = frame * pixels, (frame + 1) * pixels
+        tail = feat_ref[end - 2 * cols : end, :]
+        return jnp.concatenate([feat_ref[start : start + 4 * cols, :], tail, tail], axis=0)
+
+    rec = rec_ref[...] + weigh(edge_taps, feat_ref, frames, devices, group, size // LANES, ends)
+    blank = jnp.zeros((part_ref.shape[1] - 54, gan.shape[1]), F32)
+    total = jnp.concatenate([rec[0:27], gan[0:27], blank], axis=0).astype(BF16)
     for i in range(part_ref.shape[0]):
         part_ref[i] = total
 
@@ -640,8 +668,13 @@
     pieces = block_rows * cols // LANES
     pixels = pieces * LANES
     put_taps(unpack(plane_ref, zin, devices, group), gan_taps, frames, cols, pieces, 32)
-    inner, edges = rec_rows(inner_ref, zin, devices, group, cols, block_rows)
-    put_taps(inner + edges, rec_taps, frames, cols, pieces, 32)
+    lanes = inner_ref.shape[1]
+    above, first, last, below = edge_blocks(zin, lanes, devices, group, cols)
+    none = lambda count: jnp.zeros((above.shape[0], count), F32)
+    edges = jnp.concatenate(
+        [above, first, none((block_rows - 2) * cols), last, below, none(lanes - (block_rows + 2) * cols)], axis=1
+    )
+    put_taps(inner_ref[...] + edges, rec_taps, frames, cols, pieces, 32)
     for pair in range(frames // 2):
         for k in range(pieces):
             parts = []
@@ -754,14 +787,18 @@
     staged = stage_call(disc_first, disc_second, cols)
     arrived, inner = lax.optimization_barrier((arrived, inner))
     sent = disc_call(arrived, staged, disc_third, disc_fourth, disc_head, devices, group, cols, block_rows)
+    sent, held = lax.optimization_barrier((sent, inner))
     returned = trade(sent)
     taps_scratch = pltpu.VMEM((block_rows * cols // LANES, 32 * frames, LANES), F32)
     plane_scratch = pltpu.VMEM((lanes // LANES, devices * pitch, LANES), F32)
     flops = 4 * features.size * 27
+    rec_part = taps_call(
+        rec_kernel, [VM, VM], (held, feats), jax.ShapeDtypeStruct((32, channels), F32), [taps_scratch], *sizes, flops, "rec_taps"
+    )
     part = taps_call(
-        both_kernel, [VM, VM, VM], (inner, returned, feats),
+        both_kernel, [VM, VM, VM], (rec_part, returned, feats),
         jax.ShapeDtypeStruct((clips * lax.axis_size("near"), 56, channels), BF16),
-        [taps_scratch, taps_scratch, plane_scratch], *sizes, flops, "both_taps",
+        [taps_scratch, pltpu.VMEM((8 * cols // LANES, 32 * frames, LANES), F32), plane_scratch], *sizes, flops, "both_taps",
     )
     share = lambda values, axes: lax.all_to_all(values, axes, split_axis=0, concat_axis=0, tiled=True)
     sums = share(sum_call(share(part, ("clip", "near")), lax.axis_size("far")), "far")

time: 59.1 us -> 66.7 us (1.13)
  local copies, waits for them, and re-layouts: 1.97 us -> 11.8 us
  blocking collectives: 17.1 us -> 7.46 us
  starting transfers between devices: 10.8 us -> 14.9 us
  waiting for transfers between devices: 7.71 us -> 10.4 us
    all_to_all x1 -> x0, blocking collectives: 9.62 us -> none  [per_device(): lax.all_to_all(values.reshape(devices, pitch, lanes), row, split_axis=0,...]
    unnamed x16 -> x36, local copies, waits for them, and re-layouts: 0.93 us -> 10.1 us
    all_to_all x1 -> x2, starting transfers between devices: 7.29 us -> 11.4 us  [per_device(): lax.all_to_all(values.reshape(devices, pitch, lanes), row, split_axis=0,...]
    all_to_all x1 -> x2, waiting for transfers between devices: 5.24 us -> 7.89 us  [per_device(): lax.all_to_all(values.reshape(devices, pitch, lanes), row, split_axis=0,...]
    pallas_call x2 -> x3, Pallas kernels: 4.28 us -> 4.72 us  [taps_call(): pl.pallas_call(functools.partial(kernel, frames=frames, devices=devices,...]
  transfers between devices with their start and end apart: 2 -> 3, of which waited for: 2 -> 3; matrix products, arithmetic and copies ran while one was open for 2% -> 2% of each run, Pallas kernels for 5% -> 6%
where the time goes in v13:
time: 66.7 us; the launch traced here: 66 us
  Pallas kernels  20.6 us (31%)
  starting transfers between devices  14.9 us (22%)
  local copies, waits for them, and re-layouts  11.8 us (18%)
  waiting for transfers between devices  10.4 us (16%)
  blocking collectives  7.46 us (11%)
  between operations  0.96 us (1%)
    all_to_all x2, starting transfers between devices, per_device(): lax.all_to_all(values.reshape(devices, pitch, lanes), row, split_axis=0,...  11.4 us
    unnamed x36, local copies, waits for them, and re-layouts  10.1 us
    all_to_all x2, waiting for transfers between devices, per_device(): lax.all_to_all(values.reshape(devices, pitch, lanes), row, split_axis=0,...  7.89 us
    all_to_all x1, blocking collectives, per_device(): lax.all_to_all(values, axes, split_axis=0, concat_axis=0, tiled=True)  7.46 us
    pallas_call x1, Pallas kernels, disc_call(): pl.pallas_call(functools.partial(disc_kernel, devices=devices, group=grou...  7.42 us
    pallas_call x3, Pallas kernels, taps_call(): pl.pallas_call(functools.partial(kernel, frames=frames, devices=devices,...  4.72 us
    pallas_call x1, Pallas kernels, forward_call(): pl.pallas_call(functools.partial(forward_kernel, frames=frames, devices=d...  3.98 us
    all_to_all x1, starting transfers between devices, per_device(): lax.all_to_all(values, axes, split_axis=0, concat_axis=0, tiled=True)  3.46 us
  transfers between devices with their start and end apart: 3, of which 3 were waited for; matrix products, arithmetic and copies ran while one was open for 2% of the time, Pallas kernels for 6%

profile of v13, /device:TPU:0, one launch (start us, length us, event | category | flops | bytes accessed | tf_op | source)
XLA Modules:
  0.0 66.0 jit_solution(14480764082696297059)
XLA Ops:
  0.7 4.0 %forward_taps.1.pay_ref = bf16[64,896]{1,0:T(8,128)(2,1)} custom-call(bf16[12288,128]{1,0:T(8,128)(2,1)} %bitcast.19, bf16[16,3,16,48]{3,2,1,0:T(8,128)(2,1)} %bitcast.25, bf16[3,3,3,128]{3,2,1,0:T(4,128)(2,1)} %weight_ref.1), custom_call_target="tpu_custom_call" | custom-call | flops 84934656 | bytes 3145728 | tf_op jit(solution)/shard_map/forward_taps/pallas_call | solution.py:124
  4.7 7.3 %all-to-all-start = ((bf16[8,8,896]{2,1,0:T(8,128)(2,1)}), bf16[8,8,896]{2,1,0:T(8,128)(2,1)S(1)}, u32[]{:S(2)}, u32[]{:S(2)}) async-start(bf16[8,8,896]{2,1,0:T(8,128)(2,1)} %bitcast.24), calls=%async_computation | async-start | bytes 229376 | tf_op jit(solution)/shard_map/all_to_all | solution.py:781
  12.6 0.9 %copy-done.1 = bf16[64,896]{1,0:T(8,128)(2,1)S(1)} copy-done((bf16[64,896]{1,0:T(8,128)(2,1)S(1)}, bf16[64,896]{1,0:T(8,128)(2,1)}, u32[]{:S(2)}) %copy-start.1) | copy-done | bytes 114712
  13.8 0.7 %stage_weights.1 = (bf16[144,1024]{1,0:T(8,128)(2,1)S(1)}, bf16[512,144]{1,0:T(8,128)(2,1)S(1)}, bf16[1024,128]{1,0:T(8,128)(2,1)S(1)}, bf16[256,512]{1,0:T(8,128)(2,1)S(1)}) custom-call(bf16[4,4,3,64]{3,2,1,0:T(4,128)(2,1)S(1)} %copy.21.first_ref, bf16[1024,128]{1,0:T(8,128)(2,1)S(1)} %bitcast.30), custom_call_target="tpu_custom_call" | custom-call | flops 100000000 | bytes 4000000 | tf_op jit(solution)/shard_map/stage_weights/pallas_call | solution.py:501
  14.5 0.7 %copy-done.8 = bf16[144,1024]{1,0:T(8,128)(2,1)} copy-done((bf16[144,1024]{1,0:T(8,128)(2,1)}, bf16[144,1024]{1,0:T(8,128)(2,1)S(1)}, u32[]{:S(2)}) %copy-start.8) | copy-done | bytes 294936
  15.9 0.7 %copy-done.12 = bf16[1024,128]{1,0:T(8,128)(2,1)} copy-done((bf16[1024,128]{1,0:T(8,128)(2,1)}, bf16[1024,128]{1,0:T(8,128)(2,1)S(1)}, u32[]{:S(2)}) %copy-start.12) | copy-done | bytes 262168
  16.6 0.7 %copy-done.14 = bf16[256,512]{1,0:T(8,128)(2,1)} copy-done((bf16[256,512]{1,0:T(8,128)(2,1)}, bf16[256,512]{1,0:T(8,128)(2,1)S(1)}, u32[]{:S(2)}) %copy-start.14) | copy-done | bytes 262168
  17.3 1.8 %all-to-all-done = bf16[8,8,896]{2,1,0:T(8,128)(2,1)S(1)} async-done(((bf16[8,8,896]{2,1,0:T(8,128)(2,1)}), bf16[8,8,896]{2,1,0:T(8,128)(2,1)S(1)}, u32[]{:S(2)}, u32[]{:S(2)}) %all-to-all-start) | async-done | bytes 114720 | tf_op jit(solution)/shard_map/all_to_all | solution.py:781
  19.2 0.7 %copy-done.5 = bf16[16,512]{1,0:T(8,128)(2,1)S(1)} copy-done((bf16[16,512]{1,0:T(8,128)(2,1)S(1)}, bf16[16,512]{1,0:T(8,128)(2,1)}, u32[]{:S(2)}) %copy-start.5) | copy-done | bytes 16408
  19.9 1.2 %copy-done.6 = bf16[4,4,128,256]{3,2,1,0:T(8,128)(2,1)S(1)} copy-done((bf16[4,4,128,256]{3,2,1,0:T(8,128)(2,1)S(1)}, bf16[4,4,128,256]{3,2,1,0:T(8,128)(2,1)}, u32[]{:S(2)}) %copy-start.6) | copy-done | bytes 1048600
  21.1 1.0 %copy-done.9 = bf16[144,1024]{1,0:T(8,128)(2,1)S(1)} copy-done((bf16[144,1024]{1,0:T(8,128)(2,1)S(1)}, bf16[144,1024]{1,0:T(8,128)(2,1)}, u32[]{:S(2)}) %copy-start.9) | copy-done | bytes 294936
  22.1 0.9 %copy-done.11 = bf16[512,144]{1,0:T(8,128)(2,1)S(1)} copy-done((bf16[512,144]{1,0:T(8,128)(2,1)S(1)}, bf16[512,144]{1,0:T(8,128)(2,1)}, u32[]{:S(2)}) %copy-start.11) | copy-done | bytes 147480
  23.0 0.9 %copy-done.13 = bf16[1024,128]{1,0:T(8,128)(2,1)S(1)} copy-done((bf16[1024,128]{1,0:T(8,128)(2,1)S(1)}, bf16[1024,128]{1,0:T(8,128)(2,1)}, u32[]{:S(2)}) %copy-start.13) | copy-done | bytes 262168
  24.0 0.9 %copy-done.15 = bf16[256,512]{1,0:T(8,128)(2,1)S(1)} copy-done((bf16[256,512]{1,0:T(8,128)(2,1)S(1)}, bf16[256,512]{1,0:T(8,128)(2,1)}, u32[]{:S(2)}) %copy-start.15) | copy-done | bytes 262168
  24.9 7.4 %disc_rows.1 = bf16[64,896]{1,0:T(8,128)(2,1)S(1)} custom-call(bf16[64,896]{1,0:T(8,128)(2,1)S(1)} %bitcast.27, bf16[16,512]{1,0:T(8,128)(2,1)S(1)} %copy-done.5, bf16[144,1024]{1,0:T(8,128)(2,1)S(1)} %copy-done.9, bf16[256,512]{1,0:T(8,128)(2,1)S(1)} %copy-done.15, bf16[1024,128]{1,0:T(8,128)(2,1)S(1)} %copy-done.13, bf16[512,144]{1,0:T(8,128)(2,1)S(1)} %copy-done.11, ...), custom_call_target="tpu_custom_call" | custom-call | flops 4000000000 | bytes 8000000 | tf_op jit(solution)/shard_map/disc_rows/pallas_call | solution.py:532
  33.0 4.2 %all-to-all-start.1 = ((bf16[8,8,896]{2,1,0:T(8,128)(2,1)}), bf16[8,8,896]{2,1,0:T(8,128)(2,1)S(1)}, u32[]{:S(2)}, u32[]{:S(2)}) async-start(bf16[8,8,896]{2,1,0:T(8,128)(2,1)} %bitcast.28), calls=%async_computation.1 | async-start | bytes 229376 | tf_op jit(solution)/shard_map/all_to_all | solution.py:781
  37.2 1.2 %rec_taps.1.rec_ref = f32[32,128]{1,0:T(8,128)S(1)} custom-call(f32[48,896]{1,0:T(8,128)S(1)} %inner_rows.1.inner_ref, bf16[12288,128]{1,0:T(8,128)(2,1)S(1)} %bitcast.20), custom_call_target="tpu_custom_call" | custom-call | flops 169869312 | bytes 4000000 | tf_op jit(solution)/shard_map/rec_taps/pallas_call | solution.py:689
  38.4 6.0 %all-to-all-done.1 = bf16[8,8,896]{2,1,0:T(8,128)(2,1)S(1)} async-done(((bf16[8,8,896]{2,1,0:T(8,128)(2,1)}), bf16[8,8,896]{2,1,0:T(8,128)(2,1)S(1)}, u32[]{:S(2)}, u32[]{:S(2)}) %all-to-all-start.1) | async-done | bytes 114720 | tf_op jit(solution)/shard_map/all_to_all | solution.py:781
  44.4 1.5 %both_taps.1 = bf16[8,56,128]{2,1,0:T(8,128)(2,1)S(1)} custom-call(f32[32,128]{1,0:T(8,128)S(1)} %rec_taps.1.rec_ref, bf16[64,896]{1,0:T(8,128)(2,1)S(1)} %bitcast.22, bf16[12288,128]{1,0:T(8,128)(2,1)S(1)} %bitcast.21), custom_call_target="tpu_custom_call" | custom-call | flops 169869312 | bytes 4000000 | tf_op jit(solution)/shard_map/both_taps/pallas_call | solution.py:689
  46.0 7.5 %all_to_all.20.parts_ref = bf16[8,56,128]{2,1,0:T(8,128)(2,1)S(1)} all-to-all(bf16[8,56,128]{2,1,0:T(8,128)(2,1)S(1)} %both_taps.1), channel_id=1, replica_groups=mesh['clip'=4,'far'=4,'near'=2] {'clip','near'}, dimensions={0} | all-to-all | bytes 229376 | tf_op jit(solution)/shard_map/all_to_all | solution.py:803
  54.1 3.5 %all-to-all-start.3 = ((bf16[4,56,128]{2,1,0:T(8,128)(2,1)}), bf16[4,56,128]{2,1,0:T(8,128)(2,1)S(1)}, u32[]{:S(2)}, u32[]{:S(2)}) async-start(bf16[4,56,128]{2,1,0:T(8,128)(2,1)} %sum_parts.1), calls=%async_computation.3 | async-start | bytes 114688 | tf_op jit(solution)/shard_map/all_to_all | solution.py:803
  58.6 2.0 %turn_taps.1.taps_ref = bf16[6144,128]{1,0:T(8,128)(2,1)S(1)} custom-call(f32[48,896]{1,0:T(8,128)S(1)} %inner_rows.1.inner_ref, bf16[64,896]{1,0:T(8,128)(2,1)S(1)} %bitcast.23), custom_call_target="tpu_custom_call" | custom-call | flops 169869312 | bytes 4000000 | tf_op jit(solution)/shard_map/turn_taps/pallas_call | solution.py:689
  60.6 2.5 %all-to-all-done.3.sums_ref = bf16[4,56,128]{2,1,0:T(8,128)(2,1)S(1)} async-done(((bf16[4,56,128]{2,1,0:T(8,128)(2,1)}), bf16[4,56,128]{2,1,0:T(8,128)(2,1)S(1)}, u32[]{:S(2)}, u32[]{:S(2)}) %all-to-all-start.3) | async-done | bytes 57376 | tf_op jit(solution)/shard_map/all_to_all | solution.py:803
  63.0 2.8 %feature_pull.1 = (bf16[12288,128]{1,0:T(8,128)(2,1)}, f32[3,3,3,128]{3,2,1,0:T(4,128)}, f32[1,1]{1,0:T(1,128)}) custom-call(bf16[6144,128]{1,0:T(8,128)(2,1)S(1)} %turn_taps.1.taps_ref, bf16[4,56,128]{2,1,0:T(8,128)(2,1)S(1)} %all-to-all-done.3.sums_ref, bf16[3,3,3,128]{3,2,1,0:T(4,128)(2,1)S(1)} %copy-done.4), custom_call_target="tpu_custom_call" | custom-call | flops 201326592 | bytes 6291456 | tf_op jit(solution)/shard_map/feature_pull/pallas_call | solution.py:745
  (34 shorter events, 4.0 us)
Async XLA Ops:
  0.6 12.0 %copy-start.2 = (bf16[1,16,16,3,48]{4,2,3,1,0:T(8,128)(2,1)S(1)}, bf16[1,16,16,3,48]{4,2,3,1,0:T(8,128)(2,1)}, u32[]{:S(2)}) copy-start(bf16[1,16,16,3,48]{4,2,3,1,0:T(8,128)(2,1)} %param.9) | copy-start | bytes 221188
  0.6 11.3 %copy-start.17 = (bf16[4,4,3,64]{3,1,2,0:T(4,128)(2,1)S(1)}, bf16[4,4,3,64]{3,1,2,0:T(4,128)(2,1)}, u32[]{:S(2)}) copy-start(bf16[4,4,3,64]{3,1,2,0:T(4,128)(2,1)} %param.11) | copy-start | bytes 18436
  0.7 11.3 %copy-start.16 = (bf16[4,4,512,1]{2,1,3,0:T(4,128)(2,1)S(1)}, bf16[4,4,512,1]{2,1,3,0:T(4,128)(2,1)}, u32[]{:S(2)}) copy-start(bf16[4,4,512,1]{2,1,3,0:T(4,128)(2,1)} %param.15) | copy-start | bytes 49156
  0.7 13.2 %copy-start.7 = (bf16[4,4,64,128]{3,2,1,0:T(8,128)(2,1)S(1)}, bf16[4,4,64,128]{3,2,1,0:T(8,128)(2,1)}, u32[]{:S(2)}) copy-start(bf16[4,4,64,128]{3,2,1,0:T(8,128)(2,1)} %param.12) | copy-start | bytes 786436
  4.7 14.5 %all-to-all-start = ((bf16[8,8,896]{2,1,0:T(8,128)(2,1)}), bf16[8,8,896]{2,1,0:T(8,128)(2,1)S(1)}, u32[]{:S(2)}, u32[]{:S(2)}) async-start(bf16[8,8,896]{2,1,0:T(8,128)(2,1)} %bitcast.24), calls=%async_computation | async-start | bytes 229376 | tf_op jit(solution)/shard_map/all_to_all | solution.py:781
  12.6 0.9 %copy-start.1 = (bf16[64,896]{1,0:T(8,128)(2,1)S(1)}, bf16[64,896]{1,0:T(8,128)(2,1)}, u32[]{:S(2)}) copy-start(bf16[64,896]{1,0:T(8,128)(2,1)} %forward_taps.1.pay_ref) | copy-start | bytes 344068
  14.5 0.7 %copy-start.8 = (bf16[144,1024]{1,0:T(8,128)(2,1)}, bf16[144,1024]{1,0:T(8,128)(2,1)S(1)}, u32[]{:S(2)}) copy-start(bf16[144,1024]{1,0:T(8,128)(2,1)S(1)} %get-tuple-element.19.window) | copy-start | bytes 884740
  15.2 0.7 %copy-start.10 = (bf16[512,144]{1,0:T(8,128)(2,1)}, bf16[512,144]{1,0:T(8,128)(2,1)S(1)}, u32[]{:S(2)}) copy-start(bf16[512,144]{1,0:T(8,128)(2,1)S(1)} %get-tuple-element.22.unwindow) | copy-start | bytes 442372
  15.9 0.7 %copy-start.12 = (bf16[1024,128]{1,0:T(8,128)(2,1)}, bf16[1024,128]{1,0:T(8,128)(2,1)S(1)}, u32[]{:S(2)}) copy-start(bf16[1024,128]{1,0:T(8,128)(2,1)S(1)} %get-tuple-element.21.second) | copy-start | bytes 786436
  16.6 0.7 %copy-start.14 = (bf16[256,512]{1,0:T(8,128)(2,1)}, bf16[256,512]{1,0:T(8,128)(2,1)S(1)}, u32[]{:S(2)}) copy-start(bf16[256,512]{1,0:T(8,128)(2,1)S(1)} %get-tuple-element.20.band_ref) | copy-start | bytes 786436
  19.2 0.7 %copy-start.5 = (bf16[16,512]{1,0:T(8,128)(2,1)S(1)}, bf16[16,512]{1,0:T(8,128)(2,1)}, u32[]{:S(2)}) copy-start(bf16[16,512]{1,0:T(8,128)(2,1)} %reshape.47.head_ref) | copy-start | bytes 49156
  19.9 1.2 %copy-start.6 = (bf16[4,4,128,256]{3,2,1,0:T(8,128)(2,1)S(1)}, bf16[4,4,128,256]{3,2,1,0:T(8,128)(2,1)}, u32[]{:S(2)}) copy-start(bf16[4,4,128,256]{3,2,1,0:T(8,128)(2,1)} %param.13) | copy-start | bytes 3145732
  21.1 1.0 %copy-start.9 = (bf16[144,1024]{1,0:T(8,128)(2,1)S(1)}, bf16[144,1024]{1,0:T(8,128)(2,1)}, u32[]{:S(2)}) copy-start(bf16[144,1024]{1,0:T(8,128)(2,1)} %copy-done.8) | copy-start | bytes 884740
  22.1 0.9 %copy-start.11 = (bf16[512,144]{1,0:T(8,128)(2,1)S(1)}, bf16[512,144]{1,0:T(8,128)(2,1)}, u32[]{:S(2)}) copy-start(bf16[512,144]{1,0:T(8,128)(2,1)} %copy-done.10) | copy-start | bytes 442372
  23.0 0.9 %copy-start.13 = (bf16[1024,128]{1,0:T(8,128)(2,1)S(1)}, bf16[1024,128]{1,0:T(8,128)(2,1)}, u32[]{:S(2)}) copy-start(bf16[1024,128]{1,0:T(8,128)(2,1)} %copy-done.12) | copy-start | bytes 786436
  24.0 0.9 %copy-start.15 = (bf16[256,512]{1,0:T(8,128)(2,1)S(1)}, bf16[256,512]{1,0:T(8,128)(2,1)}, u32[]{:S(2)}) copy-start(bf16[256,512]{1,0:T(8,128)(2,1)} %copy-done.14) | copy-start | bytes 786436
  24.9 12.2 %copy-start = (bf16[1,16,16,48,128]{4,3,2,1,0:T(8,128)(2,1)S(1)}, bf16[1,16,16,48,128]{4,3,2,1,0:T(8,128)(2,1)}, u32[]{:S(2)}) copy-start(bf16[1,16,16,48,128]{4,3,2,1,0:T(8,128)(2,1)} %param.8) | copy-start | bytes 9437188
  32.4 0.6 copy-start.3
  33.0 11.4 %all-to-all-start.1 = ((bf16[8,8,896]{2,1,0:T(8,128)(2,1)}), bf16[8,8,896]{2,1,0:T(8,128)(2,1)S(1)}, u32[]{:S(2)}, u32[]{:S(2)}) async-start(bf16[8,8,896]{2,1,0:T(8,128)(2,1)} %bitcast.28), calls=%async_computation.1 | async-start | bytes 229376 | tf_op jit(solution)/shard_map/all_to_all | solution.py:781
  44.4 18.6 %copy-start.4 = (bf16[3,3,3,128]{3,2,1,0:T(4,128)(2,1)S(1)}, bf16[3,3,3,128]{3,2,1,0:T(4,128)(2,1)}, u32[]{:S(2)}) copy-start(bf16[3,3,3,128]{3,2,1,0:T(4,128)(2,1)} %weight_ref.1) | copy-start | bytes 20740
  54.1 9.0 %all-to-all-start.3 = ((bf16[4,56,128]{2,1,0:T(8,128)(2,1)}), bf16[4,56,128]{2,1,0:T(8,128)(2,1)S(1)}, u32[]{:S(2)}, u32[]{:S(2)}) async-start(bf16[4,56,128]{2,1,0:T(8,128)(2,1)} %sum_parts.1), calls=%async_computation.3 | async-start | bytes 114688 | tf_op jit(solution)/shard_map/all_to_all | solution.py:803

commit v14 on v13

--- a/solution.py
+++ b/solution.py
@@ -615,7 +615,7 @@
     return total
 
 
-def rec_kernel(inner_ref, feat_ref, part_ref, taps_ref, *, frames, devices, group, cols, block_rows):
+def rec_kernel(after_hbm, inner_ref, feat_ref, part_ref, taps_ref, *, frames, devices, group, cols, block_rows):
     pixels = block_rows * cols
     put_taps(inner_ref[...], taps_ref, frames, cols, pixels // LANES, 32)
     whole = lambda frame: feat_ref[frame * pixels : (frame + 1) * pixels, :]
@@ -787,13 +787,13 @@
     staged = stage_call(disc_first, disc_second, cols)
     arrived, inner = lax.optimization_barrier((arrived, inner))
     sent = disc_call(arrived, staged, disc_third, disc_fourth, disc_head, devices, group, cols, block_rows)
-    sent, held = lax.optimization_barrier((sent, inner))
     returned = trade(sent)
     taps_scratch = pltpu.VMEM((block_rows * cols // LANES, 32 * frames, LANES), F32)
     plane_scratch = pltpu.VMEM((lanes // LANES, devices * pitch, LANES), F32)
     flops = 4 * features.size * 27
     rec_part = taps_call(
-        rec_kernel, [VM, VM], (held, feats), jax.ShapeDtypeStruct((32, channels), F32), [taps_scratch], *sizes, flops, "rec_taps"
+        rec_kernel, [HBM, VM, VM], (sent, inner, feats), jax.ShapeDtypeStruct((32, channels), F32),
+        [taps_scratch], *sizes, flops, "rec_taps",
     )
     part = taps_call(
         both_kernel, [VM, VM, VM], (rec_part, returned, feats),

time: 66.7 us -> 66.7 us (level)
  local copies, waits for them, and re-layouts: 11.8 us -> 11.1 us
    unnamed x36 -> x34, local copies, waits for them, and re-layouts: 10.1 us -> 9.5 us
where the time goes in v14:
time: 66.7 us; the launch traced here: 66 us
  Pallas kernels  21.2 us (32%)
  starting transfers between devices  14.9 us (22%)
  local copies, waits for them, and re-layouts  11.1 us (17%)
  waiting for transfers between devices  10.3 us (15%)
  blocking collectives  7.46 us (11%)
  between operations  0.95 us (1%)
    all_to_all x2, starting transfers between devices, per_device(): lax.all_to_all(values.reshape(devices, pitch, lanes), row, split_axis=0,...  11.5 us
    unnamed x34, local copies, waits for them, and re-layouts  9.5 us
    pallas_call x1, Pallas kernels, disc_call(): pl.pallas_call(functools.partial(disc_kernel, devices=devices, group=grou...  8.07 us
    all_to_all x2, waiting for transfers between devices, per_device(): lax.all_to_all(values.reshape(devices, pitch, lanes), row, split_axis=0,...  7.86 us
    all_to_all x1, blocking collectives, per_device(): lax.all_to_all(values, axes, split_axis=0, concat_axis=0, tiled=True)  7.46 us
    pallas_call x3, Pallas kernels, taps_call(): pl.pallas_call(functools.partial(kernel, frames=frames, devices=devices,...  4.72 us
    pallas_call x1, Pallas kernels, forward_call(): pl.pallas_call(functools.partial(forward_kernel, frames=frames, devices=d...  3.98 us
    all_to_all x1, starting transfers between devices, per_device(): lax.all_to_all(values, axes, split_axis=0, concat_axis=0, tiled=True)  3.46 us
  transfers between devices with their start and end apart: 3, of which 3 were waited for; matrix products, arithmetic and copies ran while one was open for 2% of the time, Pallas kernels for 6%

profile of v14, /device:TPU:0, one launch (start us, length us, event | category | flops | bytes accessed | tf_op | source)
XLA Modules:
  0.0 66.0 jit_solution(2309499662675288447)
XLA Ops:
  0.7 4.0 %forward_taps.1.pay_ref = bf16[64,896]{1,0:T(8,128)(2,1)} custom-call(bf16[12288,128]{1,0:T(8,128)(2,1)} %bitcast.19, bf16[16,3,16,48]{3,2,1,0:T(8,128)(2,1)} %bitcast.25, bf16[3,3,3,128]{3,2,1,0:T(4,128)(2,1)} %weight_ref.1), custom_call_target="tpu_custom_call" | custom-call | flops 84934656 | bytes 3145728 | tf_op jit(solution)/shard_map/forward_taps/pallas_call | solution.py:124
  4.7 7.3 %all-to-all-start = ((bf16[8,8,896]{2,1,0:T(8,128)(2,1)}), bf16[8,8,896]{2,1,0:T(8,128)(2,1)S(1)}, u32[]{:S(2)}, u32[]{:S(2)}) async-start(bf16[8,8,896]{2,1,0:T(8,128)(2,1)} %bitcast.24), calls=%async_computation | async-start | bytes 229376 | tf_op jit(solution)/shard_map/all_to_all | solution.py:781
  12.6 0.9 %copy-done.1 = bf16[64,896]{1,0:T(8,128)(2,1)S(1)} copy-done((bf16[64,896]{1,0:T(8,128)(2,1)S(1)}, bf16[64,896]{1,0:T(8,128)(2,1)}, u32[]{:S(2)}) %copy-start.1) | copy-done | bytes 114712
  14.5 0.7 %copy-done.7 = bf16[144,1024]{1,0:T(8,128)(2,1)} copy-done((bf16[144,1024]{1,0:T(8,128)(2,1)}, bf16[144,1024]{1,0:T(8,128)(2,1)S(1)}, u32[]{:S(2)}) %copy-start.7) | copy-done | bytes 294936
  15.3 0.7 %copy-done.9 = bf16[512,144]{1,0:T(8,128)(2,1)} copy-done((bf16[512,144]{1,0:T(8,128)(2,1)}, bf16[512,144]{1,0:T(8,128)(2,1)S(1)}, u32[]{:S(2)}) %copy-start.9) | copy-done | bytes 147480
  16.0 0.7 %copy-done.11 = bf16[1024,128]{1,0:T(8,128)(2,1)} copy-done((bf16[1024,128]{1,0:T(8,128)(2,1)}, bf16[1024,128]{1,0:T(8,128)(2,1)S(1)}, u32[]{:S(2)}) %copy-start.11) | copy-done | bytes 262168
  16.7 0.7 %copy-done.13 = bf16[256,512]{1,0:T(8,128)(2,1)} copy-done((bf16[256,512]{1,0:T(8,128)(2,1)}, bf16[256,512]{1,0:T(8,128)(2,1)S(1)}, u32[]{:S(2)}) %copy-start.13) | copy-done | bytes 262168
  17.4 1.8 %all-to-all-done = bf16[8,8,896]{2,1,0:T(8,128)(2,1)S(1)} async-done(((bf16[8,8,896]{2,1,0:T(8,128)(2,1)}), bf16[8,8,896]{2,1,0:T(8,128)(2,1)S(1)}, u32[]{:S(2)}, u32[]{:S(2)}) %all-to-all-start) | async-done | bytes 114720 | tf_op jit(solution)/shard_map/all_to_all | solution.py:781
  19.2 0.7 %copy-done.4 = bf16[16,512]{1,0:T(8,128)(2,1)S(1)} copy-done((bf16[16,512]{1,0:T(8,128)(2,1)S(1)}, bf16[16,512]{1,0:T(8,128)(2,1)}, u32[]{:S(2)}) %copy-start.4) | copy-done | bytes 16408
  19.9 1.2 %copy-done.5 = bf16[4,4,128,256]{3,2,1,0:T(8,128)(2,1)S(1)} copy-done((bf16[4,4,128,256]{3,2,1,0:T(8,128)(2,1)S(1)}, bf16[4,4,128,256]{3,2,1,0:T(8,128)(2,1)}, u32[]{:S(2)}) %copy-start.5) | copy-done | bytes 1048600
  21.1 1.0 %copy-done.8 = bf16[144,1024]{1,0:T(8,128)(2,1)S(1)} copy-done((bf16[144,1024]{1,0:T(8,128)(2,1)S(1)}, bf16[144,1024]{1,0:T(8,128)(2,1)}, u32[]{:S(2)}) %copy-start.8) | copy-done | bytes 294936
  22.1 0.9 %copy-done.10 = bf16[512,144]{1,0:T(8,128)(2,1)S(1)} copy-done((bf16[512,144]{1,0:T(8,128)(2,1)S(1)}, bf16[512,144]{1,0:T(8,128)(2,1)}, u32[]{:S(2)}) %copy-start.10) | copy-done | bytes 147480
  23.0 0.9 %copy-done.12 = bf16[1024,128]{1,0:T(8,128)(2,1)S(1)} copy-done((bf16[1024,128]{1,0:T(8,128)(2,1)S(1)}, bf16[1024,128]{1,0:T(8,128)(2,1)}, u32[]{:S(2)}) %copy-start.12) | copy-done | bytes 262168
  24.0 0.9 %copy-done.14 = bf16[256,512]{1,0:T(8,128)(2,1)S(1)} copy-done((bf16[256,512]{1,0:T(8,128)(2,1)S(1)}, bf16[256,512]{1,0:T(8,128)(2,1)}, u32[]{:S(2)}) %copy-start.14) | copy-done | bytes 262168
  24.9 8.1 %disc_rows.1.after_hbm = bf16[64,896]{1,0:T(8,128)(2,1)} custom-call(bf16[64,896]{1,0:T(8,128)(2,1)S(1)} %bitcast.27, bf16[16,512]{1,0:T(8,128)(2,1)S(1)} %copy-done.4, bf16[144,1024]{1,0:T(8,128)(2,1)S(1)} %copy-done.8, bf16[256,512]{1,0:T(8,128)(2,1)S(1)} %copy-done.14, bf16[1024,128]{1,0:T(8,128)(2,1)S(1)} %copy-done.12, bf16[512,144]{1,0:T(8,128)(2,1)S(1)} %copy-done.10, ...), custom_call_target="tpu_custom_call" | custom-call | flops 4000000000 | bytes 8000000 | tf_op jit(solution)/shard_map/disc_rows/pallas_call | solution.py:532
  33.0 4.2 %all-to-all-start.1 = ((bf16[8,8,896]{2,1,0:T(8,128)(2,1)}), bf16[8,8,896]{2,1,0:T(8,128)(2,1)S(1)}, u32[]{:S(2)}, u32[]{:S(2)}) async-start(bf16[8,8,896]{2,1,0:T(8,128)(2,1)} %bitcast.9), calls=%async_computation.1 | async-start | bytes 229376 | tf_op jit(solution)/shard_map/all_to_all | solution.py:781
  37.2 1.2 %rec_taps.1.rec_ref = f32[32,128]{1,0:T(8,128)S(1)} custom-call(bf16[64,896]{1,0:T(8,128)(2,1)} %disc_rows.1.after_hbm, f32[48,896]{1,0:T(8,128)S(1)} %inner_rows.1.inner_ref, bf16[12288,128]{1,0:T(8,128)(2,1)S(1)} %bitcast.20), custom_call_target="tpu_custom_call" | custom-call | flops 169869312 | bytes 4000000 | tf_op jit(solution)/shard_map/rec_taps/pallas_call | solution.py:689
  38.4 6.0 %all-to-all-done.1 = bf16[8,8,896]{2,1,0:T(8,128)(2,1)S(1)} async-done(((bf16[8,8,896]{2,1,0:T(8,128)(2,1)}), bf16[8,8,896]{2,1,0:T(8,128)(2,1)S(1)}, u32[]{:S(2)}, u32[]{:S(2)}) %all-to-all-start.1) | async-done | bytes 114720 | tf_op jit(solution)/shard_map/all_to_all | solution.py:781
  44.5 1.5 %both_taps.1 = bf16[8,56,128]{2,1,0:T(8,128)(2,1)S(1)} custom-call(f32[32,128]{1,0:T(8,128)S(1)} %rec_taps.1.rec_ref, bf16[64,896]{1,0:T(8,128)(2,1)S(1)} %bitcast.22, bf16[12288,128]{1,0:T(8,128)(2,1)S(1)} %bitcast.21), custom_call_target="tpu_custom_call" | custom-call | flops 169869312 | bytes 4000000 | tf_op jit(solution)/shard_map/both_taps/pallas_call | solution.py:689
  46.0 7.5 %all_to_all.20.parts_ref = bf16[8,56,128]{2,1,0:T(8,128)(2,1)S(1)} all-to-all(bf16[8,56,128]{2,1,0:T(8,128)(2,1)S(1)} %both_taps.1), channel_id=1, replica_groups=mesh['clip'=4,'far'=4,'near'=2] {'clip','near'}, dimensions={0} | all-to-all | bytes 229376 | tf_op jit(solution)/shard_map/all_to_all | solution.py:803
  54.1 3.5 %all-to-all-start.3 = ((bf16[4,56,128]{2,1,0:T(8,128)(2,1)}), bf16[4,56,128]{2,1,0:T(8,128)(2,1)S(1)}, u32[]{:S(2)}, u32[]{:S(2)}) async-start(bf16[4,56,128]{2,1,0:T(8,128)(2,1)} %sum_parts.1), calls=%async_computation.3 | async-start | bytes 114688 | tf_op jit(solution)/shard_map/all_to_all | solution.py:803
  58.6 2.0 %turn_taps.1.taps_ref = bf16[6144,128]{1,0:T(8,128)(2,1)S(1)} custom-call(f32[48,896]{1,0:T(8,128)S(1)} %inner_rows.1.inner_ref, bf16[64,896]{1,0:T(8,128)(2,1)S(1)} %bitcast.23), custom_call_target="tpu_custom_call" | custom-call | flops 169869312 | bytes 4000000 | tf_op jit(solution)/shard_map/turn_taps/pallas_call | solution.py:689
  60.6 2.5 %all-to-all-done.3.sums_ref = bf16[4,56,128]{2,1,0:T(8,128)(2,1)S(1)} async-done(((bf16[4,56,128]{2,1,0:T(8,128)(2,1)}), bf16[4,56,128]{2,1,0:T(8,128)(2,1)S(1)}, u32[]{:S(2)}, u32[]{:S(2)}) %all-to-all-start.3) | async-done | bytes 57376 | tf_op jit(solution)/shard_map/all_to_all | solution.py:803
  63.1 2.8 %feature_pull.1 = (bf16[12288,128]{1,0:T(8,128)(2,1)}, f32[3,3,3,128]{3,2,1,0:T(4,128)}, f32[1,1]{1,0:T(1,128)}) custom-call(bf16[6144,128]{1,0:T(8,128)(2,1)S(1)} %turn_taps.1.taps_ref, bf16[4,56,128]{2,1,0:T(8,128)(2,1)S(1)} %all-to-all-done.3.sums_ref, bf16[3,3,3,128]{3,2,1,0:T(4,128)(2,1)S(1)} %copy-done.3), custom_call_target="tpu_custom_call" | custom-call | flops 201326592 | bytes 6291456 | tf_op jit(solution)/shard_map/feature_pull/pallas_call | solution.py:745
  (32 shorter events, 3.3 us)
Async XLA Ops:
  0.6 12.0 %copy-start.2 = (bf16[1,16,16,3,48]{4,2,3,1,0:T(8,128)(2,1)S(1)}, bf16[1,16,16,3,48]{4,2,3,1,0:T(8,128)(2,1)}, u32[]{:S(2)}) copy-start(bf16[1,16,16,3,48]{4,2,3,1,0:T(8,128)(2,1)} %param.9) | copy-start | bytes 221188
  0.6 11.3 %copy-start.16 = (bf16[4,4,3,64]{3,1,2,0:T(4,128)(2,1)S(1)}, bf16[4,4,3,64]{3,1,2,0:T(4,128)(2,1)}, u32[]{:S(2)}) copy-start(bf16[4,4,3,64]{3,1,2,0:T(4,128)(2,1)} %param.11) | copy-start | bytes 18436
  0.7 11.3 %copy-start.15 = (bf16[4,4,512,1]{2,1,3,0:T(4,128)(2,1)S(1)}, bf16[4,4,512,1]{2,1,3,0:T(4,128)(2,1)}, u32[]{:S(2)}) copy-start(bf16[4,4,512,1]{2,1,3,0:T(4,128)(2,1)} %param.15) | copy-start | bytes 49156
  0.7 13.2 %copy-start.6 = (bf16[4,4,64,128]{3,2,1,0:T(8,128)(2,1)S(1)}, bf16[4,4,64,128]{3,2,1,0:T(8,128)(2,1)}, u32[]{:S(2)}) copy-start(bf16[4,4,64,128]{3,2,1,0:T(8,128)(2,1)} %param.12) | copy-start | bytes 786436
  4.7 14.5 %all-to-all-start = ((bf16[8,8,896]{2,1,0:T(8,128)(2,1)}), bf16[8,8,896]{2,1,0:T(8,128)(2,1)S(1)}, u32[]{:S(2)}, u32[]{:S(2)}) async-start(bf16[8,8,896]{2,1,0:T(8,128)(2,1)} %bitcast.24), calls=%async_computation | async-start | bytes 229376 | tf_op jit(solution)/shard_map/all_to_all | solution.py:781
  12.6 0.9 %copy-start.1 = (bf16[64,896]{1,0:T(8,128)(2,1)S(1)}, bf16[64,896]{1,0:T(8,128)(2,1)}, u32[]{:S(2)}) copy-start(bf16[64,896]{1,0:T(8,128)(2,1)} %forward_taps.1.pay_ref) | copy-start | bytes 344068
  14.5 0.7 %copy-start.7 = (bf16[144,1024]{1,0:T(8,128)(2,1)}, bf16[144,1024]{1,0:T(8,128)(2,1)S(1)}, u32[]{:S(2)}) copy-start(bf16[144,1024]{1,0:T(8,128)(2,1)S(1)} %get-tuple-element.17.window) | copy-start | bytes 884740
  15.2 0.7 %copy-start.9 = (bf16[512,144]{1,0:T(8,128)(2,1)}, bf16[512,144]{1,0:T(8,128)(2,1)S(1)}, u32[]{:S(2)}) copy-start(bf16[512,144]{1,0:T(8,128)(2,1)S(1)} %get-tuple-element.20.unwindow) | copy-start | bytes 442372
  16.0 0.7 %copy-start.11 = (bf16[1024,128]{1,0:T(8,128)(2,1)}, bf16[1024,128]{1,0:T(8,128)(2,1)S(1)}, u32[]{:S(2)}) copy-start(bf16[1024,128]{1,0:T(8,128)(2,1)S(1)} %get-tuple-element.19.second) | copy-start | bytes 786436
  16.7 0.7 %copy-start.13 = (bf16[256,512]{1,0:T(8,128)(2,1)}, bf16[256,512]{1,0:T(8,128)(2,1)S(1)}, u32[]{:S(2)}) copy-start(bf16[256,512]{1,0:T(8,128)(2,1)S(1)} %get-tuple-element.18.band_ref) | copy-start | bytes 786436
  19.2 0.7 %copy-start.4 = (bf16[16,512]{1,0:T(8,128)(2,1)S(1)}, bf16[16,512]{1,0:T(8,128)(2,1)}, u32[]{:S(2)}) copy-start(bf16[16,512]{1,0:T(8,128)(2,1)} %reshape.47.head_ref) | copy-start | bytes 49156
  19.9 1.2 %copy-start.5 = (bf16[4,4,128,256]{3,2,1,0:T(8,128)(2,1)S(1)}, bf16[4,4,128,256]{3,2,1,0:T(8,128)(2,1)}, u32[]{:S(2)}) copy-start(bf16[4,4,128,256]{3,2,1,0:T(8,128)(2,1)} %param.13) | copy-start | bytes 3145732
  21.1 1.0 %copy-start.8 = (bf16[144,1024]{1,0:T(8,128)(2,1)S(1)}, bf16[144,1024]{1,0:T(8,128)(2,1)}, u32[]{:S(2)}) copy-start(bf16[144,1024]{1,0:T(8,128)(2,1)} %copy-done.7) | copy-start | bytes 884740
  22.1 0.9 %copy-start.10 = (bf16[512,144]{1,0:T(8,128)(2,1)S(1)}, bf16[512,144]{1,0:T(8,128)(2,1)}, u32[]{:S(2)}) copy-start(bf16[512,144]{1,0:T(8,128)(2,1)} %copy-done.9) | copy-start | bytes 442372
  23.0 0.9 %copy-start.12 = (bf16[1024,128]{1,0:T(8,128)(2,1)S(1)}, bf16[1024,128]{1,0:T(8,128)(2,1)}, u32[]{:S(2)}) copy-start(bf16[1024,128]{1,0:T(8,128)(2,1)} %copy-done.11) | copy-start | bytes 786436
  24.0 0.9 %copy-start.14 = (bf16[256,512]{1,0:T(8,128)(2,1)S(1)}, bf16[256,512]{1,0:T(8,128)(2,1)}, u32[]{:S(2)}) copy-start(bf16[256,512]{1,0:T(8,128)(2,1)} %copy-done.13) | copy-start | bytes 786436
  24.9 12.3 %copy-start = (bf16[1,16,16,48,128]{4,3,2,1,0:T(8,128)(2,1)S(1)}, bf16[1,16,16,48,128]{4,3,2,1,0:T(8,128)(2,1)}, u32[]{:S(2)}) copy-start(bf16[1,16,16,48,128]{4,3,2,1,0:T(8,128)(2,1)} %param.8) | copy-start | bytes 9437188
  33.0 11.4 %all-to-all-start.1 = ((bf16[8,8,896]{2,1,0:T(8,128)(2,1)}), bf16[8,8,896]{2,1,0:T(8,128)(2,1)S(1)}, u32[]{:S(2)}, u32[]{:S(2)}) async-start(bf16[8,8,896]{2,1,0:T(8,128)(2,1)} %bitcast.9), calls=%async_computation.1 | async-start | bytes 229376 | tf_op jit(solution)/shard_map/all_to_all | solution.py:781
  44.5 18.6 %copy-start.3 = (bf16[3,3,3,128]{3,2,1,0:T(4,128)(2,1)S(1)}, bf16[3,3,3,128]{3,2,1,0:T(4,128)(2,1)}, u32[]{:S(2)}) copy-start(bf16[3,3,3,128]{3,2,1,0:T(4,128)(2,1)} %weight_ref.1) | copy-start | bytes 20740
  54.1 9.0 %all-to-all-start.3 = ((bf16[4,56,128]{2,1,0:T(8,128)(2,1)}), bf16[4,56,128]{2,1,0:T(8,128)(2,1)S(1)}, u32[]{:S(2)}, u32[]{:S(2)}) async-start(bf16[4,56,128]{2,1,0:T(8,128)(2,1)} %sum_parts.1), calls=%async_computation.3 | async-start | bytes 114688 | tf_op jit(solution)/shard_map/all_to_all | solution.py:803

commit v15 on v10

--- a/solution.py
+++ b/solution.py
@@ -759,11 +759,11 @@
     flops = 4 * features.size * 27
     part = taps_call(
         both_kernel, [VM, VM, VM], (inner, returned, feats),
-        jax.ShapeDtypeStruct((clips * lax.axis_size("near"), 56, channels), BF16),
+        jax.ShapeDtypeStruct((lax.axis_size("far"), 56, channels), BF16),
         [taps_scratch, taps_scratch, plane_scratch], *sizes, flops, "both_taps",
     )
     share = lambda values, axes: lax.all_to_all(values, axes, split_axis=0, concat_axis=0, tiled=True)
-    sums = share(sum_call(share(part, ("clip", "near")), lax.axis_size("far")), "far")
+    sums = share(sum_call(share(part, "far"), clips * lax.axis_size("near")), ("clip", "near"))
     taps = taps_call(
         turn_kernel, [VM, VM], (inner, returned), jax.ShapeDtypeStruct((feats.shape[0] // 2, LANES), BF16),
         [taps_scratch, taps_scratch, plane_scratch], *sizes, flops, "turn_taps",

time: 59.2 us -> 59 us (level)
  waiting for transfers between devices: 7.71 us -> 6.84 us
  blocking collectives: 17.1 us -> 17.7 us
    all_to_all x1, waiting for transfers between devices: 2.47 us -> 1.6 us  [per_device(): lax.all_to_all(values, axes, split_axis=0, concat_axis=0, tiled=True)]
    all_to_all x1, blocking collectives: 7.44 us -> 8.08 us  [per_device(): lax.all_to_all(values, axes, split_axis=0, concat_axis=0, tiled=True)]
where the time goes in v15:
time: 59 us; the launch traced here: 58.6 us
  Pallas kernels  20.3 us (34%)
  blocking collectives  17.7 us (30%)
  starting transfers between devices  10.8 us (18%)
  waiting for transfers between devices  6.84 us (12%)
  local copies, waits for them, and re-layouts  1.97 us (3%)
  between operations  0.95 us (2%)
    all_to_all x1, blocking collectives, per_device(): lax.all_to_all(values.reshape(devices, pitch, lanes), row, split_axis=0,...  9.62 us
    all_to_all x1, blocking collectives, per_device(): lax.all_to_all(values, axes, split_axis=0, concat_axis=0, tiled=True)  8.08 us
    pallas_call x1, Pallas kernels, disc_call(): pl.pallas_call(functools.partial(disc_kernel, devices=devices, group=grou...  7.42 us
    all_to_all x1, starting transfers between devices, per_device(): lax.all_to_all(values.reshape(devices, pitch, lanes), row, split_axis=0,...  7.29 us
    all_to_all x1, waiting for transfers between devices, per_device(): lax.all_to_all(values.reshape(devices, pitch, lanes), row, split_axis=0,...  5.24 us
    pallas_call x2, Pallas kernels, taps_call(): pl.pallas_call(functools.partial(kernel, frames=frames, devices=devices,...  4.27 us
    pallas_call x1, Pallas kernels, forward_call(): pl.pallas_call(functools.partial(forward_kernel, frames=frames, devices=d...  4.13 us
    all_to_all x1, starting transfers between devices, per_device(): lax.all_to_all(values, axes, split_axis=0, concat_axis=0, tiled=True)  3.55 us
  transfers between devices with their start and end apart: 2, of which 2 were waited for; matrix products, arithmetic and copies ran while one was open for 2% of the time, Pallas kernels for 5%

profile of v15, /device:TPU:0, one launch (start us, length us, event | category | flops | bytes accessed | tf_op | source)
XLA Modules:
  0.0 58.6 jit_solution(3403188762736462082)
XLA Ops:
  0.6 0.0 copy-start.2
  0.6 0.0 copy-start.7
  0.7 0.0 copy-start.6
  0.7 4.1 %forward_taps.1.pay_ref = bf16[64,896]{1,0:T(8,128)(2,1)} custom-call(bf16[12288,128]{1,0:T(8,128)(2,1)} %bitcast.19, bf16[16,3,16,48]{3,2,1,0:T(8,128)(2,1)} %bitcast.24, bf16[3,3,3,128]{3,2,1,0:T(4,128)(2,1)} %weight_ref.1), custom_call_target="tpu_custom_call" | custom-call | flops 84934656 | bytes 3145728 | tf_op jit(solution)/shard_map/forward_taps/pallas_call | solution.py:121
  4.8 7.3 %all-to-all-start = ((bf16[8,8,896]{2,1,0:T(8,128)(2,1)}), bf16[8,8,896]{2,1,0:T(8,128)(2,1)S(1)}, u32[]{:S(2)}, u32[]{:S(2)}) async-start(bf16[8,8,896]{2,1,0:T(8,128)(2,1)} %bitcast.23), calls=%async_computation | async-start | bytes 229376 | tf_op jit(solution)/shard_map/all_to_all | solution.py:747
  12.1 0.0 copy-done.7
  12.2 0.0 copy-start.1
  12.2 0.9 %copy-done.1 = bf16[64,896]{1,0:T(8,128)(2,1)S(1)} copy-done((bf16[64,896]{1,0:T(8,128)(2,1)S(1)}, bf16[64,896]{1,0:T(8,128)(2,1)}, u32[]{:S(2)}) %copy-start.1) | copy-done | bytes 114712
  13.1 0.3 inner_rows.1.inner_ref
  13.4 0.7 %stage_weights.1 = (bf16[144,1024]{1,0:T(8,128)(2,1)S(1)}, bf16[512,144]{1,0:T(8,128)(2,1)S(1)}, bf16[1024,128]{1,0:T(8,128)(2,1)S(1)}, bf16[256,512]{1,0:T(8,128)(2,1)S(1)}) custom-call(bf16[4,4,3,64]{3,2,1,0:T(4,128)(2,1)S(1)} %copy.21.first_ref, bf16[1024,128]{1,0:T(8,128)(2,1)S(1)} %bitcast.29), custom_call_target="tpu_custom_call" | custom-call | flops 100000000 | bytes 4000000 | tf_op jit(solution)/shard_map/stage_weights/pallas_call | solution.py:498
  14.1 5.2 %all-to-all-done = bf16[8,8,896]{2,1,0:T(8,128)(2,1)S(1)} async-done(((bf16[8,8,896]{2,1,0:T(8,128)(2,1)}), bf16[8,8,896]{2,1,0:T(8,128)(2,1)S(1)}, u32[]{:S(2)}, u32[]{:S(2)}) %all-to-all-start) | async-done | bytes 114720 | tf_op jit(solution)/shard_map/all_to_all | solution.py:747
  19.3 0.0 copy-done.4
  19.4 7.4 %disc_rows.1 = bf16[64,896]{1,0:T(8,128)(2,1)S(1)} custom-call(bf16[64,896]{1,0:T(8,128)(2,1)S(1)} %bitcast.26, bf16[16,512]{1,0:T(8,128)(2,1)S(1)} %reshape.47.head_ref, bf16[144,1024]{1,0:T(8,128)(2,1)S(1)} %get-tuple-element.17.window, bf16[256,512]{1,0:T(8,128)(2,1)S(1)} %get-tuple-element.18.band_ref, bf16[1024,128]{1,0:T(8,128)(2,1)S(1)} %get-tuple-element.19.second, ...), custom_call_target="tpu_custom_call" | custom-call | flops 4000000000 | bytes 8000000 | tf_op jit(solution)/shard_map/disc_rows/pallas_call | solution.py:529
  26.8 9.6 %all_to_all.20 = bf16[8,8,896]{2,1,0:T(8,128)(2,1)S(1)} all-to-all(bf16[8,8,896]{2,1,0:T(8,128)(2,1)S(1)} %bitcast.27), channel_id=1, replica_groups=mesh['clip'=4,'far'=4,'near'=2] {'far','near'}, dimensions={0} | all-to-all | bytes 229376 | tf_op jit(solution)/shard_map/all_to_all | solution.py:747
  36.4 2.3 %both_taps.1 = bf16[4,56,128]{2,1,0:T(8,128)(2,1)S(1)} custom-call(f32[48,896]{1,0:T(8,128)S(1)} %inner_rows.1.inner_ref, bf16[64,896]{1,0:T(8,128)(2,1)S(1)} %bitcast.21, bf16[12288,128]{1,0:T(8,128)(2,1)S(1)} %bitcast.20), custom_call_target="tpu_custom_call" | custom-call | flops 169869312 | bytes 4000000 | tf_op jit(solution)/shard_map/both_taps/pallas_call | solution.py:655
  38.7 8.1 %all_to_all.21.parts_ref = bf16[4,56,128]{2,1,0:T(8,128)(2,1)S(1)} all-to-all(bf16[4,56,128]{2,1,0:T(8,128)(2,1)S(1)} %both_taps.1), channel_id=1, replica_groups=mesh['clip'=4,'far'=4,'near'=2] {'far'}, dimensions={0} | all-to-all | bytes 114688 | tf_op jit(solution)/shard_map/all_to_all | solution.py:765
  46.8 0.7 %sum_parts.1 = bf16[8,56,128]{2,1,0:T(8,128)(2,1)} custom-call(bf16[4,56,128]{2,1,0:T(8,128)(2,1)S(1)} %all_to_all.21.parts_ref), custom_call_target="tpu_custom_call" | custom-call | tf_op jit(solution)/shard_map/sum_parts/pallas_call | solution.py:788
  47.4 3.5 %all-to-all-start.3 = ((bf16[8,56,128]{2,1,0:T(8,128)(2,1)}), bf16[8,56,128]{2,1,0:T(8,128)(2,1)S(1)}, u32[]{:S(2)}, u32[]{:S(2)}) async-start(bf16[8,56,128]{2,1,0:T(8,128)(2,1)} %sum_parts.1), calls=%async_computation.3 | async-start | bytes 229376 | tf_op jit(solution)/shard_map/all_to_all | solution.py:765
  51.0 0.1 slice.4
  51.1 0.2 reshape.54
  51.3 0.7 %copy.23 = bf16[8,2,16,3,48]{4,2,3,1,0:T(8,128)(2,1)} copy(bf16[8,2,16,3,48]{4,2,0,1,3:T(8,128)(2,1)S(1)} %bitcast.30) | data formatting | bytes 147456 | tf_op jit(solution)/shard_map/transpose | solution.py:772
  52.0 2.0 %turn_taps.1.taps_ref = bf16[6144,128]{1,0:T(8,128)(2,1)S(1)} custom-call(f32[48,896]{1,0:T(8,128)S(1)} %inner_rows.1.inner_ref, bf16[64,896]{1,0:T(8,128)(2,1)S(1)} %bitcast.22), custom_call_target="tpu_custom_call" | custom-call | flops 169869312 | bytes 4000000 | tf_op jit(solution)/shard_map/turn_taps/pallas_call | solution.py:655
  54.0 1.6 %all-to-all-done.3.sums_ref = bf16[8,56,128]{2,1,0:T(8,128)(2,1)S(1)} async-done(((bf16[8,56,128]{2,1,0:T(8,128)(2,1)}), bf16[8,56,128]{2,1,0:T(8,128)(2,1)S(1)}, u32[]{:S(2)}, u32[]{:S(2)}) %all-to-all-start.3) | async-done | bytes 114720 | tf_op jit(solution)/shard_map/all_to_all | solution.py:765
  55.6 2.8 %feature_pull.1 = (bf16[12288,128]{1,0:T(8,128)(2,1)}, f32[3,3,3,128]{3,2,1,0:T(4,128)}, f32[1,1]{1,0:T(1,128)}) custom-call(bf16[6144,128]{1,0:T(8,128)(2,1)S(1)} %turn_taps.1.taps_ref, bf16[8,56,128]{2,1,0:T(8,128)(2,1)S(1)} %all-to-all-done.3.sums_ref, bf16[3,3,3,128]{3,2,1,0:T(4,128)(2,1)S(1)} %copy-done.3), custom_call_target="tpu_custom_call" | custom-call | flops 201326592 | bytes 6291456 | tf_op jit(solution)/shard_map/feature_pull/pallas_call | solution.py:711
  (12 shorter events, 0.1 us)
Async XLA Ops:
  0.6 11.5 %copy-start.2 = (bf16[1,16,16,3,48]{4,2,3,1,0:T(8,128)(2,1)S(1)}, bf16[1,16,16,3,48]{4,2,3,1,0:T(8,128)(2,1)}, u32[]{:S(2)}) copy-start(bf16[1,16,16,3,48]{4,2,3,1,0:T(8,128)(2,1)} %param.9) | copy-start | bytes 221188
  0.6 11.5 %copy-start.7 = (bf16[4,4,3,64]{3,1,2,0:T(4,128)(2,1)S(1)}, bf16[4,4,3,64]{3,1,2,0:T(4,128)(2,1)}, u32[]{:S(2)}) copy-start(bf16[4,4,3,64]{3,1,2,0:T(4,128)(2,1)} %param.11) | copy-start | bytes 18436
  0.7 11.5 %copy-start.6 = (bf16[4,4,512,1]{2,1,3,0:T(4,128)(2,1)S(1)}, bf16[4,4,512,1]{2,1,3,0:T(4,128)(2,1)}, u32[]{:S(2)}) copy-start(bf16[4,4,512,1]{2,1,3,0:T(4,128)(2,1)} %param.15) | copy-start | bytes 49156
  0.7 12.7 %copy-start.5 = (bf16[4,4,64,128]{3,2,1,0:T(8,128)(2,1)S(1)}, bf16[4,4,64,128]{3,2,1,0:T(8,128)(2,1)}, u32[]{:S(2)}) copy-start(bf16[4,4,64,128]{3,2,1,0:T(8,128)(2,1)} %param.12) | copy-start | bytes 786436
  0.7 18.7 %copy-start.4 = (bf16[4,4,128,256]{3,2,1,0:T(8,128)(2,1)S(1)}, bf16[4,4,128,256]{3,2,1,0:T(8,128)(2,1)}, u32[]{:S(2)}) copy-start(bf16[4,4,128,256]{3,2,1,0:T(8,128)(2,1)} %param.13) | copy-start | bytes 3145732
  4.8 14.5 %all-to-all-start = ((bf16[8,8,896]{2,1,0:T(8,128)(2,1)}), bf16[8,8,896]{2,1,0:T(8,128)(2,1)S(1)}, u32[]{:S(2)}, u32[]{:S(2)}) async-start(bf16[8,8,896]{2,1,0:T(8,128)(2,1)} %bitcast.23), calls=%async_computation | async-start | bytes 229376 | tf_op jit(solution)/shard_map/all_to_all | solution.py:747
  12.2 0.9 %copy-start.1 = (bf16[64,896]{1,0:T(8,128)(2,1)S(1)}, bf16[64,896]{1,0:T(8,128)(2,1)}, u32[]{:S(2)}) copy-start(bf16[64,896]{1,0:T(8,128)(2,1)} %forward_taps.1.pay_ref) | copy-start | bytes 344068
  19.3 17.1 %copy-start = (bf16[1,16,16,48,128]{4,3,2,1,0:T(8,128)(2,1)S(1)}, bf16[1,16,16,48,128]{4,3,2,1,0:T(8,128)(2,1)}, u32[]{:S(2)}) copy-start(bf16[1,16,16,48,128]{4,3,2,1,0:T(8,128)(2,1)} %param.8) | copy-start | bytes 9437188
  36.4 19.2 %copy-start.3 = (bf16[3,3,3,128]{3,2,1,0:T(4,128)(2,1)S(1)}, bf16[3,3,3,128]{3,2,1,0:T(4,128)(2,1)}, u32[]{:S(2)}) copy-start(bf16[3,3,3,128]{3,2,1,0:T(4,128)(2,1)} %weight_ref.1) | copy-start | bytes 20740
  47.4 8.2 %all-to-all-start.3 = ((bf16[8,56,128]{2,1,0:T(8,128)(2,1)}), bf16[8,56,128]{2,1,0:T(8,128)(2,1)S(1)}, u32[]{:S(2)}, u32[]{:S(2)}) async-start(bf16[8,56,128]{2,1,0:T(8,128)(2,1)} %sum_parts.1), calls=%async_computation.3 | async-start | bytes 229376 | tf_op jit(solution)/shard_map/all_to_all | solution.py:765
